TPU v7x, 32 devices: a whole 2x2x4 slice. The times are simulated.
32 devices in a mesh: seq: 8 (over y, x, core), tp: 4 (over z).
Axes of the slice: x: 2, y: 2, z: 4, core: 2. Of those that a mesh axis runs over, the one named last changes fastest.
Arguments:
- tokens: bfloat16 [4, 4096, 1024], P(None, 'seq'), may hold values from -6 to 6
- lengths: int32 [4], replicated, may hold values from 1024 to 4096, as said below
- attention_norm_gain: float32 [1024], replicated, may hold values from 0.5 to 1.5
- query_weight: bfloat16 [1024, 1024], P(None, 'tp'), may hold values from -0.1875 to 0.1875
- key_weight: bfloat16 [1024, 1024], P(None, 'tp'), may hold values from -0.1875 to 0.1875
- value_weight: bfloat16 [1024, 1024], P(None, 'tp'), may hold values from -0.1875 to 0.1875
- output_weight: bfloat16 [1024, 1024], P('tp'), may hold values from -0.75 to 0.75
- state_key_weight: bfloat16 [1024, 1024], P(None, 'tp'), may hold values from -0.1875 to 0.1875
- state_value_weight: bfloat16 [1024, 1024], P(None, 'tp'), may hold values from -0.1875 to 0.1875
- state_coefficient: float32 [1024, 16], P(('seq', 'tp')), may hold values from -0.06 to 0.06
- state_rate: float32 [1024, 16], P(('seq', 'tp')), may hold values from 0.0002 to 0.03
- feedforward_norm_gain: float32 [1024], replicated, may hold values from 0.5 to 1.5
- hidden_weight: bfloat16 [1024, 4096], P(None, 'tp'), may hold values from -0.1875 to 0.1875
- return_weight: bfloat16 [4096, 1024], P('tp'), may hold values from -0.09375 to 0.09375
- cotangent: bfloat16 [4, 4096, 1024], P(None, 'seq'), may hold values from -6 to 6
Outputs:
- output: bfloat16 [4, 4096, 1024], P(None, 'seq')
- grad_tokens: float32 [4, 4096, 1024], P(None, 'seq')
- grad_attn_gain: float32 [1024], replicated
- grad_query_weight: float32 [1024, 1024], P(None, 'tp')
- grad_key_weight: float32 [1024, 1024], P(None, 'tp')
- grad_value_weight: float32 [1024, 1024], P(None, 'tp')
- grad_output_weight: float32 [1024, 1024], P('tp')
- grad_state_key_weight: float32 [1024, 1024], P(None, 'tp')
- grad_state_value_weight: float32 [1024, 1024], P(None, 'tp')
- grad_state_coefficient: float32 [1024, 16], P(('seq', 'tp'))
- grad_state_rate: float32 [1024, 16], P(('seq', 'tp'))
- grad_mlp_gain: float32 [1024], replicated
- grad_hidden_weight: float32 [1024, 4096], P(None, 'tp')
- grad_return_weight: float32 [4096, 1024], P('tp')
Inputs may be any that keep to these rules, and one draw needn't show every extreme that they name: `lengths`: valid length of each sequence; one of the 4 sequences, which one drawn from the seed, has the full length 4096; positions at or past a length are padding.
All inputs are finite; a program needn't handle non-finite values.
Results may differ from a plain program's by a relative error of at most 0.023.
Values may be sent and summed in bfloat16 or wider, within the bound.
No kernel may reach another device: no remote copies, remote signals or barrier semaphores. Data moves between devices by JAX's collectives and lax.ppermute only.
A program may use at most 256 MiB of HBM per device.

v0:
```python
from functools import partial
import math

import jax
import jax.numpy as jnp
from jax import lax
from jax.sharding import PartitionSpec as P

DH = 128
CTX = 128


EPS = 1e-05
NEGATIVE = -1e30
HIGH_ACCURACY = lax.Precision.HIGHEST


def shifted(value, axis, steps):
    count = lax.axis_size(axis)
    first, last = (max(0, -steps), min(count, count - steps))
    return lax.ppermute(value, axis, [(source, source + steps) for source in range(first, last)])


def normalize(values):
    center = values - jnp.mean(values, axis=-1, keepdims=True)
    inverse = lax.rsqrt(jnp.mean(center * center, axis=-1, keepdims=True) + EPS)
    return (center * inverse, inverse)


def norm_back(normed, inverse, grad_normed):
    mean_grad = jnp.mean(grad_normed, axis=-1, keepdims=True)
    mean_cross = jnp.mean(grad_normed * normed, axis=-1, keepdims=True)
    return inverse * (grad_normed - mean_grad - normed * mean_cross)


def kernel_rows(kernel_coefficient, kernel_decay_rate, seq_len):
    offsets = jnp.arange(seq_len).astype(jnp.float32)
    return jnp.einsum(
        "cn,cnk->ck",
        kernel_coefficient,
        jnp.exp(-kernel_decay_rate[:, :, None] * offsets),
        precision=HIGH_ACCURACY,
    )


def dot_high(matrix, table):
    return jnp.matmul(matrix, table, precision=HIGH_ACCURACY)


def dft_table(count, sign):
    index = jnp.arange(count)
    phase = (index[:, None] * index[None, :] % count).astype(jnp.float32) * (2.0 * math.pi / count)
    return (jnp.cos(phase), sign * jnp.sin(phase))


def twiddle(outer_len, inner_len, sign):
    product = (jnp.arange(outer_len)[:, None] * jnp.arange(inner_len)[None, :]).astype(jnp.float32)
    phase = product * (2.0 * math.pi / (outer_len * inner_len))
    return (jnp.cos(phase), sign * jnp.sin(phase))


def transform_forward(signal, outer_len, inner_len):
    grid = signal.reshape(signal.shape[:-1] + (outer_len, inner_len))
    cos_outer, sin_outer = dft_table(outer_len, -1.0)
    real_a = jnp.einsum("kt,...tj->...kj", cos_outer, grid, precision=HIGH_ACCURACY)
    imag_a = jnp.einsum("kt,...tj->...kj", sin_outer, grid, precision=HIGH_ACCURACY)
    cos_turn, sin_turn = twiddle(outer_len, inner_len, -1.0)
    real_b = real_a * cos_turn - imag_a * sin_turn
    imag_b = real_a * sin_turn + imag_a * cos_turn
    cos_inner, sin_inner = dft_table(inner_len, -1.0)
    real_c = dot_high(real_b, cos_inner) - dot_high(imag_b, sin_inner)
    imag_c = dot_high(real_b, sin_inner) + dot_high(imag_b, cos_inner)
    return (real_c, imag_c)


def transform_inverse(real_in, imag_in, outer_len, inner_len):
    cos_inner, sin_inner = dft_table(inner_len, 1.0)
    real_a = dot_high(real_in, cos_inner) - dot_high(imag_in, sin_inner)
    imag_a = dot_high(real_in, sin_inner) + dot_high(imag_in, cos_inner)
    cos_turn, sin_turn = twiddle(outer_len, inner_len, 1.0)
    real_b = real_a * cos_turn - imag_a * sin_turn
    imag_b = real_a * sin_turn + imag_a * cos_turn
    cos_outer, sin_outer = dft_table(outer_len, 1.0)
    joined = jnp.einsum("tk,...kj->...tj", cos_outer, real_b, precision=HIGH_ACCURACY) - jnp.einsum(
        "tk,...kj->...tj", sin_outer, imag_b, precision=HIGH_ACCURACY
    )
    return joined.reshape(joined.shape[:-2] + (outer_len * inner_len,)) / (outer_len * inner_len)


def to_channels(values):
    return lax.all_to_all(values, "seq", split_axis=1, concat_axis=2, tiled=True)


def to_positions(values):
    return lax.all_to_all(values, "seq", split_axis=2, concat_axis=1, tiled=True)


def tp_total(values):
    return lax.psum(values.astype(jnp.bfloat16), "tp").astype(jnp.float32)


def body(
    tokens,
    lengths,
    attention_norm_gain,
    query_weight,
    key_weight,
    value_weight,
    output_weight,
    state_key_weight,
    state_value_weight,
    state_coefficient,
    state_rate,
    feedforward_norm_gain,
    hidden_weight,
    return_weight,
    cotangent,
):
    sequences, block_len, features = tokens.shape
    seq_count = lax.axis_size("seq")
    tp_count = lax.axis_size("tp")
    seq_index = lax.axis_index("seq")
    tp_index = lax.axis_index("tp")
    channels = features // (seq_count * tp_count)
    full_len = block_len * seq_count
    padded_len = 2 * full_len
    inner_len = math.gcd(padded_len, 128)
    outer_len = padded_len // inner_len
    local_heads = query_weight.shape[1] // DH
    score_scale = DH ** (-0.5)
    share = block_len // tp_count
    positions = seq_index * block_len + jnp.arange(block_len)
    valid = (positions[None, :] < lengths[:, None]).astype(jnp.float32)[:, :, None]
    inputs = tokens.astype(jnp.float32)
    normed_in, inverse_in = normalize(inputs)
    attn_input = (normed_in * attention_norm_gain).astype(jnp.bfloat16)
    masked = (attn_input.astype(jnp.float32) * valid).astype(jnp.bfloat16)
    split_view = masked.reshape(sequences, block_len, seq_count, tp_count, channels)
    own_slice = lax.dynamic_index_in_dim(split_view, tp_index, 3, keepdims=False)
    own_slice = jnp.transpose(
        own_slice.reshape(sequences, block_len, seq_count * channels), (0, 2, 1)
    )
    along = to_channels(own_slice)
    spread = ((0, 0), (0, 0), (0, full_len))
    in_real, in_imag = transform_forward(
        jnp.pad(along.astype(jnp.float32), spread), outer_len, inner_len
    )
    kernel, kernel_back = jax.vjp(
        partial(kernel_rows, seq_len=full_len), state_coefficient, state_rate
    )
    ker_real, ker_imag = transform_forward(
        jnp.pad(kernel, ((0, 0), (0, full_len))), outer_len, inner_len
    )
    convolved = transform_inverse(
        in_real * ker_real - in_imag * ker_imag,
        in_real * ker_imag + in_imag * ker_real,
        outer_len,
        inner_len,
    )[:, :, :full_len]
    outgoing = convolved.astype(jnp.bfloat16)
    returned = to_positions(outgoing)
    context_part = shifted(returned[:, :, block_len - CTX :], "seq", 1)
    gathered = lax.all_gather(context_part, "tp", axis=1, tiled=True)
    context_carry = jnp.transpose(
        gathered.reshape(sequences, tp_count, seq_count, channels, CTX), (0, 4, 2, 1, 3)
    ).reshape(sequences, CTX, features)
    queries = jnp.einsum(
        "bwd,de->bwe", attn_input, query_weight, preferred_element_type=jnp.float32
    ).astype(jnp.bfloat16)
    token_keys = jnp.einsum(
        "bwd,de->bwe", attn_input, key_weight, preferred_element_type=jnp.float32
    ).astype(jnp.bfloat16)
    token_values = jnp.einsum(
        "bwd,de->bwe", attn_input, value_weight, preferred_element_type=jnp.float32
    ).astype(jnp.bfloat16)
    context_state_keys = jnp.einsum(
        "bsd,de->bse", context_carry, state_key_weight, preferred_element_type=jnp.float32
    ).astype(jnp.bfloat16)
    state_values = jnp.einsum(
        "bsd,de->bse", context_carry, state_value_weight, preferred_element_type=jnp.float32
    ).astype(jnp.bfloat16)
    query_heads = queries.reshape(sequences, block_len, local_heads, DH)
    key_heads = jnp.concatenate([token_keys, context_state_keys], axis=1).reshape(
        sequences, block_len + CTX, local_heads, DH
    )
    value_heads = jnp.concatenate([token_values, state_values], axis=1).reshape(
        sequences, block_len + CTX, local_heads, DH
    )
    causal = jnp.arange(block_len)[:, None] >= jnp.arange(block_len)[None, :]
    allowed = jnp.concatenate([causal, jnp.broadcast_to(seq_index > 0, (block_len, CTX))], axis=1)

    def score_block():
        raw_scores = (
            jnp.einsum(
                "bqhd,bkhd->bhqk", query_heads, key_heads, preferred_element_type=jnp.float32
            )
            * score_scale
        )
        return jnp.where(allowed, raw_scores, NEGATIVE)

    scores = score_block()
    row_max = jnp.max(scores, axis=-1, keepdims=True)
    exp_scores = jnp.exp(scores - row_max)
    row_total = jnp.sum(exp_scores, axis=-1, keepdims=True)
    log_total = row_max + jnp.log(row_total)
    attn_probs = (exp_scores / row_total).astype(jnp.bfloat16)
    head_mix = jnp.einsum(
        "bhqk,bkhd->bqhd", attn_probs, value_heads, preferred_element_type=jnp.float32
    )
    head_mix = head_mix.reshape(sequences, block_len, local_heads * DH).astype(jnp.bfloat16)
    attn_part = jnp.einsum(
        "bwe,ed->bwd", head_mix, output_weight, preferred_element_type=jnp.float32
    )
    residual = inputs + tp_total(attn_part)
    normed_mid, inverse_mid = normalize(residual)
    mlp_input = (normed_mid * feedforward_norm_gain).astype(jnp.bfloat16)
    pre_act = jnp.einsum(
        "bwd,df->bwf", mlp_input, hidden_weight, preferred_element_type=jnp.float32
    )
    activated, gelu_back = jax.vjp(partial(jax.nn.gelu, approximate=False), pre_act)
    activated = activated.astype(jnp.bfloat16)
    mlp_part = jnp.einsum(
        "bwf,fd->bwd", activated, return_weight, preferred_element_type=jnp.float32
    )
    output = ((residual + tp_total(mlp_part)) * valid).astype(jnp.bfloat16)
    grad_out = cotangent.astype(jnp.float32) * valid
    grad_out_b = grad_out.astype(jnp.bfloat16)
    grad_return = jnp.einsum(
        "bwf,bwd->fd", activated, grad_out_b, preferred_element_type=jnp.float32
    )
    grad_act = jnp.einsum(
        "bwd,fd->bwf", grad_out_b, return_weight, preferred_element_type=jnp.float32
    )
    grad_pre = gelu_back(grad_act)[0].astype(jnp.bfloat16)
    grad_hidden = jnp.einsum("bwd,bwf->df", mlp_input, grad_pre, preferred_element_type=jnp.float32)
    mid_part = jnp.einsum(
        "bwf,df->bwd", grad_pre, hidden_weight, preferred_element_type=jnp.float32
    )
    grad_mid = tp_total(mid_part)
    gain_part = jnp.sum(
        lax.dynamic_slice_in_dim(grad_mid * normed_mid, tp_index * share, share, 1), axis=(0, 1)
    )
    grad_resid = grad_out + norm_back(normed_mid, inverse_mid, grad_mid * feedforward_norm_gain)
    grad_resid_b = grad_resid.astype(jnp.bfloat16)
    grad_output = jnp.einsum(
        "bwe,bwd->ed", head_mix, grad_resid_b, preferred_element_type=jnp.float32
    )
    grad_heads = jnp.einsum(
        "bwd,ed->bwe", grad_resid_b, output_weight, preferred_element_type=jnp.float32
    ).astype(jnp.bfloat16)
    grad_heads = grad_heads.reshape(sequences, block_len, local_heads, DH)
    grad_probs = jnp.einsum(
        "bqhd,bkhd->bhqk", grad_heads, value_heads, preferred_element_type=jnp.float32
    )
    probs_full = jnp.exp(score_block() - log_total)
    delta = jnp.sum(probs_full * grad_probs, axis=-1, keepdims=True)
    grad_scores = (probs_full * (grad_probs - delta)).astype(jnp.bfloat16)
    grad_queries = (
        jnp.einsum("bhqk,bkhd->bqhd", grad_scores, key_heads, preferred_element_type=jnp.float32)
        * score_scale
    )
    grad_queries = grad_queries.astype(jnp.bfloat16).reshape(sequences, block_len, local_heads * DH)
    grad_keys_all = (
        jnp.einsum("bhqk,bqhd->bkhd", grad_scores, query_heads, preferred_element_type=jnp.float32)
        * score_scale
    )
    grad_keys_all = grad_keys_all.astype(jnp.bfloat16).reshape(
        sequences, block_len + CTX, local_heads * DH
    )
    grad_values_all = jnp.einsum(
        "bhqk,bqhd->bkhd", attn_probs, grad_heads, preferred_element_type=jnp.float32
    )
    grad_values_all = grad_values_all.astype(jnp.bfloat16).reshape(
        sequences, block_len + CTX, local_heads * DH
    )
    grad_token_keys = grad_keys_all[:, :block_len]
    grad_state_keys = grad_keys_all[:, block_len:]
    grad_token_values = grad_values_all[:, :block_len]
    grad_state_values = grad_values_all[:, block_len:]
    grad_query = jnp.einsum(
        "bwd,bwe->de", attn_input, grad_queries, preferred_element_type=jnp.float32
    )
    grad_key = jnp.einsum(
        "bwd,bwe->de", attn_input, grad_token_keys, preferred_element_type=jnp.float32
    )
    grad_value = jnp.einsum(
        "bwd,bwe->de", attn_input, grad_token_values, preferred_element_type=jnp.float32
    )
    grad_state_key = jnp.einsum(
        "bsd,bse->de", context_carry, grad_state_keys, preferred_element_type=jnp.float32
    )
    grad_state_value = jnp.einsum(
        "bsd,bse->de", context_carry, grad_state_values, preferred_element_type=jnp.float32
    )
    grad_context = jnp.einsum(
        "bse,de->bsd", grad_state_keys, state_key_weight, preferred_element_type=jnp.float32
    ) + jnp.einsum(
        "bse,de->bsd", grad_state_values, state_value_weight, preferred_element_type=jnp.float32
    )
    ordered = jnp.transpose(
        grad_context.reshape(sequences, CTX, seq_count, tp_count, channels), (0, 3, 2, 4, 1)
    ).reshape(sequences, tp_count * seq_count * channels, CTX)
    grad_ctx_part = lax.psum_scatter(
        ordered.astype(jnp.bfloat16), "tp", scatter_dimension=1, tiled=True
    )
    moved_back = shifted(grad_ctx_part, "seq", -1)
    incoming = jnp.pad(moved_back, ((0, 0), (0, 0), (block_len - CTX, 0)))
    arrived = to_channels(incoming).astype(jnp.float32)
    grad_real, grad_imag = transform_forward(jnp.pad(arrived, spread), outer_len, inner_len)
    grad_signal = transform_inverse(
        ker_real * grad_real + ker_imag * grad_imag,
        ker_real * grad_imag - ker_imag * grad_real,
        outer_len,
        inner_len,
    )[:, :, :full_len]
    kernel_real = jnp.sum(grad_real * in_real + grad_imag * in_imag, axis=0)
    kernel_imag = jnp.sum(grad_imag * in_real - grad_real * in_imag, axis=0)
    grad_kernel = transform_inverse(kernel_real, kernel_imag, outer_len, inner_len)[:, :full_len]
    grad_coefficient, grad_rate = kernel_back(grad_kernel)
    grad_seq = to_positions(grad_signal.astype(jnp.bfloat16))
    tp_slot = (jnp.arange(tp_count) == tp_index).astype(jnp.float32)
    placed = jnp.transpose(grad_seq.astype(jnp.float32), (0, 2, 1)).reshape(
        sequences, block_len, seq_count, 1, channels
    )
    placed = (placed * tp_slot[:, None]).reshape(sequences, block_len, features) * valid
    input_part = (
        jnp.einsum("bwe,de->bwd", grad_queries, query_weight, preferred_element_type=jnp.float32)
        + jnp.einsum("bwe,de->bwd", grad_token_keys, key_weight, preferred_element_type=jnp.float32)
        + jnp.einsum(
            "bwe,de->bwd", grad_token_values, value_weight, preferred_element_type=jnp.float32
        )
        + placed
    )
    grad_in, grad_mlp_gain = (
        lax.psum(input_part.astype(jnp.bfloat16), "tp").astype(jnp.float32),
        lax.psum(gain_part.astype(jnp.bfloat16), "tp").astype(jnp.float32),
    )
    grad_attn_gain = jnp.sum(grad_in * normed_in, axis=(0, 1))
    grad_tokens = grad_resid + norm_back(normed_in, inverse_in, grad_in * attention_norm_gain)
    summed = (
        lax.psum(grad_attn_gain.astype(jnp.bfloat16), "seq").astype(jnp.float32),
        lax.psum(grad_query.astype(jnp.bfloat16), "seq").astype(jnp.float32),
        lax.psum(grad_key.astype(jnp.bfloat16), "seq").astype(jnp.float32),
        lax.psum(grad_value.astype(jnp.bfloat16), "seq").astype(jnp.float32),
        lax.psum(grad_output.astype(jnp.bfloat16), "seq").astype(jnp.float32),
        lax.psum(grad_state_key.astype(jnp.bfloat16), "seq").astype(jnp.float32),
        lax.psum(grad_state_value.astype(jnp.bfloat16), "seq").astype(jnp.float32),
        lax.psum(grad_mlp_gain.astype(jnp.bfloat16), "seq").astype(jnp.float32),
        lax.psum(grad_hidden.astype(jnp.bfloat16), "seq").astype(jnp.float32),
        lax.psum(grad_return.astype(jnp.bfloat16), "seq").astype(jnp.float32),
    )
    return (
        output,
        grad_tokens,
        summed[0],
        summed[1],
        summed[2],
        summed[3],
        summed[4],
        summed[5],
        summed[6],
        grad_coefficient,
        grad_rate,
        summed[7],
        summed[8],
        summed[9],
    )


def solution(mesh):
    placed = (
        P(None, "seq", None),
        P(),
        P(),
        P(None, "tp"),
        P(None, "tp"),
        P(None, "tp"),
        P("tp", None),
        P(None, "tp"),
        P(None, "tp"),
        P(("seq", "tp"), None),
        P(("seq", "tp"), None),
        P(),
        P(None, "tp"),
        P("tp", None),
        P(None, "seq", None),
    )
    return jax.shard_map(
        body,
        mesh=mesh,
        in_specs=placed,
        out_specs=(
            P(None, "seq", None),
            P(None, "seq", None),
            P(),
            P(None, "tp"),
            P(None, "tp"),
            P(None, "tp"),
            P("tp", None),
            P(None, "tp"),
            P(None, "tp"),
            P(("seq", "tp"), None),
            P(("seq", "tp"), None),
            P(),
            P(None, "tp"),
            P("tp", None),
        ),
        check_vma=False,
    )
```

profile of v0, /device:TPU:17, one launch (start us, length us, event | category | flops | bytes accessed | tf_op | source)
XLA Modules:
  0.0 1145.0 jit_solution(3905105662586762539)
XLA Ops:
  15.8 6.2 copy.193
  25.1 4.8 all-to-all-start
  30.4 5.9 fusion.25
  85.4 5.2 fusion.40
  90.7 6.1 fusion.55
  96.8 9.4 copy.257
  106.1 5.3 slice_bitcast_fusion.2
  111.4 7.0 reshape.336
  118.4 18.2 %all_to_all.45 = bf16[8,2,32768]{2,1,0:T(2,128)(2,1)} all-to-all(bf16[8,2,32768]{2,1,0:T(2,128)(2,1)S(1)} %reshape.336), channel_id=1, replica_groups=mesh['seq'=8,'tp'=4] {'seq'}, dimensions={0} | all-to-all | bytes 2097152 | tf_op jit(solution)/shard_map/all_to_all | solution.py:95
  136.6 7.0 reshape.337
  143.6 5.5 copy.259
  156.7 5.3 convolution_convert_fusion.6
  167.3 18.6 %all-gather.2.cloned.1.call-done = bf16[4,1024,128]{2,1,0:T(8,128)(2,1)} async-done(((bf16[4,256,128]{2,1,0:T(8,128)(2,1)}), bf16[4,1024,128]{2,1,0:T(8,128)(2,1)}) %all-gather.2.cloned.1.call-update) | async-done | bytes 1048592 | tf_op jit(solution)/shard_map/all_gather | solution.py:163
  211.9 154.1 %all-reduce.13.cloned.1.call-done = bf16[4,512,1024]{2,1,0:T(8,128)(2,1)} async-done(((bf16[4,512,1024]{2,1,0:T(8,128)(2,1)}), bf16[4,512,1024]{2,1,0:T(8,128)(2,1)}) %all-reduce.13.cloned.1.call-update) | async-done | bytes 4194320 | tf_op jit(solution)/shard_map/psum | solution.py:99
  366.0 4.8 fusion.26
  375.5 7.9 fusion.84
  383.4 21.0 %multiply_convert_fusion.2 = (bf16[4,512,1024]{2,1,0:T(8,128)(2,1)}, f32[4,512,1024]{2,1,0:T(8,128)}) fusion(f32[4,512,1024]{2,1,0:T(8,128)S(1)} %get-tuple-element.71, u8[512,1024]{1,0:T(8,128)(4,1)} %get-tuple-element.47, u8[512,1024]{1,0:T(8,128)(4,1)} %get-tuple-element.46), kind=kLoop, calls=%fused_computation.43 | loop fusion | flops 146800640 | bytes 22020096 | tf_op jit(solution)/shard_map/convert_element_type | solution.py:221
  404.4 11.6 %add_convert_fusion.1 = bf16[4,512,1024]{2,1,0:T(8,128)(2,1)} fusion(f32[4,512,1024]{2,1,0:T(8,128)} %get-tuple-element.64, f32[4,512,1024]{2,1,0:T(8,128)S(1)} %get-tuple-element.71, bf16[4,512,1024]{2,1,0:T(8,128)(2,1)S(1)} %copy-done.41, f32[4,512]{1,0:T(4,128)S(1)} %compare_convert_fusion, bf16[1024,1024]{1,0:T(8,128)(2,1)} %param.28), kind=kOutput, calls=%fused_computation.39 | convolution fusion | flops 4330618880 | bytes 27271168 | tf_op jit(solution)/shard_map/bwd,fd->bwf/dot_general | solution.py:231
  416.0 8.3 convolution_convert_fusion
  425.7 9.7 bitcast_convert_fusion
  435.5 9.4 bitcast_convert_fusion.1
  444.8 133.7 %all-reduce.15.cloned.1.call-done = bf16[4,512,1024]{2,1,0:T(8,128)(2,1)} async-done(((bf16[4,512,1024]{2,1,0:T(8,128)(2,1)}), bf16[4,512,1024]{2,1,0:T(8,128)(2,1)}) %all-reduce.15.cloned.1.call-update) | async-done | bytes 4194320 | tf_op jit(solution)/shard_map/psum | solution.py:99
  578.5 6.4 multiply_reduce_fusion.3
  585.0 7.2 multiply_add_fusion
  613.3 9.5 convolution_convert_fusion.1
  631.9 7.3 reduce-scatter.2.cloned.1.call-done
  642.2 5.4 fusion.115
  656.5 5.2 fusion.119
  673.9 5.7 fusion.108
  683.9 12.5 %subtract_reduce_fusion = (f32[32,64,128]{2,1,0:T(8,128)}, f32[32,64,128]{2,1,0:T(8,128)}, f32[4,32,64,128]{3,2,1,0:T(8,128)S(1)}) fusion(f32[4,32,64,128]{3,2,1,0:T(8,128)S(1)} %copy-done.8, f32[4,32,64,128]{3,2,1,0:T(8,128)S(1)} %convolution_add_fusion.1, f32[4,32,64,128]{3,2,1,0:T(8,128)S(1)} %copy-done.10, f32[4,32,64,128]{3,2,1,0:T(8,128)} %fusion.108, ...), kind=kOutput, calls=%fused_computation.80 | convolution fusion | flops 1622917120 | bytes 31522816 | tf_op jit(solution)/shard_map/dot_general | solution.py:47
  709.1 4.7 convolution_subtract_fusion
  713.9 4.8 fusion.32
  718.7 5.1 fusion.56
  723.8 6.8 copy.261
  730.6 5.3 slice_bitcast_fusion.1
  735.9 7.8 reshape.338
  743.8 7.2 all-to-all-start.3
  750.9 5.9 fusion.132
  761.4 12.7 %all-to-all-done.3 = bf16[8,2,32768]{2,1,0:T(2,128)(2,1)S(1)} async-done(((bf16[8,2,32768]{2,1,0:T(2,128)(2,1)}), bf16[8,2,32768]{2,1,0:T(2,128)(2,1)S(1)}, u32[]{:S(2)}, u32[]{:S(2)}) %all-to-all-start.3) | async-done | bytes 1048608 | tf_op jit(solution)/shard_map/all_to_all | solution.py:95
  778.6 5.5 copy.223
  790.5 8.9 copy.225
  799.4 12.1 %add_convert_fusion = bf16[4,512,1024]{2,1,0:T(8,128)(2,1)} fusion(f32[4,512,1024]{2,1,0:T(8,128)} %copy.225, f32[4,512,1024]{2,1,0:T(8,128)} %fusion.142, f32[4,512,1024]{2,1,0:T(8,128)} %fusion.132, f32[1024]{0:T(1024)S(1)} %copy-done.75, f32[4,512]{1,0:T(4,128)S(1)} %compare_convert_fusion, bf16[4,640,256]{1,2,0:T(8,128)(2,1)S(1)} %bitcast.419, ...), kind=kOutput, calls=%fused_computation.36 | convolution fusion | flops 1086324736 | bytes 30945280 | tf_op jit(solution)/shard_map/bwe,de->bwd/dot_general | solution.py:329
  817.5 7.2 psum.116
  833.1 11.2 fusion.24
  862.6 241.1 %all-reduce.19.cloned.1.call-done = (bf16[4,512,1024]{2,1,0:T(8,128)(2,1)}, bf16[4,512,1024]{2,1,0:T(8,128)(2,1)}) async-done(((bf16[4,512,1024]{2,1,0:T(8,128)(2,1)}, bf16[4,512,1024]{2,1,0:T(8,128)(2,1)}), (bf16[4,512,1024]{2,1,0:T(8,128)(2,1)}, bf16[4,512,1024]{2,1,0:T(8,128)(2,1)})) %all-reduce.19.cloned.1.call-update) | async-done | bytes 8388624 | tf_op jit(solution)/shard_map/psum | solution.py:99
  1103.7 7.1 fusion.14
  1110.8 11.9 %all-reduce.5 = (bf16[1024]{0:T(1024)(128)(2,1)S(1)}, bf16[1024]{0:T(1024)(128)(2,1)S(1)}) all-reduce(bf16[1024]{0:T(1024)(128)(2,1)S(1)} %get-tuple-element.44, bf16[1024]{0:T(1024)(128)(2,1)S(1)} %psum.116), channel_id=1, replica_groups=mesh['seq'=8,'tp'=4] {'seq'}, use_global_device_ids=true, to_apply=%region_17.18 | all-reduce | flops 2048 | bytes 8192 | tf_op jit(solution)/shard_map/psum | solution.py:341
  1123.8 13.8 %fusion.11 = (f32[4,512,1024]{2,1,0:T(8,128)}, bf16[4,512,1024]{2,1,0:T(8,128)(2,1)}) fusion(f32[4,512,1024]{2,1,0:T(8,128)} %copy-done.11, bf16[4,512,1024]{2,1,0:T(8,128)(2,1)} %param.15, bf16[4,512,1024]{2,1,0:T(8,128)(2,1)} %get-tuple-element.62, f32[4,512]{1,0:T(4,128)S(1)} %broadcast_multiply_fusion.1, f32[4,512]{1,0:T(4,128)S(1)} %broadcast_multiply_fusion.2, ...), kind=kLoop, calls=%fused_computation.23 | loop fusion | flops 33554432 | bytes 37793792 | tf_op jit(solution)/shard_map/add | solution.py:339
  (325 shorter events, 225.8 us)
Async XLA Ops:
  7.2 368.3 %copy-start = (bf16[1024,1024]{1,0:T(8,128)(2,1)S(1)}, bf16[1024,1024]{1,0:T(8,128)(2,1)}, u32[]{:S(2)}) copy-start(bf16[1024,1024]{1,0:T(8,128)(2,1)} %param.27) | copy-start | bytes 6291460
  22.0 8.2 copy-start.82
  22.0 8.3 copy-start.73
  25.1 20.1 %all-to-all-start = ((bf16[4,256,512]{2,0,1:T(4,128)(2,1)}), bf16[4,256,512]{2,0,1:T(4,128)(2,1)}, u32[]{:S(2)}, u32[]{:S(2)}) async-start(bf16[4,256,512]{2,0,1:T(4,128)(2,1)} %copy.194), calls=%async_computation | async-start | bytes 2097152 | tf_op jit(solution)/shard_map/all_to_all | solution.py:91
  29.9 156.0 %all-gather.2.cloned.1.call-start = ((), (), s32[]{:S(2)}) async-start(), calls=%async_computation.5 | async-start | bytes 1310720 | tf_op jit(solution)/shard_map/all_gather | solution.py:163
  30.1 60.6 %copy-start.51 = (f32[64,128]{1,0:T(8,128)}, f32[64,128]{1,0:T(8,128)S(1)}, u32[]{:S(2)}) copy-start(f32[64,128]{1,0:T(8,128)S(1)} %fusion.249) | copy-start | bytes 98308
  30.2 34.0 %copy-start.34 = (f32[64,128]{1,0:T(8,128)}, f32[64,128]{1,0:T(8,128)S(1)}, u32[]{:S(2)}) copy-start(f32[64,128]{1,0:T(8,128)S(1)} %get-tuple-element.76) | copy-start | bytes 98308
  30.3 60.4 %copy-start.26 = (f32[64,128]{1,0:T(8,128)}, f32[64,128]{1,0:T(8,128)S(1)}, u32[]{:S(2)}) copy-start(f32[64,128]{1,0:T(8,128)S(1)} %get-tuple-element.75) | copy-start | bytes 98308
  43.0 38.2 %copy-start.15 = (f32[32,64,128]{2,1,0:T(8,128)}, f32[32,64,128]{2,1,0:T(8,128)S(1)}, u32[]{:S(2)}) copy-start(f32[32,64,128]{2,1,0:T(8,128)S(1)} %convolution_add_fusion.5) | copy-start | bytes 3145732
  64.2 17.0 %copy-start.7 = (f32[4,32,64,128]{3,2,1,0:T(8,128)}, f32[4,32,64,128]{3,2,1,0:T(8,128)S(1)}, u32[]{:S(2)}) copy-start(f32[4,32,64,128]{3,2,1,0:T(8,128)S(1)} %convolution_add_fusion.3) | copy-start | bytes 12582916
  68.4 12.8 %copy-start.9 = (f32[4,32,64,128]{3,2,1,0:T(8,128)}, f32[4,32,64,128]{3,2,1,0:T(8,128)S(1)}, u32[]{:S(2)}) copy-start(f32[4,32,64,128]{3,2,1,0:T(8,128)S(1)} %convolution_subtract_fusion.3) | copy-start | bytes 12582916
  149.1 6.7 collective-permute-start
  156.6 209.4 %all-reduce.13.cloned.1.call-start = ((), (), s32[]{:S(2)}) async-start(), calls=%async_computation.6 | async-start | bytes 8388608 | tf_op jit(solution)/shard_map/psum | solution.py:99
  164.7 22.6 %copy-start.45 = (bf16[1024,256]{1,0:T(8,128)(2,1)S(1)}, bf16[1024,256]{1,0:T(8,128)(2,1)}, u32[]{:S(2)}) copy-start(bf16[1024,256]{1,0:T(8,128)(2,1)} %param.23) | copy-start | bytes 1572868
  211.8 366.6 %all-reduce.15.cloned.1.call-start = ((), (), s32[]{:S(2)}) async-start(), calls=%async_computation.7 | async-start | bytes 8388608 | tf_op jit(solution)/shard_map/psum | solution.py:99
  375.5 7.9 copy-start.14
  383.4 21.0 %copy-start.41 = (bf16[4,512,1024]{2,1,0:T(8,128)(2,1)S(1)}, bf16[4,512,1024]{2,1,0:T(8,128)(2,1)}, u32[]{:S(2)}) copy-start(bf16[4,512,1024]{2,1,0:T(8,128)(2,1)} %param.29) | copy-start | bytes 12582916
  424.3 214.9 %reduce-scatter.2.cloned.1.call-start = ((), (), s32[]{:S(2)}) async-start(), calls=%async_computation.8 | async-start | bytes 1310720 | tf_op jit(solution)/shard_map/reduce_scatter | solution.py:303
  425.7 9.7 copy-start.84
  435.4 143.0 %copy-start.81 = (f32[1024]{0:T(1024)S(1)}, f32[1024]{0:T(1024)}, u32[]{:S(2)}) copy-start(f32[1024]{0:T(1024)} %param.26) | copy-start | bytes 12292
  444.8 140.1 %copy-start.69 = (f32[4,512]{1,0:T(4,128)S(1)}, f32[4,512]{1,0:T(4,128)}, u32[]{:S(2)}) copy-start(f32[4,512]{1,0:T(4,128)} %copy-done.68) | copy-start | bytes 24580
  584.9 14.4 %slice-start = ((s8[10485760]{0:T(1024)(128)(4,1)}), s8[4194304]{0:T(1024)(128)(4,1)S(1)}, s32[]{:S(2)}) async-start(s8[10485760]{0:T(1024)(128)(4,1)} %bitcast.382), calls=%async_computation.11 | async-start | bytes 8388608
  585.0 14.4 %slice-start.1 = ((s8[10485760]{0:T(1024)(128)(4,1)}), s8[4194304]{0:T(1024)(128)(4,1)S(1)}, s32[]{:S(2)}) async-start(s8[10485760]{0:T(1024)(128)(4,1)} %bitcast.382), calls=%async_computation.12 | async-start | bytes 8388608
  599.3 9.8 copy-start.36
  613.2 9.6 slice-start.3
  613.3 9.6 slice-start.4
  613.3 9.6 copy-start.23
  628.5 13.7 %copy-start.40 = (bf16[4,2,128,512]{3,2,1,0:T(8,128)(2,1)S(1)}, bf16[4,2,128,512]{3,2,1,0:T(8,128)(2,1)}, u32[]{:S(2)}) copy-start(bf16[4,2,128,512]{3,2,1,0:T(8,128)(2,1)} %copy-done.39) | copy-start | bytes 3145732
  631.9 21.1 %copy-start.32 = (bf16[4,128,8,4,32]{1,4,3,2,0:T(8,128)(2,1)S(1)}, bf16[4,128,8,4,32]{1,4,3,2,0:T(8,128)(2,1)}, u32[]{:S(2)}) copy-start(bf16[4,128,8,4,32]{1,4,3,2,0:T(8,128)(2,1)} %copy-done.31) | copy-start | bytes 3145732
  639.3 8.4 collective-permute-start.1
  647.6 7.6 copy-start.29
  649.2 15.7 %all-to-all-start.2 = ((bf16[4,256,512]{2,0,1:T(4,128)(2,1)}), bf16[4,256,512]{2,0,1:T(4,128)(2,1)S(1)}, u32[]{:S(2)}, u32[]{:S(2)}) async-start(bf16[4,256,512]{2,0,1:T(4,128)(2,1)} %pad.20.clone), calls=%async_computation.3 | async-start | bytes 2097152 | tf_op jit(solution)/shard_map/all_to_all | solution.py:91
  653.0 194.9 %all-reduce.17.cloned.1.call-start = ((), (), s32[]{:S(2)}) async-start(), calls=%async_computation.9 | async-start | bytes 14680064 | tf_op jit(solution)/shard_map/psum | solution.py:342
  668.0 11.7 %copy-start.12 = (f32[4,32,128,64]{2,3,1,0:T(8,128)}, f32[4,32,128,64]{2,3,1,0:T(8,128)S(1)}, u32[]{:S(2)}) copy-start(f32[4,32,128,64]{2,3,1,0:T(8,128)S(1)} %fusion.59) | copy-start | bytes 12582916
  670.0 9.6 copy-start.13
  683.9 12.5 %copy-start.16 = (f32[32,64,128]{2,1,0:T(8,128)S(1)}, f32[32,64,128]{2,1,0:T(8,128)}, u32[]{:S(2)}) copy-start(f32[32,64,128]{2,1,0:T(8,128)} %copy-done.15) | copy-start | bytes 3145732
  683.9 12.5 %copy-start.18 = (f32[32,64,128]{2,1,0:T(8,128)S(1)}, f32[32,64,128]{2,1,0:T(8,128)}, u32[]{:S(2)}) copy-start(f32[32,64,128]{2,1,0:T(8,128)} %convolution_subtract_fusion.6) | copy-start | bytes 3145732
  743.8 30.4 %all-to-all-start.3 = ((bf16[8,2,32768]{2,1,0:T(2,128)(2,1)}), bf16[8,2,32768]{2,1,0:T(2,128)(2,1)S(1)}, u32[]{:S(2)}, u32[]{:S(2)}) async-start(bf16[8,2,32768]{2,1,0:T(2,128)(2,1)} %reshape.338), calls=%async_computation.4 | async-start | bytes 2097152 | tf_op jit(solution)/shard_map/all_to_all | solution.py:95
  750.9 352.8 %all-reduce.19.cloned.1.call-start = ((), (), s32[]{:S(2)}) async-start(), calls=%async_computation.10 | async-start | bytes 16777216 | tf_op jit(solution)/shard_map/psum | solution.py:99
  790.5 8.9 copy-start.38
  790.5 8.9 copy-start.57
  790.5 8.9 copy-start.75
  815.5 9.3 copy-start.33
  815.5 11.8 %copy-start.30 = (f32[32,64,128]{2,1,0:T(8,128)S(1)}, f32[32,64,128]{2,1,0:T(8,128)}, u32[]{:S(2)}) copy-start(f32[32,64,128]{2,1,0:T(8,128)} %get-tuple-element.42) | copy-start | bytes 3145732
  847.9 7.6 copy-start.59
  847.9 8.7 copy-start.58
  850.1 7.5 copy-start.44
  1123.8 13.8 %copy-start.1 = (bf16[1024,1024]{1,0:T(8,128)(2,1)S(1)}, bf16[1024,1024]{1,0:T(8,128)(2,1)}, u32[]{:S(2)}) copy-start(bf16[1024,1024]{1,0:T(8,128)(2,1)} %param.27) | copy-start | bytes 6291460
  (53 other events, 195.2 us)
Sparse Core Ops, SparseCore 0:
  156.7 29.1 all-gather.1
  212.0 153.9 all-reduce.12
  424.4 153.9 all-reduce.14
  613.4 25.8 reduce-scatter.1
  661.8 128.1 all-reduce.16
  811.6 292.0 all-reduce.18
where the time goes:
time: 1160 us; the launch traced here: 1140 us
  waiting for transfers between devices  574 us (49%)
  matrix products  274 us (24%)
  local copies, waits for them, and re-layouts  116 us (10%)
  other arithmetic  105 us (9%)
  blocking collectives  37.3 us (3%)
  starting transfers between devices  22.2 us (2%)
  between operations  16 us (1%)
    psum x3, waiting for transfers between devices, tp_total(): return lax.psum(values.astype(jnp.bfloat16), 'tp').astype(jnp.float32)  529 us
    dot_general x24, matrix products, dot_high(): return jnp.matmul(matrix, table, precision=HIGH_ACCURACY)  87.8 us
    unnamed x196, local copies, waits for them, and re-layouts  52.7 us
  transfers between devices with their start and end apart: 11, of which 8 were waited for; matrix products, arithmetic and copies ran while one was open for 22% of the time, Pallas kernels for 0%

commit v1 on v0

v1 whole, which is shorter than its diff:
```python
from functools import partial
import math

import jax
import jax.numpy as jnp
from jax import lax
from jax.experimental import pallas as pl
from jax.experimental.pallas import tpu as pltpu
from jax.sharding import PartitionSpec as P

DH = 128
CTX = 128
EPS = 1e-05
NEGATIVE = -1e30
F32 = jnp.float32
BF16 = jnp.bfloat16


def normalize(values):
    center = values - jnp.mean(values, axis=-1, keepdims=True)
    inverse = lax.rsqrt(jnp.mean(center * center, axis=-1, keepdims=True) + EPS)
    return (center * inverse, inverse)


def norm_back(normed, inverse, grad_normed):
    mean_grad = jnp.mean(grad_normed, axis=-1, keepdims=True)
    mean_cross = jnp.mean(grad_normed * normed, axis=-1, keepdims=True)
    return inverse * (grad_normed - mean_grad - normed * mean_cross)


def flip(value, mask):
    count = lax.axis_size("seq")
    return lax.ppermute(value, "seq", [(i, i ^ mask) for i in range(count)])


def shifted(value, steps):
    count = lax.axis_size("seq")
    first, last = (max(0, -steps), min(count, count - steps))
    return lax.ppermute(value, "seq", [(i, i + steps) for i in range(first, last)])


def line_gather(value):
    count = lax.axis_size("tp")
    place = lax.axis_index("tp")
    lefts, rights = [value], [value]
    for k in range(1, count):
        lefts.append(lax.ppermute(lefts[-1], "tp", [(i, i + 1) for i in range(k - 1, count - 1)]))
        rights.append(
            lax.ppermute(rights[-1], "tp", [(i, i - 1) for i in range(1, count - k + 1)])
        )
    return [value] + [
        jnp.where(place >= j, lefts[j], rights[count - j]) for j in range(1, count)
    ]


def line_reduce(chunks):
    count = lax.axis_size("tp")
    add = lambda a, b: a if b is None else (a.astype(F32) + b.astype(F32)).astype(BF16)
    going, coming = None, None
    for k in range(1, count):
        going = lax.ppermute(add(chunks[k], going), "tp", [(i, i + 1) for i in range(k)])
        coming = lax.ppermute(
            add(chunks[count - k], coming), "tp", [(i, i - 1) for i in range(count - k, count)]
        )
    return (chunks[0].astype(F32) + going.astype(F32) + coming.astype(F32)).astype(BF16)


def plane_bits(reverse):
    count = lax.axis_size("seq") // 2
    bits = [1 << b for b in range(count.bit_length() - 1)]
    return bits[::-1] if reverse else bits


def plane_gather(value, reverse):
    held = {0: value}
    for bit in plane_bits(reverse):
        held.update({p | bit: flip(v, 2 * bit) for p, v in list(held.items())})
    return held


def plane_reduce(pieces, reverse):
    held = dict(pieces)
    for bit in plane_bits(reverse):
        for p in [p for p in held if p & bit]:
            got = flip(held.pop(p), 2 * bit)
            held[p ^ bit] = (held[p ^ bit].astype(F32) + got.astype(F32)).astype(BF16)
    return held[0]


def scan_in(decay_ref, u_ref, state_ref, moment_ref):
    decay = decay_ref[...]

    def step(t, carry):
        h, m = carry
        return decay * h + u_ref[t], decay * (m + h)

    zero = jnp.zeros(decay.shape, F32)
    h, m = lax.fori_loop(0, u_ref.shape[0], step, (zero, zero))
    state_ref[...] = h
    moment_ref[...] = m


def scan_out(decay_ref, gain_ref, start_ref, u_ref, y_ref):
    decay, gain = decay_ref[...], gain_ref[...]

    def step(t, h):
        h = decay * h + u_ref[t]
        y_ref[t] = jnp.sum(gain * h, axis=0)
        return h

    lax.fori_loop(0, u_ref.shape[0], step, start_ref[...])


def scan_back_in(decay_ref, g_ref, state_ref):
    decay = decay_ref[...]
    last = g_ref.shape[0] - 1

    def step(t, lam):
        return decay * (lam + g_ref[last - t])

    state_ref[...] = lax.fori_loop(0, last + 1, step, jnp.zeros(decay.shape, F32))


def scan_back_out(decay_ref, gain_ref, end_ref, start_ref, u_ref, g_ref, y_ref, gh_ref, gm_ref):
    decay, gain = decay_ref[...], gain_ref[...]
    rows, count = y_ref.shape[0], g_ref.shape[0]

    def empty(t, lam):
        y_ref[rows - 1 - t] = jnp.sum(gain * lam, axis=0)
        return decay * lam

    def full(t, lam):
        lam = lam + g_ref[count - 1 - t]
        y_ref[count - 1 - t] = jnp.sum(gain * lam, axis=0)
        return decay * lam

    lam = lax.fori_loop(0, rows - count, empty, end_ref[...])
    lax.fori_loop(0, count, full, lam)

    def again(t, carry):
        h, m, gh, gm = carry
        h, m = decay * h + u_ref[t], decay * (m + h)
        g = g_ref[t]
        return h, m, gh + g * h, gm + g * m

    zero = jnp.zeros(decay.shape, F32)
    _, _, gh, gm = lax.fori_loop(0, count, again, (start_ref[...], zero, zero, zero))
    gh_ref[...] = gh
    gm_ref[...] = gm


def call(kernel, outs, *operands):
    return pl.pallas_call(
        kernel,
        out_shape=[jax.ShapeDtypeStruct(shape, dtype) for shape, dtype in outs],
        compiler_params=pltpu.CompilerParams(vmem_limit_bytes=44 * 2**20),
    )(*operands)


def tiles(values):
    return values.astype(F32).reshape(values.shape[0], values.shape[1] // 128, 128)


def dot(a, b, dims):
    return lax.dot_general(a, b, (dims, ((), ())), preferred_element_type=F32)


NN = ((1,), (0,))
NT = ((1,), (1,))
TN = ((0,), (0,))


def body(
    tokens,
    lengths,
    attention_norm_gain,
    query_weight,
    key_weight,
    value_weight,
    output_weight,
    state_key_weight,
    state_value_weight,
    state_coefficient,
    state_rate,
    feedforward_norm_gain,
    hidden_weight,
    return_weight,
    cotangent,
):
    sequences, block_len, features = tokens.shape
    seq_count = lax.axis_size("seq")
    tp_count = lax.axis_size("tp")
    seq_index = lax.axis_index("seq")
    tp_index = lax.axis_index("tp")
    planes = seq_count // 2
    copies = tp_count // sequences
    sequence = tp_index // copies
    head_cols = query_weight.shape[1]
    hidden_cols = hidden_weight.shape[1]
    heads = head_cols * tp_count // DH
    head_rows = head_cols // seq_count
    hidden_rows = hidden_cols // seq_count
    scale = DH ** (-0.5)

    shard_a = [query_weight.T, key_weight.T, value_weight.T]
    shard_b = [state_key_weight.T, state_value_weight.T, output_weight]
    shard_m = [hidden_weight.T, return_weight]

    def head_slice(shard, relative):
        other = seq_index ^ relative
        at = (other & 1) * planes + (other >> 1)
        return lax.dynamic_slice_in_dim(shard, at * head_rows, head_rows, 0)

    def hidden_slice(shard, relative):
        return lax.dynamic_slice_in_dim(
            shard, (seq_index ^ relative) * hidden_rows, hidden_rows, 0
        )

    def gather_heads(shards, reverse):
        mine = jnp.stack([head_slice(w, 0) for w in shards])
        line = jnp.stack(line_gather(mine)[1:])
        plane = plane_gather(line, reverse)
        other = {p: flip(v, 1) for p, v in plane.items()}
        far = jnp.stack(
            [jnp.stack([group[p] for p in range(planes)]) for group in (plane, other)]
        )
        far = jnp.transpose(far, (3, 2, 0, 1, 4, 5))
        own = jnp.stack(
            [
                jnp.concatenate([head_slice(w, 2 * p + c) for c in range(2) for p in range(planes)])
                for w in shards
            ]
        )
        far = far.reshape(len(shards), (tp_count - 1) * head_cols, features)
        return jnp.concatenate([own, far], axis=1)

    def gather_hidden(shard, reverse):
        line = line_gather(hidden_slice(shard, 0))
        plane = plane_gather(jnp.concatenate(line[1:]), reverse)
        return jnp.concatenate(
            [
                piece
                for p in range(planes)
                for piece in (hidden_slice(shard, 2 * p), plane[p])
            ]
        )

    wq, wk, wv = gather_heads(shard_a, False)
    wsk, wsv, wo = gather_heads(shard_b, True)
    wh = gather_hidden(shard_m[0], False)
    wr = gather_hidden(shard_m[1], True)

    own_tokens = lax.dynamic_index_in_dim(tokens, sequence, 0, keepdims=False)
    own_cot = lax.dynamic_index_in_dim(cotangent, sequence, 0, keepdims=False)
    length = lax.dynamic_index_in_dim(lengths, sequence, 0, keepdims=False)
    before = shifted(own_tokens[block_len - CTX :], 1)
    positions = seq_index * block_len - CTX + jnp.arange(block_len + CTX)
    live = ((positions < length) & (positions >= 0)).astype(F32)[:, None]
    valid = live[CTX:]
    inputs = own_tokens.astype(F32)
    normed_in, inverse_in = normalize(inputs)
    attn_input = (normed_in * attention_norm_gain).astype(BF16)
    early = (normalize(before.astype(F32))[0] * attention_norm_gain).astype(BF16)
    window = jnp.concatenate([early, attn_input[: block_len - CTX]]).astype(F32) * live[:block_len]
    signal = tiles(window)

    both = jnp.stack([state_rate, state_coefficient])
    both = lax.all_gather(both, ("seq", "tp"), axis=1, tiled=True)
    states = both.shape[2]
    both = jnp.transpose(both, (0, 2, 1)).reshape(2, states, features // 128, 128)
    rate, gain = both[0], both[1]
    decay = jnp.exp(-rate)
    grid = rate.shape
    local_state, local_moment = call(scan_in, [(grid, F32)] * 2, decay, signal)
    start = 0.0
    for m in range(1, seq_count):
        start = start + jnp.exp(-rate * (block_len * (m - 1))) * shifted(local_state, m)
    (context,) = call(
        scan_out, [((CTX,) + grid[1:], F32)], decay, gain, start, signal[:CTX]
    )
    context = context.reshape(CTX, features).astype(BF16)

    queries = dot(attn_input, wq, NT).astype(BF16)
    token_keys = dot(attn_input, wk, NT).astype(BF16)
    token_values = dot(attn_input, wv, NT).astype(BF16)
    state_keys = dot(context, wsk, NT).astype(BF16)
    state_values = dot(context, wsv, NT).astype(BF16)
    query_heads = queries.reshape(block_len, heads, DH)
    key_heads = jnp.concatenate([token_keys, state_keys]).reshape(-1, heads, DH)
    value_heads = jnp.concatenate([token_values, state_values]).reshape(-1, heads, DH)
    causal = jnp.arange(block_len)[:, None] >= jnp.arange(block_len)[None, :]
    allowed = jnp.concatenate([causal, jnp.broadcast_to(seq_index > 0, (block_len, CTX))], axis=1)
    raw = jnp.einsum("qhd,khd->hqk", query_heads, key_heads, preferred_element_type=F32) * scale
    scores = jnp.where(allowed, raw, NEGATIVE)
    row_max = jnp.max(scores, axis=-1, keepdims=True)
    exp_scores = jnp.exp(scores - row_max)
    row_total = jnp.sum(exp_scores, axis=-1, keepdims=True)
    probs_full = exp_scores / row_total
    attn_probs = probs_full.astype(BF16)
    head_mix = jnp.einsum("hqk,khd->qhd", attn_probs, value_heads, preferred_element_type=F32)
    head_mix = head_mix.reshape(block_len, heads * DH).astype(BF16)
    residual = inputs + dot(head_mix, wo, NN)
    normed_mid, inverse_mid = normalize(residual)
    mlp_input = (normed_mid * feedforward_norm_gain).astype(BF16)

    grad_out = own_cot.astype(F32) * valid
    grad_out_b = grad_out.astype(BF16)
    mlp_rows = jnp.concatenate([mlp_input, flip(mlp_input, 1)])
    out_rows = jnp.concatenate([grad_out_b, flip(grad_out_b, 1)])
    pre_act = dot(mlp_rows, wh, NT)
    activated, gelu_back = jax.vjp(partial(jax.nn.gelu, approximate=False), pre_act)
    activated = activated.astype(BF16)
    mlp_part = dot(activated, wr, NN)
    grad_act = dot(out_rows, wr, NT)
    grad_pre = gelu_back(grad_act)[0].astype(BF16)
    mid_part = dot(grad_pre, wh, NN)
    grad_mid = mid_part[:block_len] + flip(mid_part[block_len:].astype(BF16), 1).astype(F32)
    mlp_out = mlp_part[:block_len] + flip(mlp_part[block_len:].astype(BF16), 1).astype(F32)
    output = ((residual + mlp_out) * valid).astype(BF16)
    output_line = line_gather(output)
    grad_return = dot(activated, out_rows, TN).astype(BF16)
    grad_hidden = dot(grad_pre, mlp_rows, TN).astype(BF16)

    def reduce_hidden(grad, reverse):
        grad = grad.reshape(planes, tp_count * hidden_rows, features)
        mine = plane_reduce({p: grad[p] for p in range(planes)}, reverse)
        mine = mine.reshape(tp_count, hidden_rows, features)
        return line_reduce([mine[j] for j in range(tp_count)])

    sum_hidden = reduce_hidden(grad_hidden, False)
    sum_return = reduce_hidden(grad_return, True)

    grad_mlp_gain = jnp.sum(grad_mid * normed_mid, axis=0)
    grad_resid = grad_out + norm_back(normed_mid, inverse_mid, grad_mid * feedforward_norm_gain)
    grad_resid_b = grad_resid.astype(BF16)
    grad_heads = dot(grad_resid_b, wo, NT).astype(BF16).reshape(block_len, heads, DH)
    grad_probs = jnp.einsum("qhd,khd->hqk", grad_heads, value_heads, preferred_element_type=F32)
    delta = jnp.sum(probs_full * grad_probs, axis=-1, keepdims=True)
    grad_scores = (probs_full * (grad_probs - delta)).astype(BF16)
    grad_queries = (
        jnp.einsum("hqk,khd->qhd", grad_scores, key_heads, preferred_element_type=F32) * scale
    )
    grad_keys_all = (
        jnp.einsum("hqk,qhd->khd", grad_scores, query_heads, preferred_element_type=F32) * scale
    )
    grad_values_all = jnp.einsum(
        "hqk,qhd->khd", attn_probs, grad_heads, preferred_element_type=F32
    )
    wide = heads * DH
    grad_queries = grad_queries.reshape(block_len, wide).astype(BF16)
    grad_keys_all = grad_keys_all.reshape(block_len + CTX, wide).astype(BF16)
    grad_values_all = grad_values_all.reshape(block_len + CTX, wide).astype(BF16)
    grad_token_keys, grad_state_keys = grad_keys_all[:block_len], grad_keys_all[block_len:]
    grad_token_values, grad_state_values = grad_values_all[:block_len], grad_values_all[block_len:]
    grad_context = (
        dot(grad_state_keys, wsk, NN) + dot(grad_state_values, wsv, NN)
    ).astype(BF16)

    grad_conv = tiles(grad_context)
    (local_back,) = call(scan_back_in, [(grid, F32)], decay, grad_conv)
    end = 0.0
    for m in range(1, seq_count):
        end = end + jnp.exp(-rate * (block_len * (m - 1))) * shifted(local_back, -m)
    grad_signal, grad_gain, grad_moment = call(
        scan_back_out,
        [((block_len,) + grid[1:], F32), (grid, F32), (grid, F32)],
        decay,
        gain,
        end,
        start,
        signal[:CTX],
        grad_conv,
    )
    end_moment = block_len * jnp.exp(-rate * block_len) * start + local_moment
    grad_rate = -gain * (grad_moment + end * end_moment)
    grad_signal = grad_signal.reshape(block_len, features).astype(BF16)
    grad_signal = jnp.concatenate([grad_signal[CTX:], shifted(grad_signal[:CTX], -1)])

    grad_in = (
        dot(grad_queries, wq, NN)
        + dot(grad_token_keys, wk, NN)
        + dot(grad_token_values, wv, NN)
        + grad_signal.astype(F32) * valid
    )
    grad_attn_gain = jnp.sum(grad_in * normed_in, axis=0)
    grad_tokens = grad_resid + norm_back(normed_in, inverse_in, grad_in * attention_norm_gain)
    tokens_line = line_gather(grad_tokens.astype(BF16))

    def split(values):
        return values.reshape(values.shape[0], tp_count, 2, head_cols // 2)

    def both_rows(values):
        values = split(values)
        mine, other = values[:, :, 0], values[:, :, 1]
        joined = jnp.concatenate([mine, flip(other, 1)])
        return joined.reshape(joined.shape[0], -1)

    def both_full(values):
        return jnp.concatenate([values, flip(values, 1)])

    x_rows, c_rows, r_rows = both_full(attn_input), both_full(context), both_full(grad_resid_b)
    grads_a = [
        dot(both_rows(grad_queries), x_rows, TN),
        dot(both_rows(grad_token_keys), x_rows, TN),
        dot(both_rows(grad_token_values), x_rows, TN),
    ]
    grads_b = [
        dot(both_rows(grad_state_keys), c_rows, TN),
        dot(both_rows(grad_state_values), c_rows, TN),
        dot(both_rows(head_mix), r_rows, TN),
    ]

    def reduce_heads(grads, reverse):
        stack = jnp.stack([g.astype(BF16) for g in grads]).reshape(
            len(grads), tp_count, planes, head_rows, features
        )
        mine = plane_reduce(
            {p: jnp.transpose(stack[:, :, p], (1, 0, 2, 3)) for p in range(planes)}, reverse
        )
        return line_reduce([mine[j] for j in range(tp_count)])

    sum_a = reduce_heads(grads_a, False)
    sum_b = reduce_heads(grads_b, True)

    def spread(value, reverse):
        plane = plane_gather(value, reverse)
        other = {p: flip(v, 1) for p, v in plane.items()}
        return jnp.stack([(plane, other)[i & 1][i >> 1] for i in range(seq_count)])

    def ordered(stack):
        return [
            lax.dynamic_index_in_dim(stack, seq_index ^ i, 0, keepdims=False)
            for i in range(seq_count)
        ]

    fix = 1.0 / copies

    def head_grads(value, reverse):
        parts = ordered(spread(value, reverse))
        parts = [parts[2 * p + c] for c in range(2) for p in range(planes)]
        return jnp.concatenate(parts, axis=1).astype(F32) * fix

    def hidden_grads(value, reverse):
        return jnp.concatenate(ordered(spread(value, reverse))).astype(F32) * fix

    full_a = head_grads(sum_a, False)
    full_b = head_grads(sum_b, True)
    full_hidden = hidden_grads(sum_hidden, False)
    full_return = hidden_grads(sum_return, True)

    gains = lax.psum(jnp.stack([grad_attn_gain, grad_mlp_gain]), ("seq", "tp")) * fix
    kernel_grads = jnp.stack([grad_gain, grad_rate]).reshape(2, states, features)
    kernel_grads = lax.psum_scatter(
        jnp.transpose(kernel_grads, (2, 0, 1)).reshape(features, 2 * states),
        ("seq", "tp"),
        scatter_dimension=0,
        tiled=True,
    )
    kernel_grads = kernel_grads * fix

    def lined(line, dtype):
        stack = jnp.stack(line)
        return jnp.stack(
            [
                lax.dynamic_index_in_dim(
                    stack, (tp_index - b * copies) % tp_count, 0, keepdims=False
                )
                for b in range(sequences)
            ]
        ).astype(dtype)

    return (
        lined(output_line, BF16),
        lined(tokens_line, F32),
        gains[0],
        full_a[0].T,
        full_a[1].T,
        full_a[2].T,
        full_b[2],
        full_b[0].T,
        full_b[1].T,
        kernel_grads[:, :states],
        kernel_grads[:, states:],
        gains[1],
        full_hidden.T,
        full_return,
    )


LOG2E = math.log2(math.e)
SCALE = DH ** (-0.5)


def params(limit=44):
    return pltpu.CompilerParams(vmem_limit_bytes=limit * 2**20)


def like(shape, dtype=BF16):
    return jax.ShapeDtypeStruct(shape, dtype)


def whole(shape):
    return pl.BlockSpec(shape, lambda *_: (0,) * len(shape))


def launch(kernel, place, grid, in_specs, out_specs, outs, operands, scratch=(), flops=0):
    return pl.pallas_call(
        kernel,
        grid_spec=pltpu.PrefetchScalarGridSpec(
            num_scalar_prefetch=1,
            grid=grid,
            in_specs=in_specs,
            out_specs=out_specs,
            scratch_shapes=list(scratch),
        ),
        out_shape=outs,
        compiler_params=params(),
        cost_estimate=pl.CostEstimate(flops=flops, bytes_accessed=0, transcendentals=0),
    )(place, *operands)


def cycle(value, steps):
    count = lax.axis_size("tp")
    return lax.ppermute(value, "tp", [(i, (i + steps) % count) for i in range(count)])


def pack_heads(place, wq, wk, wv, wsk, wsv, wo, a_ref, b_ref, turned):
    core, chip = place[0] & 1, place[0] >> 1
    rows = a_ref.shape[2]

    def cut(p):
        return pl.ds(pl.multiple_of((chip ^ p) * rows, rows), rows)

    for out, refs in ((a_ref, (wq, wk, wv)), (b_ref, (wsk, wsv))):
        for w, ref in enumerate(refs):
            turned[...] = ref[...].astype(F32).T
            for p in range(4):
                out[p, w] = turned[cut(p), :].astype(BF16)
    turned[...] = wo[...].astype(F32)
    for p in range(4):
        b_ref[p, 2] = turned[cut(p), :].astype(BF16)


def pack_hidden(place, wh, wr, h_ref, r_ref, turned):
    chip = place[0] >> 1
    rows = h_ref.shape[1]
    for out, turn in ((h_ref, True), (r_ref, False)):
        turned[...] = wh[...].astype(F32).T if turn else wr[...].astype(F32)
        for p in range(4):
            cut = pl.ds(pl.multiple_of((chip ^ p) * rows, rows), rows)
            out[p] = turned[cut, :].astype(BF16)


def load_heads(j, own, far, into, base):
    rows = own.shape[2]

    @pl.when(j == 0)
    def _():
        for p in range(4):
            for w in range(3):
                into[base + w, p * rows : (p + 1) * rows] = own[p, w]

    @pl.when(j > 0)
    def _():
        for p in range(4):
            for w in range(3):
                into[base + w, p * rows : (p + 1) * rows] = far[p][0, w]


def masked(raw, r, block):
    n = raw.shape[1]
    column = lax.broadcasted_iota(jnp.int32, raw.shape, 1)
    row = lax.broadcasted_iota(jnp.int32, raw.shape, 0)
    keep = (column - (n - 128) <= row) & ((column >= CTX) | (block > 0))
    return jnp.where(keep, raw * (SCALE * LOG2E), NEGATIVE)


def attend(place, x0, x1, c0, c1, own_a, own_b, a0, a1, a2, a3, b0, b1, b2, b3,
           part0, part1, q_ref, k_ref, v_ref, s_ref, o_ref, lse_ref,
           weight, keys, values, total):
    j = pl.program_id(0)
    load_heads(j, own_a, (a0, a1, a2, a3), weight, 0)
    load_heads(j, own_b, (b0, b1, b2, b3), weight, 3)
    rows = x0.shape[0]

    @pl.when(j == 0)
    def _():
        total[...] = jnp.zeros_like(total)

    qkv_w = weight[0:3].reshape(3 * DH, -1)
    st_w = weight[3:5].reshape(2 * DH, -1)
    for half, (x, c) in enumerate(((x0, c0), (x1, c1))):
        base = half * rows
        qkv = dot(x[...], qkv_w, NT).astype(BF16)
        q_ref[base : base + rows] = qkv[:, :DH]
        k_ref[base : base + rows] = qkv[:, DH : 2 * DH]
        v_ref[base : base + rows] = qkv[:, 2 * DH :]
        state = dot(c[...], st_w, NT).astype(BF16)
        s_ref[half * CTX : (half + 1) * CTX] = state
        keys[half, 0:CTX] = state[:, :DH]
        values[half, 0:CTX] = state[:, DH:]
        keys[half, CTX:] = qkv[:, DH : 2 * DH]
        values[half, CTX:] = qkv[:, 2 * DH :]
    for half in range(2):
        block = place[0] ^ half
        base = half * rows
        for r in range(rows // 128):
            saved = slice(base + r * 128, base + (r + 1) * 128)
            n = CTX + (r + 1) * 128
            scores = masked(dot(q_ref[saved], keys[half, 0:n], NT), r, block)
            top = jnp.max(scores, axis=1, keepdims=True)
            power = jnp.exp2(scores - top)
            summed = jnp.sum(power, axis=1, keepdims=True)
            lse_ref[0, saved] = top + jnp.log2(summed)
            probs = (power * (1.0 / summed)).astype(BF16)
            o_ref[saved] = dot(probs, values[half, 0:n], NN).astype(BF16)
    for half in range(2):
        base = half * rows
        total[base : base + rows] += dot(o_ref[base : base + rows], weight[5], NN)

    @pl.when(j == pl.num_programs(0) - 1)
    def _():
        part0[...] = total[0:rows].astype(part0.dtype)
        part1[...] = total[rows:].astype(part1.dtype)


def attend_back(place, g0, g1, own_a, own_b, a0, a1, a2, a3, b0, b1, b2, b3,
                q_ref, k_ref, v_ref, s_ref, lse_ref,
                in0, in1, ctx0, ctx1, d_ref, ds_ref,
                weight, keys, values, heads, grad_k, grad_v, total, ctx_total):
    j = pl.program_id(0)
    load_heads(j, own_a, (a0, a1, a2, a3), weight, 0)
    load_heads(j, own_b, (b0, b1, b2, b3), weight, 3)
    rows = g0.shape[0]

    @pl.when(j == 0)
    def _():
        total[...] = jnp.zeros_like(total)
        ctx_total[...] = jnp.zeros_like(ctx_total)

    qkv_w = weight[0:3].reshape(3 * DH, -1)
    st_w = weight[3:5].reshape(2 * DH, -1)
    for half, g in enumerate((g0, g1)):
        base = half * rows
        keys[half, 0:CTX] = s_ref[half * CTX : (half + 1) * CTX, :DH]
        values[half, 0:CTX] = s_ref[half * CTX : (half + 1) * CTX, DH:]
        keys[half, CTX:] = k_ref[base : base + rows]
        values[half, CTX:] = v_ref[base : base + rows]
        heads[half] = dot(g[...], weight[5], NT).astype(BF16)
    for half in range(2):
        block = place[0] ^ half
        base = half * rows
        for r in reversed(range(rows // 128)):
            saved = slice(base + r * 128, base + (r + 1) * 128)
            n = CTX + (r + 1) * 128
            q = q_ref[saved]
            own = heads[half, r * 128 : (r + 1) * 128]
            probs = jnp.exp2(masked(dot(q, keys[half, 0:n], NT), r, block) - lse_ref[0, saved])
            grad = dot(own, values[half, 0:n], NT)
            delta = jnp.sum(probs * grad, axis=1, keepdims=True)
            scores = (probs * (grad - delta)).astype(BF16)
            d_ref[saved, 0:DH] = (dot(scores, keys[half, 0:n], NN) * SCALE).astype(BF16)
            to_k = dot(scores, q, TN)
            to_v = dot(probs.astype(BF16), own, TN)
            if r == rows // 128 - 1:
                grad_k[half, 0:n] = to_k
                grad_v[half, 0:n] = to_v
            else:
                grad_k[half, 0:n] += to_k
                grad_v[half, 0:n] += to_v
    for half in range(2):
        base = half * rows
        d_ref[base : base + rows, DH : 2 * DH] = (grad_k[half, CTX:] * SCALE).astype(BF16)
        d_ref[base : base + rows, 2 * DH :] = grad_v[half, CTX:].astype(BF16)
        state = slice(half * CTX, (half + 1) * CTX)
        ds_ref[state, :DH] = (grad_k[half, 0:CTX] * SCALE).astype(BF16)
        ds_ref[state, DH:] = grad_v[half, 0:CTX].astype(BF16)
        ctx_total[state] += dot(ds_ref[state], st_w, NN)
        total[base : base + rows] += dot(d_ref[base : base + rows], qkv_w, NN)

    @pl.when(j == pl.num_programs(0) - 1)
    def _():
        in0[...] = total[0:rows].astype(in0.dtype)
        in1[...] = total[rows:].astype(in1.dtype)
        ctx0[...] = ctx_total[0:CTX].astype(ctx0.dtype)
        ctx1[...] = ctx_total[CTX:].astype(ctx1.dtype)


def attend_weights(place, x0, x1, c0, c1, g0, g1, d_ref, ds_ref, o_ref, keep_a, send_a, keep_b, send_b):
    rows = x0.shape[0]
    cut = keep_a.shape[3]
    to_qkv = (dot(d_ref[0:rows], x0[...], TN) + dot(d_ref[rows:], x1[...], TN)).astype(BF16)
    to_state = (dot(ds_ref[0:CTX], c0[...], TN) + dot(ds_ref[CTX:], c1[...], TN)).astype(BF16)
    to_out = (dot(o_ref[0:rows], g0[...], TN) + dot(o_ref[rows:], g1[...], TN)).astype(BF16)
    spots_a = {0: (keep_a, 0), 2: (keep_a, 1), 1: (send_a, 0), 3: (send_a, 1)}
    spots_b = {0: (keep_b, 0), 1: (keep_b, 1), 2: (send_b, 0), 3: (send_b, 1)}
    for p in range(4):
        out, at = spots_a[p]
        for w in range(3):
            out[at, 0, w] = to_qkv[w * DH + p * cut : w * DH + (p + 1) * cut]
        out, at = spots_b[p]
        for w in range(2):
            out[at, 0, w] = to_state[w * DH + p * cut : w * DH + (p + 1) * cut]
        out[at, 0, 2] = to_out[p * cut : (p + 1) * cut]


def gelu_parts(x):
    size = jnp.abs(x) * math.sqrt(0.5)
    bell = jnp.exp2(x * x * (-0.5 * LOG2E))
    t = 1.0 / (1.0 + 0.3275911 * size)
    poly = 1.061405429 * t - 1.453152027
    poly = poly * t + 1.421413741
    poly = poly * t - 0.284496736
    poly = poly * t + 0.254829592
    tail = 0.5 * poly * t * bell
    return jnp.where(x >= 0, 1.0 - tail, tail), bell * (1.0 / math.sqrt(2.0 * math.pi))


def load_hidden(j, own, far, into):
    rows = own.shape[1]

    @pl.when(j == 0)
    def _():
        for p in range(4):
            into[p * rows : (p + 1) * rows] = own[p]

    @pl.when(j > 0)
    def _():
        for p in range(4):
            into[p * rows : (p + 1) * rows] = far[p][0]


def feed(place, m0, m1, g0, g1, own_h, own_r, h0, h1, h2, h3, r0, r1, r2, r3,
         mlp0, mlp1, mid0, mid1, act_ref, pre_ref, wh, wr, mlp, mid):
    j = pl.program_id(0)
    load_hidden(j, own_h, (h0, h1, h2, h3), wh)
    load_hidden(j, own_r, (r0, r1, r2, r3), wr)
    rows = m0.shape[0]

    @pl.when(j == 0)
    def _():
        mlp[...] = jnp.zeros_like(mlp)
        mid[...] = jnp.zeros_like(mid)

    for half, (m, g) in enumerate(((m0, g0), (m1, g1))):
        saved = slice(half * rows, (half + 1) * rows)
        pre = dot(m[...], wh[...], NT)
        back = dot(g[...], wr[...], NT)
        part, bell = gelu_parts(pre)
        act_ref[saved] = (pre * part).astype(BF16)
        pre_ref[saved] = (back * (part + pre * bell)).astype(BF16)
        mlp[saved] += dot(act_ref[saved], wr[...], NN)
        mid[saved] += dot(pre_ref[saved], wh[...], NN)

    @pl.when(j == pl.num_programs(0) - 1)
    def _():
        mlp0[...] = mlp[0:rows].astype(mlp0.dtype)
        mlp1[...] = mlp[rows:].astype(mlp1.dtype)
        mid0[...] = mid[0:rows].astype(mid0.dtype)
        mid1[...] = mid[rows:].astype(mid1.dtype)


def feed_weights(place, m0, m1, g0, g1, act_ref, pre_ref, keep_h, send_h, keep_r, send_r):
    rows = m0.shape[0]
    cut = keep_h.shape[2]
    to_h = (dot(pre_ref[0:rows], m0[...], TN) + dot(pre_ref[rows:], m1[...], TN)).astype(BF16)
    to_r = (dot(act_ref[0:rows], g0[...], TN) + dot(act_ref[rows:], g1[...], TN)).astype(BF16)
    spots_h = {0: (keep_h, 0), 2: (keep_h, 1), 1: (send_h, 0), 3: (send_h, 1)}
    spots_r = {0: (keep_r, 0), 1: (keep_r, 1), 2: (send_r, 0), 3: (send_r, 1)}
    for p in range(4):
        out, at = spots_h[p]
        out[at, 0] = to_h[p * cut : (p + 1) * cut]
        out, at = spots_r[p]
        out[at, 0] = to_r[p * cut : (p + 1) * cut]


def live_rows(place, count):
    at = place[0] * (count * pl.num_programs(0)) + pl.program_id(0) * count
    position = at + lax.broadcasted_iota(jnp.int32, (count, 1), 0)
    return (position < place[2]).astype(F32)


def middle(place, tokens, own, got, gain, residual, m_ref):
    value = tokens[0].astype(F32) + own[...] + got[...].astype(F32)
    residual[...] = value
    m_ref[...] = (normalize(value)[0] * gain[...]).astype(BF16)


def finish(place, residual, own, got, out):
    value = residual[...] + own[...] + got[...].astype(F32)
    out[...] = (value * live_rows(place, value.shape[0])).astype(BF16)


def middle_back(place, residual, own, got, cot, gain, grad, grad_b, sums):
    value = residual[...]
    normed, inverse = normalize(value)
    valid = live_rows(place, value.shape[0])
    back = own[...] + got[...].astype(F32)
    total = jnp.sum(back * normed, axis=0, keepdims=True)

    @pl.when(pl.program_id(0) == 0)
    def _():
        sums[...] = total

    @pl.when(pl.program_id(0) > 0)
    def _():
        sums[...] += total

    value = cot[0].astype(F32) * valid + norm_back(normed, inverse, back * gain[...])
    grad[...] = value
    grad_b[...] = value.astype(BF16)


def first_back(place, tokens, own, got, signal, grad, gain, out, sums):
    normed, inverse = normalize(tokens[0].astype(F32))
    valid = live_rows(place, out.shape[0])
    back = own[...] + got[...].astype(F32) + signal[...].astype(F32) * valid
    total = jnp.sum(back * normed, axis=0, keepdims=True)

    @pl.when(pl.program_id(0) == 0)
    def _():
        sums[...] = total

    @pl.when(pl.program_id(0) > 0)
    def _():
        sums[...] += total

    out[...] = (grad[...] + norm_back(normed, inverse, back * gain[...])).astype(BF16)


def unpack_heads(place, n0, n1, n2, n3, f0, f1, f2, f3, q, k, v, o, sk, sv, rows_ref):
    core, chip = place[0] & 1, place[0] >> 1
    cut = n0.shape[1]
    for w, out in ((0, q), (1, k), (2, v), (3, sk), (4, sv), (5, o)):
        for other, pieces in ((0, (n0, n1, n2, n3)), (1, (f0, f1, f2, f3))):
            for p, piece in enumerate(pieces):
                at = (core ^ other) * DH + (chip ^ p) * cut
                rows_ref[pl.ds(pl.multiple_of(at, cut), cut), :] = piece[w].astype(F32)
        out[...] = rows_ref[...] if out is o else rows_ref[...].T


def unpack_hidden(place, pieces, h, r):
    cut = pieces.shape[2]
    for i in range(8):
        at = ((i & 1) * 4 + (i >> 1)) * cut
        r[at : at + cut, :] = pieces[i, 1].astype(F32)
        h[:, at : at + cut] = pieces[i, 0].astype(F32).T


def add(a, b):
    return (a.astype(F32) + b.astype(F32)).astype(BF16)


def after(value, *earlier):
    return lax.optimization_barrier((value, *earlier))[0]


def states_around(local, rate, length, sign, first):
    group = local
    for m in (1, 2):
        group = group + jnp.exp(-rate * (length * m)) * shifted(local, sign * m)
    total = shifted(group, sign * first)
    for m in range(first + 3, 8, 3):
        total = total + jnp.exp(-rate * (length * (m - first))) * shifted(group, sign * m)
    return total


def scan_rows(decay_ref, gain_ref, late_ref, g_ref, y_ref, end_ref):
    decay, gain = decay_ref[...], gain_ref[...]
    rows, count = y_ref.shape[0], g_ref.shape[0]

    def full(t, lam):
        lam = lam + g_ref[count - 1 - t]
        y_ref[rows - 1 - t] = jnp.sum(gain * lam, axis=0)
        return decay * lam

    def empty(t, lam):
        y_ref[rows - count - 1 - t] = jnp.sum(gain * lam, axis=0)
        return decay * lam

    lam = lax.fori_loop(0, count, full, late_ref[...], unroll=8)
    end_ref[...] = lam
    lax.fori_loop(0, rows - count, empty, lam, unroll=8)


def scan_sums(decay_ref, start_ref, u_ref, g_ref, gh_ref, gm_ref):
    decay = decay_ref[...]

    def again(t, carry):
        h, m, gh, gm = carry
        h, m = decay * h + u_ref[t], decay * (m + h)
        g = g_ref[t]
        return h, m, gh + g * h, gm + g * m

    zero = jnp.zeros(decay.shape, F32)
    _, _, gh, gm = lax.fori_loop(0, u_ref.shape[0], again, (start_ref[...], zero, zero, zero))
    gh_ref[...] = gh
    gm_ref[...] = gm


def fast_body(
    tokens, lengths, attention_norm_gain, query_weight, key_weight, value_weight, output_weight,
    state_key_weight, state_value_weight, state_coefficient, state_rate, feedforward_norm_gain,
    hidden_weight, return_weight, cotangent,
):
    sequences, block_len, features = tokens.shape
    tp_count = lax.axis_size("tp")
    seq_index = lax.axis_index("seq")
    tp_index = lax.axis_index("tp")
    hidden_cols = hidden_weight.shape[1]
    cut = DH // 4
    wide = hidden_cols // 8
    length = lax.dynamic_index_in_dim(lengths, tp_index, 0, keepdims=False)
    place = jnp.stack([seq_index, tp_index, length]).astype(jnp.int32)

    column = pl.BlockSpec((features, DH), lambda i, place: (0, place[0] & 1))
    own_a, own_b = launch(
        pack_heads, place, (1,),
        [column] * 5 + [pl.BlockSpec((DH, features), lambda i, place: (place[0] & 1, 0))],
        [whole((4, 3, cut, features))] * 2,
        [like((4, 3, cut, features))] * 2,
        (query_weight, key_weight, value_weight, state_key_weight, state_value_weight, output_weight),
        [pltpu.VMEM((DH, features), F32)],
    )
    own_h, own_r = launch(
        pack_hidden, place, (1,),
        [
            pl.BlockSpec((features, hidden_cols // 2), lambda i, place: (0, place[0] & 1)),
            pl.BlockSpec((hidden_cols // 2, features), lambda i, place: (place[0] & 1, 0)),
        ],
        [whole((4, wide, features))] * 2,
        [like((4, wide, features))] * 2,
        (hidden_weight, return_weight),
        [pltpu.VMEM((hidden_cols // 2, features), F32)],
    )

    def line_of(own):
        return jnp.stack([cycle(own[0], j) for j in range(1, tp_count)])

    def plane_of(line, across):
        near = {2: flip(line, 2), 4: flip(line, 4)}
        return [line, near[2], near[4], flip(near[6 - across], across)]

    line_a, line_b, line_h, line_r = map(line_of, (own_a, own_b, own_h, own_r))
    far_a, far_b = plane_of(line_a, 2), plane_of(line_b, 4)
    far_h, far_r = plane_of(line_h, 2), plane_of(line_r, 4)

    own_tokens = lax.dynamic_index_in_dim(tokens, tp_index, 0, keepdims=False)
    own_cot = lax.dynamic_index_in_dim(cotangent, tp_index, 0, keepdims=False)
    before = shifted(own_tokens[block_len - CTX :], 1)
    positions = seq_index * block_len - CTX + jnp.arange(block_len + CTX)
    live = ((positions < length) & (positions >= 0)).astype(F32)[:, None]
    x = (normalize(own_tokens.astype(F32))[0] * attention_norm_gain).astype(BF16)
    x_other = flip(x, 1)
    grad_out = (own_cot.astype(F32) * live[CTX:]).astype(BF16)
    grad_out_other = flip(grad_out, 1)
    early = (normalize(before.astype(F32))[0] * attention_norm_gain).astype(BF16)
    signal = tiles(
        jnp.concatenate([early, x[: block_len - CTX]]).astype(F32) * live[:block_len]
    )

    states = state_rate.shape[1]
    channels = state_rate.shape[0]
    both = jnp.stack([state_rate, state_coefficient]).reshape(1, -1, 128)
    devices = features // channels
    both = lax.all_to_all(
        jnp.broadcast_to(both, (devices,) + both.shape[1:]), ("seq", "tp"), 0, 0
    )
    both = jnp.transpose(both.reshape(devices, 2, channels, states), (1, 3, 0, 2))
    both = both.reshape(2, states, features // 128, 128)
    rate, gain = both[0], both[1]
    decay = jnp.exp(-rate)
    grid = rate.shape
    local_state, local_moment = call(scan_in, [(grid, F32)] * 2, decay, signal)
    start = states_around(local_state, rate, block_len, 1, 1)
    (context,) = call(scan_out, [((CTX,) + grid[1:], F32)], decay, gain, start, signal[:CTX])
    context = context.reshape(CTX, features).astype(BF16)
    context_other = flip(context, 1)

    rows = 2 * block_len
    slots = tp_count
    own_spec = whole((4, 3, cut, features))
    far_spec = pl.BlockSpec(
        (1, 3, cut, features), lambda j, place: (jnp.maximum(j - 1, 0), 0, 0, 0)
    )
    full = whole((block_len, features))
    ctx_spec = whole((CTX, features))
    head = lambda n, width: pl.BlockSpec((n, width), lambda j, place: (0, j))
    lse_spec = pl.BlockSpec((1, rows, 1), lambda j, place: (j, 0, 0))
    weight_specs = [own_spec] * 2 + [far_spec] * 8
    weights = (own_a, own_b, *far_a, *far_b)
    part, part_other, q, k, v, state, mix, lse = launch(
        attend, place, (slots,),
        [full] * 2 + [ctx_spec] * 2 + weight_specs,
        [full] * 2 + [head(rows, DH)] * 3 + [head(2 * CTX, 2 * DH), head(rows, DH), lse_spec],
        [like((block_len, features), F32), like((block_len, features))]
        + [like((rows, slots * DH))] * 3
        + [like((2 * CTX, slots * 2 * DH)), like((rows, slots * DH)), like((slots, rows, 1), F32)],
        (after(x, line_h, line_r), x_other, context, context_other, *weights),
        [
            pltpu.VMEM((6, DH, features), BF16),
            pltpu.VMEM((2, CTX + block_len, DH), BF16),
            pltpu.VMEM((2, CTX + block_len, DH), BF16),
            pltpu.VMEM((rows, features), F32),
        ],
    )
    group = 128
    steps = block_len // group
    row_spec = pl.BlockSpec((group, features), lambda i, place: (i, 0))
    seq_spec = pl.BlockSpec((1, group, features), lambda i, place: (place[1], i, 0))
    gain_spec = whole((1, features))
    mid_gain = feedforward_norm_gain.reshape(1, -1)
    residual, m = launch(
        middle, place, (steps,),
        [seq_spec, row_spec, row_spec, gain_spec], [row_spec] * 2,
        [like((block_len, features), F32), like((block_len, features))],
        (tokens, part, flip(part_other, 1), mid_gain),
    )
    m_other = flip(m, 1)

    hidden_own = whole((4, wide, features))
    hidden_far = pl.BlockSpec(
        (1, wide, features), lambda j, place: (jnp.maximum(j - 1, 0), 0, 0)
    )
    chunk = 4 * wide
    mlp, mlp_other, mid, mid_other, act, pre = launch(
        feed, place, (slots,),
        [full] * 4 + [hidden_own] * 2 + [hidden_far] * 8,
        [full] * 4 + [head(rows, chunk)] * 2,
        [like((block_len, features), F32), like((block_len, features))] * 2
        + [like((rows, slots * chunk))] * 2,
        (m, m_other, grad_out, grad_out_other, own_h, own_r, *far_h, *far_r),
        [pltpu.VMEM((chunk, features), BF16)] * 2 + [pltpu.VMEM((rows, features), F32)] * 2,
    )
    mid_got, mlp_got = flip(mid_other, 1), flip(mlp_other, 1)
    (output,) = launch(
        finish, place, (steps,),
        [row_spec] * 3, [row_spec], [like((block_len, features))], (residual, mlp, mlp_got),
    )
    output_all = lax.all_gather(output, "tp")
    resid, resid_b, sums_mid = launch(
        middle_back, place, (steps,),
        [row_spec] * 3 + [seq_spec, gain_spec], [row_spec] * 2 + [gain_spec],
        [
            like((block_len, features), F32), like((block_len, features)),
            like((1, features), F32),
        ],
        (residual, mid, mid_got, cotangent, mid_gain),
    )
    resid_other = flip(resid_b, 1)
    grad_spec = pl.BlockSpec(
        (2, 1, wide, features), lambda j, place: (0, (place[1] - j + slots) % slots, 0, 0)
    )
    keep_h, send_h, keep_r, send_r = launch(
        feed_weights, place, (slots,),
        [full] * 4 + [head(rows, chunk)] * 2, [grad_spec] * 4,
        [like((2, slots, wide, features))] * 4,
        (m, m_other, grad_out, grad_out_other, act, after(pre, resid_b, output)),
    )

    grad_in, grad_in_other, grad_ctx, grad_ctx_other, d, ds = launch(
        attend_back, place, (slots,),
        [full] * 2 + weight_specs + [head(rows, DH)] * 3 + [head(2 * CTX, 2 * DH), lse_spec],
        [full] * 2 + [ctx_spec] * 2 + [head(rows, 3 * DH), head(2 * CTX, 2 * DH)],
        [
            like((block_len, features), F32), like((block_len, features)),
            like((CTX, features), F32), like((CTX, features)),
            like((rows, slots * 3 * DH)), like((2 * CTX, slots * 2 * DH)),
        ],
        (after(resid_b, keep_h), resid_other, *weights, q, k, v, state, lse),
        [
            pltpu.VMEM((6, DH, features), BF16),
            pltpu.VMEM((2, CTX + block_len, DH), BF16),
            pltpu.VMEM((2, CTX + block_len, DH), BF16),
            pltpu.VMEM((2, block_len, DH), BF16),
            pltpu.VMEM((2, CTX + block_len, DH), F32),
            pltpu.VMEM((2, CTX + block_len, DH), F32),
            pltpu.VMEM((rows, features), F32),
            pltpu.VMEM((2 * CTX, features), F32),
        ],
    )
    grad_ctx_got = flip(grad_ctx_other, 1)
    grad_in_got = flip(grad_in_other, 1)
    part_spec = pl.BlockSpec(
        (2, 1, 3, cut, features), lambda j, place: (0, (place[1] - j + slots) % slots, 0, 0, 0)
    )
    keep_a, send_a, keep_b, send_b = launch(
        attend_weights, place, (slots,),
        [full] * 2 + [ctx_spec] * 2 + [full] * 2
        + [head(rows, 3 * DH), head(2 * CTX, 2 * DH), head(rows, DH)],
        [part_spec] * 4,
        [like((2, slots, 3, cut, features))] * 4,
        (x, x_other, context, context_other, resid_b, resid_other, d, ds, mix),
    )

    grad_context = (grad_ctx + grad_ctx_got.astype(F32)).astype(BF16)
    grad_conv = tiles(grad_context)
    grad_later = tiles(shifted(grad_context, -1))
    (local_back,) = call(scan_back_in, [(grid, F32)], decay, grad_conv)
    late = states_around(local_back, rate, block_len, -1, 2)
    late = jnp.exp(-rate * (block_len - CTX)) * late
    grad_signal, end = call(
        scan_rows, [((block_len,) + grid[1:], F32), (grid, F32)], decay, gain, late, grad_later
    )
    grad_signal = grad_signal.reshape(block_len, features).astype(BF16)
    grad_gain, grad_moment = call(
        scan_sums, [(grid, F32)] * 2, decay, start, signal[:CTX], grad_conv
    )
    end_moment = block_len * jnp.exp(-rate * block_len) * start + local_moment
    grad_rate = -gain * (grad_moment + end * end_moment)
    grad_tokens, sums_in = launch(
        first_back, place, (steps,),
        [seq_spec] + [row_spec] * 4 + [gain_spec], [row_spec, gain_spec],
        [like((block_len, features)), like((1, features), F32)],
        (tokens, grad_in, grad_in_got, grad_signal, resid, attention_norm_gain.reshape(1, -1)),
    )

    def reduce(keep_first, send_first, keep_second, send_second, begin, then):
        got = after(flip(after(send_first, begin), 2), then)
        near, away = add(keep_first[0], got[0]), add(keep_first[1], got[1])
        first = (near, flip(away, 4))
        got = after(flip(after(send_second, begin), 4), then)
        near, away = add(keep_second[0], got[0]), add(keep_second[1], got[1])
        second = (near, flip(away, 2))
        chunks = jnp.stack([add(*first), add(*second)], axis=1)
        chunks = lax.all_to_all(after(chunks, grad_tokens), "tp", 0, 0)
        return jnp.sum(chunks.astype(F32), axis=0).astype(BF16)

    def regather(total):
        held = [total, flip(total, 2), flip(total, 4), flip(total, 6)]
        return held + [flip(value, 1) for value in held]

    pieces_m = lax.all_gather(reduce(keep_h, send_h, keep_r, send_r, resid_b, late), "seq")
    total_a = reduce(keep_a, send_a, keep_b, send_b, late, grad_tokens)
    pieces_a = regather(total_a.reshape(6, cut, features))
    grad_hidden, grad_return = launch(
        unpack_hidden, place, (1,),
        [whole((8, 2, wide, features))],
        [whole((features, hidden_cols)), whole((hidden_cols, features))],
        [like((features, hidden_cols), F32), like((hidden_cols, features), F32)],
        (pieces_m,),
    )
    grad_q, grad_k, grad_v, grad_o, grad_sk, grad_sv = launch(
        unpack_heads, place, (1,),
        [whole((6, cut, features))] * 8,
        [whole((features, 2 * DH))] * 3 + [whole((2 * DH, features))] + [whole((features, 2 * DH))] * 2,
        [like((features, 2 * DH), F32)] * 3
        + [like((2 * DH, features), F32)]
        + [like((features, 2 * DH), F32)] * 2,
        pieces_a,
        [pltpu.VMEM((2 * DH, features), F32)],
    )

    small = jnp.stack([grad_gain, grad_rate]).reshape(2, states, devices, channels)
    small = jnp.transpose(small, (2, 3, 0, 1)).reshape(devices, -1, 128)
    sums = jnp.concatenate([sums_in, sums_mid]).reshape(1, -1, 128)
    sums = jnp.broadcast_to(sums, (devices,) + sums.shape[1:])
    count = small.shape[1]
    small = jnp.sum(
        lax.all_to_all(jnp.concatenate([small, sums], axis=1), ("seq", "tp"), 0, 0), axis=0
    )
    kernel_grads = small[:count].reshape(channels, 2, states)
    gains = small[count:].reshape(2, features)

    line = line_gather(grad_tokens)
    stack = jnp.stack(line)
    grad_tokens = jnp.stack(
        [
            lax.dynamic_index_in_dim(stack, (tp_index - b) % tp_count, 0, keepdims=False)
            for b in range(sequences)
        ]
    ).astype(F32)
    return (
        output_all, grad_tokens, gains[0], grad_q, grad_k, grad_v, grad_o, grad_sk, grad_sv,
        kernel_grads[:, 0], kernel_grads[:, 1], gains[1], grad_hidden, grad_return,
    )


def choose(tokens, *others):
    query_weight = others[2]
    fits = (
        lax.axis_size("seq") == 8
        and lax.axis_size("tp") == tokens.shape[0]
        and query_weight.shape[1] == 2 * DH
        and others[11].shape[1] % 1024 == 0
        and tokens.shape[1] % 512 == 0
        and tokens.shape[2] == 1024
    )
    return (fast_body if fits else body)(tokens, *others)


def solution(mesh):
    rows = P(None, "seq", None)
    columns = P(None, "tp")
    heads = P("tp", None)
    channels = P(("seq", "tp"), None)
    return jax.shard_map(
        choose,
        mesh=mesh,
        in_specs=(
            rows, P(), P(), columns, columns, columns, heads, columns, columns,
            channels, channels, P(), columns, heads, rows,
        ),
        out_specs=(
            rows, rows, P(), columns, columns, columns, heads, columns, columns,
            channels, channels, P(), columns, heads,
        ),
        check_vma=False,
    )
```

time: 1160 us -> 700 us (0.60)
  waiting for transfers between devices: 574 us -> 250 us
  matrix products: 274 us -> 0 us
  Pallas kernels: 0 us -> 153 us
  starting transfers between devices: 22.2 us -> 106 us
  other arithmetic: 105 us -> 51.5 us
  local copies, waits for them, and re-layouts: 116 us -> 67.7 us
    psum x4 -> x0, waiting for transfers between devices: 529 us -> none  [the longest x3 529 us: tp_total(): return lax.psum(values.astype(jnp.bfloat16), 'tp').astype(jnp.float32)]
    dot_general x68 -> x0, matrix products: 274 us -> none  [the longest x24 87.8 us: dot_high(): return jnp.matmul(matrix, table, precision=HIGH_ACCURACY)]
    ppermute x2 -> x66, waiting for transfers between devices: 3.16 us -> 227 us  [the longest x37 112 us: flip(): return lax.ppermute(value, 'seq', [(i, i ^ mask) for i in range(count)])]
    pallas_call x0 -> x18, Pallas kernels: none -> 153 us  [the longest x13 130 us: launch(): pl.pallas_call(kernel, grid_spec=pltpu.PrefetchScalarGridSpec(num_scalar_...]
    ppermute x2 -> x66, starting transfers between devices: 6.33 us -> 90.5 us  [the longest x37 34.3 us: flip(): return lax.ppermute(value, 'seq', [(i, i ^ mask) for i in range(count)])]
    convert_element_type x18 -> x11, other arithmetic: 49 us -> 17.2 us  [the longest x4 8.51 us: add(): return (a.astype(F32) + b.astype(F32)).astype(BF16)]
    all_to_all x1, blocking collectives: 18.2 us -> 46.5 us  [reduce(): chunks = lax.all_to_all(after(chunks, grad_tokens), 'tp', 0, 0)]
    add x4 -> x3, other arithmetic: 21.7 us -> 2.47 us  [the longest x2 1.58 us: states_around(): group = group + jnp.exp(-rate * (length * m)) * shifted(local, sign * m)]
  transfers between devices with their start and end apart: 11 -> 71, of which waited for: 8 -> 24; matrix products, arithmetic and copies ran while one was open for 22% -> 12% of each run, Pallas kernels for 0% -> 13%
where the time goes in v1:
time: 700 us; the launch traced here: 691 us
  waiting for transfers between devices  250 us (36%)
  Pallas kernels  153 us (22%)
  starting transfers between devices  106 us (15%)
  local copies, waits for them, and re-layouts  67.7 us (10%)
  other arithmetic  51.5 us (7%)
  blocking collectives  46.5 us (7%)
  between operations  16 us (2%)
    pallas_call x13, Pallas kernels, launch(): pl.pallas_call(kernel, grid_spec=pltpu.PrefetchScalarGridSpec(num_scalar_...  130 us
    ppermute x37, waiting for transfers between devices, flip(): return lax.ppermute(value, 'seq', [(i, i ^ mask) for i in range(count)])  112 us
    ppermute x3, waiting for transfers between devices, line_gather(): lax.ppermute(lefts[-1], 'tp', [(i, i + 1) for i in range(k - 1, count - 1)])  62.1 us
    all_to_all x1, blocking collectives, reduce(): chunks = lax.all_to_all(after(chunks, grad_tokens), 'tp', 0, 0)  46.5 us
    ppermute x11, waiting for transfers between devices, shifted(): lax.ppermute(value, 'seq', [(i, i + steps) for i in range(first, last)])  46.2 us
    unnamed x196, local copies, waits for them, and re-layouts  36.7 us
    ppermute x37, starting transfers between devices, flip(): return lax.ppermute(value, 'seq', [(i, i ^ mask) for i in range(count)])  34.3 us
    ppermute x11, starting transfers between devices, shifted(): lax.ppermute(value, 'seq', [(i, i + steps) for i in range(first, last)])  26.8 us
  transfers between devices with their start and end apart: 71, of which 24 were waited for; matrix products, arithmetic and copies ran while one was open for 12% of the time, Pallas kernels for 13%

profile of v1, /device:TPU:17, one launch (start us, length us, event | category | flops | bytes accessed | tf_op | source)
XLA Modules:
  0.0 690.6 jit_solution(11230690824203718388)
XLA Ops:
  18.3 3.2 collective-permute-start.21
  26.3 6.4 all-to-all-start
  48.6 3.6 collective-permute-start.7
  53.6 8.9 %all-to-all-done = f32[32,8,128]{2,1,0:T(8,128)S(1)} async-done(((f32[32,8,128]{2,1,0:T(8,128)}), f32[32,8,128]{2,1,0:T(8,128)S(1)}, u32[]{:S(2)}, u32[]{:S(2)}) %all-to-all-start) | async-done | bytes 131104 | tf_op jit(solution)/shard_map/all_to_all | solution.py:966
  65.1 3.6 convert_multiply_fusion.1.u_ref
  68.7 8.5 %shard_map.255 = (f32[16,8,128]{2,1,0:T(8,128)S(1)}, f32[16,8,128]{2,1,0:T(8,128)S(1)}) custom-call(f32[16,8,128]{2,1,0:T(8,128)S(1)} %exp.40.decay_ref, f32[512,8,128]{2,1,0:T(8,128)S(1)} %convert_multiply_fusion.1.u_ref), custom_call_target="tpu_custom_call" | custom-call | tf_op jit(solution)/shard_map/pallas_call | solution.py:153
  77.3 3.3 collective-permute-start.9
  80.6 4.4 collective-permute-start.8
  106.7 3.0 collective-permute-start.1
  109.8 4.4 collective-permute-start.10
  114.5 8.7 %collective-permute-done.10 = f32[16,8,128]{2,1,0:T(8,128)S(1)} collective-permute-done((f32[16,8,128]{2,1,0:T(8,128)S(1)}, f32[16,8,128]{2,1,0:T(8,128)S(1)}, u32[]{:S(2)}, u32[]{:S(2)}) %collective-permute-start.10) | collective-permute-done | bytes 65568 | tf_op jit(solution)/shard_map/ppermute | solution.py:39
  128.0 6.2 collective-permute-done
  134.2 3.2 collective-permute-start.17
  141.3 9.0 %collective-permute-done.17.a1 = bf16[3,3,32,1024]{3,2,1,0:T(8,128)(2,1)S(1)} collective-permute-done((bf16[3,3,32,1024]{3,2,1,0:T(8,128)(2,1)S(1)}, bf16[3,3,32,1024]{3,2,1,0:T(8,128)(2,1)S(1)}, u32[]{:S(2)}, u32[]{:S(2)}) %collective-permute-start.17) | collective-permute-done | bytes 589856 | tf_op jit(solution)/shard_map/ppermute | solution.py:33
  151.2 11.8 %collective-permute-done.19.a3 = bf16[3,3,32,1024]{3,2,1,0:T(8,128)(2,1)S(1)} collective-permute-done((bf16[3,3,32,1024]{3,2,1,0:T(8,128)(2,1)S(1)}, bf16[3,3,32,1024]{3,2,1,0:T(8,128)(2,1)S(1)}, u32[]{:S(2)}, u32[]{:S(2)}) %collective-permute-start.19) | collective-permute-done | bytes 589856 | tf_op jit(solution)/shard_map/ppermute | solution.py:33
  163.8 24.7 %shard_map.258 = (f32[512,1024]{1,0:T(8,128)}, bf16[512,1024]{1,0:T(8,128)(2,1)S(1)}, bf16[1024,512]{1,0:T(8,128)(2,1)S(1)}, bf16[1024,512]{1,0:T(8,128)(2,1)}, ...) custom-call(s32[3]{0:T(128)S(1)} %pad_add_fusion.place, ...), custom_call_target="tpu_custom_call" | custom-call | tf_op jit(solution)/shard_map/pallas_call | solution.py:507
  198.1 3.3 shard_map.259
  203.0 11.5 %collective-permute-done.30.h2 = bf16[3,128,1024]{2,1,0:T(8,128)(2,1)S(1)} collective-permute-done((bf16[3,128,1024]{2,1,0:T(8,128)(2,1)S(1)}, bf16[3,128,1024]{2,1,0:T(8,128)(2,1)S(1)}, u32[]{:S(2)}, u32[]{:S(2)}) %collective-permute-start.30) | collective-permute-done | bytes 786464 | tf_op jit(solution)/shard_map/ppermute | solution.py:33
  216.9 15.2 %collective-permute-done.29.h1 = bf16[3,128,1024]{2,1,0:T(8,128)(2,1)S(1)} collective-permute-done((bf16[3,128,1024]{2,1,0:T(8,128)(2,1)S(1)}, bf16[3,128,1024]{2,1,0:T(8,128)(2,1)S(1)}, u32[]{:S(2)}, u32[]{:S(2)}) %collective-permute-start.29) | collective-permute-done | bytes 786464 | tf_op jit(solution)/shard_map/ppermute | solution.py:33
  232.1 16.8 %collective-permute-done.31.h3 = bf16[3,128,1024]{2,1,0:T(8,128)(2,1)S(1)} collective-permute-done((bf16[3,128,1024]{2,1,0:T(8,128)(2,1)S(1)}, bf16[3,128,1024]{2,1,0:T(8,128)(2,1)S(1)}, u32[]{:S(2)}, u32[]{:S(2)}) %collective-permute-start.31) | collective-permute-done | bytes 786464 | tf_op jit(solution)/shard_map/ppermute | solution.py:33
  249.9 29.4 %shard_map.260 = (f32[512,1024]{1,0:T(8,128)}, bf16[512,1024]{1,0:T(8,128)(2,1)S(1)}, f32[512,1024]{1,0:T(8,128)}, bf16[512,1024]{1,0:T(8,128)(2,1)S(1)}, bf16[1...) custom-call(s32[3]{0:T(128)S(1)} %pad_add_fusion.place, bf16[512,1024]{1,0:T(8,128)(2,1)S(1)} %get-tuple-element.89.m0, ...), custom_call_target="tpu_custom_call" | custom-call | tf_op jit(solution)/shard_map/pallas_call | solution.py:507
  285.7 5.1 shard_map.262
  298.6 13.4 %shard_map.263 = (bf16[2,4,128,1024]{3,2,1,0:T(8,128)(2,1)S(1)}, bf16[2,4,128,1024]{3,2,1,0:T(8,128)(2,1)}, bf16[2,4,128,1024]{3,2,1,0:T(8,128)(2,1)}, bf16[2,4,128,1024]{3,2,1,0:T(8,128)(2,1)}) custom-call(s32[3]{0:T(128)S(1)} %pad_add_fusion.place, bf16[512,1024]{1,0:T(8,128)(2,1)S(1)} %copy-done.9, bf16[512,1024]{1,0:T(8,128)(2,1)S(1)} %copy-done.11, ...), custom_call_target="tpu_custom_call" | custom-call | tf_op jit(solution)/shard_map/pallas_call | solution.py:507
  314.8 25.8 %shard_map.264 = (f32[512,1024]{1,0:T(8,128)}, bf16[512,1024]{1,0:T(8,128)(2,1)S(1)}, f32[128,1024]{1,0:T(8,128)S(1)}, bf16[128,1024]{1,0:T(8,128)(2,1)S(1)}, bf...) custom-call(s32[3]{0:T(128)S(1)} %pad_add_fusion.place, bf16[512,1024]{1,0:T(8,128)(2,1)} %get-tuple-element.99.g0, ...), custom_call_target="tpu_custom_call" | custom-call | tf_op jit(solution)/shard_map/pallas_call | solution.py:507
  349.8 12.5 %collective-permute-done.41 = f32[16,8,128]{2,1,0:T(8,128)S(1)} collective-permute-done((f32[16,8,128]{2,1,0:T(8,128)S(1)}, f32[16,8,128]{2,1,0:T(8,128)S(1)}, u32[]{:S(2)}, u32[]{:S(2)}) %collective-permute-start.41) | collective-permute-done | bytes 65568 | tf_op jit(solution)/shard_map/ppermute | solution.py:39
  377.8 3.0 collective-permute-start.44
  380.8 21.8 %collective-permute-done.44 = bf16[128,1024]{1,0:T(8,128)(2,1)S(1)} collective-permute-done((bf16[128,1024]{1,0:T(8,128)(2,1)S(1)}, bf16[128,1024]{1,0:T(8,128)(2,1)S(1)}, u32[]{:S(2)}, u32[]{:S(2)}) %collective-permute-start.44) | collective-permute-done | bytes 262176 | tf_op jit(solution)/shard_map/ppermute | solution.py:39
  402.7 4.7 shard_map.266
  409.7 4.2 shard_map.267
  418.5 46.5 %all_to_all.20 = bf16[4,2,128,1024]{3,2,1,0:T(8,128)(2,1)} all-to-all(bf16[4,2,128,1024]{3,2,1,0:T(8,128)(2,1)S(1)} %copy.71), channel_id=1, replica_groups=mesh['seq'=8,'tp'=4] {'tp'}, dimensions={0} | all-to-all | bytes 4194304 | tf_op jit(solution)/shard_map/all_to_all | solution.py:1126
  464.9 3.1 reduce_sum.75
  470.5 10.1 %shard_map.269 = (bf16[2,4,3,32,1024]{4,3,2,1,0:T(8,128)(2,1)S(1)}, bf16[2,4,3,32,1024]{4,3,2,1,0:T(8,128)(2,1)}, bf16[2,4,3,32,1024]{4,3,2,1,0:T(8,128)(2,1)}, bf16[2,4,3,32,1024]{4,3,2,1,0:T(8,128)(2,1)}) custom-call(s32[3]{0:T(128)S(1)} %pad_add_fusion.place, bf16[512,1024]{1,0:T(8,128)(2,1)S(1)} %copy-done.1, bf16[512,1024]{1,0:T(8,128)(2,1)S(1)} %copy-done.5, ...), custom_call_target="tpu_custom_call" | custom-call | tf_op jit(solution)/shard_map/pallas_call | solution.py:507
  481.8 5.0 collective-permute-start.53
  486.8 5.5 shard_map.268
  492.6 3.3 collective-permute-start.46
  495.9 37.4 %collective-permute-done.53 = bf16[2,4,3,32,1024]{4,3,2,1,0:T(8,128)(2,1)} collective-permute-done((bf16[2,4,3,32,1024]{4,3,2,1,0:T(8,128)(2,1)}, bf16[2,4,3,32,1024]{4,3,2,1,0:T(8,128)(2,1)}, u32[]{:S(2)}, u32[]{:S(2)}) %collective-permute-start.53) | collective-permute-done | bytes 1572896 | tf_op jit(solution)/shard_map/ppermute | solution.py:33
  540.2 3.0 collective-permute-start.45
  544.1 5.6 all-to-all-start.1
  549.7 3.2 collective-permute-start.47
  562.3 14.1 %all-to-all-done.1 = f32[32,24,128]{2,1,0:T(8,128)S(1)} async-done(((f32[32,24,128]{2,1,0:T(8,128)}), f32[32,24,128]{2,1,0:T(8,128)S(1)}, u32[]{:S(2)}, u32[]{:S(2)}) %all-to-all-start.1) | async-done | bytes 393248 | tf_op jit(solution)/shard_map/all_to_all | solution.py:1160
  576.4 3.9 all-to-all-start.2
  580.4 3.1 collective-permute-start.49
  585.1 51.1 %collective-permute-done.49 = bf16[512,1024]{1,0:T(8,128)(2,1)} collective-permute-done((bf16[512,1024]{1,0:T(8,128)(2,1)S(1)}, bf16[512,1024]{1,0:T(8,128)(2,1)}, u32[]{:S(2)}, u32[]{:S(2)}) %collective-permute-start.49) | collective-permute-done | bytes 1048608 | tf_op jit(solution)/shard_map/ppermute | solution.py:47
  647.1 11.0 %collective-permute-done.50 = bf16[512,1024]{1,0:T(8,128)(2,1)} collective-permute-done((bf16[512,1024]{1,0:T(8,128)(2,1)}, bf16[512,1024]{1,0:T(8,128)(2,1)}, u32[]{:S(2)}, u32[]{:S(2)}) %collective-permute-start.50) | collective-permute-done | bytes 1048608 | tf_op jit(solution)/shard_map/ppermute | solution.py:47
  660.3 3.2 collective-permute-start.58
  665.8 3.8 maximum_convert_fusion
  669.6 4.8 shard_map.270
  676.5 4.7 shard_map.271
  (404 shorter events, 172.6 us)
Async XLA Ops:
  18.2 29.2 %collective-permute-start.22 = (bf16[3,32,1024]{2,1,0:T(8,128)(2,1)}, bf16[3,32,1024]{2,1,0:T(8,128)(2,1)S(1)}, u32[]{:S(2)}, u32[]{:S(2)}) collective-permute-start(bf16[3,32,1024]{2,1,0:T(8,128)(2,1)} %slice_bitcast_fusion.2), channel_id=1, source_target_pairs={{0,3},{1,0},{2,1},{3,2},{4,7},{5,4},{6,5},{7,6},{8,11},{9,8},{10,9... | collective-permute-start | bytes 589832 | tf_op jit(solution)/shard_map/ppermute | solution.py:524
  18.3 30.3 %collective-permute-start.21 = (bf16[3,32,1024]{2,1,0:T(8,128)(2,1)}, bf16[3,32,1024]{2,1,0:T(8,128)(2,1)}, u32[]{:S(2)}, u32[]{:S(2)}) collective-permute-start(bf16[3,32,1024]{2,1,0:T(8,128)(2,1)} %slice_bitcast_fusion.2), channel_id=1, source_target_pairs={{0,2},{1,3},{2,0},{3,1},{4,6},{5,7},{6,4},{7,5},{8,10},{9,11},{10,... | collective-permute-start | bytes 589832 | tf_op jit(solution)/shard_map/ppermute | solution.py:524
  21.6 30.7 %collective-permute-start.20 = (bf16[3,32,1024]{2,1,0:T(8,128)(2,1)}, bf16[3,32,1024]{2,1,0:T(8,128)(2,1)}, u32[]{:S(2)}, u32[]{:S(2)}) collective-permute-start(bf16[3,32,1024]{2,1,0:T(8,128)(2,1)} %slice_bitcast_fusion.2), channel_id=1, source_target_pairs={{0,1},{1,2},{2,3},{3,0},{4,5},{5,6},{6,7},{7,4},{8,9},{9,10},{10,1... | collective-permute-start | bytes 589832 | tf_op jit(solution)/shard_map/ppermute | solution.py:524
  22.2 55.0 %collective-permute-start.16 = (bf16[3,32,1024]{2,1,0:T(8,128)(2,1)}, bf16[3,32,1024]{2,1,0:T(8,128)(2,1)}, u32[]{:S(2)}, u32[]{:S(2)}) collective-permute-start(bf16[3,32,1024]{2,1,0:T(8,128)(2,1)} %slice_bitcast_fusion.3), channel_id=1, source_target_pairs={{0,3},{1,0},{2,1},{3,2},{4,7},{5,4},{6,5},{7,6},{8,11},{9,8},{10,9... | collective-permute-start | bytes 589832 | tf_op jit(solution)/shard_map/ppermute | solution.py:524
  23.7 53.6 %collective-permute-start.15 = (bf16[3,32,1024]{2,1,0:T(8,128)(2,1)}, bf16[3,32,1024]{2,1,0:T(8,128)(2,1)}, u32[]{:S(2)}, u32[]{:S(2)}) collective-permute-start(bf16[3,32,1024]{2,1,0:T(8,128)(2,1)} %slice_bitcast_fusion.3), channel_id=1, source_target_pairs={{0,2},{1,3},{2,0},{3,1},{4,6},{5,7},{6,4},{7,5},{8,10},{9,11},{10,... | collective-permute-start | bytes 589832 | tf_op jit(solution)/shard_map/ppermute | solution.py:524
  26.3 36.2 %all-to-all-start = ((f32[32,8,128]{2,1,0:T(8,128)}), f32[32,8,128]{2,1,0:T(8,128)S(1)}, u32[]{:S(2)}, u32[]{:S(2)}) async-start(f32[32,8,128]{2,1,0:T(8,128)} %broadcast_in_dim.11), calls=%async_computation | async-start | bytes 262144 | tf_op jit(solution)/shard_map/all_to_all | solution.py:966
  32.7 636.8 %all-gather.5.cloned.1.call-start = ((), (), s32[]{:S(2)}) async-start(), calls=%async_computation.4 | async-start | bytes 5242880 | tf_op jit(solution)/shard_map/all_gather | solution.py:1040
  47.4 33.2 %collective-permute-start.14 = (bf16[3,32,1024]{2,1,0:T(8,128)(2,1)}, bf16[3,32,1024]{2,1,0:T(8,128)(2,1)}, u32[]{:S(2)}, u32[]{:S(2)}) collective-permute-start(bf16[3,32,1024]{2,1,0:T(8,128)(2,1)} %slice_bitcast_fusion.3), channel_id=1, source_target_pairs={{0,1},{1,2},{2,3},{3,0},{4,5},{5,6},{6,7},{7,4},{8,9},{9,10},{10,1... | collective-permute-start | bytes 589832 | tf_op jit(solution)/shard_map/ppermute | solution.py:524
  52.3 53.2 %collective-permute-start.5 = (bf16[128,1024]{1,0:T(8,128)(2,1)}, bf16[128,1024]{1,0:T(8,128)(2,1)}, u32[]{:S(2)}, u32[]{:S(2)}) collective-permute-start(bf16[128,1024]{1,0:T(8,128)(2,1)} %slice_bitcast_fusion), channel_id=1, source_target_pairs={{0,3},{1,0},{2,1},{3,2},{4,7},{5,4},{6,5},{7,6},{8,11},{9,8},{10,9... | collective-permute-start | bytes 786440 | tf_op jit(solution)/shard_map/ppermute | solution.py:524
  64.3 42.4 %collective-permute-start.4 = (bf16[128,1024]{1,0:T(8,128)(2,1)}, bf16[128,1024]{1,0:T(8,128)(2,1)}, u32[]{:S(2)}, u32[]{:S(2)}) collective-permute-start(bf16[128,1024]{1,0:T(8,128)(2,1)} %slice_bitcast_fusion), channel_id=1, source_target_pairs={{0,2},{1,3},{2,0},{3,1},{4,6},{5,7},{6,4},{7,5},{8,10},{9,11},{10,... | collective-permute-start | bytes 786440 | tf_op jit(solution)/shard_map/ppermute | solution.py:524
  77.2 32.5 %collective-permute-start.3 = (bf16[128,1024]{1,0:T(8,128)(2,1)}, bf16[128,1024]{1,0:T(8,128)(2,1)}, u32[]{:S(2)}, u32[]{:S(2)}) collective-permute-start(bf16[128,1024]{1,0:T(8,128)(2,1)} %slice_bitcast_fusion), channel_id=1, source_target_pairs={{0,1},{1,2},{2,3},{3,0},{4,5},{5,6},{6,7},{7,4},{8,9},{9,10},{10,1... | collective-permute-start | bytes 786440 | tf_op jit(solution)/shard_map/ppermute | solution.py:524
  77.3 24.3 %collective-permute-start.9 = (f32[16,8,128]{2,1,0:T(8,128)S(1)}, f32[16,8,128]{2,1,0:T(8,128)}, u32[]{:S(2)}, u32[]{:S(2)}) collective-permute-start(f32[16,8,128]{2,1,0:T(8,128)S(1)} %get-tuple-element.83), channel_id=1, source_target_pairs={{0,8},{4,12},{8,16},{12,20},{16,24},{20,28},{1,9},{5,13},{9,17},{1... | collective-permute-start | bytes 196616 | tf_op jit(solution)/shard_map/ppermute | solution.py:39
  80.6 21.1 %collective-permute-start.8 = (f32[16,8,128]{2,1,0:T(8,128)S(1)}, f32[16,8,128]{2,1,0:T(8,128)}, u32[]{:S(2)}, u32[]{:S(2)}) collective-permute-start(f32[16,8,128]{2,1,0:T(8,128)S(1)} %get-tuple-element.83), channel_id=1, source_target_pairs={{0,4},{4,8},{8,12},{12,16},{16,20},{20,24},{24,28},{1,5},{5,9},{9,... | collective-permute-start | bytes 196616 | tf_op jit(solution)/shard_map/ppermute | solution.py:39
  105.5 21.3 %collective-permute-start.2 = (bf16[128,1024]{1,0:T(8,128)(2,1)}, bf16[128,1024]{1,0:T(8,128)(2,1)S(1)}, u32[]{:S(2)}, u32[]{:S(2)}) collective-permute-start(bf16[128,1024]{1,0:T(8,128)(2,1)} %slice_bitcast_fusion.1), channel_id=1, source_target_pairs={{0,3},{1,0},{2,1},{3,2},{4,7},{5,4},{6,5},{7,6},{8,11},{9,8},{10,9... | collective-permute-start | bytes 786440 | tf_op jit(solution)/shard_map/ppermute | solution.py:524
  106.7 20.5 %collective-permute-start.1 = (bf16[128,1024]{1,0:T(8,128)(2,1)}, bf16[128,1024]{1,0:T(8,128)(2,1)S(1)}, u32[]{:S(2)}, u32[]{:S(2)}) collective-permute-start(bf16[128,1024]{1,0:T(8,128)(2,1)} %slice_bitcast_fusion.1), channel_id=1, source_target_pairs={{0,2},{1,3},{2,0},{3,1},{4,6},{5,7},{6,4},{7,5},{8,10},{9,11},{10,... | collective-permute-start | bytes 786440 | tf_op jit(solution)/shard_map/ppermute | solution.py:524
  109.7 28.8 %collective-permute-start.18 = (bf16[3,3,32,1024]{3,2,1,0:T(8,128)(2,1)S(1)}, bf16[3,3,32,1024]{3,2,1,0:T(8,128)(2,1)S(1)}, u32[]{:S(2)}, u32[]{:S(2)}) collective-permute-start(bf16[3,3,32,1024]{3,2,1,0:T(8,128)(2,1)S(1)} %pad_maximum_fusion.5.a0), channel_id=1, source_target_pairs={{0,16},{4,20},{8,24},{12,28},{16,0},{20,4},{24,8},{28,12},{1,17},{... | collective-permute-start | bytes 1769480 | tf_op jit(solution)/shard_map/ppermute | solution.py:33
  109.7 30.1 %collective-permute-start.23 = (bf16[3,3,32,1024]{3,2,1,0:T(8,128)(2,1)S(1)}, bf16[3,3,32,1024]{3,2,1,0:T(8,128)(2,1)S(1)}, u32[]{:S(2)}, u32[]{:S(2)}) collective-permute-start(bf16[3,3,32,1024]{3,2,1,0:T(8,128)(2,1)S(1)} %pad_maximum_fusion.6.b0), channel_id=1, source_target_pairs={{0,8},{4,12},{8,0},{12,4},{16,24},{20,28},{24,16},{28,20},{1,9},{5... | collective-permute-start | bytes 1769480 | tf_op jit(solution)/shard_map/ppermute | solution.py:33
  123.2 28.0 %collective-permute-start.6 = (bf16[512,1024]{1,0:T(8,128)(2,1)S(1)}, bf16[512,1024]{1,0:T(8,128)(2,1)S(1)}, u32[]{:S(2)}, u32[]{:S(2)}) collective-permute-start(bf16[512,1024]{1,0:T(8,128)(2,1)S(1)} %fusion.5.x0), channel_id=1, source_target_pairs={{0,4},{4,0},{8,12},{12,8},{16,20},{20,16},{24,28},{28,24},{1,5},{5... | collective-permute-start | bytes 3145736 | tf_op jit(solution)/shard_map/ppermute | solution.py:33
  138.5 24.5 %collective-permute-start.19 = (bf16[3,3,32,1024]{3,2,1,0:T(8,128)(2,1)S(1)}, bf16[3,3,32,1024]{3,2,1,0:T(8,128)(2,1)S(1)}, u32[]{:S(2)}, u32[]{:S(2)}) collective-permute-start(bf16[3,3,32,1024]{3,2,1,0:T(8,128)(2,1)S(1)} %collective-permute-done.18.a2), channel_id=1, source_target_pairs={{0,8},{4,12},{8,0},{12,4},{16,24},{20,28},{24,16},{28,20},{1,9},{5... | collective-permute-start | bytes 1769480 | tf_op jit(solution)/shard_map/ppermute | solution.py:33
  139.8 24.0 %collective-permute-start.25 = (bf16[3,3,32,1024]{3,2,1,0:T(8,128)(2,1)S(1)}, bf16[3,3,32,1024]{3,2,1,0:T(8,128)(2,1)S(1)}, u32[]{:S(2)}, u32[]{:S(2)}) collective-permute-start(bf16[3,3,32,1024]{3,2,1,0:T(8,128)(2,1)S(1)} %collective-permute-done.23.b1), channel_id=1, source_target_pairs={{0,16},{4,20},{8,24},{12,28},{16,0},{20,4},{24,8},{28,12},{1,17},{... | collective-permute-start | bytes 1769480 | tf_op jit(solution)/shard_map/ppermute | solution.py:33
  201.4 47.5 %collective-permute-start.27 = (bf16[512,1024]{1,0:T(8,128)(2,1)S(1)}, bf16[512,1024]{1,0:T(8,128)(2,1)S(1)}, u32[]{:S(2)}, u32[]{:S(2)}) collective-permute-start(bf16[512,1024]{1,0:T(8,128)(2,1)S(1)} %get-tuple-element.89.m0), channel_id=1, source_target_pairs={{0,4},{4,0},{8,12},{12,8},{16,20},{20,16},{24,28},{28,24},{1,5},{5... | collective-permute-start | bytes 3145736 | tf_op jit(solution)/shard_map/ppermute | solution.py:33
  202.4 29.7 %collective-permute-start.29 = (bf16[3,128,1024]{2,1,0:T(8,128)(2,1)S(1)}, bf16[3,128,1024]{2,1,0:T(8,128)(2,1)S(1)}, u32[]{:S(2)}, u32[]{:S(2)}) collective-permute-start(bf16[3,128,1024]{2,1,0:T(8,128)(2,1)S(1)} %pad_maximum_fusion.3.h0), channel_id=1, source_target_pairs={{0,8},{4,12},{8,0},{12,4},{16,24},{20,28},{24,16},{28,20},{1,9},{5... | collective-permute-start | bytes 2359304 | tf_op jit(solution)/shard_map/ppermute | solution.py:33
  202.6 29.5 %collective-permute-start.33 = (bf16[3,128,1024]{2,1,0:T(8,128)(2,1)S(1)}, bf16[3,128,1024]{2,1,0:T(8,128)(2,1)S(1)}, u32[]{:S(2)}, u32[]{:S(2)}) collective-permute-start(bf16[3,128,1024]{2,1,0:T(8,128)(2,1)S(1)} %pad_maximum_fusion.4.r0), channel_id=1, source_target_pairs={{0,16},{4,20},{8,24},{12,28},{16,0},{20,4},{24,8},{28,12},{1,17},{... | collective-permute-start | bytes 2359304 | tf_op jit(solution)/shard_map/ppermute | solution.py:33
  214.5 34.5 %collective-permute-start.31 = (bf16[3,128,1024]{2,1,0:T(8,128)(2,1)S(1)}, bf16[3,128,1024]{2,1,0:T(8,128)(2,1)S(1)}, u32[]{:S(2)}, u32[]{:S(2)}) collective-permute-start(bf16[3,128,1024]{2,1,0:T(8,128)(2,1)S(1)} %collective-permute-done.30.h2), channel_id=1, source_target_pairs={{0,8},{4,12},{8,0},{12,4},{16,24},{20,28},{24,16},{28,20},{1,9},{5... | collective-permute-start | bytes 2359304 | tf_op jit(solution)/shard_map/ppermute | solution.py:33
  215.4 33.5 %collective-permute-start.34 = (bf16[3,128,1024]{2,1,0:T(8,128)(2,1)S(1)}, bf16[3,128,1024]{2,1,0:T(8,128)(2,1)S(1)}, u32[]{:S(2)}, u32[]{:S(2)}) collective-permute-start(bf16[3,128,1024]{2,1,0:T(8,128)(2,1)S(1)} %collective-permute-done.32.r1), channel_id=1, source_target_pairs={{0,16},{4,20},{8,24},{12,28},{16,0},{20,4},{24,8},{28,12},{1,17},{... | collective-permute-start | bytes 2359304 | tf_op jit(solution)/shard_map/ppermute | solution.py:33
  292.2 22.5 %collective-permute-start.37 = (bf16[512,1024]{1,0:T(8,128)(2,1)}, bf16[512,1024]{1,0:T(8,128)(2,1)}, u32[]{:S(2)}, u32[]{:S(2)}) collective-permute-start(bf16[512,1024]{1,0:T(8,128)(2,1)} %get-tuple-element.99.g0), channel_id=1, source_target_pairs={{0,4},{4,0},{8,12},{12,8},{16,20},{20,16},{24,28},{28,24},{1,5},{5... | collective-permute-start | bytes 3145736 | tf_op jit(solution)/shard_map/ppermute | solution.py:33
  313.4 58.4 %collective-permute-start.64 = (bf16[2,4,128,1024]{3,2,1,0:T(8,128)(2,1)}, bf16[2,4,128,1024]{3,2,1,0:T(8,128)(2,1)}, u32[]{:S(2)}, u32[]{:S(2)}) collective-permute-start(bf16[2,4,128,1024]{3,2,1,0:T(8,128)(2,1)} %get-tuple-element.141), channel_id=1, source_target_pairs={{0,16},{4,20},{8,24},{12,28},{16,0},{20,4},{24,8},{28,12},{1,17},{... | collective-permute-start | bytes 6291464 | tf_op jit(solution)/shard_map/ppermute | solution.py:33
  313.8 62.2 %collective-permute-start.62 = (bf16[2,4,128,1024]{3,2,1,0:T(8,128)(2,1)}, bf16[2,4,128,1024]{3,2,1,0:T(8,128)(2,1)}, u32[]{:S(2)}, u32[]{:S(2)}) collective-permute-start(bf16[2,4,128,1024]{3,2,1,0:T(8,128)(2,1)} %get-tuple-element.137), channel_id=1, source_target_pairs={{0,8},{4,12},{8,0},{12,4},{16,24},{20,28},{24,16},{28,20},{1,9},{5... | collective-permute-start | bytes 6291464 | tf_op jit(solution)/shard_map/ppermute | solution.py:33
  343.1 331.3 %all-gather.7.cloned.1.call-start = ((), (), s32[]{:S(2)}) async-start(), calls=%async_computation.5 | async-start | bytes 4718592 | tf_op jit(solution)/shard_map/all_gather | solution.py:1133
  370.1 37.7 %collective-permute-start.38 = (bf16[512,1024]{1,0:T(8,128)(2,1)}, bf16[512,1024]{1,0:T(8,128)(2,1)S(1)}, u32[]{:S(2)}, u32[]{:S(2)}) collective-permute-start(bf16[512,1024]{1,0:T(8,128)(2,1)} %copy-done.71), channel_id=1, source_target_pairs={{0,4},{4,0},{8,12},{12,8},{16,20},{20,16},{24,28},{28,24},{1,5},{5... | collective-permute-start | bytes 3145736 | tf_op jit(solution)/shard_map/ppermute | solution.py:33
  373.8 40.1 %collective-permute-start.65 = (bf16[4,128,1024]{2,1,0:T(8,128)(2,1)S(1)}, bf16[4,128,1024]{2,1,0:T(8,128)(2,1)S(1)}, u32[]{:S(2)}, u32[]{:S(2)}) collective-permute-start(bf16[4,128,1024]{2,1,0:T(8,128)(2,1)S(1)} %fusion.14), channel_id=1, source_target_pairs={{0,8},{4,12},{8,0},{12,4},{16,24},{20,28},{24,16},{28,20},{1,9},{5... | collective-permute-start | bytes 3145736 | tf_op jit(solution)/shard_map/ppermute | solution.py:33
  377.6 38.6 %collective-permute-start.63 = (bf16[4,128,1024]{2,1,0:T(8,128)(2,1)S(1)}, bf16[4,128,1024]{2,1,0:T(8,128)(2,1)S(1)}, u32[]{:S(2)}, u32[]{:S(2)}) collective-permute-start(bf16[4,128,1024]{2,1,0:T(8,128)(2,1)S(1)} %fusion.12), channel_id=1, source_target_pairs={{0,16},{4,20},{8,24},{12,28},{16,0},{20,4},{24,8},{28,12},{1,17},{... | collective-permute-start | bytes 3145736 | tf_op jit(solution)/shard_map/ppermute | solution.py:33
  377.8 24.8 %collective-permute-start.44 = (bf16[128,1024]{1,0:T(8,128)(2,1)S(1)}, bf16[128,1024]{1,0:T(8,128)(2,1)S(1)}, u32[]{:S(2)}, u32[]{:S(2)}) collective-permute-start(bf16[128,1024]{1,0:T(8,128)(2,1)S(1)} %copy-done.86), channel_id=1, source_target_pairs={{4,0},{8,4},{12,8},{16,12},{20,16},{24,20},{28,24},{5,1},{9,5},{13... | collective-permute-start | bytes 786440 | tf_op jit(solution)/shard_map/ppermute | solution.py:39
  481.8 51.5 %collective-permute-start.53 = (bf16[2,4,3,32,1024]{4,3,2,1,0:T(8,128)(2,1)}, bf16[2,4,3,32,1024]{4,3,2,1,0:T(8,128)(2,1)}, u32[]{:S(2)}, u32[]{:S(2)}) collective-permute-start(bf16[2,4,3,32,1024]{4,3,2,1,0:T(8,128)(2,1)} %get-tuple-element.127), channel_id=1, source_target_pairs={{0,16},{4,20},{8,24},{12,28},{16,0},{20,4},{24,8},{28,12},{1,17},{... | collective-permute-start | bytes 4718600 | tf_op jit(solution)/shard_map/ppermute | solution.py:33
  486.8 50.1 %collective-permute-start.51 = (bf16[2,4,3,32,1024]{4,3,2,1,0:T(8,128)(2,1)}, bf16[2,4,3,32,1024]{4,3,2,1,0:T(8,128)(2,1)}, u32[]{:S(2)}, u32[]{:S(2)}) collective-permute-start(bf16[2,4,3,32,1024]{4,3,2,1,0:T(8,128)(2,1)} %get-tuple-element.123), channel_id=1, source_target_pairs={{0,8},{4,12},{8,0},{12,4},{16,24},{20,28},{24,16},{28,20},{1,9},{5... | collective-permute-start | bytes 4718600 | tf_op jit(solution)/shard_map/ppermute | solution.py:33
  492.6 57.1 %collective-permute-start.46 = (bf16[512,1024]{1,0:T(8,128)(2,1)}, bf16[512,1024]{1,0:T(8,128)(2,1)}, u32[]{:S(2)}, u32[]{:S(2)}) collective-permute-start(bf16[512,1024]{1,0:T(8,128)(2,1)} %copy-done.54), channel_id=1, source_target_pairs={{1,0},{2,1},{3,2},{5,4},{6,5},{7,6},{9,8},{10,9},{11,10},{13,12},{... | collective-permute-start | bytes 3145736 | tf_op jit(solution)/shard_map/ppermute | solution.py:49
  535.9 19.3 %collective-permute-start.54 = (bf16[4,3,32,1024]{3,2,1,0:T(8,128)(2,1)}, bf16[4,3,32,1024]{3,2,1,0:T(8,128)(2,1)}, u32[]{:S(2)}, u32[]{:S(2)}) collective-permute-start(bf16[4,3,32,1024]{3,2,1,0:T(8,128)(2,1)} %fusion.20), channel_id=1, source_target_pairs={{0,8},{4,12},{8,0},{12,4},{16,24},{20,28},{24,16},{28,20},{1,9},{5... | collective-permute-start | bytes 2359304 | tf_op jit(solution)/shard_map/ppermute | solution.py:33
  539.2 19.8 %collective-permute-start.52 = (bf16[4,3,32,1024]{3,2,1,0:T(8,128)(2,1)}, bf16[4,3,32,1024]{3,2,1,0:T(8,128)(2,1)}, u32[]{:S(2)}, u32[]{:S(2)}) collective-permute-start(bf16[4,3,32,1024]{3,2,1,0:T(8,128)(2,1)} %fusion.18), channel_id=1, source_target_pairs={{0,16},{4,20},{8,24},{12,28},{16,0},{20,4},{24,8},{28,12},{1,17},{... | collective-permute-start | bytes 2359304 | tf_op jit(solution)/shard_map/ppermute | solution.py:33
  540.2 40.1 %collective-permute-start.45 = (bf16[512,1024]{1,0:T(8,128)(2,1)}, bf16[512,1024]{1,0:T(8,128)(2,1)S(1)}, u32[]{:S(2)}, u32[]{:S(2)}) collective-permute-start(bf16[512,1024]{1,0:T(8,128)(2,1)} %copy-done.54), channel_id=1, source_target_pairs={{0,1},{1,2},{2,3},{4,5},{5,6},{6,7},{8,9},{9,10},{10,11},{12,13},{... | collective-permute-start | bytes 3145736 | tf_op jit(solution)/shard_map/ppermute | solution.py:47
  544.1 32.3 %all-to-all-start.1 = ((f32[32,24,128]{2,1,0:T(8,128)}), f32[32,24,128]{2,1,0:T(8,128)S(1)}, u32[]{:S(2)}, u32[]{:S(2)}) async-start(f32[32,24,128]{2,1,0:T(8,128)} %pad_maximum_fusion.8), calls=%async_computation.1 | async-start | bytes 786432 | tf_op jit(solution)/shard_map/all_to_all | solution.py:1160
  549.7 33.8 %collective-permute-start.47 = (bf16[512,1024]{1,0:T(8,128)(2,1)}, bf16[512,1024]{1,0:T(8,128)(2,1)}, u32[]{:S(2)}, u32[]{:S(2)}) collective-permute-start(bf16[512,1024]{1,0:T(8,128)(2,1)} %collective-permute-done.46), channel_id=1, source_target_pairs={{1,0},{2,1},{5,4},{6,5},{9,8},{10,9},{13,12},{14,13},{17,16},{18,1... | collective-permute-start | bytes 3145736 | tf_op jit(solution)/shard_map/ppermute | solution.py:49
  576.4 67.6 %all-to-all-start.2 = ((bf16[4,2,3,32,1024]{4,3,2,1,0:T(8,128)(2,1)}), bf16[4,2,3,32,1024]{4,3,2,1,0:T(8,128)(2,1)S(1)}, u32[]{:S(2)}, u32[]{:S(2)}) async-start(bf16[4,2,3,32,1024]{4,3,2,1,0:T(8,128)(2,1)} %copy.70), calls=%async_computation.2 | async-start | bytes 3145728 | tf_op jit(solution)/shard_map/all_to_all | solution.py:1126
  580.4 55.9 %collective-permute-start.49 = (bf16[512,1024]{1,0:T(8,128)(2,1)S(1)}, bf16[512,1024]{1,0:T(8,128)(2,1)}, u32[]{:S(2)}, u32[]{:S(2)}) collective-permute-start(bf16[512,1024]{1,0:T(8,128)(2,1)S(1)} %collective-permute-done.45), channel_id=1, source_target_pairs={{1,2},{2,3},{5,6},{6,7},{9,10},{10,11},{13,14},{14,15},{17,18},{18... | collective-permute-start | bytes 3145736 | tf_op jit(solution)/shard_map/ppermute | solution.py:47
  583.5 59.5 %collective-permute-start.48 = (bf16[512,1024]{1,0:T(8,128)(2,1)}, bf16[512,1024]{1,0:T(8,128)(2,1)}, u32[]{:S(2)}, u32[]{:S(2)}) collective-permute-start(bf16[512,1024]{1,0:T(8,128)(2,1)} %collective-permute-done.47), channel_id=1, source_target_pairs={{1,0},{5,4},{9,8},{13,12},{17,16},{21,20},{25,24},{29,28}} | collective-permute-start | bytes 3145736 | tf_op jit(solution)/shard_map/ppermute | solution.py:49
  636.3 21.8 %collective-permute-start.50 = (bf16[512,1024]{1,0:T(8,128)(2,1)}, bf16[512,1024]{1,0:T(8,128)(2,1)}, u32[]{:S(2)}, u32[]{:S(2)}) collective-permute-start(bf16[512,1024]{1,0:T(8,128)(2,1)} %collective-permute-done.49), channel_id=1, source_target_pairs={{2,3},{6,7},{10,11},{14,15},{18,19},{22,23},{26,27},{30,31}} | collective-permute-start | bytes 3145736 | tf_op jit(solution)/shard_map/ppermute | solution.py:47
  644.4 19.2 %collective-permute-start.57 = (bf16[6,32,1024]{2,1,0:T(8,128)(2,1)S(1)}, bf16[6,32,1024]{2,1,0:T(8,128)(2,1)S(1)}, u32[]{:S(2)}, u32[]{:S(2)}) collective-permute-start(bf16[6,32,1024]{2,1,0:T(8,128)(2,1)S(1)} %bitcast.159), channel_id=1, source_target_pairs={{0,24},{4,28},{8,16},{12,20},{16,8},{20,12},{24,0},{28,4},{1,25},{... | collective-permute-start | bytes 1179656 | tf_op jit(solution)/shard_map/ppermute | solution.py:33
  645.4 19.4 %collective-permute-start.56 = (bf16[6,32,1024]{2,1,0:T(8,128)(2,1)S(1)}, bf16[6,32,1024]{2,1,0:T(8,128)(2,1)S(1)}, u32[]{:S(2)}, u32[]{:S(2)}) collective-permute-start(bf16[6,32,1024]{2,1,0:T(8,128)(2,1)S(1)} %bitcast.160), channel_id=1, source_target_pairs={{0,16},{4,20},{8,24},{12,28},{16,0},{20,4},{24,8},{28,12},{1,17},{... | collective-permute-start | bytes 1179656 | tf_op jit(solution)/shard_map/ppermute | solution.py:33
  646.1 19.2 %collective-permute-start.55 = (bf16[6,32,1024]{2,1,0:T(8,128)(2,1)S(1)}, bf16[6,32,1024]{2,1,0:T(8,128)(2,1)S(1)}, u32[]{:S(2)}, u32[]{:S(2)}) collective-permute-start(bf16[6,32,1024]{2,1,0:T(8,128)(2,1)S(1)} %bitcast.161), channel_id=1, source_target_pairs={{0,8},{4,12},{8,0},{12,4},{16,24},{20,28},{24,16},{28,20},{1,9},{5... | collective-permute-start | bytes 1179656 | tf_op jit(solution)/shard_map/ppermute | solution.py:33
  (117 other events, 1432.7 us)
Sparse Core Ops, SparseCore 0:
  343.2 81.8 all-gather.4
  468.1 52.1 all-gather.6

commit v2 on v1

--- a/solution.py
+++ b/solution.py
@@ -149,11 +149,12 @@
     gm_ref[...] = gm
 
 
-def call(kernel, outs, *operands):
+def call(kernel, outs, *operands, us=5):
     return pl.pallas_call(
         kernel,
         out_shape=[jax.ShapeDtypeStruct(shape, dtype) for shape, dtype in outs],
-        compiler_params=pltpu.CompilerParams(vmem_limit_bytes=44 * 2**20),
+        compiler_params=pltpu.CompilerParams(vmem_limit_bytes=42 * 2**20),
+        cost_estimate=pl.CostEstimate(flops=int(us * 1.1e9), bytes_accessed=0, transcendentals=0),
     )(*operands)
 
 
@@ -491,7 +492,11 @@
 SCALE = DH ** (-0.5)
 
 
-def params(limit=44):
+def cost(us):
+    return pl.CostEstimate(flops=int(us * 1.1e9), bytes_accessed=0, transcendentals=0)
+
+
+def params(limit=42):
     return pltpu.CompilerParams(vmem_limit_bytes=limit * 2**20)
 
 
@@ -503,7 +508,7 @@
     return pl.BlockSpec(shape, lambda *_: (0,) * len(shape))
 
 
-def launch(kernel, place, grid, in_specs, out_specs, outs, operands, scratch=(), flops=0):
+def launch(kernel, place, grid, in_specs, out_specs, outs, operands, scratch=(), us=5):
     return pl.pallas_call(
         kernel,
         grid_spec=pltpu.PrefetchScalarGridSpec(
@@ -515,8 +520,12 @@
         ),
         out_shape=outs,
         compiler_params=params(),
-        cost_estimate=pl.CostEstimate(flops=flops, bytes_accessed=0, transcendentals=0),
+        cost_estimate=cost(us),
     )(place, *operands)
+
+
+def timed(us):
+    return partial(launch, us=us)
 
 
 def cycle(value, steps):
@@ -524,47 +533,43 @@
     return lax.ppermute(value, "tp", [(i, (i + steps) % count) for i in range(count)])
 
 
-def pack_heads(place, wq, wk, wv, wsk, wsv, wo, a_ref, b_ref, turned):
-    core, chip = place[0] & 1, place[0] >> 1
-    rows = a_ref.shape[2]
-
-    def cut(p):
-        return pl.ds(pl.multiple_of((chip ^ p) * rows, rows), rows)
-
-    for out, refs in ((a_ref, (wq, wk, wv)), (b_ref, (wsk, wsv))):
-        for w, ref in enumerate(refs):
-            turned[...] = ref[...].astype(F32).T
-            for p in range(4):
-                out[p, w] = turned[cut(p), :].astype(BF16)
-    turned[...] = wo[...].astype(F32)
-    for p in range(4):
-        b_ref[p, 2] = turned[cut(p), :].astype(BF16)
-
-
-def pack_hidden(place, wh, wr, h_ref, r_ref, turned):
+def pack_heads(place, wq, wk, wv, wsk, wsv, wo, out, turned):
     chip = place[0] >> 1
-    rows = h_ref.shape[1]
-    for out, turn in ((h_ref, True), (r_ref, False)):
-        turned[...] = wh[...].astype(F32).T if turn else wr[...].astype(F32)
+    rows = out.shape[2]
+    for w, ref in enumerate((wq, wk, wv, wsk, wsv, wo)):
+        turned[...] = ref[...].astype(F32) if ref is wo else ref[...].astype(F32).T
         for p in range(4):
             cut = pl.ds(pl.multiple_of((chip ^ p) * rows, rows), rows)
-            out[p] = turned[cut, :].astype(BF16)
-
-
-def load_heads(j, own, far, into, base):
+            out[p, w] = turned[cut, :].astype(BF16)
+
+
+def pack_hidden(place, wh, wr, out, turned):
+    chip = place[0] >> 1
+    rows = out.shape[2]
+    for w, ref in enumerate((wh, wr)):
+        turned[...] = ref[...].astype(F32).T if ref is wh else ref[...].astype(F32)
+        for p in range(4):
+            cut = pl.ds(pl.multiple_of((chip ^ p) * rows, rows), rows)
+            out[p, w] = turned[cut, :].astype(BF16)
+
+
+def load_heads(j, own, far, into, first, count):
     rows = own.shape[2]
 
     @pl.when(j == 0)
     def _():
         for p in range(4):
-            for w in range(3):
-                into[base + w, p * rows : (p + 1) * rows] = own[p, w]
+            for w in range(count):
+                into[w, p * rows : (p + 1) * rows] = own[p, first + w]
 
     @pl.when(j > 0)
     def _():
         for p in range(4):
-            for w in range(3):
-                into[base + w, p * rows : (p + 1) * rows] = far[p][0, w]
+            for w in range(count):
+                if p < 3:
+                    into[w, p * rows : (p + 1) * rows] = far[p][0, first + w]
+                else:
+                    into[w, p * rows : (p + 1) * rows] = far[3 + (first + w) // 3][0, (first + w) % 3]
 
 
 def masked(raw, r, block):
@@ -575,32 +580,38 @@
     return jnp.where(keep, raw * (SCALE * LOG2E), NEGATIVE)
 
 
-def attend(place, x0, x1, c0, c1, own_a, own_b, a0, a1, a2, a3, b0, b1, b2, b3,
-           part0, part1, q_ref, k_ref, v_ref, s_ref, o_ref, lse_ref,
-           weight, keys, values, total):
+def project(place, x0, x1, own, f0, f1, f2, f3, f4, q_ref, k_ref, v_ref, weight):
     j = pl.program_id(0)
-    load_heads(j, own_a, (a0, a1, a2, a3), weight, 0)
-    load_heads(j, own_b, (b0, b1, b2, b3), weight, 3)
+    load_heads(j, own, (f0, f1, f2, f3, f4), weight, 0, 3)
     rows = x0.shape[0]
+    qkv_w = weight[0:3].reshape(3 * DH, -1)
+    for half, x in enumerate((x0, x1)):
+        saved = slice(half * rows, (half + 1) * rows)
+        qkv = dot(x[...], qkv_w, NT).astype(BF16)
+        q_ref[saved] = qkv[:, :DH]
+        k_ref[saved] = qkv[:, DH : 2 * DH]
+        v_ref[saved] = qkv[:, 2 * DH :]
+
+
+def attend(place, c0, c1, own, f0, f1, f2, f3, f4, q_ref, k_ref, v_ref,
+           part0, part1, s_ref, o_ref, lse_ref, weight, keys, values, total):
+    j = pl.program_id(0)
+    load_heads(j, own, (f0, f1, f2, f3, f4), weight, 3, 3)
+    rows = part0.shape[0]
 
     @pl.when(j == 0)
     def _():
         total[...] = jnp.zeros_like(total)
 
-    qkv_w = weight[0:3].reshape(3 * DH, -1)
-    st_w = weight[3:5].reshape(2 * DH, -1)
-    for half, (x, c) in enumerate(((x0, c0), (x1, c1))):
+    st_w = weight[0:2].reshape(2 * DH, -1)
+    for half, c in enumerate((c0, c1)):
         base = half * rows
-        qkv = dot(x[...], qkv_w, NT).astype(BF16)
-        q_ref[base : base + rows] = qkv[:, :DH]
-        k_ref[base : base + rows] = qkv[:, DH : 2 * DH]
-        v_ref[base : base + rows] = qkv[:, 2 * DH :]
         state = dot(c[...], st_w, NT).astype(BF16)
         s_ref[half * CTX : (half + 1) * CTX] = state
         keys[half, 0:CTX] = state[:, :DH]
         values[half, 0:CTX] = state[:, DH:]
-        keys[half, CTX:] = qkv[:, DH : 2 * DH]
-        values[half, CTX:] = qkv[:, 2 * DH :]
+        keys[half, CTX:] = k_ref[base : base + rows]
+        values[half, CTX:] = v_ref[base : base + rows]
     for half in range(2):
         block = place[0] ^ half
         base = half * rows
@@ -616,7 +627,7 @@
             o_ref[saved] = dot(probs, values[half, 0:n], NN).astype(BF16)
     for half in range(2):
         base = half * rows
-        total[base : base + rows] += dot(o_ref[base : base + rows], weight[5], NN)
+        total[base : base + rows] += dot(o_ref[base : base + rows], weight[2], NN)
 
     @pl.when(j == pl.num_programs(0) - 1)
     def _():
@@ -624,13 +635,12 @@
         part1[...] = total[rows:].astype(part1.dtype)
 
 
-def attend_back(place, g0, g1, own_a, own_b, a0, a1, a2, a3, b0, b1, b2, b3,
+def attend_back(place, g0, g1, own, f0, f1, f2, f3, f4,
                 q_ref, k_ref, v_ref, s_ref, lse_ref,
                 in0, in1, ctx0, ctx1, d_ref, ds_ref,
                 weight, keys, values, heads, grad_k, grad_v, total, ctx_total):
     j = pl.program_id(0)
-    load_heads(j, own_a, (a0, a1, a2, a3), weight, 0)
-    load_heads(j, own_b, (b0, b1, b2, b3), weight, 3)
+    load_heads(j, own, (f0, f1, f2, f3, f4), weight, 0, 6)
     rows = g0.shape[0]
 
     @pl.when(j == 0)
@@ -716,39 +726,48 @@
     return jnp.where(x >= 0, 1.0 - tail, tail), bell * (1.0 / math.sqrt(2.0 * math.pi))
 
 
-def load_hidden(j, own, far, into):
-    rows = own.shape[1]
+def load_hidden(j, w, own, far, into):
+    rows = own.shape[2]
 
     @pl.when(j == 0)
     def _():
         for p in range(4):
-            into[p * rows : (p + 1) * rows] = own[p]
+            into[p * rows : (p + 1) * rows] = own[p, w]
 
     @pl.when(j > 0)
     def _():
-        for p in range(4):
-            into[p * rows : (p + 1) * rows] = far[p][0]
-
-
-def feed(place, m0, m1, g0, g1, own_h, own_r, h0, h1, h2, h3, r0, r1, r2, r3,
-         mlp0, mlp1, mid0, mid1, act_ref, pre_ref, wh, wr, mlp, mid):
+        for p in range(3):
+            into[p * rows : (p + 1) * rows] = far[p][0, w]
+        into[3 * rows :] = far[3 + w][0]
+
+
+def feed_in(place, m0, m1, own, f0, f1, f2, f3, act_ref, slope_ref, wh):
+    load_hidden(pl.program_id(0), 0, own, (f0, f1, f2, f3), wh)
+    rows = m0.shape[0]
+    for half, m in enumerate((m0, m1)):
+        saved = slice(half * rows, (half + 1) * rows)
+        pre = dot(m[...], wh[...], NT)
+        part, bell = gelu_parts(pre)
+        act_ref[saved] = (pre * part).astype(BF16)
+        slope_ref[saved] = (part + pre * bell).astype(BF16)
+
+
+def feed_out(place, g0, g1, own, f0, f1, f2, f3, f4, act_ref, slope_ref,
+             mlp0, mlp1, mid0, mid1, pre_ref, wh, wr, mlp, mid):
     j = pl.program_id(0)
-    load_hidden(j, own_h, (h0, h1, h2, h3), wh)
-    load_hidden(j, own_r, (r0, r1, r2, r3), wr)
-    rows = m0.shape[0]
+    load_hidden(j, 0, own, (f0, f1, f2, f3, f4), wh)
+    load_hidden(j, 1, own, (f0, f1, f2, f3, f4), wr)
+    rows = g0.shape[0]
 
     @pl.when(j == 0)
     def _():
         mlp[...] = jnp.zeros_like(mlp)
         mid[...] = jnp.zeros_like(mid)
 
-    for half, (m, g) in enumerate(((m0, g0), (m1, g1))):
+    for half, g in enumerate((g0, g1)):
         saved = slice(half * rows, (half + 1) * rows)
-        pre = dot(m[...], wh[...], NT)
         back = dot(g[...], wr[...], NT)
-        part, bell = gelu_parts(pre)
-        act_ref[saved] = (pre * part).astype(BF16)
-        pre_ref[saved] = (back * (part + pre * bell)).astype(BF16)
+        pre_ref[saved] = (back * slope_ref[saved].astype(F32)).astype(BF16)
         mlp[saved] += dot(act_ref[saved], wr[...], NN)
         mid[saved] += dot(pre_ref[saved], wh[...], NN)
 
@@ -760,18 +779,14 @@
         mid1[...] = mid[rows:].astype(mid1.dtype)
 
 
-def feed_weights(place, m0, m1, g0, g1, act_ref, pre_ref, keep_h, send_h, keep_r, send_r):
-    rows = m0.shape[0]
-    cut = keep_h.shape[2]
-    to_h = (dot(pre_ref[0:rows], m0[...], TN) + dot(pre_ref[rows:], m1[...], TN)).astype(BF16)
-    to_r = (dot(act_ref[0:rows], g0[...], TN) + dot(act_ref[rows:], g1[...], TN)).astype(BF16)
-    spots_h = {0: (keep_h, 0), 2: (keep_h, 1), 1: (send_h, 0), 3: (send_h, 1)}
-    spots_r = {0: (keep_r, 0), 1: (keep_r, 1), 2: (send_r, 0), 3: (send_r, 1)}
+def feed_weights(keeps, place, a0, a1, b_ref, keep, send):
+    rows = a0.shape[0]
+    cut = keep.shape[2]
+    sends = [p for p in range(4) if p not in keeps]
+    grad = (dot(b_ref[0:rows], a0[...], TN) + dot(b_ref[rows:], a1[...], TN)).astype(BF16)
     for p in range(4):
-        out, at = spots_h[p]
-        out[at, 0] = to_h[p * cut : (p + 1) * cut]
-        out, at = spots_r[p]
-        out[at, 0] = to_r[p * cut : (p + 1) * cut]
+        out, at = (keep, keeps.index(p)) if p in keeps else (send, sends.index(p))
+        out[at, 0] = grad[p * cut : (p + 1) * cut]
 
 
 def live_rows(place, count):
@@ -839,12 +854,14 @@
         out[...] = rows_ref[...] if out is o else rows_ref[...].T
 
 
-def unpack_hidden(place, pieces, h, r):
-    cut = pieces.shape[2]
-    for i in range(8):
-        at = ((i & 1) * 4 + (i >> 1)) * cut
-        r[at : at + cut, :] = pieces[i, 1].astype(F32)
-        h[:, at : at + cut] = pieces[i, 0].astype(F32).T
+def unpack_hidden(place, n0, n1, n2, n3, f0, f1, f2, f3, h, r):
+    core, chip = place[0] & 1, place[0] >> 1
+    cut = n0.shape[1]
+    for other, pieces in ((0, (n0, n1, n2, n3)), (1, (f0, f1, f2, f3))):
+        for p, piece in enumerate(pieces):
+            at = pl.multiple_of((core ^ other) * 4 * cut + (chip ^ p) * cut, cut)
+            r[pl.ds(at, cut), :] = piece[1].astype(F32)
+            h[:, pl.ds(at, cut)] = piece[0].astype(F32).T
 
 
 def add(a, b):
@@ -855,13 +872,19 @@
     return lax.optimization_barrier((value, *earlier))[0]
 
 
-def states_around(local, rate, length, sign, first):
+def powers(lengths, rate_ref, *outs):
+    for length, out in zip(lengths, outs):
+        out[...] = jnp.exp(-rate_ref[...] * float(length))
+
+
+def states_around(local, power, sign, first, *earlier):
     group = local
     for m in (1, 2):
-        group = group + jnp.exp(-rate * (length * m)) * shifted(local, sign * m)
+        group = group + power[m] * shifted(local, sign * m)
+    group = after(group, *earlier)
     total = shifted(group, sign * first)
     for m in range(first + 3, 8, 3):
-        total = total + jnp.exp(-rate * (length * (m - first))) * shifted(group, sign * m)
+        total = total + power[m - first] * shifted(group, sign * m)
     return total
 
 
@@ -914,36 +937,25 @@
     place = jnp.stack([seq_index, tp_index, length]).astype(jnp.int32)
 
     column = pl.BlockSpec((features, DH), lambda i, place: (0, place[0] & 1))
-    own_a, own_b = launch(
+    (own_w,) = timed(4)(
         pack_heads, place, (1,),
         [column] * 5 + [pl.BlockSpec((DH, features), lambda i, place: (place[0] & 1, 0))],
-        [whole((4, 3, cut, features))] * 2,
-        [like((4, 3, cut, features))] * 2,
+        [whole((4, 6, cut, features))],
+        [like((4, 6, cut, features))],
         (query_weight, key_weight, value_weight, state_key_weight, state_value_weight, output_weight),
         [pltpu.VMEM((DH, features), F32)],
     )
-    own_h, own_r = launch(
+    (own_m,) = timed(5)(
         pack_hidden, place, (1,),
         [
             pl.BlockSpec((features, hidden_cols // 2), lambda i, place: (0, place[0] & 1)),
             pl.BlockSpec((hidden_cols // 2, features), lambda i, place: (place[0] & 1, 0)),
         ],
-        [whole((4, wide, features))] * 2,
-        [like((4, wide, features))] * 2,
+        [whole((4, 2, wide, features))],
+        [like((4, 2, wide, features))],
         (hidden_weight, return_weight),
         [pltpu.VMEM((hidden_cols // 2, features), F32)],
     )
-
-    def line_of(own):
-        return jnp.stack([cycle(own[0], j) for j in range(1, tp_count)])
-
-    def plane_of(line, across):
-        near = {2: flip(line, 2), 4: flip(line, 4)}
-        return [line, near[2], near[4], flip(near[6 - across], across)]
-
-    line_a, line_b, line_h, line_r = map(line_of, (own_a, own_b, own_h, own_r))
-    far_a, far_b = plane_of(line_a, 2), plane_of(line_b, 4)
-    far_h, far_r = plane_of(line_h, 2), plane_of(line_r, 4)
 
     own_tokens = lax.dynamic_index_in_dim(tokens, tp_index, 0, keepdims=False)
     own_cot = lax.dynamic_index_in_dim(cotangent, tp_index, 0, keepdims=False)
@@ -969,96 +981,140 @@
     both = jnp.transpose(both.reshape(devices, 2, channels, states), (1, 3, 0, 2))
     both = both.reshape(2, states, features // 128, 128)
     rate, gain = both[0], both[1]
-    decay = jnp.exp(-rate)
     grid = rate.shape
-    local_state, local_moment = call(scan_in, [(grid, F32)] * 2, decay, signal)
-    start = states_around(local_state, rate, block_len, 1, 1)
-    (context,) = call(scan_out, [((CTX,) + grid[1:], F32)], decay, gain, start, signal[:CTX])
+    spans = [1, block_len - CTX] + [block_len * m for m in (1, 2, 3, 6)]
+    decay, tail_power, *blocks = call(
+        partial(powers, spans), [(grid, F32)] * len(spans), rate, us=1
+    )
+    block_power = dict(zip((1, 2, 3, 6), blocks))
+
+    def line_of(own):
+        return jnp.stack([cycle(own[0], j) for j in range(1, tp_count)])
+
+    def plane_of(line, by_x, by_y, half):
+        return [line, by_x, by_y, flip(by_y[:, :half], 2), flip(by_x[:, half:], 4)]
+
+    line_w = line_of(own_w)
+    near_w = flip(line_w, 2), flip(line_w, 4)
+    far_w = plane_of(line_w, *near_w, 3)
+    line_m = line_of(after(own_m, line_w))
+    near_m = flip(line_m, 2), flip(line_m, 4)
+    far_m = plane_of(line_m, *near_m, 1)
+    far_m[3:] = [value[:, 0] for value in far_m[3:]]
+
+    local_state, local_moment = call(
+        scan_in, [(grid, F32)] * 2, decay, after(signal, line_w, own_m), us=8
+    )
+    start = states_around(after(local_state, *near_w), block_power, 1, 1)
+    (context,) = call(scan_out, [((CTX,) + grid[1:], F32)], decay, gain, start, signal[:CTX], us=3)
     context = context.reshape(CTX, features).astype(BF16)
     context_other = flip(context, 1)
 
     rows = 2 * block_len
     slots = tp_count
-    own_spec = whole((4, 3, cut, features))
-    far_spec = pl.BlockSpec(
-        (1, 3, cut, features), lambda j, place: (jnp.maximum(j - 1, 0), 0, 0, 0)
-    )
+    own_spec = whole((4, 6, cut, features))
+
+    def slot_spec(*shape):
+        return pl.BlockSpec(
+            (1, *shape, features),
+            lambda j, place: (jnp.maximum(j - 1, 0),) + (0,) * (len(shape) + 1),
+        )
+
+    weight_specs = [own_spec] + [slot_spec(6, cut)] * 3 + [slot_spec(3, cut)] * 2
+    weights = (own_w, *far_w)
     full = whole((block_len, features))
     ctx_spec = whole((CTX, features))
     head = lambda n, width: pl.BlockSpec((n, width), lambda j, place: (0, j))
     lse_spec = pl.BlockSpec((1, rows, 1), lambda j, place: (j, 0, 0))
-    weight_specs = [own_spec] * 2 + [far_spec] * 8
-    weights = (own_a, own_b, *far_a, *far_b)
-    part, part_other, q, k, v, state, mix, lse = launch(
+    q, k, v = timed(8)(
+        project, place, (slots,),
+        [full] * 2 + weight_specs,
+        [head(rows, DH)] * 3,
+        [like((rows, slots * DH))] * 3,
+        (x, x_other, *weights),
+        [pltpu.VMEM((3, DH, features), BF16)],
+    )
+    attended = timed(20)(
         attend, place, (slots,),
-        [full] * 2 + [ctx_spec] * 2 + weight_specs,
-        [full] * 2 + [head(rows, DH)] * 3 + [head(2 * CTX, 2 * DH), head(rows, DH), lse_spec],
+        [ctx_spec] * 2 + weight_specs + [head(rows, DH)] * 3,
+        [full] * 2 + [head(2 * CTX, 2 * DH), head(rows, DH), lse_spec],
         [like((block_len, features), F32), like((block_len, features))]
-        + [like((rows, slots * DH))] * 3
         + [like((2 * CTX, slots * 2 * DH)), like((rows, slots * DH)), like((slots, rows, 1), F32)],
-        (after(x, line_h, line_r), x_other, context, context_other, *weights),
+        (after(context, line_m), context_other, *weights, q, k, v),
         [
-            pltpu.VMEM((6, DH, features), BF16),
+            pltpu.VMEM((3, DH, features), BF16),
             pltpu.VMEM((2, CTX + block_len, DH), BF16),
             pltpu.VMEM((2, CTX + block_len, DH), BF16),
             pltpu.VMEM((rows, features), F32),
         ],
     )
+    part, part_other, state, mix, lse = attended
     group = 128
     steps = block_len // group
     row_spec = pl.BlockSpec((group, features), lambda i, place: (i, 0))
     seq_spec = pl.BlockSpec((1, group, features), lambda i, place: (place[1], i, 0))
     gain_spec = whole((1, features))
     mid_gain = feedforward_norm_gain.reshape(1, -1)
-    residual, m = launch(
+    residual, m = timed(4)(
         middle, place, (steps,),
         [seq_spec, row_spec, row_spec, gain_spec], [row_spec] * 2,
         [like((block_len, features), F32), like((block_len, features))],
-        (tokens, part, flip(part_other, 1), mid_gain),
+        (tokens, part, after(flip(part_other, 1), *near_m), mid_gain),
     )
     m_other = flip(m, 1)
 
-    hidden_own = whole((4, wide, features))
-    hidden_far = pl.BlockSpec(
-        (1, wide, features), lambda j, place: (jnp.maximum(j - 1, 0), 0, 0)
-    )
+    hidden_own = whole((4, 2, wide, features))
+    hidden_far = [slot_spec(2, wide)] * 3 + [slot_spec(wide)]
     chunk = 4 * wide
-    mlp, mlp_other, mid, mid_other, act, pre = launch(
-        feed, place, (slots,),
-        [full] * 4 + [hidden_own] * 2 + [hidden_far] * 8,
-        [full] * 4 + [head(rows, chunk)] * 2,
+    act, slope = timed(14)(
+        feed_in, place, (slots,),
+        [full] * 2 + [hidden_own] + hidden_far,
+        [head(rows, chunk)] * 2,
+        [like((rows, slots * chunk))] * 2,
+        (m, m_other, own_m, *far_m[:4]),
+        [pltpu.VMEM((chunk, features), BF16)],
+    )
+    mlp, mlp_other, mid, mid_other, pre = timed(21)(
+        feed_out, place, (slots,),
+        [full] * 2 + [hidden_own] + hidden_far + hidden_far[3:] + [head(rows, chunk)] * 2,
+        [full] * 4 + [head(rows, chunk)],
         [like((block_len, features), F32), like((block_len, features))] * 2
-        + [like((rows, slots * chunk))] * 2,
-        (m, m_other, grad_out, grad_out_other, own_h, own_r, *far_h, *far_r),
+        + [like((rows, slots * chunk))],
+        (grad_out, grad_out_other, own_m, *far_m, act, slope),
         [pltpu.VMEM((chunk, features), BF16)] * 2 + [pltpu.VMEM((rows, features), F32)] * 2,
     )
     mid_got, mlp_got = flip(mid_other, 1), flip(mlp_other, 1)
-    (output,) = launch(
+    grad_spec = pl.BlockSpec((2, 1, wide, features), lambda j, place: (0, j, 0, 0))
+    hidden_grads = partial(
+        launch, place=place, grid=(slots,), us=8,
+        in_specs=[full] * 2 + [head(rows, chunk)], out_specs=[grad_spec] * 2,
+        outs=[like((2, slots, wide, features))] * 2,
+    )
+    keep_r, send_r = hidden_grads(
+        partial(feed_weights, (0, 1)), operands=(grad_out, grad_out_other, after(act, pre))
+    )
+    mlp_got = after(mlp_got, keep_r)
+    mid_got = after(mid_got, keep_r)
+    (output,) = timed(3)(
         finish, place, (steps,),
         [row_spec] * 3, [row_spec], [like((block_len, features))], (residual, mlp, mlp_got),
     )
     output_all = lax.all_gather(output, "tp")
-    resid, resid_b, sums_mid = launch(
+    resid, resid_b, sums_mid = timed(5)(
         middle_back, place, (steps,),
         [row_spec] * 3 + [seq_spec, gain_spec], [row_spec] * 2 + [gain_spec],
         [
             like((block_len, features), F32), like((block_len, features)),
             like((1, features), F32),
         ],
-        (residual, mid, mid_got, cotangent, mid_gain),
+        (after(residual, output), mid, mid_got, cotangent, mid_gain),
     )
     resid_other = flip(resid_b, 1)
-    grad_spec = pl.BlockSpec(
-        (2, 1, wide, features), lambda j, place: (0, (place[1] - j + slots) % slots, 0, 0)
-    )
-    keep_h, send_h, keep_r, send_r = launch(
-        feed_weights, place, (slots,),
-        [full] * 4 + [head(rows, chunk)] * 2, [grad_spec] * 4,
-        [like((2, slots, wide, features))] * 4,
-        (m, m_other, grad_out, grad_out_other, act, after(pre, resid_b, output)),
-    )
-
-    grad_in, grad_in_other, grad_ctx, grad_ctx_other, d, ds = launch(
+    keep_h, send_h = hidden_grads(
+        partial(feed_weights, (0, 2)), operands=(m, m_other, after(pre, resid_b))
+    )
+
+    grad_in, grad_in_other, grad_ctx, grad_ctx_other, d, ds = timed(27)(
         attend_back, place, (slots,),
         [full] * 2 + weight_specs + [head(rows, DH)] * 3 + [head(2 * CTX, 2 * DH), lse_spec],
         [full] * 2 + [ctx_spec] * 2 + [head(rows, 3 * DH), head(2 * CTX, 2 * DH)],
@@ -1081,10 +1137,8 @@
     )
     grad_ctx_got = flip(grad_ctx_other, 1)
     grad_in_got = flip(grad_in_other, 1)
-    part_spec = pl.BlockSpec(
-        (2, 1, 3, cut, features), lambda j, place: (0, (place[1] - j + slots) % slots, 0, 0, 0)
-    )
-    keep_a, send_a, keep_b, send_b = launch(
+    part_spec = pl.BlockSpec((2, 1, 3, cut, features), lambda j, place: (0, j, 0, 0, 0))
+    keep_a, send_a, keep_b, send_b = timed(10)(
         attend_weights, place, (slots,),
         [full] * 2 + [ctx_spec] * 2 + [full] * 2
         + [head(rows, 3 * DH), head(2 * CTX, 2 * DH), head(rows, DH)],
@@ -1093,12 +1147,13 @@
         (x, x_other, context, context_other, resid_b, resid_other, d, ds, mix),
     )
 
+    got_r = flip(after(send_r, resid_b), 4)
+    got_h = flip(after(send_h, resid_b), 2)
     grad_context = (grad_ctx + grad_ctx_got.astype(F32)).astype(BF16)
-    grad_conv = tiles(grad_context)
+    grad_conv = tiles(after(grad_context, got_r, got_h))
     grad_later = tiles(shifted(grad_context, -1))
     (local_back,) = call(scan_back_in, [(grid, F32)], decay, grad_conv)
-    late = states_around(local_back, rate, block_len, -1, 2)
-    late = jnp.exp(-rate * (block_len - CTX)) * late
+    late = tail_power * states_around(local_back, block_power, -1, 2, keep_a)
     grad_signal, end = call(
         scan_rows, [((block_len,) + grid[1:], F32), (grid, F32)], decay, gain, late, grad_later
     )
@@ -1106,41 +1161,44 @@
     grad_gain, grad_moment = call(
         scan_sums, [(grid, F32)] * 2, decay, start, signal[:CTX], grad_conv
     )
-    end_moment = block_len * jnp.exp(-rate * block_len) * start + local_moment
+    end_moment = block_len * block_power[1] * start + local_moment
     grad_rate = -gain * (grad_moment + end * end_moment)
-    grad_tokens, sums_in = launch(
+    grad_tokens, sums_in = timed(5)(
         first_back, place, (steps,),
         [seq_spec] + [row_spec] * 4 + [gain_spec], [row_spec, gain_spec],
         [like((block_len, features)), like((1, features), F32)],
-        (tokens, grad_in, grad_in_got, grad_signal, resid, attention_norm_gain.reshape(1, -1)),
-    )
-
-    def reduce(keep_first, send_first, keep_second, send_second, begin, then):
-        got = after(flip(after(send_first, begin), 2), then)
+        (tokens, grad_in, grad_in_got, grad_signal, after(resid, output_all), attention_norm_gain.reshape(1, -1)),
+    )
+
+    def plane_sum(keep_first, got_first, keep_second, got_second, then, end):
+        got = after(got_first, *then)
         near, away = add(keep_first[0], got[0]), add(keep_first[1], got[1])
-        first = (near, flip(away, 4))
-        got = after(flip(after(send_second, begin), 4), then)
+        first = (near, after(flip(away, 4), *end))
+        got = after(got_second, *then)
         near, away = add(keep_second[0], got[0]), add(keep_second[1], got[1])
-        second = (near, flip(away, 2))
-        chunks = jnp.stack([add(*first), add(*second)], axis=1)
-        chunks = lax.all_to_all(after(chunks, grad_tokens), "tp", 0, 0)
-        return jnp.sum(chunks.astype(F32), axis=0).astype(BF16)
+        second = (near, after(flip(away, 2), *end))
+        return [
+            jnp.stack([add(a[j], b[j]) for a, b in (first, second)]) for j in range(slots)
+        ]
 
     def regather(total):
         held = [total, flip(total, 2), flip(total, 4), flip(total, 6)]
         return held + [flip(value, 1) for value in held]
 
-    pieces_m = lax.all_gather(reduce(keep_h, send_h, keep_r, send_r, resid_b, late), "seq")
-    total_a = reduce(keep_a, send_a, keep_b, send_b, late, grad_tokens)
+    ready = (late, grad_later)
+    got_a, got_b = flip(after(send_a, *ready), 2), flip(after(send_b, *ready), 4)
+    total_m = line_reduce(plane_sum(keep_h, got_h, keep_r, got_r, ready, (grad_tokens,)))
+    pieces_m = regather(total_m)
+    total_a = line_reduce(plane_sum(keep_a, got_a, keep_b, got_b, (grad_tokens,), ()))
     pieces_a = regather(total_a.reshape(6, cut, features))
-    grad_hidden, grad_return = launch(
+    grad_hidden, grad_return = timed(5)(
         unpack_hidden, place, (1,),
-        [whole((8, 2, wide, features))],
+        [whole((2, wide, features))] * 8,
         [whole((features, hidden_cols)), whole((hidden_cols, features))],
         [like((features, hidden_cols), F32), like((hidden_cols, features), F32)],
-        (pieces_m,),
-    )
-    grad_q, grad_k, grad_v, grad_o, grad_sk, grad_sv = launch(
+        pieces_m,
+    )
+    grad_q, grad_k, grad_v, grad_o, grad_sk, grad_sv = timed(5)(
         unpack_heads, place, (1,),
         [whole((6, cut, features))] * 8,
         [whole((features, 2 * DH))] * 3 + [whole((2 * DH, features))] + [whole((features, 2 * DH))] * 2,
@@ -1162,14 +1220,7 @@
     kernel_grads = small[:count].reshape(channels, 2, states)
     gains = small[count:].reshape(2, features)
 
-    line = line_gather(grad_tokens)
-    stack = jnp.stack(line)
-    grad_tokens = jnp.stack(
-        [
-            lax.dynamic_index_in_dim(stack, (tp_index - b) % tp_count, 0, keepdims=False)
-            for b in range(sequences)
-        ]
-    ).astype(F32)
+    grad_tokens = lax.all_gather(grad_tokens, "tp").astype(F32)
     return (
         output_all, grad_tokens, gains[0], grad_q, grad_k, grad_v, grad_o, grad_sk, grad_sv,
         kernel_grads[:, 0], kernel_grads[:, 1], gains[1], grad_hidden, grad_return,

time: 700 us -> 598 us (0.85)
  waiting for transfers between devices: 250 us -> 154 us
  blocking collectives: 46.5 us -> 0 us
  starting transfers between devices: 106 us -> 130 us
  Pallas kernels: 153 us -> 163 us
    all_to_all x1 -> x0, blocking collectives: 46.5 us -> none  [reduce(): chunks = lax.all_to_all(after(chunks, grad_tokens), 'tp', 0, 0)]
    ppermute x6 -> x12, waiting for transfers between devices: 62.1 us -> 19.9 us  [the longest x6 18 us: line_reduce(): lax.ppermute(add(chunks[count - k], coming), 'tp', [(i, i - 1) for i in r...]
    ppermute x11, waiting for transfers between devices: 46.2 us -> 7.7 us  [shifted(): lax.ppermute(value, 'seq', [(i, i + steps) for i in range(first, last)])]
    ppermute x6 -> x12, starting transfers between devices: 16.5 us -> 47.8 us  [the longest x6 36.9 us: line_reduce(): lax.ppermute(add(chunks[count - k], coming), 'tp', [(i, i - 1) for i in r...]
    exp x12 -> x0, local copies, waits for them, and re-layouts: 15.2 us -> none  [the longest x4 7.03 us: states_around(): jnp.exp(-rate * (length * (m - first))) * shifted(group, sign * m)]
    all_to_all x1, waiting for transfers between devices: 14.1 us -> 0.01 us  [fast_body(): lax.all_to_all(jnp.concatenate([small, sums], axis=1), ('seq', 'tp'), 0, 0)]
    convert_element_type x1 -> x10, other arithmetic: 3.76 us -> 16.7 us  [the longest x6 7.06 us: line_reduce(): (a.astype(F32) + b.astype(F32)).astype(BF16)]
    another operation x10 -> x4, other arithmetic: 13.8 us -> 1.66 us  [plane_sum(): jnp.stack([add(a[j], b[j]) for a, b in (first, second)])]
  transfers between devices with their start and end apart: 71 -> 73, of which waited for: 24 -> 25; matrix products, arithmetic and copies ran while one was open for 12% -> 12% of each run, Pallas kernels for 13% -> 23%
where the time goes in v2:
time: 598 us; the launch traced here: 588 us
  Pallas kernels  163 us (27%)
  waiting for transfers between devices  154 us (26%)
  starting transfers between devices  130 us (22%)
  local copies, waits for them, and re-layouts  70.8 us (12%)
  other arithmetic  54.2 us (9%)
  between operations  15.8 us (3%)
    pallas_call x16, Pallas kernels, launch(): pl.pallas_call(kernel, grid_spec=pltpu.PrefetchScalarGridSpec(num_scalar_...  141 us
    ppermute x40, waiting for transfers between devices, flip(): return lax.ppermute(value, 'seq', [(i, i ^ mask) for i in range(count)])  103 us
    unnamed x192, local copies, waits for them, and re-layouts  46 us
    ppermute x6, starting transfers between devices, line_reduce(): lax.ppermute(add(chunks[count - k], coming), 'tp', [(i, i - 1) for i in r...  36.9 us
    ppermute x40, starting transfers between devices, flip(): return lax.ppermute(value, 'seq', [(i, i ^ mask) for i in range(count)])  31.7 us
    ppermute x11, starting transfers between devices, shifted(): lax.ppermute(value, 'seq', [(i, i + steps) for i in range(first, last)])  28.6 us
    pallas_call x6, Pallas kernels, call(): pl.pallas_call(kernel, out_shape=[jax.ShapeDtypeStruct(shape, dtype) for...  22.6 us
    ppermute x6, waiting for transfers between devices, line_reduce(): lax.ppermute(add(chunks[count - k], coming), 'tp', [(i, i - 1) for i in r...  18 us
  transfers between devices with their start and end apart: 73, of which 25 were waited for; matrix products, arithmetic and copies ran while one was open for 12% of the time, Pallas kernels for 23%

profile of v2, /device:TPU:17, one launch (start us, length us, event | category | flops | bytes accessed | tf_op | source)
XLA Modules:
  0.0 588.2 jit_solution(4809478432857288476)
XLA Ops:
  18.8 3.2 collective-permute-start.2
  22.8 6.7 %all-to-all-start = ((f32[32,8,128]{2,1,0:T(8,128)}), f32[32,8,128]{2,1,0:T(8,128)S(1)}, u32[]{:S(2)}, u32[]{:S(2)}) async-start(f32[32,8,128]{2,1,0:T(8,128)} %broadcast_in_dim.11), calls=%async_computation | async-start | bytes 262144 | tf_op jit(solution)/shard_map/all_to_all | solution.py:978
  31.2 3.3 collective-permute-start
  47.6 13.2 %all-to-all-done = f32[32,8,128]{2,1,0:T(8,128)S(1)} async-done(((f32[32,8,128]{2,1,0:T(8,128)}), f32[32,8,128]{2,1,0:T(8,128)S(1)}, u32[]{:S(2)}, u32[]{:S(2)}) %all-to-all-start) | async-done | bytes 131104 | tf_op jit(solution)/shard_map/all_to_all | solution.py:978
  72.7 3.1 collective-permute-start.12
  75.8 8.5 %shard_map.257 = (f32[16,8,128]{2,1,0:T(8,128)S(1)}, f32[16,8,128]{2,1,0:T(8,128)S(1)}) custom-call(f32[16,8,128]{2,1,0:T(8,128)S(1)} %get-tuple-element.94.decay_ref, f32[512,8,128]{2,1,0:T(8,128)S(1)} %convert_multiply_fusion.1.u_ref), custom_call_target="tpu_custom_call" | custom-call | flops 8800000000 | tf_op jit(solution)/shard_map/pallas_call | solution.py:153
  84.3 14.3 %collective-permute-done.5.f2 = bf16[3,6,32,1024]{3,2,1,0:T(8,128)(2,1)S(1)} collective-permute-done((bf16[3,6,32,1024]{3,2,1,0:T(8,128)(2,1)S(1)}, bf16[3,6,32,1024]{3,2,1,0:T(8,128)(2,1)S(1)}, u32[]{:S(2)}, u32[]{:S(2)}) %collective-permute-start.5) | collective-permute-done | bytes 1179680 | tf_op jit(solution)/shard_map/ppermute | solution.py:33
  100.9 5.5 collective-permute-start.6
  109.2 7.8 %collective-permute-done.12 = bf16[2,128,1024]{2,1,0:T(8,128)(2,1)S(1)} collective-permute-done((bf16[2,128,1024]{2,1,0:T(8,128)(2,1)S(1)}, bf16[2,128,1024]{2,1,0:T(8,128)(2,1)S(1)}, u32[]{:S(2)}, u32[]{:S(2)}) %collective-permute-start.12) | collective-permute-done | bytes 524320 | tf_op jit(solution)/shard_map/ppermute | solution.py:533
  118.3 2.7 collective-permute-done.11
  121.0 3.1 collective-permute-start.9
  124.1 4.4 collective-permute-start.8
  137.0 3.0 collective-permute-start.14
  140.0 6.3 %shard_map.259 = (bf16[1024,512]{1,0:T(8,128)(2,1)S(1)}, bf16[1024,512]{1,0:T(8,128)(2,1)S(1)}, bf16[1024,512]{1,0:T(8,128)(2,1)S(1)}) custom-call(s32[3]{0:T(128)S(1)} %pad_add_fusion.place, bf16[512,1024]{1,0:T(8,128)(2,1)S(1)} %fusion.5.x0, bf16[512,1024]{1,0:T(8,128)(2,1)S(1)} %collective-permute-done.17.x1, bf16[4,6,32,1024]{3,2,1,0:T(8,128)(2,1)S(1)} %copy-done.26, ...), custom_call_target="tpu_custom_call" | custom-call | flops 8800000000 | tf_op jit(solution)/shard_map/pallas_call | solution.py:512
  146.5 22.1 %shard_map.260 = (f32[512,1024]{1,0:T(8,128)}, bf16[512,1024]{1,0:T(8,128)(2,1)S(1)}, bf16[256,1024]{1,0:T(8,128)(2,1)S(1)}, bf16[1024,512]{1,0:T(8,128)(2,1)S(1)}, f32[4,1024,1]{2,1,0:T(8,128)}) custom-call(s32[3]{0:T(128)S(1)} %pad_add_fusion.place, bf16[128,1024]{1,0:T(8,128)(2,1)S(1)} %bitcast.185, bf16[128,1024]{1,0:T(8,128)(2,1)S(1)} %collective-permute-done.14.c1, ...), custom_call_target="tpu_custom_call" | custom-call | flops 22000001024 | tf_op jit(solution)/shard_map/pallas_call | solution.py:512
  187.8 9.5 %collective-permute-done.22 = bf16[3,1,128,1024]{3,2,0,1:T(8,128)(2,1)S(1)} collective-permute-done((bf16[3,1,128,1024]{3,2,0,1:T(8,128)(2,1)S(1)}, bf16[3,1,128,1024]{3,2,0,1:T(8,128)(2,1)S(1)}, u32[]{:S(2)}, u32[]{:S(2)}) %collective-permute-start.22) | collective-permute-done | bytes 786464 | tf_op jit(solution)/shard_map/ppermute | solution.py:33
  197.3 13.8 %shard_map.262 = (bf16[1024,2048]{1,0:T(8,128)(2,1)}, bf16[1024,2048]{1,0:T(8,128)(2,1)}) custom-call(s32[3]{0:T(128)S(1)} %pad_add_fusion.place, bf16[512,1024]{1,0:T(8,128)(2,1)S(1)} %get-tuple-element.111.m0.a0, bf16[512,1024]{1,0:T(8,128)(2,1)S(1)} %collective-permute-done.24.m1.a1, bf16[4,2,128,1024]{3,2,1,0:T(8,128)(2,1)S(1)} %shard_map.256.own, ...), custom_call_target="tpu_custom_call" | custom-call | flops 15399999488 | tf_op jit(solution)/shard_map/pallas_call | solution.py:512
  211.0 21.8 %shard_map.263 = (f32[512,1024]{1,0:T(8,128)}, bf16[512,1024]{1,0:T(8,128)(2,1)S(1)}, f32[512,1024]{1,0:T(8,128)}, bf16[512,1024]{1,0:T(8,128)(2,1)}, bf16[1024,2048]{1,0:T(8,128)(2,1)}) custom-call(s32[3]{0:T(128)S(1)} %pad_add_fusion.place, bf16[512,1024]{1,0:T(8,128)(2,1)S(1)} %fusion.6.g0.a0, bf16[512,1024]{1,0:T(8,128)(2,1)S(1)} %collective-permute-done.21.g1.a1, ...), custom_call_target="tpu_custom_call" | custom-call | flops 23100000256 | tf_op jit(solution)/shard_map/pallas_call | solution.py:512
  236.4 6.4 %shard_map.264 = (bf16[2,4,128,1024]{3,2,1,0:T(8,128)(2,1)S(1)}, bf16[2,4,128,1024]{3,2,1,0:T(8,128)(2,1)S(1)}) custom-call(s32[3]{0:T(128)S(1)} %pad_add_fusion.place, bf16[512,1024]{1,0:T(8,128)(2,1)S(1)} %fusion.6.g0.a0, bf16[512,1024]{1,0:T(8,128)(2,1)S(1)} %collective-permute-done.21.g1.a1, bf16[1024,2048]{1,0:T(8,128)(2,1)S(1)} %copy-done.63), custom_call_target="tpu_custom_call" | custom-call | flops 8800000000 | tf_op jit(solution)/shard_map/pallas_call | solution.py:512
  249.3 5.1 shard_map.266
  260.9 6.5 %shard_map.267 = (bf16[2,4,128,1024]{3,2,1,0:T(8,128)(2,1)S(1)}, bf16[2,4,128,1024]{3,2,1,0:T(8,128)(2,1)S(1)}) custom-call(s32[3]{0:T(128)S(1)} %pad_add_fusion.place, bf16[512,1024]{1,0:T(8,128)(2,1)S(1)} %copy-done.38, bf16[512,1024]{1,0:T(8,128)(2,1)S(1)} %copy-done.40, bf16[1024,2048]{1,0:T(8,128)(2,1)S(1)} %copy-done.62), custom_call_target="tpu_custom_call" | custom-call | flops 8800000000 | tf_op jit(solution)/shard_map/pallas_call | solution.py:512
  274.3 26.9 %shard_map.268 = (f32[512,1024]{1,0:T(8,128)}, bf16[512,1024]{1,0:T(8,128)(2,1)}, f32[128,1024]{1,0:T(8,128)S(1)}, bf16[128,1024]{1,0:T(8,128)(2,1)S(1)}, bf16[1...) custom-call(s32[3]{0:T(128)S(1)} %pad_add_fusion.place, bf16[512,1024]{1,0:T(8,128)(2,1)} %get-tuple-element.127.g0, ...), custom_call_target="tpu_custom_call" | custom-call | flops 29699999744 | tf_op jit(solution)/shard_map/pallas_call | solution.py:512
  305.1 9.7 %collective-permute-done.31 = bf16[2,4,128,1024]{3,2,1,0:T(8,128)(2,1)} collective-permute-done((bf16[2,4,128,1024]{3,2,1,0:T(8,128)(2,1)S(1)}, bf16[2,4,128,1024]{3,2,1,0:T(8,128)(2,1)}, u32[]{:S(2)}, u32[]{:S(2)}) %collective-permute-start.31) | collective-permute-done | bytes 2097184 | tf_op jit(solution)/shard_map/ppermute | solution.py:33
  318.0 3.1 collective-permute-start.32
  321.2 9.8 %shard_map.270 = (bf16[2,4,3,32,1024]{4,3,2,1,0:T(8,128)(2,1)S(1)}, bf16[2,4,3,32,1024]{4,3,2,1,0:T(8,128)(2,1)}, bf16[2,4,3,32,1024]{4,3,2,1,0:T(8,128)(2,1)S(1)}, bf16[2,4,3,32,1024]{4,3,2,1,0:T(8,128)(2,1)}) custom-call(s32[3]{0:T(128)S(1)} %pad_add_fusion.place, bf16[512,1024]{1,0:T(8,128)(2,1)S(1)} %fusion.5.x0, bf16[512,1024]{1,0:T(8,128)(2,1)S(1)} %copy-done.36, ...), custom_call_target="tpu_custom_call" | custom-call | flops 11000000512 | tf_op jit(solution)/shard_map/pallas_call | solution.py:512
  334.0 5.9 %collective-permute-done.35 = f32[16,8,128]{2,1,0:T(8,128)S(1)} collective-permute-done((f32[16,8,128]{2,1,0:T(8,128)S(1)}, f32[16,8,128]{2,1,0:T(8,128)S(1)}, u32[]{:S(2)}, u32[]{:S(2)}) %collective-permute-start.35) | collective-permute-done | bytes 65568 | tf_op jit(solution)/shard_map/ppermute | solution.py:39
  339.9 3.6 collective-permute-start.37
  343.7 3.8 fusion.10
  347.6 4.0 fusion.9
  353.0 5.9 %shard_map.273 = (f32[16,8,128]{2,1,0:T(8,128)S(1)}, f32[16,8,128]{2,1,0:T(8,128)S(1)}) custom-call(f32[16,8,128]{2,1,0:T(8,128)S(1)} %copy-done.65, f32[16,8,128]{2,1,0:T(8,128)S(1)} %copy-done.19, f32[128,8,128]{2,1,0:T(8,128)S(1)} %bitcast.175, f32[128,8,128]{2,1,0:T(8,128)S(1)} %bitcast.177), custom_call_target="tpu_custom_call" | custom-call | flops 5500000256 | tf_op jit(solution)/shard_map/pallas_call | solution.py:153
  359.9 4.5 shard_map.271
  370.4 5.0 shard_map.272
  375.5 25.1 %collective-permute-done.55 = bf16[4,128,1024]{2,1,0:T(8,128)(2,1)} collective-permute-done((bf16[4,128,1024]{2,1,0:T(8,128)(2,1)}, bf16[4,128,1024]{2,1,0:T(8,128)(2,1)}, u32[]{:S(2)}, u32[]{:S(2)}) %collective-permute-start.55) | collective-permute-done | bytes 1048608 | tf_op jit(solution)/shard_map/ppermute | solution.py:33
  407.6 3.3 fusion.26
  413.0 7.7 %collective-permute-done.38 = bf16[4,3,32,1024]{3,2,1,0:T(8,128)(2,1)S(1)} collective-permute-done((bf16[4,3,32,1024]{3,2,1,0:T(8,128)(2,1)S(1)}, bf16[4,3,32,1024]{3,2,1,0:T(8,128)(2,1)S(1)}, u32[]{:S(2)}, u32[]{:S(2)}) %collective-permute-start.38) | collective-permute-done | bytes 786464 | tf_op jit(solution)/shard_map/ppermute | solution.py:33
  429.6 7.6 %collective-permute-done.59 = bf16[2,128,1024]{2,1,0:T(8,128)(2,1)S(1)} collective-permute-done((bf16[2,128,1024]{2,1,0:T(8,128)(2,1)S(1)}, bf16[2,128,1024]{2,1,0:T(8,128)(2,1)S(1)}, u32[]{:S(2)}, u32[]{:S(2)}) %collective-permute-start.59) | collective-permute-done | bytes 524320 | tf_op jit(solution)/shard_map/ppermute | solution.py:62
  440.1 4.9 collective-permute-start.60
  445.3 8.8 %collective-permute-done.44 = bf16[2,3,32,1024]{3,2,1,0:T(8,128)(2,1)} collective-permute-done((bf16[2,3,32,1024]{3,2,1,0:T(8,128)(2,1)}, bf16[2,3,32,1024]{3,2,1,0:T(8,128)(2,1)}, u32[]{:S(2)}, u32[]{:S(2)}) %collective-permute-start.44) | collective-permute-done | bytes 393248 | tf_op jit(solution)/shard_map/ppermute | solution.py:62
  461.9 22.2 %collective-permute-start.45 = (bf16[2,3,32,1024]{3,2,1,0:T(8,128)(2,1)S(1)}, bf16[2,3,32,1024]{3,2,1,0:T(8,128)(2,1)S(1)}, u32[]{:S(2)}, u32[]{:S(2)}) collective-permute-start(bf16[2,3,32,1024]{3,2,1,0:T(8,128)(2,1)S(1)} %get-tuple-element.247), channel_id=1, source_target_pairs={{2,1},{3,2},{6,5},{7,6},{10,9},{11,10},{14,13},{15,14},{18,17},{19... | collective-permute-start | bytes 1179656 | tf_op jit(solution)/shard_map/ppermute | solution.py:62
  488.4 4.1 collective-permute-start.43
  494.3 5.2 collective-permute-start.46
  500.3 8.6 %all-to-all-start.1 = ((f32[32,24,128]{2,1,0:T(8,128)}), f32[32,24,128]{2,1,0:T(8,128)}, u32[]{:S(2)}, u32[]{:S(2)}) async-start(f32[32,24,128]{2,1,0:T(8,128)} %pad_maximum_fusion.6), calls=%async_computation.1 | async-start | bytes 786432 | tf_op jit(solution)/shard_map/all_to_all | solution.py:1218
  517.7 10.7 %collective-permute-done.64.n3 = bf16[2,128,1024]{2,1,0:T(8,128)(2,1)S(1)} collective-permute-done((bf16[2,128,1024]{2,1,0:T(8,128)(2,1)S(1)}, bf16[2,128,1024]{2,1,0:T(8,128)(2,1)S(1)}, u32[]{:S(2)}, u32[]{:S(2)}) %collective-permute-start.64) | collective-permute-done | bytes 524320 | tf_op jit(solution)/shard_map/ppermute | solution.py:33
  529.5 10.0 %collective-permute-done.63.n2 = bf16[2,128,1024]{2,1,0:T(8,128)(2,1)S(1)} collective-permute-done((bf16[2,128,1024]{2,1,0:T(8,128)(2,1)S(1)}, bf16[2,128,1024]{2,1,0:T(8,128)(2,1)S(1)}, u32[]{:S(2)}, u32[]{:S(2)}) %collective-permute-start.63) | collective-permute-done | bytes 524320 | tf_op jit(solution)/shard_map/ppermute | solution.py:33
  542.6 5.6 collective-permute-done.49.n3
  560.4 5.9 shard_map.275
  566.3 6.0 %shard_map.274 = (f32[1024,256]{1,0:T(8,128)}, f32[1024,256]{1,0:T(8,128)}, f32[1024,256]{1,0:T(8,128)}, f32[256,1024]{1,0:T(8,128)}, f32[1024,256]{1,0:T(8,128)}, /*index=5*/f32[1024,256]{1,0:T(8,128)}) custom-call(s32[3]{0:T(128)S(1)} %pad_add_fusion.place, bf16[6,32,1024]{2,1,0:T(8,128)(2,1)S(1)} %bitcast.183, ...), custom_call_target="tpu_custom_call" | custom-call | flops 5500000256 | tf_op jit(solution)/shard_map/pallas_call | solution.py:512
  572.3 6.8 %convert.20 = f32[4,512,1024]{2,1,0:T(8,128)} convert(bf16[4,512,1024]{2,1,0:T(8,128)(2,1)} %bitcast.193) | non-fusion elementwise | flops 2097152 | bytes 12582912 | tf_op jit(solution)/shard_map/convert_element_type | solution.py:1223
  (401 shorter events, 177.4 us)
Async XLA Ops:
  18.6 51.3 %collective-permute-start.3 = (bf16[6,32,1024]{2,1,0:T(8,128)(2,1)}, bf16[6,32,1024]{2,1,0:T(8,128)(2,1)}, u32[]{:S(2)}, u32[]{:S(2)}) collective-permute-start(bf16[6,32,1024]{2,1,0:T(8,128)(2,1)} %slice_bitcast_fusion.1), channel_id=1, source_target_pairs={{0,3},{1,0},{2,1},{3,2},{4,7},{5,4},{6,5},{7,6},{8,11},{9,8},{10,9... | collective-permute-start | bytes 1179656 | tf_op jit(solution)/shard_map/ppermute | solution.py:533
  18.8 51.2 %collective-permute-start.2 = (bf16[6,32,1024]{2,1,0:T(8,128)(2,1)}, bf16[6,32,1024]{2,1,0:T(8,128)(2,1)}, u32[]{:S(2)}, u32[]{:S(2)}) collective-permute-start(bf16[6,32,1024]{2,1,0:T(8,128)(2,1)} %slice_bitcast_fusion.1), channel_id=1, source_target_pairs={{0,2},{1,3},{2,0},{3,1},{4,6},{5,7},{6,4},{7,5},{8,10},{9,11},{10,... | collective-permute-start | bytes 1179656 | tf_op jit(solution)/shard_map/ppermute | solution.py:533
  22.0 48.0 %collective-permute-start.1 = (bf16[6,32,1024]{2,1,0:T(8,128)(2,1)}, bf16[6,32,1024]{2,1,0:T(8,128)(2,1)}, u32[]{:S(2)}, u32[]{:S(2)}) collective-permute-start(bf16[6,32,1024]{2,1,0:T(8,128)(2,1)} %slice_bitcast_fusion.1), channel_id=1, source_target_pairs={{0,1},{1,2},{2,3},{3,0},{4,5},{5,6},{6,7},{7,4},{8,9},{9,10},{10,1... | collective-permute-start | bytes 1179656 | tf_op jit(solution)/shard_map/ppermute | solution.py:533
  22.8 38.0 %all-to-all-start = ((f32[32,8,128]{2,1,0:T(8,128)}), f32[32,8,128]{2,1,0:T(8,128)S(1)}, u32[]{:S(2)}, u32[]{:S(2)}) async-start(f32[32,8,128]{2,1,0:T(8,128)} %broadcast_in_dim.11), calls=%async_computation | async-start | bytes 262144 | tf_op jit(solution)/shard_map/all_to_all | solution.py:978
  29.5 335.3 %all-gather.5.cloned.1.call-start = ((), (), s32[]{:S(2)}) async-start(), calls=%async_computation.2 | async-start | bytes 5242880 | tf_op jit(solution)/shard_map/all_gather | solution.py:1102
  31.2 35.1 %collective-permute-start = (bf16[128,1024]{1,0:T(8,128)(2,1)}, bf16[128,1024]{1,0:T(8,128)(2,1)}, u32[]{:S(2)}, u32[]{:S(2)}) collective-permute-start(bf16[128,1024]{1,0:T(8,128)(2,1)} %dynamic-slice_bitcast_fusion), channel_id=1, source_target_pairs={{0,4},{4,8},{8,12},{12,16},{16,20},{20,24},{24,28},{1,5},{5,9},{9,... | collective-permute-start | bytes 786440 | tf_op jit(solution)/shard_map/ppermute | solution.py:39
  71.3 27.3 %collective-permute-start.5 = (bf16[3,6,32,1024]{3,2,1,0:T(8,128)(2,1)S(1)}, bf16[3,6,32,1024]{3,2,1,0:T(8,128)(2,1)S(1)}, u32[]{:S(2)}, u32[]{:S(2)}) collective-permute-start(bf16[3,6,32,1024]{3,2,1,0:T(8,128)(2,1)S(1)} %pad_maximum_fusion.1.f0), channel_id=1, source_target_pairs={{0,16},{4,20},{8,24},{12,28},{16,0},{20,4},{24,8},{28,12},{1,17},{... | collective-permute-start | bytes 3538952 | tf_op jit(solution)/shard_map/ppermute | solution.py:33
  71.6 27.0 %collective-permute-start.4 = (bf16[3,6,32,1024]{3,2,1,0:T(8,128)(2,1)S(1)}, bf16[3,6,32,1024]{3,2,1,0:T(8,128)(2,1)S(1)}, u32[]{:S(2)}, u32[]{:S(2)}) collective-permute-start(bf16[3,6,32,1024]{3,2,1,0:T(8,128)(2,1)S(1)} %pad_maximum_fusion.1.f0), channel_id=1, source_target_pairs={{0,8},{4,12},{8,0},{12,4},{16,24},{20,28},{24,16},{28,20},{1,9},{5... | collective-permute-start | bytes 3538952 | tf_op jit(solution)/shard_map/ppermute | solution.py:33
  72.7 36.1 %collective-permute-start.13 = (bf16[2,128,1024]{2,1,0:T(8,128)(2,1)S(1)}, bf16[2,128,1024]{2,1,0:T(8,128)(2,1)S(1)}, u32[]{:S(2)}, u32[]{:S(2)}) collective-permute-start(bf16[2,128,1024]{2,1,0:T(8,128)(2,1)S(1)} %slice_bitcast_fusion), channel_id=1, source_target_pairs={{0,3},{1,0},{2,1},{3,2},{4,7},{5,4},{6,5},{7,6},{8,11},{9,8},{10,9... | collective-permute-start | bytes 1572872 | tf_op jit(solution)/shard_map/ppermute | solution.py:533
  72.7 44.3 %collective-permute-start.12 = (bf16[2,128,1024]{2,1,0:T(8,128)(2,1)S(1)}, bf16[2,128,1024]{2,1,0:T(8,128)(2,1)S(1)}, u32[]{:S(2)}, u32[]{:S(2)}) collective-permute-start(bf16[2,128,1024]{2,1,0:T(8,128)(2,1)S(1)} %slice_bitcast_fusion), channel_id=1, source_target_pairs={{0,2},{1,3},{2,0},{3,1},{4,6},{5,7},{6,4},{7,5},{8,10},{9,11},{10,... | collective-permute-start | bytes 1572872 | tf_op jit(solution)/shard_map/ppermute | solution.py:533
  75.8 45.1 %collective-permute-start.11 = (bf16[2,128,1024]{2,1,0:T(8,128)(2,1)S(1)}, bf16[2,128,1024]{2,1,0:T(8,128)(2,1)S(1)}, u32[]{:S(2)}, u32[]{:S(2)}) collective-permute-start(bf16[2,128,1024]{2,1,0:T(8,128)(2,1)S(1)} %slice_bitcast_fusion), channel_id=1, source_target_pairs={{0,1},{1,2},{2,3},{3,0},{4,5},{5,6},{6,7},{7,4},{8,9},{9,10},{10,1... | collective-permute-start | bytes 1572872 | tf_op jit(solution)/shard_map/ppermute | solution.py:533
  107.6 29.4 %collective-permute-start.17 = (bf16[512,1024]{1,0:T(8,128)(2,1)S(1)}, bf16[512,1024]{1,0:T(8,128)(2,1)S(1)}, u32[]{:S(2)}, u32[]{:S(2)}) collective-permute-start(bf16[512,1024]{1,0:T(8,128)(2,1)S(1)} %fusion.5.x0), channel_id=1, source_target_pairs={{0,4},{4,0},{8,12},{12,8},{16,20},{20,16},{24,28},{28,24},{1,5},{5... | collective-permute-start | bytes 3145736 | tf_op jit(solution)/shard_map/ppermute | solution.py:33
  108.8 31.2 %collective-permute-start.15 = (bf16[3,3,32,1024]{3,2,1,0:T(8,128)(2,1)S(1)}, bf16[3,3,32,1024]{3,2,1,0:T(8,128)(2,1)S(1)}, u32[]{:S(2)}, u32[]{:S(2)}) collective-permute-start(bf16[3,3,32,1024]{3,2,1,0:T(8,128)(2,1)S(1)} %slice.307), channel_id=1, source_target_pairs={{0,8},{4,12},{8,0},{12,4},{16,24},{20,28},{24,16},{28,20},{1,9},{5... | collective-permute-start | bytes 1769480 | tf_op jit(solution)/shard_map/ppermute | solution.py:33
  117.1 23.0 %collective-permute-start.16 = (bf16[3,3,32,1024]{3,2,1,0:T(8,128)(2,1)S(1)}, bf16[3,3,32,1024]{3,2,1,0:T(8,128)(2,1)S(1)}, u32[]{:S(2)}, u32[]{:S(2)}) collective-permute-start(bf16[3,3,32,1024]{3,2,1,0:T(8,128)(2,1)S(1)} %slice.308), channel_id=1, source_target_pairs={{0,16},{4,20},{8,24},{12,28},{16,0},{20,4},{24,8},{28,12},{1,17},{... | collective-permute-start | bytes 1769480 | tf_op jit(solution)/shard_map/ppermute | solution.py:33
  131.5 39.0 %collective-permute-start.20 = (bf16[3,2,128,1024]{3,2,0,1:T(8,128)(2,1)}, bf16[3,2,128,1024]{3,2,0,1:T(8,128)(2,1)}, u32[]{:S(2)}, u32[]{:S(2)}) collective-permute-start(bf16[3,2,128,1024]{3,2,0,1:T(8,128)(2,1)} %pad_maximum_fusion), channel_id=1, source_target_pairs={{0,16},{4,20},{8,24},{12,28},{16,0},{20,4},{24,8},{28,12},{1,17},{... | collective-permute-start | bytes 4718600 | tf_op jit(solution)/shard_map/ppermute | solution.py:33
  133.7 36.8 %collective-permute-start.19 = (bf16[3,2,128,1024]{3,2,0,1:T(8,128)(2,1)}, bf16[3,2,128,1024]{3,2,0,1:T(8,128)(2,1)}, u32[]{:S(2)}, u32[]{:S(2)}) collective-permute-start(bf16[3,2,128,1024]{3,2,0,1:T(8,128)(2,1)} %pad_maximum_fusion), channel_id=1, source_target_pairs={{0,8},{4,12},{8,0},{12,4},{16,24},{20,28},{24,16},{28,20},{1,9},{5... | collective-permute-start | bytes 4718600 | tf_op jit(solution)/shard_map/ppermute | solution.py:33
  176.4 20.8 %collective-permute-start.24 = (bf16[512,1024]{1,0:T(8,128)(2,1)S(1)}, bf16[512,1024]{1,0:T(8,128)(2,1)S(1)}, u32[]{:S(2)}, u32[]{:S(2)}) collective-permute-start(bf16[512,1024]{1,0:T(8,128)(2,1)S(1)} %get-tuple-element.111.m0.a0), channel_id=1, source_target_pairs={{0,4},{4,0},{8,12},{12,8},{16,20},{20,16},{24,28},{28,24},{1,5},{5... | collective-permute-start | bytes 3145736 | tf_op jit(solution)/shard_map/ppermute | solution.py:33
  180.9 30.1 %collective-permute-start.21 = (bf16[512,1024]{1,0:T(8,128)(2,1)S(1)}, bf16[512,1024]{1,0:T(8,128)(2,1)S(1)}, u32[]{:S(2)}, u32[]{:S(2)}) collective-permute-start(bf16[512,1024]{1,0:T(8,128)(2,1)S(1)} %fusion.6.g0.a0), channel_id=1, source_target_pairs={{0,4},{4,0},{8,12},{12,8},{16,20},{20,16},{24,28},{28,24},{1,5},{5... | collective-permute-start | bytes 3145736 | tf_op jit(solution)/shard_map/ppermute | solution.py:33
  184.5 26.6 %collective-permute-start.23 = (bf16[3,1,128,1024]{3,2,0,1:T(8,128)(2,1)S(1)}, bf16[3,1,128,1024]{3,2,0,1:T(8,128)(2,1)S(1)}, u32[]{:S(2)}, u32[]{:S(2)}) collective-permute-start(bf16[3,1,128,1024]{3,2,0,1:T(8,128)(2,1)S(1)} %slice.310), channel_id=1, source_target_pairs={{0,16},{4,20},{8,24},{12,28},{16,0},{20,4},{24,8},{28,12},{1,17},{... | collective-permute-start | bytes 2359304 | tf_op jit(solution)/shard_map/ppermute | solution.py:33
  256.2 316.2 %all-gather.7.cloned.1.call-start = ((), (), s32[]{:S(2)}) async-start(), calls=%async_computation.3 | async-start | bytes 5242880 | tf_op jit(solution)/shard_map/all_gather | solution.py:1223
  267.4 47.4 %collective-permute-start.31 = (bf16[2,4,128,1024]{3,2,1,0:T(8,128)(2,1)S(1)}, bf16[2,4,128,1024]{3,2,1,0:T(8,128)(2,1)}, u32[]{:S(2)}, u32[]{:S(2)}) collective-permute-start(bf16[2,4,128,1024]{3,2,1,0:T(8,128)(2,1)S(1)} %get-tuple-element.138), channel_id=1, source_target_pairs={{0,8},{4,12},{8,0},{12,4},{16,24},{20,28},{24,16},{28,20},{1,9},{5... | collective-permute-start | bytes 6291464 | tf_op jit(solution)/shard_map/ppermute | solution.py:33
  268.5 47.0 %collective-permute-start.30 = (bf16[2,4,128,1024]{3,2,1,0:T(8,128)(2,1)S(1)}, bf16[2,4,128,1024]{3,2,1,0:T(8,128)(2,1)}, u32[]{:S(2)}, u32[]{:S(2)}) collective-permute-start(bf16[2,4,128,1024]{3,2,1,0:T(8,128)(2,1)S(1)} %copy-done.34), channel_id=1, source_target_pairs={{0,16},{4,20},{8,24},{12,28},{16,0},{20,4},{24,8},{28,12},{1,17},{... | collective-permute-start | bytes 6291464 | tf_op jit(solution)/shard_map/ppermute | solution.py:33
  301.6 63.3 %collective-permute-start.28 = (bf16[512,1024]{1,0:T(8,128)(2,1)}, bf16[512,1024]{1,0:T(8,128)(2,1)}, u32[]{:S(2)}, u32[]{:S(2)}) collective-permute-start(bf16[512,1024]{1,0:T(8,128)(2,1)} %get-tuple-element.131), channel_id=1, source_target_pairs={{0,4},{4,0},{8,12},{12,8},{16,20},{20,16},{24,28},{28,24},{1,5},{5... | collective-permute-start | bytes 3145736 | tf_op jit(solution)/shard_map/ppermute | solution.py:33
  302.8 31.0 %collective-permute-start.36 = (bf16[128,1024]{1,0:T(8,128)(2,1)S(1)}, bf16[128,1024]{1,0:T(8,128)(2,1)S(1)}, u32[]{:S(2)}, u32[]{:S(2)}) collective-permute-start(bf16[128,1024]{1,0:T(8,128)(2,1)S(1)} %add_convert_fusion.14), channel_id=1, source_target_pairs={{4,0},{8,4},{12,8},{16,12},{20,16},{24,20},{28,24},{5,1},{9,5},{13... | collective-permute-start | bytes 786440 | tf_op jit(solution)/shard_map/ppermute | solution.py:39
  339.9 61.4 %collective-permute-start.37 = (bf16[2,4,3,32,1024]{4,3,2,1,0:T(8,128)(2,1)}, bf16[2,4,3,32,1024]{4,3,2,1,0:T(8,128)(2,1)}, u32[]{:S(2)}, u32[]{:S(2)}) collective-permute-start(bf16[2,4,3,32,1024]{4,3,2,1,0:T(8,128)(2,1)} %get-tuple-element.156), channel_id=1, source_target_pairs={{0,8},{4,12},{8,0},{12,4},{16,24},{20,28},{24,16},{28,20},{1,9},{5... | collective-permute-start | bytes 4718600 | tf_op jit(solution)/shard_map/ppermute | solution.py:33
  343.5 57.8 %collective-permute-start.39 = (bf16[2,4,3,32,1024]{4,3,2,1,0:T(8,128)(2,1)}, bf16[2,4,3,32,1024]{4,3,2,1,0:T(8,128)(2,1)}, u32[]{:S(2)}, u32[]{:S(2)}) collective-permute-start(bf16[2,4,3,32,1024]{4,3,2,1,0:T(8,128)(2,1)} %get-tuple-element.160), channel_id=1, source_target_pairs={{0,16},{4,20},{8,24},{12,28},{16,0},{20,4},{24,8},{28,12},{1,17},{... | collective-permute-start | bytes 4718600 | tf_op jit(solution)/shard_map/ppermute | solution.py:33
  351.5 49.8 %collective-permute-start.54 = (bf16[4,128,1024]{2,1,0:T(8,128)(2,1)}, bf16[4,128,1024]{2,1,0:T(8,128)(2,1)}, u32[]{:S(2)}, u32[]{:S(2)}) collective-permute-start(bf16[4,128,1024]{2,1,0:T(8,128)(2,1)} %get-tuple-element.216), channel_id=1, source_target_pairs={{0,16},{4,20},{8,24},{12,28},{16,0},{20,4},{24,8},{28,12},{1,17},{... | collective-permute-start | bytes 3145736 | tf_op jit(solution)/shard_map/ppermute | solution.py:33
  352.8 47.7 %collective-permute-start.55 = (bf16[4,128,1024]{2,1,0:T(8,128)(2,1)}, bf16[4,128,1024]{2,1,0:T(8,128)(2,1)}, u32[]{:S(2)}, u32[]{:S(2)}) collective-permute-start(bf16[4,128,1024]{2,1,0:T(8,128)(2,1)} %get-tuple-element.218), channel_id=1, source_target_pairs={{0,8},{4,12},{8,0},{12,4},{16,24},{20,28},{24,16},{28,20},{1,9},{5... | collective-permute-start | bytes 3145736 | tf_op jit(solution)/shard_map/ppermute | solution.py:33
  410.9 26.3 %collective-permute-start.59 = (bf16[2,128,1024]{2,1,0:T(8,128)(2,1)S(1)}, bf16[2,128,1024]{2,1,0:T(8,128)(2,1)S(1)}, u32[]{:S(2)}, u32[]{:S(2)}) collective-permute-start(bf16[2,128,1024]{2,1,0:T(8,128)(2,1)S(1)} %pad_maximum_fusion.3), channel_id=1, source_target_pairs={{3,2},{7,6},{11,10},{15,14},{19,18},{23,22},{27,26},{31,30}} | collective-permute-start | bytes 1572872 | tf_op jit(solution)/shard_map/ppermute | solution.py:62
  412.3 24.9 %collective-permute-start.56 = (bf16[2,128,1024]{2,1,0:T(8,128)(2,1)S(1)}, bf16[2,128,1024]{2,1,0:T(8,128)(2,1)S(1)}, u32[]{:S(2)}, u32[]{:S(2)}) collective-permute-start(bf16[2,128,1024]{2,1,0:T(8,128)(2,1)S(1)} %pad_maximum_fusion.5), channel_id=1, source_target_pairs={{0,1},{4,5},{8,9},{12,13},{16,17},{20,21},{24,25},{28,29}} | collective-permute-start | bytes 1572872 | tf_op jit(solution)/shard_map/ppermute | solution.py:61
  426.0 28.1 %collective-permute-start.44 = (bf16[2,3,32,1024]{3,2,1,0:T(8,128)(2,1)}, bf16[2,3,32,1024]{3,2,1,0:T(8,128)(2,1)}, u32[]{:S(2)}, u32[]{:S(2)}) collective-permute-start(bf16[2,3,32,1024]{3,2,1,0:T(8,128)(2,1)} %pad_maximum_fusion.7), channel_id=1, source_target_pairs={{3,2},{7,6},{11,10},{15,14},{19,18},{23,22},{27,26},{31,30}} | collective-permute-start | bytes 1179656 | tf_op jit(solution)/shard_map/ppermute | solution.py:62
  428.1 26.0 %collective-permute-start.41 = (bf16[2,3,32,1024]{3,2,1,0:T(8,128)(2,1)}, bf16[2,3,32,1024]{3,2,1,0:T(8,128)(2,1)}, u32[]{:S(2)}, u32[]{:S(2)}) collective-permute-start(bf16[2,3,32,1024]{3,2,1,0:T(8,128)(2,1)} %pad_maximum_fusion.9), channel_id=1, source_target_pairs={{0,1},{4,5},{8,9},{12,13},{16,17},{20,21},{24,25},{28,29}} | collective-permute-start | bytes 1179656 | tf_op jit(solution)/shard_map/ppermute | solution.py:61
  438.5 20.2 %collective-permute-start.57 = (bf16[2,128,1024]{2,1,0:T(8,128)(2,1)}, bf16[2,128,1024]{2,1,0:T(8,128)(2,1)}, u32[]{:S(2)}, u32[]{:S(2)}) collective-permute-start(bf16[2,128,1024]{2,1,0:T(8,128)(2,1)} %get-tuple-element.242), channel_id=1, source_target_pairs={{0,1},{1,2},{4,5},{5,6},{8,9},{9,10},{12,13},{13,14},{16,17},{17,1... | collective-permute-start | bytes 1572872 | tf_op jit(solution)/shard_map/ppermute | solution.py:61
  440.1 44.0 %collective-permute-start.60 = (bf16[2,128,1024]{2,1,0:T(8,128)(2,1)}, bf16[2,128,1024]{2,1,0:T(8,128)(2,1)}, u32[]{:S(2)}, u32[]{:S(2)}) collective-permute-start(bf16[2,128,1024]{2,1,0:T(8,128)(2,1)} %get-tuple-element.243), channel_id=1, source_target_pairs={{2,1},{3,2},{6,5},{7,6},{10,9},{11,10},{14,13},{15,14},{18,17},{19... | collective-permute-start | bytes 1572872 | tf_op jit(solution)/shard_map/ppermute | solution.py:62
  455.6 31.8 %collective-permute-start.42 = (bf16[2,3,32,1024]{3,2,1,0:T(8,128)(2,1)S(1)}, bf16[2,3,32,1024]{3,2,1,0:T(8,128)(2,1)S(1)}, u32[]{:S(2)}, u32[]{:S(2)}) collective-permute-start(bf16[2,3,32,1024]{3,2,1,0:T(8,128)(2,1)S(1)} %get-tuple-element.246), channel_id=1, source_target_pairs={{0,1},{1,2},{4,5},{5,6},{8,9},{9,10},{12,13},{13,14},{16,17},{17,1... | collective-permute-start | bytes 1179656 | tf_op jit(solution)/shard_map/ppermute | solution.py:61
  460.0 49.0 %collective-permute-start.58 = (bf16[2,128,1024]{2,1,0:T(8,128)(2,1)S(1)}, bf16[2,128,1024]{2,1,0:T(8,128)(2,1)}, u32[]{:S(2)}, u32[]{:S(2)}) collective-permute-start(bf16[2,128,1024]{2,1,0:T(8,128)(2,1)S(1)} %add_convert_fusion.10), channel_id=1, source_target_pairs={{0,1},{1,2},{2,3},{4,5},{5,6},{6,7},{8,9},{9,10},{10,11},{12,13},{... | collective-permute-start | bytes 1572872 | tf_op jit(solution)/shard_map/ppermute | solution.py:61
  461.9 31.5 %collective-permute-start.45 = (bf16[2,3,32,1024]{3,2,1,0:T(8,128)(2,1)S(1)}, bf16[2,3,32,1024]{3,2,1,0:T(8,128)(2,1)S(1)}, u32[]{:S(2)}, u32[]{:S(2)}) collective-permute-start(bf16[2,3,32,1024]{3,2,1,0:T(8,128)(2,1)S(1)} %get-tuple-element.247), channel_id=1, source_target_pairs={{2,1},{3,2},{6,5},{7,6},{10,9},{11,10},{14,13},{15,14},{18,17},{19... | collective-permute-start | bytes 1179656 | tf_op jit(solution)/shard_map/ppermute | solution.py:62
  485.4 23.6 %collective-permute-start.61 = (bf16[2,128,1024]{2,1,0:T(8,128)(2,1)S(1)}, bf16[2,128,1024]{2,1,0:T(8,128)(2,1)}, u32[]{:S(2)}, u32[]{:S(2)}) collective-permute-start(bf16[2,128,1024]{2,1,0:T(8,128)(2,1)S(1)} %add_convert_fusion.9), channel_id=1, source_target_pairs={{1,0},{2,1},{3,2},{5,4},{6,5},{7,6},{9,8},{10,9},{11,10},{13,12},{... | collective-permute-start | bytes 1572872 | tf_op jit(solution)/shard_map/ppermute | solution.py:62
  488.4 24.9 %collective-permute-start.43 = (bf16[2,3,32,1024]{3,2,1,0:T(8,128)(2,1)}, bf16[2,3,32,1024]{3,2,1,0:T(8,128)(2,1)}, u32[]{:S(2)}, u32[]{:S(2)}) collective-permute-start(bf16[2,3,32,1024]{3,2,1,0:T(8,128)(2,1)} %add_convert_fusion.13), channel_id=1, source_target_pairs={{0,1},{1,2},{2,3},{4,5},{5,6},{6,7},{8,9},{9,10},{10,11},{12,13},{... | collective-permute-start | bytes 1179656 | tf_op jit(solution)/shard_map/ppermute | solution.py:61
  494.3 20.0 %collective-permute-start.46 = (bf16[2,3,32,1024]{3,2,1,0:T(8,128)(2,1)}, bf16[2,3,32,1024]{3,2,1,0:T(8,128)(2,1)}, u32[]{:S(2)}, u32[]{:S(2)}) collective-permute-start(bf16[2,3,32,1024]{3,2,1,0:T(8,128)(2,1)} %add_convert_fusion.12), channel_id=1, source_target_pairs={{1,0},{2,1},{3,2},{5,4},{6,5},{7,6},{9,8},{10,9},{11,10},{13,12},{... | collective-permute-start | bytes 1179656 | tf_op jit(solution)/shard_map/ppermute | solution.py:62
  500.3 40.1 %all-to-all-start.1 = ((f32[32,24,128]{2,1,0:T(8,128)}), f32[32,24,128]{2,1,0:T(8,128)}, u32[]{:S(2)}, u32[]{:S(2)}) async-start(f32[32,24,128]{2,1,0:T(8,128)} %pad_maximum_fusion.6), calls=%async_computation.1 | async-start | bytes 786432 | tf_op jit(solution)/shard_map/all_to_all | solution.py:1218
  510.5 31.6 %collective-permute-start.65 = (bf16[2,128,1024]{2,1,0:T(8,128)(2,1)S(1)}, bf16[2,128,1024]{2,1,0:T(8,128)(2,1)S(1)}, u32[]{:S(2)}, u32[]{:S(2)}) collective-permute-start(bf16[2,128,1024]{2,1,0:T(8,128)(2,1)S(1)} %add_convert_fusion.8.n0), channel_id=1, source_target_pairs={{0,4},{4,0},{8,12},{12,8},{16,20},{20,16},{24,28},{28,24},{1,5},{5... | collective-permute-start | bytes 1572872 | tf_op jit(solution)/shard_map/ppermute | solution.py:33
  513.0 26.5 %collective-permute-start.63 = (bf16[2,128,1024]{2,1,0:T(8,128)(2,1)S(1)}, bf16[2,128,1024]{2,1,0:T(8,128)(2,1)S(1)}, u32[]{:S(2)}, u32[]{:S(2)}) collective-permute-start(bf16[2,128,1024]{2,1,0:T(8,128)(2,1)S(1)} %add_convert_fusion.8.n0), channel_id=1, source_target_pairs={{0,16},{4,20},{8,24},{12,28},{16,0},{20,4},{24,8},{28,12},{1,17},{... | collective-permute-start | bytes 1572872 | tf_op jit(solution)/shard_map/ppermute | solution.py:33
  513.3 26.7 %collective-permute-start.62 = (bf16[2,128,1024]{2,1,0:T(8,128)(2,1)S(1)}, bf16[2,128,1024]{2,1,0:T(8,128)(2,1)S(1)}, u32[]{:S(2)}, u32[]{:S(2)}) collective-permute-start(bf16[2,128,1024]{2,1,0:T(8,128)(2,1)S(1)} %add_convert_fusion.8.n0), channel_id=1, source_target_pairs={{0,8},{4,12},{8,0},{12,4},{16,24},{20,28},{24,16},{28,20},{1,9},{5... | collective-permute-start | bytes 1572872 | tf_op jit(solution)/shard_map/ppermute | solution.py:33
  515.7 32.6 %collective-permute-start.49 = (bf16[6,32,1024]{2,1,0:T(8,128)(2,1)S(1)}, bf16[6,32,1024]{2,1,0:T(8,128)(2,1)}, u32[]{:S(2)}, u32[]{:S(2)}) collective-permute-start(bf16[6,32,1024]{2,1,0:T(8,128)(2,1)S(1)} %bitcast.179), channel_id=1, source_target_pairs={{0,24},{4,28},{8,16},{12,20},{16,8},{20,12},{24,0},{28,4},{1,25},{... | collective-permute-start | bytes 1179656 | tf_op jit(solution)/shard_map/ppermute | solution.py:33
  528.5 31.4 %collective-permute-start.68 = (bf16[2,128,1024]{2,1,0:T(8,128)(2,1)S(1)}, bf16[2,128,1024]{2,1,0:T(8,128)(2,1)S(1)}, u32[]{:S(2)}, u32[]{:S(2)}) collective-permute-start(bf16[2,128,1024]{2,1,0:T(8,128)(2,1)S(1)} %collective-permute-done.64.n3), channel_id=1, source_target_pairs={{0,4},{4,0},{8,12},{12,8},{16,20},{20,16},{24,28},{28,24},{1,5},{5... | collective-permute-start | bytes 1572872 | tf_op jit(solution)/shard_map/ppermute | solution.py:33
  539.5 20.4 %collective-permute-start.67 = (bf16[2,128,1024]{2,1,0:T(8,128)(2,1)S(1)}, bf16[2,128,1024]{2,1,0:T(8,128)(2,1)}, u32[]{:S(2)}, u32[]{:S(2)}) collective-permute-start(bf16[2,128,1024]{2,1,0:T(8,128)(2,1)S(1)} %collective-permute-done.63.n2), channel_id=1, source_target_pairs={{0,4},{4,0},{8,12},{12,8},{16,20},{20,16},{24,28},{28,24},{1,5},{5... | collective-permute-start | bytes 1572872 | tf_op jit(solution)/shard_map/ppermute | solution.py:33
  540.0 20.4 %collective-permute-start.66 = (bf16[2,128,1024]{2,1,0:T(8,128)(2,1)S(1)}, bf16[2,128,1024]{2,1,0:T(8,128)(2,1)}, u32[]{:S(2)}, u32[]{:S(2)}) collective-permute-start(bf16[2,128,1024]{2,1,0:T(8,128)(2,1)S(1)} %collective-permute-done.62.n1), channel_id=1, source_target_pairs={{0,4},{4,0},{8,12},{12,8},{16,20},{20,16},{24,28},{28,24},{1,5},{5... | collective-permute-start | bytes 1572872 | tf_op jit(solution)/shard_map/ppermute | solution.py:33
  (117 other events, 1685.4 us)
Sparse Core Ops, SparseCore 0:
  256.3 78.6 all-gather.4
  375.6 119.9 all-gather.6

commit v3 on v2

--- a/solution.py
+++ b/solution.py
@@ -39,28 +39,39 @@
     return lax.ppermute(value, "seq", [(i, i + steps) for i in range(first, last)])
 
 
-def line_gather(value):
+def line_steps(value):
     count = lax.axis_size("tp")
-    place = lax.axis_index("tp")
     lefts, rights = [value], [value]
     for k in range(1, count):
         lefts.append(lax.ppermute(lefts[-1], "tp", [(i, i + 1) for i in range(k - 1, count - 1)]))
         rights.append(
             lax.ppermute(rights[-1], "tp", [(i, i - 1) for i in range(1, count - k + 1)])
         )
+    return lefts, rights
+
+
+def line_gather(value):
+    count = lax.axis_size("tp")
+    place = lax.axis_index("tp")
+    lefts, rights = line_steps(value)
     return [value] + [
         jnp.where(place >= j, lefts[j], rights[count - j]) for j in range(1, count)
     ]
 
 
-def line_reduce(chunks):
+def line_reduce(chunks, pace=None):
     count = lax.axis_size("tp")
-    add = lambda a, b: a if b is None else (a.astype(F32) + b.astype(F32)).astype(BF16)
+
+    def add(a, b, k):
+        if pace:
+            a = lax.optimization_barrier((a, *pace[k - 1]))[0]
+        return a if b is None else (a.astype(F32) + b.astype(F32)).astype(BF16)
+
     going, coming = None, None
     for k in range(1, count):
-        going = lax.ppermute(add(chunks[k], going), "tp", [(i, i + 1) for i in range(k)])
+        going = lax.ppermute(add(chunks[k], going, k), "tp", [(i, i + 1) for i in range(k)])
         coming = lax.ppermute(
-            add(chunks[count - k], coming), "tp", [(i, i - 1) for i in range(count - k, count)]
+            add(chunks[count - k], coming, k), "tp", [(i, i - 1) for i in range(count - k, count)]
         )
     return (chunks[0].astype(F32) + going.astype(F32) + coming.astype(F32)).astype(BF16)
 
@@ -989,27 +1000,26 @@
     block_power = dict(zip((1, 2, 3, 6), blocks))
 
     def line_of(own):
-        return jnp.stack([cycle(own[0], j) for j in range(1, tp_count)])
+        return jnp.stack([cycle(own, j) for j in range(1, tp_count)])
 
     def plane_of(line, by_x, by_y, half):
         return [line, by_x, by_y, flip(by_y[:, :half], 2), flip(by_x[:, half:], 4)]
 
-    line_w = line_of(own_w)
+    line_w = line_of(own_w[0])
     near_w = flip(line_w, 2), flip(line_w, 4)
     far_w = plane_of(line_w, *near_w, 3)
-    line_m = line_of(after(own_m, line_w))
-    near_m = flip(line_m, 2), flip(line_m, 4)
+    line_m = line_of(after(own_m[0], line_w))
+    near_m = flip(after(line_m, *near_w), 2), flip(after(line_m, *near_w), 4)
     far_m = plane_of(line_m, *near_m, 1)
     far_m[3:] = [value[:, 0] for value in far_m[3:]]
 
     local_state, local_moment = call(
-        scan_in, [(grid, F32)] * 2, decay, after(signal, line_w, own_m), us=8
+        scan_in, [(grid, F32)] * 2, decay, after(signal, line_w, own_m, x_other, grad_out_other), us=8
     )
     start = states_around(after(local_state, *near_w), block_power, 1, 1)
     (context,) = call(scan_out, [((CTX,) + grid[1:], F32)], decay, gain, start, signal[:CTX], us=3)
     context = context.reshape(CTX, features).astype(BF16)
     context_other = flip(context, 1)
-
     rows = 2 * block_len
     slots = tp_count
     own_spec = whole((4, 6, cut, features))
@@ -1149,20 +1159,17 @@
 
     got_r = flip(after(send_r, resid_b), 4)
     got_h = flip(after(send_h, resid_b), 2)
+    near_h, away_h = add(keep_h[0], got_h[0]), add(keep_h[1], got_h[1])
+    near_r, away_r = add(keep_r[0], got_r[0]), add(keep_r[1], got_r[1])
     grad_context = (grad_ctx + grad_ctx_got.astype(F32)).astype(BF16)
     grad_conv = tiles(after(grad_context, got_r, got_h))
     grad_later = tiles(shifted(grad_context, -1))
     (local_back,) = call(scan_back_in, [(grid, F32)], decay, grad_conv)
-    late = tail_power * states_around(local_back, block_power, -1, 2, keep_a)
+    late = tail_power * states_around(local_back, block_power, -1, 2, keep_a, away_h, away_r)
     grad_signal, end = call(
         scan_rows, [((block_len,) + grid[1:], F32), (grid, F32)], decay, gain, late, grad_later
     )
     grad_signal = grad_signal.reshape(block_len, features).astype(BF16)
-    grad_gain, grad_moment = call(
-        scan_sums, [(grid, F32)] * 2, decay, start, signal[:CTX], grad_conv
-    )
-    end_moment = block_len * block_power[1] * start + local_moment
-    grad_rate = -gain * (grad_moment + end * end_moment)
     grad_tokens, sums_in = timed(5)(
         first_back, place, (steps,),
         [seq_spec] + [row_spec] * 4 + [gain_spec], [row_spec, gain_spec],
@@ -1170,26 +1177,44 @@
         (tokens, grad_in, grad_in_got, grad_signal, after(resid, output_all), attention_norm_gain.reshape(1, -1)),
     )
 
-    def plane_sum(keep_first, got_first, keep_second, got_second, then, end):
-        got = after(got_first, *then)
-        near, away = add(keep_first[0], got[0]), add(keep_first[1], got[1])
-        first = (near, after(flip(away, 4), *end))
-        got = after(got_second, *then)
-        near, away = add(keep_second[0], got[0]), add(keep_second[1], got[1])
-        second = (near, after(flip(away, 2), *end))
-        return [
-            jnp.stack([add(a[j], b[j]) for a, b in (first, second)]) for j in range(slots)
+    lefts, rights = line_steps(grad_tokens)
+    line = [grad_tokens] + [
+        jnp.where(tp_index >= j, lefts[j], rights[slots - j]) for j in range(1, slots)
+    ]
+    line = jnp.stack(line)
+    tokens_all = jnp.stack(
+        [
+            lax.dynamic_index_in_dim(line, (tp_index - b) % slots, 0, keepdims=False)
+            for b in range(sequences)
         ]
+    ).astype(F32)
+    grad_gain, grad_moment = call(
+        scan_sums, [(grid, F32)] * 2, decay, after(start, grad_tokens), signal[:CTX], grad_conv
+    )
+    end_moment = block_len * block_power[1] * start + local_moment
+    grad_rate = -gain * (grad_moment + end * end_moment)
 
     def regather(total):
         held = [total, flip(total, 2), flip(total, 4), flip(total, 6)]
         return held + [flip(value, 1) for value in held]
 
     ready = (late, grad_later)
-    got_a, got_b = flip(after(send_a, *ready), 2), flip(after(send_b, *ready), 4)
-    total_m = line_reduce(plane_sum(keep_h, got_h, keep_r, got_r, ready, (grad_tokens,)))
+    more_h, more_r = flip(after(away_h, *ready), 4), flip(after(away_r, *ready), 2)
+    more_h, more_r = after(more_h, grad_tokens), after(more_r, grad_tokens)
+    got_a = flip(after(send_a, more_h, more_r), 2)
+    got_b = flip(after(send_b, more_h, more_r), 4)
+    pairs = (near_h, more_h), (near_r, more_r)
+    total_m = line_reduce(
+        [jnp.stack([add(a[j], b[j]) for a, b in pairs]) for j in range(slots)],
+        list(zip(lefts[1:], rights[1:])),
+    )
+    near_a, away_a = add(keep_a[0], got_a[0]), add(keep_a[1], got_a[1])
+    near_b, away_b = add(keep_b[0], got_b[0]), add(keep_b[1], got_b[1])
+    pairs = (near_a, flip(away_a, 4)), (near_b, flip(away_b, 2))
+    total_a = line_reduce(
+        [jnp.stack([add(a[j], b[j]) for a, b in pairs]) for j in range(slots)]
+    )
     pieces_m = regather(total_m)
-    total_a = line_reduce(plane_sum(keep_a, got_a, keep_b, got_b, (grad_tokens,), ()))
     pieces_a = regather(total_a.reshape(6, cut, features))
     grad_hidden, grad_return = timed(5)(
         unpack_hidden, place, (1,),
@@ -1215,14 +1240,16 @@
     sums = jnp.broadcast_to(sums, (devices,) + sums.shape[1:])
     count = small.shape[1]
     small = jnp.sum(
-        lax.all_to_all(jnp.concatenate([small, sums], axis=1), ("seq", "tp"), 0, 0), axis=0
+        lax.all_to_all(
+            after(jnp.concatenate([small, sums], axis=1), total_a), ("seq", "tp"), 0, 0
+        ),
+        axis=0,
     )
     kernel_grads = small[:count].reshape(channels, 2, states)
     gains = small[count:].reshape(2, features)
 
-    grad_tokens = lax.all_gather(grad_tokens, "tp").astype(F32)
     return (
-        output_all, grad_tokens, gains[0], grad_q, grad_k, grad_v, grad_o, grad_sk, grad_sv,
+        output_all, tokens_all, gains[0], grad_q, grad_k, grad_v, grad_o, grad_sk, grad_sv,
         kernel_grads[:, 0], kernel_grads[:, 1], gains[1], grad_hidden, grad_return,
     )
 

time: 598 us -> 558 us (0.933)
  waiting for transfers between devices: 154 us -> 124 us
  starting transfers between devices: 130 us -> 119 us
  local copies, waits for them, and re-layouts: 70.8 us -> 79.8 us
  other arithmetic: 54.2 us -> 46.7 us
    ppermute x40, waiting for transfers between devices: 103 us -> 54.8 us  [flip(): return lax.ppermute(value, 'seq', [(i, i ^ mask) for i in range(count)])]
    ppermute x12 -> x18, waiting for transfers between devices: 19.9 us -> 41.4 us  [the longest x6 25.5 us: line_reduce(): lax.ppermute(add(chunks[count - k], coming, k), 'tp', [(i, i - 1) for i i...]
    ppermute x12 -> x18, starting transfers between devices: 47.8 us -> 37.2 us  [the longest x6 11.4 us: line_reduce(): lax.ppermute(add(chunks[k], going, k), 'tp', [(i, i + 1) for i in range(k)])]
    convert_element_type x7, other arithmetic: 13.9 us -> 5.93 us  [the longest x1 3.95 us: fast_body(): tokens_all = jnp.stack([lax.dynamic_index_in_dim(line, (tp_index - b) % s...]
    unnamed x192 -> x198, local copies, waits for them, and re-layouts: 46 us -> 53.8 us
    convert_element_type x7 -> x8, other arithmetic: 17.4 us -> 16.9 us  [add(): return (a.astype(F32) + b.astype(F32)).astype(BF16)]
  transfers between devices with their start and end apart: 73 -> 78, of which waited for: 25 -> 21; matrix products, arithmetic and copies ran while one was open for 12% -> 14% of each run, Pallas kernels for 23% -> 23%
where the time goes in v3:
time: 558 us; the launch traced here: 549 us
  Pallas kernels  163 us (29%)
  waiting for transfers between devices  124 us (22%)
  starting transfers between devices  119 us (21%)
  local copies, waits for them, and re-layouts  79.8 us (14%)
  other arithmetic  46.7 us (8%)
  between operations  16.1 us (3%)
    pallas_call x16, Pallas kernels, launch(): pl.pallas_call(kernel, grid_spec=pltpu.PrefetchScalarGridSpec(num_scalar_...  141 us
    ppermute x40, waiting for transfers between devices, flip(): return lax.ppermute(value, 'seq', [(i, i ^ mask) for i in range(count)])  54.8 us
    unnamed x198, local copies, waits for them, and re-layouts  53.8 us
    ppermute x40, starting transfers between devices, flip(): return lax.ppermute(value, 'seq', [(i, i ^ mask) for i in range(count)])  35.7 us
    ppermute x11, starting transfers between devices, shifted(): lax.ppermute(value, 'seq', [(i, i + steps) for i in range(first, last)])  26.2 us
    ppermute x6, waiting for transfers between devices, line_reduce(): lax.ppermute(add(chunks[count - k], coming, k), 'tp', [(i, i - 1) for i i...  25.5 us
    pallas_call x6, Pallas kernels, call(): pl.pallas_call(kernel, out_shape=[jax.ShapeDtypeStruct(shape, dtype) for...  22.3 us
    convert_element_type x8, other arithmetic, add(): return (a.astype(F32) + b.astype(F32)).astype(BF16)  16.9 us
  transfers between devices with their start and end apart: 78, of which 21 were waited for; matrix products, arithmetic and copies ran while one was open for 14% of the time, Pallas kernels for 23%

profile of v3, /device:TPU:17, one launch (start us, length us, event | category | flops | bytes accessed | tf_op | source)
XLA Modules:
  0.0 548.6 jit_solution(13931790750995904036)
XLA Ops:
  18.7 3.2 collective-permute-start.2
  22.7 6.7 %all-to-all-start = ((f32[32,8,128]{2,1,0:T(8,128)}), f32[32,8,128]{2,1,0:T(8,128)S(1)}, u32[]{:S(2)}, u32[]{:S(2)}) async-start(f32[32,8,128]{2,1,0:T(8,128)} %broadcast_in_dim.11), calls=%async_computation | async-start | bytes 262144 | tf_op jit(solution)/shard_map/all_to_all | solution.py:989
  31.2 3.3 collective-permute-start
  50.4 10.3 %all-to-all-done = f32[32,8,128]{2,1,0:T(8,128)S(1)} async-done(((f32[32,8,128]{2,1,0:T(8,128)}), f32[32,8,128]{2,1,0:T(8,128)S(1)}, u32[]{:S(2)}, u32[]{:S(2)}) %all-to-all-start) | async-done | bytes 131104 | tf_op jit(solution)/shard_map/all_to_all | solution.py:989
  74.1 3.5 collective-permute-start.14
  77.7 8.5 %shard_map.257 = (f32[16,8,128]{2,1,0:T(8,128)S(1)}, f32[16,8,128]{2,1,0:T(8,128)S(1)}) custom-call(f32[16,8,128]{2,1,0:T(8,128)S(1)} %get-tuple-element.100.decay_ref, f32[512,8,128]{2,1,0:T(8,128)S(1)} %convert_multiply_fusion.1.u_ref), custom_call_target="tpu_custom_call" | custom-call | flops 8800000000 | tf_op jit(solution)/shard_map/pallas_call | solution.py:164
  86.2 12.7 %collective-permute-done.6.f1 = bf16[3,6,32,1024]{3,2,1,0:T(8,128)(2,1)S(1)} collective-permute-done((bf16[3,6,32,1024]{3,2,1,0:T(8,128)(2,1)S(1)}, bf16[3,6,32,1024]{3,2,1,0:T(8,128)(2,1)S(1)}, u32[]{:S(2)}, u32[]{:S(2)}) %collective-permute-start.6) | collective-permute-done | bytes 1179680 | tf_op jit(solution)/shard_map/ppermute | solution.py:33
  102.0 3.8 collective-permute-start.8
  108.2 10.5 %collective-permute-done.14 = bf16[2,128,1024]{2,1,0:T(8,128)(2,1)S(1)} collective-permute-done((bf16[2,128,1024]{2,1,0:T(8,128)(2,1)S(1)}, bf16[2,128,1024]{2,1,0:T(8,128)(2,1)S(1)}, u32[]{:S(2)}, u32[]{:S(2)}) %collective-permute-start.14) | collective-permute-done | bytes 524320 | tf_op jit(solution)/shard_map/ppermute | solution.py:544
  118.7 4.3 collective-permute-start.10
  123.0 3.1 collective-permute-start.11
  132.6 6.3 %shard_map.259 = (bf16[1024,512]{1,0:T(8,128)(2,1)S(1)}, bf16[1024,512]{1,0:T(8,128)(2,1)S(1)}, bf16[1024,512]{1,0:T(8,128)(2,1)S(1)}) custom-call(s32[3]{0:T(128)S(1)} %pad_add_fusion.place, bf16[512,1024]{1,0:T(8,128)(2,1)S(1)} %fusion.5.x0, bf16[512,1024]{1,0:T(8,128)(2,1)S(1)} %copy-done.39, bf16[4,6,32,1024]{3,2,1,0:T(8,128)(2,1)S(1)} %copy-done.31, ...), custom_call_target="tpu_custom_call" | custom-call | flops 8800000000 | tf_op jit(solution)/shard_map/pallas_call | solution.py:523
  139.1 22.1 %shard_map.260 = (f32[512,1024]{1,0:T(8,128)}, bf16[512,1024]{1,0:T(8,128)(2,1)S(1)}, bf16[256,1024]{1,0:T(8,128)(2,1)S(1)}, bf16[1024,512]{1,0:T(8,128)(2,1)S(1)}, f32[4,1024,1]{2,1,0:T(8,128)}) custom-call(s32[3]{0:T(128)S(1)} %pad_add_fusion.place, bf16[128,1024]{1,0:T(8,128)(2,1)S(1)} %bitcast.191, bf16[128,1024]{1,0:T(8,128)(2,1)S(1)} %collective-permute-done.16.c1, ...), custom_call_target="tpu_custom_call" | custom-call | flops 22000001024 | tf_op jit(solution)/shard_map/pallas_call | solution.py:523
  179.4 10.3 %collective-permute-done.22 = bf16[3,1,128,1024]{3,2,0,1:T(8,128)(2,1)S(1)} collective-permute-done((bf16[3,1,128,1024]{3,2,0,1:T(8,128)(2,1)S(1)}, bf16[3,1,128,1024]{3,2,0,1:T(8,128)(2,1)S(1)}, u32[]{:S(2)}, u32[]{:S(2)}) %collective-permute-start.22) | collective-permute-done | bytes 786464 | tf_op jit(solution)/shard_map/ppermute | solution.py:33
  189.8 13.7 %shard_map.262 = (bf16[1024,2048]{1,0:T(8,128)(2,1)}, bf16[1024,2048]{1,0:T(8,128)(2,1)}) custom-call(s32[3]{0:T(128)S(1)} %pad_add_fusion.place, bf16[512,1024]{1,0:T(8,128)(2,1)S(1)} %get-tuple-element.118.m0.a0, bf16[512,1024]{1,0:T(8,128)(2,1)S(1)} %collective-permute-done.24.m1.a1, bf16[4,2,128,1024]{3,2,1,0:T(8,128)(2,1)S(1)} %copy-done.29, ...), custom_call_target="tpu_custom_call" | custom-call | flops 15399999488 | tf_op jit(solution)/shard_map/pallas_call | solution.py:523
  203.5 21.8 %shard_map.263 = (f32[512,1024]{1,0:T(8,128)}, bf16[512,1024]{1,0:T(8,128)(2,1)S(1)}, f32[512,1024]{1,0:T(8,128)}, bf16[512,1024]{1,0:T(8,128)(2,1)}, bf16[1024,2048]{1,0:T(8,128)(2,1)}) custom-call(s32[3]{0:T(128)S(1)} %pad_add_fusion.place, bf16[512,1024]{1,0:T(8,128)(2,1)S(1)} %fusion.6.g0.a0, bf16[512,1024]{1,0:T(8,128)(2,1)S(1)} %copy-done.42, ...), custom_call_target="tpu_custom_call" | custom-call | flops 23100000256 | tf_op jit(solution)/shard_map/pallas_call | solution.py:523
  229.9 6.3 %shard_map.264 = (bf16[2,4,128,1024]{3,2,1,0:T(8,128)(2,1)S(1)}, bf16[2,4,128,1024]{3,2,1,0:T(8,128)(2,1)S(1)}) custom-call(s32[3]{0:T(128)S(1)} %pad_add_fusion.place, bf16[512,1024]{1,0:T(8,128)(2,1)S(1)} %copy-done.9, bf16[512,1024]{1,0:T(8,128)(2,1)S(1)} %copy-done.42, bf16[1024,2048]{1,0:T(8,128)(2,1)S(1)} %copy-done.71), custom_call_target="tpu_custom_call" | custom-call | flops 8800000000 | tf_op jit(solution)/shard_map/pallas_call | solution.py:523
  242.8 5.1 shard_map.266
  254.4 6.3 %shard_map.267 = (bf16[2,4,128,1024]{3,2,1,0:T(8,128)(2,1)S(1)}, bf16[2,4,128,1024]{3,2,1,0:T(8,128)(2,1)S(1)}) custom-call(s32[3]{0:T(128)S(1)} %pad_add_fusion.place, bf16[512,1024]{1,0:T(8,128)(2,1)S(1)} %copy-done.44, bf16[512,1024]{1,0:T(8,128)(2,1)S(1)} %copy-done.46, bf16[1024,2048]{1,0:T(8,128)(2,1)S(1)} %copy-done.70), custom_call_target="tpu_custom_call" | custom-call | flops 8800000000 | tf_op jit(solution)/shard_map/pallas_call | solution.py:523
  268.7 27.3 %shard_map.268 = (f32[512,1024]{1,0:T(8,128)}, bf16[512,1024]{1,0:T(8,128)(2,1)}, f32[128,1024]{1,0:T(8,128)S(1)}, bf16[128,1024]{1,0:T(8,128)(2,1)S(1)}, bf16[1...) custom-call(s32[3]{0:T(128)S(1)} %pad_add_fusion.place, bf16[512,1024]{1,0:T(8,128)(2,1)} %get-tuple-element.134.g0, ...), custom_call_target="tpu_custom_call" | custom-call | flops 29699999744 | tf_op jit(solution)/shard_map/pallas_call | solution.py:523
  299.2 9.9 %shard_map.270 = (bf16[2,4,3,32,1024]{4,3,2,1,0:T(8,128)(2,1)S(1)}, bf16[2,4,3,32,1024]{4,3,2,1,0:T(8,128)(2,1)}, bf16[2,4,3,32,1024]{4,3,2,1,0:T(8,128)(2,1)S(1)}, bf16[2,4,3,32,1024]{4,3,2,1,0:T(8,128)(2,1)}) custom-call(s32[3]{0:T(128)S(1)} %pad_add_fusion.place, bf16[512,1024]{1,0:T(8,128)(2,1)S(1)} %fusion.5.x0, bf16[512,1024]{1,0:T(8,128)(2,1)S(1)} %copy-done.40, ...), custom_call_target="tpu_custom_call" | custom-call | flops 11000000512 | tf_op jit(solution)/shard_map/pallas_call | solution.py:523
  317.1 3.9 add_convert_fusion.1
  321.0 3.9 add_convert_fusion
  327.7 3.7 collective-permute-done.34
  331.4 3.7 collective-permute-done.35
  335.3 4.5 shard_map.271
  345.8 4.1 shard_map.272
  350.0 10.1 %collective-permute-done.43 = bf16[4,128,1024]{2,1,0:T(8,128)(2,1)} collective-permute-done((bf16[4,128,1024]{2,1,0:T(8,128)(2,1)}, bf16[4,128,1024]{2,1,0:T(8,128)(2,1)}, u32[]{:S(2)}, u32[]{:S(2)}) %collective-permute-start.43) | collective-permute-done | bytes 1048608 | tf_op jit(solution)/shard_map/ppermute | solution.py:33
  363.5 3.4 collective-permute-start.38
  367.7 5.6 %shard_map.273 = (f32[16,8,128]{2,1,0:T(8,128)S(1)}, f32[16,8,128]{2,1,0:T(8,128)S(1)}) custom-call(f32[16,8,128]{2,1,0:T(8,128)S(1)} %copy-done.74, f32[16,8,128]{2,1,0:T(8,128)S(1)} %copy-done.23, f32[128,8,128]{2,1,0:T(8,128)S(1)} %bitcast.181, f32[128,8,128]{2,1,0:T(8,128)S(1)} %bitcast.183), custom_call_target="tpu_custom_call" | custom-call | flops 5500000256 | tf_op jit(solution)/shard_map/pallas_call | solution.py:164
  376.9 9.6 %collective-permute-done.37 = bf16[512,1024]{1,0:T(8,128)(2,1)} collective-permute-done((bf16[512,1024]{1,0:T(8,128)(2,1)S(1)}, bf16[512,1024]{1,0:T(8,128)(2,1)}, u32[]{:S(2)}, u32[]{:S(2)}) %collective-permute-start.37) | collective-permute-done | bytes 1048608 | tf_op jit(solution)/shard_map/ppermute | solution.py:46
  388.8 3.2 collective-permute-start.39
  392.0 4.0 collective-permute-done.47
  405.1 5.7 %collective-permute-done.41 = bf16[512,1024]{1,0:T(8,128)(2,1)S(1)} collective-permute-done((bf16[512,1024]{1,0:T(8,128)(2,1)}, bf16[512,1024]{1,0:T(8,128)(2,1)S(1)}, u32[]{:S(2)}, u32[]{:S(2)}) %collective-permute-start.41) | collective-permute-done | bytes 1048608 | tf_op jit(solution)/shard_map/ppermute | solution.py:46
  412.1 4.1 collective-permute-start.42
  426.3 5.7 %collective-permute-done.52 = bf16[2,3,32,1024]{3,2,1,0:T(8,128)(2,1)S(1)} collective-permute-done((bf16[2,3,32,1024]{3,2,1,0:T(8,128)(2,1)S(1)}, bf16[2,3,32,1024]{3,2,1,0:T(8,128)(2,1)S(1)}, u32[]{:S(2)}, u32[]{:S(2)}) %collective-permute-start.52) | collective-permute-done | bytes 393248 | tf_op jit(solution)/shard_map/ppermute | solution.py:73
  436.1 7.1 %collective-permute-done.66 = bf16[2,128,1024]{2,1,0:T(8,128)(2,1)S(1)} collective-permute-done((bf16[2,128,1024]{2,1,0:T(8,128)(2,1)S(1)}, bf16[2,128,1024]{2,1,0:T(8,128)(2,1)S(1)}, u32[]{:S(2)}, u32[]{:S(2)}) %collective-permute-start.66) | collective-permute-done | bytes 524320 | tf_op jit(solution)/shard_map/ppermute | solution.py:73
  446.4 4.1 collective-permute-start.64
  454.1 3.4 collective-permute-start.51
  461.2 10.2 %collective-permute-done.54 = bf16[2,3,32,1024]{3,2,1,0:T(8,128)(2,1)S(1)} collective-permute-done((bf16[2,3,32,1024]{3,2,1,0:T(8,128)(2,1)S(1)}, bf16[2,3,32,1024]{3,2,1,0:T(8,128)(2,1)S(1)}, u32[]{:S(2)}, u32[]{:S(2)}) %collective-permute-start.54) | collective-permute-done | bytes 393248 | tf_op jit(solution)/shard_map/ppermute | solution.py:73
  474.6 7.6 %collective-permute-start.57 = (bf16[6,32,1024]{2,1,0:T(8,128)(2,1)S(1)}, bf16[6,32,1024]{2,1,0:T(8,128)(2,1)}, u32[]{:S(2)}, u32[]{:S(2)}) collective-permute-start(bf16[6,32,1024]{2,1,0:T(8,128)(2,1)S(1)} %bitcast.187), channel_id=1, source_target_pairs={{0,24},{4,28},{8,16},{12,20},{16,8},{20,12},{24,0},{28,4},{1,25},{... | collective-permute-start | bytes 1179656 | tf_op jit(solution)/shard_map/ppermute | solution.py:33
  482.1 5.8 %all-to-all-start.1 = ((f32[32,24,128]{2,1,0:T(8,128)}), f32[32,24,128]{2,1,0:T(8,128)S(1)}, u32[]{:S(2)}, u32[]{:S(2)}) async-start(f32[32,24,128]{2,1,0:T(8,128)} %pad_maximum_fusion.7), calls=%async_computation.1 | async-start | bytes 786432 | tf_op jit(solution)/shard_map/all_to_all | solution.py:1243
  495.1 4.3 collective-permute-start.70
  499.8 3.9 maximum_convert_fusion
  503.8 4.3 collective-permute-done.68.n1
  510.8 9.5 %collective-permute-done.70.n3 = bf16[2,128,1024]{2,1,0:T(8,128)(2,1)S(1)} collective-permute-done((bf16[2,128,1024]{2,1,0:T(8,128)(2,1)S(1)}, bf16[2,128,1024]{2,1,0:T(8,128)(2,1)S(1)}, u32[]{:S(2)}, u32[]{:S(2)}) %collective-permute-start.70) | collective-permute-done | bytes 524320 | tf_op jit(solution)/shard_map/ppermute | solution.py:33
  526.9 6.3 %shard_map.274 = (f32[1024,256]{1,0:T(8,128)}, f32[1024,256]{1,0:T(8,128)}, f32[1024,256]{1,0:T(8,128)}, f32[256,1024]{1,0:T(8,128)}, f32[1024,256]{1,0:T(8,128)}, /*index=5*/f32[1024,256]{1,0:T(8,128)}) custom-call(s32[3]{0:T(128)S(1)} %pad_add_fusion.place, bf16[6,32,1024]{2,1,0:T(8,128)(2,1)S(1)} %bitcast.189, ...), custom_call_target="tpu_custom_call" | custom-call | flops 5500000256 | tf_op jit(solution)/shard_map/pallas_call | solution.py:523
  533.3 6.1 %shard_map.275 = (f32[1024,1024]{1,0:T(8,128)}, f32[1024,1024]{1,0:T(8,128)}) custom-call(s32[3]{0:T(128)S(1)} %pad_add_fusion.place, bf16[2,128,1024]{2,1,0:T(8,128)(2,1)S(1)} %add_convert_fusion.8.n0, bf16[2,128,1024]{2,1,0:T(8,128)(2,1)S(1)} %collective-permute-done.68.n1, bf16[2,128,1024]{2,1,0:T(8,128)(2,1)S(1)} %collective-permute-done.69.n2, ...), custom_call_target="tpu_custom_call" | custom-call | flops 5500000256 | tf_op jit(solution)/shard_map/pallas_call | solution.py:523
  (422 shorter events, 185.5 us)
Async XLA Ops:
  18.5 51.5 %collective-permute-start.3 = (bf16[6,32,1024]{2,1,0:T(8,128)(2,1)}, bf16[6,32,1024]{2,1,0:T(8,128)(2,1)}, u32[]{:S(2)}, u32[]{:S(2)}) collective-permute-start(bf16[6,32,1024]{2,1,0:T(8,128)(2,1)} %slice_bitcast_fusion.1), channel_id=1, source_target_pairs={{0,3},{1,0},{2,1},{3,2},{4,7},{5,4},{6,5},{7,6},{8,11},{9,8},{10,9... | collective-permute-start | bytes 1179656 | tf_op jit(solution)/shard_map/ppermute | solution.py:544
  18.7 51.4 %collective-permute-start.2 = (bf16[6,32,1024]{2,1,0:T(8,128)(2,1)}, bf16[6,32,1024]{2,1,0:T(8,128)(2,1)}, u32[]{:S(2)}, u32[]{:S(2)}) collective-permute-start(bf16[6,32,1024]{2,1,0:T(8,128)(2,1)} %slice_bitcast_fusion.1), channel_id=1, source_target_pairs={{0,2},{1,3},{2,0},{3,1},{4,6},{5,7},{6,4},{7,5},{8,10},{9,11},{10,... | collective-permute-start | bytes 1179656 | tf_op jit(solution)/shard_map/ppermute | solution.py:544
  21.9 48.2 %collective-permute-start.1 = (bf16[6,32,1024]{2,1,0:T(8,128)(2,1)}, bf16[6,32,1024]{2,1,0:T(8,128)(2,1)}, u32[]{:S(2)}, u32[]{:S(2)}) collective-permute-start(bf16[6,32,1024]{2,1,0:T(8,128)(2,1)} %slice_bitcast_fusion.1), channel_id=1, source_target_pairs={{0,1},{1,2},{2,3},{3,0},{4,5},{5,6},{6,7},{7,4},{8,9},{9,10},{10,1... | collective-permute-start | bytes 1179656 | tf_op jit(solution)/shard_map/ppermute | solution.py:544
  22.7 38.0 %all-to-all-start = ((f32[32,8,128]{2,1,0:T(8,128)}), f32[32,8,128]{2,1,0:T(8,128)S(1)}, u32[]{:S(2)}, u32[]{:S(2)}) async-start(f32[32,8,128]{2,1,0:T(8,128)} %broadcast_in_dim.11), calls=%async_computation | async-start | bytes 262144 | tf_op jit(solution)/shard_map/all_to_all | solution.py:989
  29.4 310.8 %all-gather.3.cloned.1.call-start = ((), (), s32[]{:S(2)}) async-start(), calls=%async_computation.2 | async-start | bytes 5242880 | tf_op jit(solution)/shard_map/all_gather | solution.py:1112
  31.2 35.0 %collective-permute-start = (bf16[128,1024]{1,0:T(8,128)(2,1)}, bf16[128,1024]{1,0:T(8,128)(2,1)}, u32[]{:S(2)}, u32[]{:S(2)}) collective-permute-start(bf16[128,1024]{1,0:T(8,128)(2,1)} %dynamic-slice_bitcast_fusion), channel_id=1, source_target_pairs={{0,4},{4,8},{8,12},{12,16},{16,20},{20,24},{24,28},{1,5},{5,9},{9,... | collective-permute-start | bytes 786440 | tf_op jit(solution)/shard_map/ppermute | solution.py:39
  39.2 34.9 %collective-permute-start.4 = (bf16[512,1024]{1,0:T(8,128)(2,1)S(1)}, bf16[512,1024]{1,0:T(8,128)(2,1)S(1)}, u32[]{:S(2)}, u32[]{:S(2)}) collective-permute-start(bf16[512,1024]{1,0:T(8,128)(2,1)S(1)} %fusion.5.x0), channel_id=1, source_target_pairs={{0,4},{4,0},{8,12},{12,8},{16,20},{20,16},{24,28},{28,24},{1,5},{5... | collective-permute-start | bytes 3145736 | tf_op jit(solution)/shard_map/ppermute | solution.py:33
  71.5 27.4 %collective-permute-start.6 = (bf16[3,6,32,1024]{3,2,1,0:T(8,128)(2,1)S(1)}, bf16[3,6,32,1024]{3,2,1,0:T(8,128)(2,1)S(1)}, u32[]{:S(2)}, u32[]{:S(2)}) collective-permute-start(bf16[3,6,32,1024]{3,2,1,0:T(8,128)(2,1)S(1)} %pad_maximum_fusion.2.f0), channel_id=1, source_target_pairs={{0,8},{4,12},{8,0},{12,4},{16,24},{20,28},{24,16},{28,20},{1,9},{5... | collective-permute-start | bytes 3538952 | tf_op jit(solution)/shard_map/ppermute | solution.py:33
  72.0 27.1 %collective-permute-start.7 = (bf16[3,6,32,1024]{3,2,1,0:T(8,128)(2,1)S(1)}, bf16[3,6,32,1024]{3,2,1,0:T(8,128)(2,1)S(1)}, u32[]{:S(2)}, u32[]{:S(2)}) collective-permute-start(bf16[3,6,32,1024]{3,2,1,0:T(8,128)(2,1)S(1)} %pad_maximum_fusion.2.f0), channel_id=1, source_target_pairs={{0,16},{4,20},{8,24},{12,28},{16,0},{20,4},{24,8},{28,12},{1,17},{... | collective-permute-start | bytes 3538952 | tf_op jit(solution)/shard_map/ppermute | solution.py:33
  74.1 33.5 %collective-permute-start.15 = (bf16[2,128,1024]{2,1,0:T(8,128)(2,1)S(1)}, bf16[2,128,1024]{2,1,0:T(8,128)(2,1)S(1)}, u32[]{:S(2)}, u32[]{:S(2)}) collective-permute-start(bf16[2,128,1024]{2,1,0:T(8,128)(2,1)S(1)} %copy-done.90), channel_id=1, source_target_pairs={{0,3},{1,0},{2,1},{3,2},{4,7},{5,4},{6,5},{7,6},{8,11},{9,8},{10,9... | collective-permute-start | bytes 1572872 | tf_op jit(solution)/shard_map/ppermute | solution.py:544
  74.1 44.5 %collective-permute-start.14 = (bf16[2,128,1024]{2,1,0:T(8,128)(2,1)S(1)}, bf16[2,128,1024]{2,1,0:T(8,128)(2,1)S(1)}, u32[]{:S(2)}, u32[]{:S(2)}) collective-permute-start(bf16[2,128,1024]{2,1,0:T(8,128)(2,1)S(1)} %copy-done.90), channel_id=1, source_target_pairs={{0,2},{1,3},{2,0},{3,1},{4,6},{5,7},{6,4},{7,5},{8,10},{9,11},{10,... | collective-permute-start | bytes 1572872 | tf_op jit(solution)/shard_map/ppermute | solution.py:544
  77.6 45.4 %collective-permute-start.13 = (bf16[2,128,1024]{2,1,0:T(8,128)(2,1)S(1)}, bf16[2,128,1024]{2,1,0:T(8,128)(2,1)S(1)}, u32[]{:S(2)}, u32[]{:S(2)}) collective-permute-start(bf16[2,128,1024]{2,1,0:T(8,128)(2,1)S(1)} %copy-done.90), channel_id=1, source_target_pairs={{0,1},{1,2},{2,3},{3,0},{4,5},{5,6},{6,7},{7,4},{8,9},{9,10},{10,1... | collective-permute-start | bytes 1572872 | tf_op jit(solution)/shard_map/ppermute | solution.py:544
  106.1 26.5 %collective-permute-start.17 = (bf16[3,3,32,1024]{3,2,1,0:T(8,128)(2,1)S(1)}, bf16[3,3,32,1024]{3,2,1,0:T(8,128)(2,1)S(1)}, u32[]{:S(2)}, u32[]{:S(2)}) collective-permute-start(bf16[3,3,32,1024]{3,2,1,0:T(8,128)(2,1)S(1)} %slice.304), channel_id=1, source_target_pairs={{0,8},{4,12},{8,0},{12,4},{16,24},{20,28},{24,16},{28,20},{1,9},{5... | collective-permute-start | bytes 1769480 | tf_op jit(solution)/shard_map/ppermute | solution.py:33
  107.5 25.1 %collective-permute-start.18 = (bf16[3,3,32,1024]{3,2,1,0:T(8,128)(2,1)S(1)}, bf16[3,3,32,1024]{3,2,1,0:T(8,128)(2,1)S(1)}, u32[]{:S(2)}, u32[]{:S(2)}) collective-permute-start(bf16[3,3,32,1024]{3,2,1,0:T(8,128)(2,1)S(1)} %slice.305), channel_id=1, source_target_pairs={{0,16},{4,20},{8,24},{12,28},{16,0},{20,4},{24,8},{28,12},{1,17},{... | collective-permute-start | bytes 1769480 | tf_op jit(solution)/shard_map/ppermute | solution.py:33
  107.5 20.0 %collective-permute-start.12 = (f32[16,8,128]{2,1,0:T(8,128)S(1)}, f32[16,8,128]{2,1,0:T(8,128)S(1)}, u32[]{:S(2)}, u32[]{:S(2)}) collective-permute-start(f32[16,8,128]{2,1,0:T(8,128)S(1)} %multiply_add_fusion.2), channel_id=1, source_target_pairs={{0,28},{1,29},{2,30},{3,31}} | collective-permute-start | bytes 196616 | tf_op jit(solution)/shard_map/ppermute | solution.py:39
  127.5 35.6 %collective-permute-start.20 = (bf16[3,2,128,1024]{3,2,0,1:T(8,128)(2,1)}, bf16[3,2,128,1024]{3,2,0,1:T(8,128)(2,1)}, u32[]{:S(2)}, u32[]{:S(2)}) collective-permute-start(bf16[3,2,128,1024]{3,2,0,1:T(8,128)(2,1)} %pad_maximum_fusion.1), channel_id=1, source_target_pairs={{0,8},{4,12},{8,0},{12,4},{16,24},{20,28},{24,16},{28,20},{1,9},{5... | collective-permute-start | bytes 4718600 | tf_op jit(solution)/shard_map/ppermute | solution.py:33
  127.8 35.2 %collective-permute-start.21 = (bf16[3,2,128,1024]{3,2,0,1:T(8,128)(2,1)}, bf16[3,2,128,1024]{3,2,0,1:T(8,128)(2,1)}, u32[]{:S(2)}, u32[]{:S(2)}) collective-permute-start(bf16[3,2,128,1024]{3,2,0,1:T(8,128)(2,1)} %pad_maximum_fusion.1), channel_id=1, source_target_pairs={{0,16},{4,20},{8,24},{12,28},{16,0},{20,4},{24,8},{28,12},{1,17},{... | collective-permute-start | bytes 4718600 | tf_op jit(solution)/shard_map/ppermute | solution.py:33
  168.9 20.8 %collective-permute-start.24 = (bf16[512,1024]{1,0:T(8,128)(2,1)S(1)}, bf16[512,1024]{1,0:T(8,128)(2,1)S(1)}, u32[]{:S(2)}, u32[]{:S(2)}) collective-permute-start(bf16[512,1024]{1,0:T(8,128)(2,1)S(1)} %get-tuple-element.118.m0.a0), channel_id=1, source_target_pairs={{0,4},{4,0},{8,12},{12,8},{16,20},{20,16},{24,28},{28,24},{1,5},{5... | collective-permute-start | bytes 3145736 | tf_op jit(solution)/shard_map/ppermute | solution.py:33
  170.9 18.8 %collective-permute-start.22 = (bf16[3,1,128,1024]{3,2,0,1:T(8,128)(2,1)S(1)}, bf16[3,1,128,1024]{3,2,0,1:T(8,128)(2,1)S(1)}, u32[]{:S(2)}, u32[]{:S(2)}) collective-permute-start(bf16[3,1,128,1024]{3,2,0,1:T(8,128)(2,1)S(1)} %slice.306), channel_id=1, source_target_pairs={{0,8},{4,12},{8,0},{12,4},{16,24},{20,28},{24,16},{28,20},{1,9},{5... | collective-permute-start | bytes 2359304 | tf_op jit(solution)/shard_map/ppermute | solution.py:33
  174.2 29.3 %collective-permute-start.23 = (bf16[3,1,128,1024]{3,2,0,1:T(8,128)(2,1)S(1)}, bf16[3,1,128,1024]{3,2,0,1:T(8,128)(2,1)S(1)}, u32[]{:S(2)}, u32[]{:S(2)}) collective-permute-start(bf16[3,1,128,1024]{3,2,0,1:T(8,128)(2,1)S(1)} %slice.307), channel_id=1, source_target_pairs={{0,16},{4,20},{8,24},{12,28},{16,0},{20,4},{24,8},{28,12},{1,17},{... | collective-permute-start | bytes 2359304 | tf_op jit(solution)/shard_map/ppermute | solution.py:33
  260.7 51.9 %collective-permute-start.30 = (bf16[2,4,128,1024]{3,2,1,0:T(8,128)(2,1)S(1)}, bf16[2,4,128,1024]{3,2,1,0:T(8,128)(2,1)}, u32[]{:S(2)}, u32[]{:S(2)}) collective-permute-start(bf16[2,4,128,1024]{3,2,1,0:T(8,128)(2,1)S(1)} %copy-done.37), channel_id=1, source_target_pairs={{0,16},{4,20},{8,24},{12,28},{16,0},{20,4},{24,8},{28,12},{1,17},{... | collective-permute-start | bytes 6291464 | tf_op jit(solution)/shard_map/ppermute | solution.py:33
  262.5 50.1 %collective-permute-start.31 = (bf16[2,4,128,1024]{3,2,1,0:T(8,128)(2,1)S(1)}, bf16[2,4,128,1024]{3,2,1,0:T(8,128)(2,1)}, u32[]{:S(2)}, u32[]{:S(2)}) collective-permute-start(bf16[2,4,128,1024]{3,2,1,0:T(8,128)(2,1)S(1)} %get-tuple-element.145), channel_id=1, source_target_pairs={{0,8},{4,12},{8,0},{12,4},{16,24},{20,28},{24,16},{28,20},{1,9},{5... | collective-permute-start | bytes 6291464 | tf_op jit(solution)/shard_map/ppermute | solution.py:33
  296.1 44.1 %collective-permute-start.28 = (bf16[512,1024]{1,0:T(8,128)(2,1)}, bf16[512,1024]{1,0:T(8,128)(2,1)}, u32[]{:S(2)}, u32[]{:S(2)}) collective-permute-start(bf16[512,1024]{1,0:T(8,128)(2,1)} %get-tuple-element.138), channel_id=1, source_target_pairs={{0,4},{4,0},{8,12},{12,8},{16,20},{20,16},{24,28},{28,24},{1,5},{5... | collective-permute-start | bytes 3145736 | tf_op jit(solution)/shard_map/ppermute | solution.py:33
  335.1 24.9 %collective-permute-start.43 = (bf16[4,128,1024]{2,1,0:T(8,128)(2,1)}, bf16[4,128,1024]{2,1,0:T(8,128)(2,1)}, u32[]{:S(2)}, u32[]{:S(2)}) collective-permute-start(bf16[4,128,1024]{2,1,0:T(8,128)(2,1)} %get-tuple-element.164), channel_id=1, source_target_pairs={{0,16},{4,20},{8,24},{12,28},{16,0},{20,4},{24,8},{28,12},{1,17},{... | collective-permute-start | bytes 3145736 | tf_op jit(solution)/shard_map/ppermute | solution.py:33
  335.2 25.2 %collective-permute-start.44 = (bf16[4,128,1024]{2,1,0:T(8,128)(2,1)}, bf16[4,128,1024]{2,1,0:T(8,128)(2,1)}, u32[]{:S(2)}, u32[]{:S(2)}) collective-permute-start(bf16[4,128,1024]{2,1,0:T(8,128)(2,1)} %get-tuple-element.166), channel_id=1, source_target_pairs={{0,8},{4,12},{8,0},{12,4},{16,24},{20,28},{24,16},{28,20},{1,9},{5... | collective-permute-start | bytes 3145736 | tf_op jit(solution)/shard_map/ppermute | solution.py:33
  360.5 35.5 %collective-permute-start.47 = (bf16[2,4,3,32,1024]{4,3,2,1,0:T(8,128)(2,1)}, bf16[2,4,3,32,1024]{4,3,2,1,0:T(8,128)(2,1)}, u32[]{:S(2)}, u32[]{:S(2)}) collective-permute-start(bf16[2,4,3,32,1024]{4,3,2,1,0:T(8,128)(2,1)} %get-tuple-element.171), channel_id=1, source_target_pairs={{0,16},{4,20},{8,24},{12,28},{16,0},{20,4},{24,8},{28,12},{1,17},{... | collective-permute-start | bytes 4718600 | tf_op jit(solution)/shard_map/ppermute | solution.py:33
  361.5 36.7 %collective-permute-start.45 = (bf16[2,4,3,32,1024]{4,3,2,1,0:T(8,128)(2,1)}, bf16[2,4,3,32,1024]{4,3,2,1,0:T(8,128)(2,1)}, u32[]{:S(2)}, u32[]{:S(2)}) collective-permute-start(bf16[2,4,3,32,1024]{4,3,2,1,0:T(8,128)(2,1)} %get-tuple-element.168), channel_id=1, source_target_pairs={{0,8},{4,12},{8,0},{12,4},{16,24},{20,28},{24,16},{28,20},{1,9},{5... | collective-permute-start | bytes 4718600 | tf_op jit(solution)/shard_map/ppermute | solution.py:33
  361.5 25.0 %collective-permute-start.37 = (bf16[512,1024]{1,0:T(8,128)(2,1)S(1)}, bf16[512,1024]{1,0:T(8,128)(2,1)}, u32[]{:S(2)}, u32[]{:S(2)}) collective-permute-start(bf16[512,1024]{1,0:T(8,128)(2,1)S(1)} %get-tuple-element.155), channel_id=1, source_target_pairs={{0,1},{1,2},{2,3},{4,5},{5,6},{6,7},{8,9},{9,10},{10,11},{12,13},{... | collective-permute-start | bytes 3145736 | tf_op jit(solution)/shard_map/ppermute | solution.py:46
  363.5 25.3 %collective-permute-start.38 = (bf16[512,1024]{1,0:T(8,128)(2,1)S(1)}, bf16[512,1024]{1,0:T(8,128)(2,1)}, u32[]{:S(2)}, u32[]{:S(2)}) collective-permute-start(bf16[512,1024]{1,0:T(8,128)(2,1)S(1)} %get-tuple-element.155), channel_id=1, source_target_pairs={{1,0},{2,1},{3,2},{5,4},{6,5},{7,6},{9,8},{10,9},{11,10},{13,12},{... | collective-permute-start | bytes 3145736 | tf_op jit(solution)/shard_map/ppermute | solution.py:48
  386.6 24.2 %collective-permute-start.41 = (bf16[512,1024]{1,0:T(8,128)(2,1)}, bf16[512,1024]{1,0:T(8,128)(2,1)S(1)}, u32[]{:S(2)}, u32[]{:S(2)}) collective-permute-start(bf16[512,1024]{1,0:T(8,128)(2,1)} %collective-permute-done.37), channel_id=1, source_target_pairs={{1,2},{2,3},{5,6},{6,7},{9,10},{10,11},{13,14},{14,15},{17,18},{18... | collective-permute-start | bytes 3145736 | tf_op jit(solution)/shard_map/ppermute | solution.py:46
  388.8 23.3 %collective-permute-start.39 = (bf16[512,1024]{1,0:T(8,128)(2,1)}, bf16[512,1024]{1,0:T(8,128)(2,1)S(1)}, u32[]{:S(2)}, u32[]{:S(2)}) collective-permute-start(bf16[512,1024]{1,0:T(8,128)(2,1)} %collective-permute-done.38), channel_id=1, source_target_pairs={{1,0},{2,1},{5,4},{6,5},{9,8},{10,9},{13,12},{14,13},{17,16},{18,1... | collective-permute-start | bytes 3145736 | tf_op jit(solution)/shard_map/ppermute | solution.py:48
  412.1 22.7 %collective-permute-start.42 = (bf16[512,1024]{1,0:T(8,128)(2,1)S(1)}, bf16[512,1024]{1,0:T(8,128)(2,1)S(1)}, u32[]{:S(2)}, u32[]{:S(2)}) collective-permute-start(bf16[512,1024]{1,0:T(8,128)(2,1)S(1)} %collective-permute-done.41), channel_id=1, source_target_pairs={{2,3},{6,7},{10,11},{14,15},{18,19},{22,23},{26,27},{30,31}} | collective-permute-start | bytes 3145736 | tf_op jit(solution)/shard_map/ppermute | solution.py:46
  416.2 19.9 %collective-permute-start.40 = (bf16[512,1024]{1,0:T(8,128)(2,1)S(1)}, bf16[512,1024]{1,0:T(8,128)(2,1)S(1)}, u32[]{:S(2)}, u32[]{:S(2)}) collective-permute-start(bf16[512,1024]{1,0:T(8,128)(2,1)S(1)} %collective-permute-done.39), channel_id=1, source_target_pairs={{1,0},{5,4},{9,8},{13,12},{17,16},{21,20},{25,24},{29,28}} | collective-permute-start | bytes 3145736 | tf_op jit(solution)/shard_map/ppermute | solution.py:48
  423.0 20.3 %collective-permute-start.66 = (bf16[2,128,1024]{2,1,0:T(8,128)(2,1)S(1)}, bf16[2,128,1024]{2,1,0:T(8,128)(2,1)S(1)}, u32[]{:S(2)}, u32[]{:S(2)}) collective-permute-start(bf16[2,128,1024]{2,1,0:T(8,128)(2,1)S(1)} %get-tuple-element.259), channel_id=1, source_target_pairs={{2,1},{3,2},{6,5},{7,6},{10,9},{11,10},{14,13},{15,14},{18,17},{19... | collective-permute-start | bytes 1572872 | tf_op jit(solution)/shard_map/ppermute | solution.py:73
  425.0 20.4 %collective-permute-start.63 = (bf16[2,128,1024]{2,1,0:T(8,128)(2,1)S(1)}, bf16[2,128,1024]{2,1,0:T(8,128)(2,1)S(1)}, u32[]{:S(2)}, u32[]{:S(2)}) collective-permute-start(bf16[2,128,1024]{2,1,0:T(8,128)(2,1)S(1)} %get-tuple-element.258), channel_id=1, source_target_pairs={{0,1},{1,2},{4,5},{5,6},{8,9},{9,10},{12,13},{13,14},{16,17},{17,1... | collective-permute-start | bytes 1572872 | tf_op jit(solution)/shard_map/ppermute | solution.py:72
  432.3 19.6 %collective-permute-start.53 = (bf16[2,3,32,1024]{3,2,1,0:T(8,128)(2,1)S(1)}, bf16[2,3,32,1024]{3,2,1,0:T(8,128)(2,1)S(1)}, u32[]{:S(2)}, u32[]{:S(2)}) collective-permute-start(bf16[2,3,32,1024]{3,2,1,0:T(8,128)(2,1)S(1)} %get-tuple-element.263), channel_id=1, source_target_pairs={{2,1},{3,2},{6,5},{7,6},{10,9},{11,10},{14,13},{15,14},{18,17},{19... | collective-permute-start | bytes 1179656 | tf_op jit(solution)/shard_map/ppermute | solution.py:73
  434.8 19.2 %collective-permute-start.50 = (bf16[2,3,32,1024]{3,2,1,0:T(8,128)(2,1)S(1)}, bf16[2,3,32,1024]{3,2,1,0:T(8,128)(2,1)S(1)}, u32[]{:S(2)}, u32[]{:S(2)}) collective-permute-start(bf16[2,3,32,1024]{3,2,1,0:T(8,128)(2,1)S(1)} %get-tuple-element.262), channel_id=1, source_target_pairs={{0,1},{1,2},{4,5},{5,6},{8,9},{9,10},{12,13},{13,14},{16,17},{17,1... | collective-permute-start | bytes 1179656 | tf_op jit(solution)/shard_map/ppermute | solution.py:72
  443.5 44.5 %collective-permute-start.67 = (bf16[2,128,1024]{2,1,0:T(8,128)(2,1)S(1)}, bf16[2,128,1024]{2,1,0:T(8,128)(2,1)}, u32[]{:S(2)}, u32[]{:S(2)}) collective-permute-start(bf16[2,128,1024]{2,1,0:T(8,128)(2,1)S(1)} %add_convert_fusion.9), channel_id=1, source_target_pairs={{1,0},{2,1},{3,2},{5,4},{6,5},{7,6},{9,8},{10,9},{11,10},{13,12},{... | collective-permute-start | bytes 1572872 | tf_op jit(solution)/shard_map/ppermute | solution.py:73
  446.4 42.0 %collective-permute-start.64 = (bf16[2,128,1024]{2,1,0:T(8,128)(2,1)}, bf16[2,128,1024]{2,1,0:T(8,128)(2,1)}, u32[]{:S(2)}, u32[]{:S(2)}) collective-permute-start(bf16[2,128,1024]{2,1,0:T(8,128)(2,1)} %add_convert_fusion.10), channel_id=1, source_target_pairs={{0,1},{1,2},{2,3},{4,5},{5,6},{6,7},{8,9},{9,10},{10,11},{12,13},{... | collective-permute-start | bytes 1572872 | tf_op jit(solution)/shard_map/ppermute | solution.py:72
  452.1 19.3 %collective-permute-start.54 = (bf16[2,3,32,1024]{3,2,1,0:T(8,128)(2,1)S(1)}, bf16[2,3,32,1024]{3,2,1,0:T(8,128)(2,1)S(1)}, u32[]{:S(2)}, u32[]{:S(2)}) collective-permute-start(bf16[2,3,32,1024]{3,2,1,0:T(8,128)(2,1)S(1)} %add_convert_fusion.12), channel_id=1, source_target_pairs={{1,0},{2,1},{3,2},{5,4},{6,5},{7,6},{9,8},{10,9},{11,10},{13,12},{... | collective-permute-start | bytes 1179656 | tf_op jit(solution)/shard_map/ppermute | solution.py:73
  471.6 22.2 %collective-permute-start.55 = (bf16[6,32,1024]{2,1,0:T(8,128)(2,1)S(1)}, bf16[6,32,1024]{2,1,0:T(8,128)(2,1)}, u32[]{:S(2)}, u32[]{:S(2)}) collective-permute-start(bf16[6,32,1024]{2,1,0:T(8,128)(2,1)S(1)} %bitcast.185), channel_id=1, source_target_pairs={{0,8},{4,12},{8,0},{12,4},{16,24},{20,28},{24,16},{28,20},{1,9},{5... | collective-permute-start | bytes 1179656 | tf_op jit(solution)/shard_map/ppermute | solution.py:33
  474.1 20.9 %collective-permute-start.56 = (bf16[6,32,1024]{2,1,0:T(8,128)(2,1)S(1)}, bf16[6,32,1024]{2,1,0:T(8,128)(2,1)}, u32[]{:S(2)}, u32[]{:S(2)}) collective-permute-start(bf16[6,32,1024]{2,1,0:T(8,128)(2,1)S(1)} %bitcast.186), channel_id=1, source_target_pairs={{0,16},{4,20},{8,24},{12,28},{16,0},{20,4},{24,8},{28,12},{1,17},{... | collective-permute-start | bytes 1179656 | tf_op jit(solution)/shard_map/ppermute | solution.py:33
  474.6 24.8 %collective-permute-start.57 = (bf16[6,32,1024]{2,1,0:T(8,128)(2,1)S(1)}, bf16[6,32,1024]{2,1,0:T(8,128)(2,1)}, u32[]{:S(2)}, u32[]{:S(2)}) collective-permute-start(bf16[6,32,1024]{2,1,0:T(8,128)(2,1)S(1)} %bitcast.187), channel_id=1, source_target_pairs={{0,24},{4,28},{8,16},{12,20},{16,8},{20,12},{24,0},{28,4},{1,25},{... | collective-permute-start | bytes 1179656 | tf_op jit(solution)/shard_map/ppermute | solution.py:33
  482.1 21.7 %all-to-all-start.1 = ((f32[32,24,128]{2,1,0:T(8,128)}), f32[32,24,128]{2,1,0:T(8,128)S(1)}, u32[]{:S(2)}, u32[]{:S(2)}) async-start(f32[32,24,128]{2,1,0:T(8,128)} %pad_maximum_fusion.7), calls=%async_computation.1 | async-start | bytes 786432 | tf_op jit(solution)/shard_map/all_to_all | solution.py:1243
  495.1 25.2 %collective-permute-start.70 = (bf16[2,128,1024]{2,1,0:T(8,128)(2,1)S(1)}, bf16[2,128,1024]{2,1,0:T(8,128)(2,1)S(1)}, u32[]{:S(2)}, u32[]{:S(2)}) collective-permute-start(bf16[2,128,1024]{2,1,0:T(8,128)(2,1)S(1)} %add_convert_fusion.8.n0), channel_id=1, source_target_pairs={{0,24},{4,28},{8,16},{12,20},{16,8},{20,12},{24,0},{28,4},{1,25},{... | collective-permute-start | bytes 1572872 | tf_op jit(solution)/shard_map/ppermute | solution.py:33
  499.3 21.9 %collective-permute-start.59 = (bf16[6,32,1024]{2,1,0:T(8,128)(2,1)}, bf16[6,32,1024]{2,1,0:T(8,128)(2,1)}, u32[]{:S(2)}, u32[]{:S(2)}) collective-permute-start(bf16[6,32,1024]{2,1,0:T(8,128)(2,1)} %collective-permute-done.55.n1), channel_id=1, source_target_pairs={{0,4},{4,0},{8,12},{12,8},{16,20},{20,16},{24,28},{28,24},{1,5},{5... | collective-permute-start | bytes 1179656 | tf_op jit(solution)/shard_map/ppermute | solution.py:33
  499.7 21.5 %collective-permute-start.60 = (bf16[6,32,1024]{2,1,0:T(8,128)(2,1)}, bf16[6,32,1024]{2,1,0:T(8,128)(2,1)}, u32[]{:S(2)}, u32[]{:S(2)}) collective-permute-start(bf16[6,32,1024]{2,1,0:T(8,128)(2,1)} %collective-permute-done.56.n2), channel_id=1, source_target_pairs={{0,4},{4,0},{8,12},{12,8},{16,20},{20,16},{24,28},{28,24},{1,5},{5... | collective-permute-start | bytes 1179656 | tf_op jit(solution)/shard_map/ppermute | solution.py:33
  510.8 22.5 %collective-permute-start.71 = (bf16[2,128,1024]{2,1,0:T(8,128)(2,1)S(1)}, bf16[2,128,1024]{2,1,0:T(8,128)(2,1)S(1)}, u32[]{:S(2)}, u32[]{:S(2)}) collective-permute-start(bf16[2,128,1024]{2,1,0:T(8,128)(2,1)S(1)} %add_convert_fusion.8.n0), channel_id=1, source_target_pairs={{0,4},{4,0},{8,12},{12,8},{16,20},{20,16},{24,28},{28,24},{1,5},{5... | collective-permute-start | bytes 1572872 | tf_op jit(solution)/shard_map/ppermute | solution.py:33
  (125 other events, 1656.3 us)
Sparse Core Ops, SparseCore 0:
  249.9 78.5 all-gather.2

commit v4 on v3

--- a/solution.py
+++ b/solution.py
@@ -507,7 +507,7 @@
     return pl.CostEstimate(flops=int(us * 1.1e9), bytes_accessed=0, transcendentals=0)
 
 
-def params(limit=42):
+def params(limit=50):
     return pltpu.CompilerParams(vmem_limit_bytes=limit * 2**20)
 
 
@@ -875,6 +875,10 @@
             h[:, pl.ds(at, cut)] = piece[0].astype(F32).T
 
 
+def far_away(value):
+    return pltpu.with_memory_space_constraint(value, pltpu.HBM)
+
+
 def add(a, b):
     return (a.astype(F32) + b.astype(F32)).astype(BF16)
 
@@ -953,7 +957,9 @@
         [column] * 5 + [pl.BlockSpec((DH, features), lambda i, place: (place[0] & 1, 0))],
         [whole((4, 6, cut, features))],
         [like((4, 6, cut, features))],
-        (query_weight, key_weight, value_weight, state_key_weight, state_value_weight, output_weight),
+        tuple(map(far_away, (
+            query_weight, key_weight, value_weight, state_key_weight, state_value_weight, output_weight
+        ))),
         [pltpu.VMEM((DH, features), F32)],
     )
     (own_m,) = timed(5)(
@@ -964,7 +970,7 @@
         ],
         [whole((4, 2, wide, features))],
         [like((4, 2, wide, features))],
-        (hidden_weight, return_weight),
+        (far_away(hidden_weight), far_away(return_weight)),
         [pltpu.VMEM((hidden_cols // 2, features), F32)],
     )
 
@@ -1101,7 +1107,7 @@
         outs=[like((2, slots, wide, features))] * 2,
     )
     keep_r, send_r = hidden_grads(
-        partial(feed_weights, (0, 1)), operands=(grad_out, grad_out_other, after(act, pre))
+        partial(feed_weights, (0, 1)), operands=(grad_out, grad_out_other, far_away(after(act, pre)))
     )
     mlp_got = after(mlp_got, keep_r)
     mid_got = after(mid_got, keep_r)
@@ -1121,7 +1127,7 @@
     )
     resid_other = flip(resid_b, 1)
     keep_h, send_h = hidden_grads(
-        partial(feed_weights, (0, 2)), operands=(m, m_other, after(pre, resid_b))
+        partial(feed_weights, (0, 2)), operands=(m, m_other, far_away(after(pre, resid_b)))
     )
 
     grad_in, grad_in_other, grad_ctx, grad_ctx_other, d, ds = timed(27)(
@@ -1133,7 +1139,7 @@
             like((CTX, features), F32), like((CTX, features)),
             like((rows, slots * 3 * DH)), like((2 * CTX, slots * 2 * DH)),
         ],
-        (after(resid_b, keep_h), resid_other, *weights, q, k, v, state, lse),
+        (after(resid_b, keep_h), resid_other, *map(far_away, weights), q, k, v, state, lse),
         [
             pltpu.VMEM((6, DH, features), BF16),
             pltpu.VMEM((2, CTX + block_len, DH), BF16),

time: 558 us -> 536 us (0.961)
  local copies, waits for them, and re-layouts: 79.8 us -> 28.4 us
  Pallas kernels: 163 us -> 184 us
  waiting for transfers between devices: 124 us -> 137 us
  other arithmetic: 46.7 us -> 39.8 us
    unnamed x198 -> x120, local copies, waits for them, and re-layouts: 53.8 us -> 11.3 us
    pallas_call x16, Pallas kernels: 141 us -> 162 us  [launch(): pl.pallas_call(kernel, grid_spec=pltpu.PrefetchScalarGridSpec(num_scalar_...]
    ppermute x40, waiting for transfers between devices: 54.8 us -> 65.3 us  [flip(): return lax.ppermute(value, 'seq', [(i, i ^ mask) for i in range(count)])]
  transfers between devices with their start and end apart: 78 -> 78, of which waited for: 21 -> 22; matrix products, arithmetic and copies ran while one was open for 14% -> 11% of each run, Pallas kernels for 23% -> 27%
where the time goes in v4:
time: 536 us; the launch traced here: 528 us
  Pallas kernels  184 us (34%)
  waiting for transfers between devices  137 us (26%)
  starting transfers between devices  122 us (23%)
  other arithmetic  39.8 us (7%)
  local copies, waits for them, and re-layouts  28.4 us (5%)
  between operations  15.9 us (3%)
    pallas_call x16, Pallas kernels, launch(): pl.pallas_call(kernel, grid_spec=pltpu.PrefetchScalarGridSpec(num_scalar_...  162 us
    ppermute x40, waiting for transfers between devices, flip(): return lax.ppermute(value, 'seq', [(i, i ^ mask) for i in range(count)])  65.3 us
    ppermute x40, starting transfers between devices, flip(): return lax.ppermute(value, 'seq', [(i, i ^ mask) for i in range(count)])  37.6 us
    ppermute x11, starting transfers between devices, shifted(): lax.ppermute(value, 'seq', [(i, i + steps) for i in range(first, last)])  27.5 us
    ppermute x6, waiting for transfers between devices, line_reduce(): lax.ppermute(add(chunks[count - k], coming, k), 'tp', [(i, i - 1) for i i...  24.3 us
    pallas_call x6, Pallas kernels, call(): pl.pallas_call(kernel, out_shape=[jax.ShapeDtypeStruct(shape, dtype) for...  22.1 us
    ppermute x3, waiting for transfers between devices, line_steps(): lax.ppermute(lefts[-1], 'tp', [(i, i + 1) for i in range(k - 1, count - 1)])  18.7 us
    convert_element_type x8, other arithmetic, add(): return (a.astype(F32) + b.astype(F32)).astype(BF16)  14.2 us
  transfers between devices with their start and end apart: 78, of which 22 were waited for; matrix products, arithmetic and copies ran while one was open for 11% of the time, Pallas kernels for 27%

profile of v4, /device:TPU:17, one launch (start us, length us, event | category | flops | bytes accessed | tf_op | source)
XLA Modules:
  0.0 528.1 jit_solution(6919803779247515694)
XLA Ops:
  13.7 3.2 collective-permute-start.2
  17.8 6.7 %all-to-all-start = ((f32[32,8,128]{2,1,0:T(8,128)}), f32[32,8,128]{2,1,0:T(8,128)S(1)}, u32[]{:S(2)}, u32[]{:S(2)}) async-start(f32[32,8,128]{2,1,0:T(8,128)} %broadcast_in_dim.11), calls=%async_computation | async-start | bytes 262144 | tf_op jit(solution)/shard_map/all_to_all | solution.py:995
  26.2 3.3 collective-permute-start
  43.7 12.0 %all-to-all-done = f32[32,8,128]{2,1,0:T(8,128)S(1)} async-done(((f32[32,8,128]{2,1,0:T(8,128)}), f32[32,8,128]{2,1,0:T(8,128)S(1)}, u32[]{:S(2)}, u32[]{:S(2)}) %all-to-all-start) | async-done | bytes 131104 | tf_op jit(solution)/shard_map/all_to_all | solution.py:995
  62.5 3.5 collective-permute-start.14
  66.0 8.5 %shard_map.257 = (f32[16,8,128]{2,1,0:T(8,128)S(1)}, f32[16,8,128]{2,1,0:T(8,128)S(1)}) custom-call(f32[16,8,128]{2,1,0:T(8,128)S(1)} %get-tuple-element.100.decay_ref, f32[512,8,128]{2,1,0:T(8,128)S(1)} %convert_multiply_fusion.1.u_ref), custom_call_target="tpu_custom_call" | custom-call | flops 8800000000 | tf_op jit(solution)/shard_map/pallas_call | solution.py:164
  74.5 13.6 %collective-permute-done.6.f1 = bf16[3,6,32,1024]{3,2,1,0:T(8,128)(2,1)S(1)} collective-permute-done((bf16[3,6,32,1024]{3,2,1,0:T(8,128)(2,1)S(1)}, bf16[3,6,32,1024]{3,2,1,0:T(8,128)(2,1)S(1)}, u32[]{:S(2)}, u32[]{:S(2)}) %collective-permute-start.6) | collective-permute-done | bytes 1179680 | tf_op jit(solution)/shard_map/ppermute | solution.py:33
  91.2 3.8 collective-permute-start.8
  97.5 9.5 %collective-permute-done.14 = bf16[2,128,1024]{2,1,0:T(8,128)(2,1)S(1)} collective-permute-done((bf16[2,128,1024]{2,1,0:T(8,128)(2,1)S(1)}, bf16[2,128,1024]{2,1,0:T(8,128)(2,1)S(1)}, u32[]{:S(2)}, u32[]{:S(2)}) %collective-permute-start.14) | collective-permute-done | bytes 524320 | tf_op jit(solution)/shard_map/ppermute | solution.py:544
  107.0 4.3 collective-permute-start.10
  120.5 9.4 %shard_map.259 = (bf16[1024,512]{1,0:T(8,128)(2,1)S(1)}, bf16[1024,512]{1,0:T(8,128)(2,1)S(1)}, bf16[1024,512]{1,0:T(8,128)(2,1)}) custom-call(s32[3]{0:T(128)S(1)} %pad_add_fusion.place, bf16[512,1024]{1,0:T(8,128)(2,1)} %copy-done, bf16[512,1024]{1,0:T(8,128)(2,1)} %collective-permute-done.4.x1, bf16[4,6,32,1024]{3,2,1,0:T(8,128)(2,1)} %copy-done.17, ...), custom_call_target="tpu_custom_call" | custom-call | flops 8800000000 | tf_op jit(solution)/shard_map/pallas_call | solution.py:523
  131.8 21.0 %shard_map.260 = (f32[512,1024]{1,0:T(8,128)}, bf16[512,1024]{1,0:T(8,128)(2,1)S(1)}, bf16[256,1024]{1,0:T(8,128)(2,1)S(1)}, bf16[1024,512]{1,0:T(8,128)(2,1)}, f32[4,1024,1]{2,1,0:T(8,128)}) custom-call(s32[3]{0:T(128)S(1)} %pad_add_fusion.place, bf16[128,1024]{1,0:T(8,128)(2,1)S(1)} %bitcast.191, bf16[128,1024]{1,0:T(8,128)(2,1)S(1)} %collective-permute-done.16.c1, ...), custom_call_target="tpu_custom_call" | custom-call | flops 22000001024 | tf_op jit(solution)/shard_map/pallas_call | solution.py:523
  155.6 4.8 shard_map.261
  167.9 11.5 %collective-permute-done.22 = bf16[3,1,128,1024]{3,2,0,1:T(8,128)(2,1)S(1)} collective-permute-done((bf16[3,1,128,1024]{3,2,0,1:T(8,128)(2,1)S(1)}, bf16[3,1,128,1024]{3,2,0,1:T(8,128)(2,1)S(1)}, u32[]{:S(2)}, u32[]{:S(2)}) %collective-permute-start.22) | collective-permute-done | bytes 786464 | tf_op jit(solution)/shard_map/ppermute | solution.py:33
  179.4 15.9 %shard_map.262 = (bf16[1024,2048]{1,0:T(8,128)(2,1)}, bf16[1024,2048]{1,0:T(8,128)(2,1)}) custom-call(s32[3]{0:T(128)S(1)} %pad_add_fusion.place, bf16[512,1024]{1,0:T(8,128)(2,1)S(1)} %get-tuple-element.118.m0.a0, bf16[512,1024]{1,0:T(8,128)(2,1)S(1)} %collective-permute-done.24.m1.a1, bf16[4,2,128,1024]{3,2,1,0:T(8,128)(2,1)} %copy-done.16, ...), custom_call_target="tpu_custom_call" | custom-call | flops 15399999488 | tf_op jit(solution)/shard_map/pallas_call | solution.py:523
  195.3 23.1 %shard_map.263 = (f32[512,1024]{1,0:T(8,128)}, bf16[512,1024]{1,0:T(8,128)(2,1)S(1)}, f32[512,1024]{1,0:T(8,128)}, bf16[512,1024]{1,0:T(8,128)(2,1)}, bf16[1024,2048]{1,0:T(8,128)(2,1)}) custom-call(s32[3]{0:T(128)S(1)} %pad_add_fusion.place, bf16[512,1024]{1,0:T(8,128)(2,1)} %copy-done.2, bf16[512,1024]{1,0:T(8,128)(2,1)} %copy-done.20, ...), custom_call_target="tpu_custom_call" | custom-call | flops 23100000256 | tf_op jit(solution)/shard_map/pallas_call | solution.py:523
  219.7 8.4 %shard_map.264 = (bf16[2,4,128,1024]{3,2,1,0:T(8,128)(2,1)}, bf16[2,4,128,1024]{3,2,1,0:T(8,128)(2,1)}) custom-call(s32[3]{0:T(128)S(1)} %pad_add_fusion.place, bf16[512,1024]{1,0:T(8,128)(2,1)S(1)} %copy-done.3, bf16[512,1024]{1,0:T(8,128)(2,1)S(1)} %copy-done.21, bf16[1024,2048]{1,0:T(8,128)(2,1)} %get-tuple-element.124.act_ref.b_ref), custom_call_target="tpu_custom_call" | custom-call | flops 8800000000 | tf_op jit(solution)/shard_map/pallas_call | solution.py:523
  228.1 4.6 shard_map.265
  232.8 6.3 %shard_map.266 = (f32[512,1024]{1,0:T(8,128)}, bf16[512,1024]{1,0:T(8,128)(2,1)}, f32[1,1024]{1,0:T(1,128)S(1)}) custom-call(s32[3]{0:T(128)S(1)} %pad_add_fusion.place, f32[512,1024]{1,0:T(8,128)} %get-tuple-element.127.residual, f32[512,1024]{1,0:T(8,128)} %get-tuple-element.128.own, bf16[512,1024]{1,0:T(8,128)(2,1)} %collective-permute-done.26.got, ...), custom_call_target="tpu_custom_call" | custom-call | flops 5500000256 | tf_op jit(solution)/shard_map/pallas_call | solution.py:523
  239.5 8.4 %shard_map.267 = (bf16[2,4,128,1024]{3,2,1,0:T(8,128)(2,1)}, bf16[2,4,128,1024]{3,2,1,0:T(8,128)(2,1)}) custom-call(s32[3]{0:T(128)S(1)} %pad_add_fusion.place, bf16[512,1024]{1,0:T(8,128)(2,1)S(1)} %get-tuple-element.118.m0.a0, bf16[512,1024]{1,0:T(8,128)(2,1)S(1)} %copy-done.23, bf16[1024,2048]{1,0:T(8,128)(2,1)} %get-tuple-element.132.b_ref), custom_call_target="tpu_custom_call" | custom-call | flops 8800000000 | tf_op jit(solution)/shard_map/pallas_call | solution.py:523
  251.1 27.1 %shard_map.268 = (f32[512,1024]{1,0:T(8,128)}, bf16[512,1024]{1,0:T(8,128)(2,1)S(1)}, f32[128,1024]{1,0:T(8,128)S(1)}, bf16[128,1024]{1,0:T(8,128)(2,1)S(1)}, bf...) custom-call(s32[3]{0:T(128)S(1)} %pad_add_fusion.place, bf16[512,1024]{1,0:T(8,128)(2,1)} %get-tuple-element.134.g0, ...), custom_call_target="tpu_custom_call" | custom-call | flops 29699999744 | tf_op jit(solution)/shard_map/pallas_call | solution.py:523
  278.9 10.5 %shard_map.270 = (bf16[2,4,3,32,1024]{4,3,2,1,0:T(8,128)(2,1)}, bf16[2,4,3,32,1024]{4,3,2,1,0:T(8,128)(2,1)}, bf16[2,4,3,32,1024]{4,3,2,1,0:T(8,128)(2,1)}, bf16[2,4,3,32,1024]{4,3,2,1,0:T(8,128)(2,1)}) custom-call(s32[3]{0:T(128)S(1)} %pad_add_fusion.place, bf16[512,1024]{1,0:T(8,128)(2,1)S(1)} %copy-done.1, bf16[512,1024]{1,0:T(8,128)(2,1)} %collective-permute-done.4.x1, ...), custom_call_target="tpu_custom_call" | custom-call | flops 11000000512 | tf_op jit(solution)/shard_map/pallas_call | solution.py:523
  291.9 4.5 collective-permute-done.30
  310.6 4.1 collective-permute-done.34
  317.6 4.5 shard_map.271
  322.8 5.1 shard_map.272
  327.9 15.0 %collective-permute-done.43 = bf16[4,128,1024]{2,1,0:T(8,128)(2,1)} collective-permute-done((bf16[4,128,1024]{2,1,0:T(8,128)(2,1)}, bf16[4,128,1024]{2,1,0:T(8,128)(2,1)}, u32[]{:S(2)}, u32[]{:S(2)}) %collective-permute-start.43) | collective-permute-done | bytes 1048608 | tf_op jit(solution)/shard_map/ppermute | solution.py:33
  346.2 3.4 collective-permute-start.38
  349.7 5.5 %shard_map.273 = (f32[16,8,128]{2,1,0:T(8,128)S(1)}, f32[16,8,128]{2,1,0:T(8,128)S(1)}) custom-call(f32[16,8,128]{2,1,0:T(8,128)S(1)} %copy-done.32, f32[16,8,128]{2,1,0:T(8,128)S(1)} %copy-done.11, f32[128,8,128]{2,1,0:T(8,128)S(1)} %bitcast.181, f32[128,8,128]{2,1,0:T(8,128)S(1)} %bitcast.183), custom_call_target="tpu_custom_call" | custom-call | flops 5500000256 | tf_op jit(solution)/shard_map/pallas_call | solution.py:164
  358.7 11.1 %collective-permute-done.37 = bf16[512,1024]{1,0:T(8,128)(2,1)} collective-permute-done((bf16[512,1024]{1,0:T(8,128)(2,1)S(1)}, bf16[512,1024]{1,0:T(8,128)(2,1)}, u32[]{:S(2)}, u32[]{:S(2)}) %collective-permute-start.37) | collective-permute-done | bytes 1048608 | tf_op jit(solution)/shard_map/ppermute | solution.py:46
  372.0 3.2 collective-permute-start.39
  375.2 3.4 collective-permute-done.47
  388.4 6.1 %collective-permute-done.41 = bf16[512,1024]{1,0:T(8,128)(2,1)S(1)} collective-permute-done((bf16[512,1024]{1,0:T(8,128)(2,1)}, bf16[512,1024]{1,0:T(8,128)(2,1)S(1)}, u32[]{:S(2)}, u32[]{:S(2)}) %collective-permute-start.41) | collective-permute-done | bytes 1048608 | tf_op jit(solution)/shard_map/ppermute | solution.py:46
  395.8 4.1 collective-permute-start.42
  403.3 3.5 collective-permute-done.65
  410.5 4.8 collective-permute-done.52
  420.5 6.0 %collective-permute-done.66 = bf16[2,128,1024]{2,1,0:T(8,128)(2,1)S(1)} collective-permute-done((bf16[2,128,1024]{2,1,0:T(8,128)(2,1)S(1)}, bf16[2,128,1024]{2,1,0:T(8,128)(2,1)S(1)}, u32[]{:S(2)}, u32[]{:S(2)}) %collective-permute-start.66) | collective-permute-done | bytes 524320 | tf_op jit(solution)/shard_map/ppermute | solution.py:73
  429.6 4.2 collective-permute-start.64
  437.4 3.4 collective-permute-start.51
  444.4 10.1 %collective-permute-done.54 = bf16[2,3,32,1024]{3,2,1,0:T(8,128)(2,1)S(1)} collective-permute-done((bf16[2,3,32,1024]{3,2,1,0:T(8,128)(2,1)S(1)}, bf16[2,3,32,1024]{3,2,1,0:T(8,128)(2,1)S(1)}, u32[]{:S(2)}, u32[]{:S(2)}) %collective-permute-start.54) | collective-permute-done | bytes 393248 | tf_op jit(solution)/shard_map/ppermute | solution.py:73
  457.0 7.5 %collective-permute-start.57 = (bf16[6,32,1024]{2,1,0:T(8,128)(2,1)S(1)}, bf16[6,32,1024]{2,1,0:T(8,128)(2,1)}, u32[]{:S(2)}, u32[]{:S(2)}) collective-permute-start(bf16[6,32,1024]{2,1,0:T(8,128)(2,1)S(1)} %bitcast.187), channel_id=1, source_target_pairs={{0,24},{4,28},{8,16},{12,20},{16,8},{20,12},{24,0},{28,4},{1,25},{... | collective-permute-start | bytes 1179656 | tf_op jit(solution)/shard_map/ppermute | solution.py:33
  464.5 5.9 %all-to-all-start.1 = ((f32[32,24,128]{2,1,0:T(8,128)}), f32[32,24,128]{2,1,0:T(8,128)}, u32[]{:S(2)}, u32[]{:S(2)}) async-start(f32[32,24,128]{2,1,0:T(8,128)} %pad_maximum_fusion.7), calls=%async_computation.1 | async-start | bytes 786432 | tf_op jit(solution)/shard_map/all_to_all | solution.py:1249
  477.5 4.3 collective-permute-start.70
  482.3 3.7 maximum_convert_fusion
  487.1 3.5 collective-permute-done.68.n1
  492.6 10.0 %collective-permute-done.70.n3 = bf16[2,128,1024]{2,1,0:T(8,128)(2,1)S(1)} collective-permute-done((bf16[2,128,1024]{2,1,0:T(8,128)(2,1)S(1)}, bf16[2,128,1024]{2,1,0:T(8,128)(2,1)S(1)}, u32[]{:S(2)}, u32[]{:S(2)}) %collective-permute-start.70) | collective-permute-done | bytes 524320 | tf_op jit(solution)/shard_map/ppermute | solution.py:33
  506.4 6.2 %shard_map.274 = (f32[1024,256]{1,0:T(8,128)}, f32[1024,256]{1,0:T(8,128)}, f32[1024,256]{1,0:T(8,128)}, f32[256,1024]{1,0:T(8,128)}, f32[1024,256]{1,0:T(8,128)}, /*index=5*/f32[1024,256]{1,0:T(8,128)}) custom-call(s32[3]{0:T(128)S(1)} %pad_add_fusion.place, bf16[6,32,1024]{2,1,0:T(8,128)(2,1)S(1)} %bitcast.189, ...), custom_call_target="tpu_custom_call" | custom-call | flops 5500000256 | tf_op jit(solution)/shard_map/pallas_call | solution.py:523
  512.7 6.3 %shard_map.275 = (f32[1024,1024]{1,0:T(8,128)}, f32[1024,1024]{1,0:T(8,128)}) custom-call(s32[3]{0:T(128)S(1)} %pad_add_fusion.place, bf16[2,128,1024]{2,1,0:T(8,128)(2,1)S(1)} %add_convert_fusion.8.n0, bf16[2,128,1024]{2,1,0:T(8,128)(2,1)S(1)} %collective-permute-done.68.n1, bf16[2,128,1024]{2,1,0:T(8,128)(2,1)S(1)} %collective-permute-done.69.n2, ...), custom_call_target="tpu_custom_call" | custom-call | flops 5500000256 | tf_op jit(solution)/shard_map/pallas_call | solution.py:523
  (344 shorter events, 143.7 us)
Async XLA Ops:
  13.5 45.8 %collective-permute-start.3 = (bf16[6,32,1024]{2,1,0:T(8,128)(2,1)}, bf16[6,32,1024]{2,1,0:T(8,128)(2,1)}, u32[]{:S(2)}, u32[]{:S(2)}) collective-permute-start(bf16[6,32,1024]{2,1,0:T(8,128)(2,1)} %slice_bitcast_fusion.1), channel_id=1, source_target_pairs={{0,3},{1,0},{2,1},{3,2},{4,7},{5,4},{6,5},{7,6},{8,11},{9,8},{10,9... | collective-permute-start | bytes 1179656 | tf_op jit(solution)/shard_map/ppermute | solution.py:544
  13.7 45.6 %collective-permute-start.2 = (bf16[6,32,1024]{2,1,0:T(8,128)(2,1)}, bf16[6,32,1024]{2,1,0:T(8,128)(2,1)}, u32[]{:S(2)}, u32[]{:S(2)}) collective-permute-start(bf16[6,32,1024]{2,1,0:T(8,128)(2,1)} %slice_bitcast_fusion.1), channel_id=1, source_target_pairs={{0,2},{1,3},{2,0},{3,1},{4,6},{5,7},{6,4},{7,5},{8,10},{9,11},{10,... | collective-permute-start | bytes 1179656 | tf_op jit(solution)/shard_map/ppermute | solution.py:544
  16.9 42.4 %collective-permute-start.1 = (bf16[6,32,1024]{2,1,0:T(8,128)(2,1)}, bf16[6,32,1024]{2,1,0:T(8,128)(2,1)}, u32[]{:S(2)}, u32[]{:S(2)}) collective-permute-start(bf16[6,32,1024]{2,1,0:T(8,128)(2,1)} %slice_bitcast_fusion.1), channel_id=1, source_target_pairs={{0,1},{1,2},{2,3},{3,0},{4,5},{5,6},{6,7},{7,4},{8,9},{9,10},{10,1... | collective-permute-start | bytes 1179656 | tf_op jit(solution)/shard_map/ppermute | solution.py:544
  17.8 38.0 %all-to-all-start = ((f32[32,8,128]{2,1,0:T(8,128)}), f32[32,8,128]{2,1,0:T(8,128)S(1)}, u32[]{:S(2)}, u32[]{:S(2)}) async-start(f32[32,8,128]{2,1,0:T(8,128)} %broadcast_in_dim.11), calls=%async_computation | async-start | bytes 262144 | tf_op jit(solution)/shard_map/all_to_all | solution.py:995
  24.5 298.1 %all-gather.3.cloned.1.call-start = ((), (), s32[]{:S(2)}) async-start(), calls=%async_computation.2 | async-start | bytes 5242880 | tf_op jit(solution)/shard_map/all_gather | solution.py:1118
  26.2 32.2 %collective-permute-start = (bf16[128,1024]{1,0:T(8,128)(2,1)}, bf16[128,1024]{1,0:T(8,128)(2,1)S(1)}, u32[]{:S(2)}, u32[]{:S(2)}) collective-permute-start(bf16[128,1024]{1,0:T(8,128)(2,1)} %dynamic-slice_bitcast_fusion), channel_id=1, source_target_pairs={{0,4},{4,8},{8,12},{12,16},{16,20},{20,24},{24,28},{1,5},{5,9},{9,... | collective-permute-start | bytes 786440 | tf_op jit(solution)/shard_map/ppermute | solution.py:39
  34.3 28.2 %collective-permute-start.4 = (bf16[512,1024]{1,0:T(8,128)(2,1)S(1)}, bf16[512,1024]{1,0:T(8,128)(2,1)}, u32[]{:S(2)}, u32[]{:S(2)}) collective-permute-start(bf16[512,1024]{1,0:T(8,128)(2,1)S(1)} %fusion.5.x0), channel_id=1, source_target_pairs={{0,4},{4,0},{8,12},{12,8},{16,20},{20,16},{24,28},{28,24},{1,5},{5... | collective-permute-start | bytes 3145736 | tf_op jit(solution)/shard_map/ppermute | solution.py:33
  60.8 27.4 %collective-permute-start.6 = (bf16[3,6,32,1024]{3,2,1,0:T(8,128)(2,1)S(1)}, bf16[3,6,32,1024]{3,2,1,0:T(8,128)(2,1)S(1)}, u32[]{:S(2)}, u32[]{:S(2)}) collective-permute-start(bf16[3,6,32,1024]{3,2,1,0:T(8,128)(2,1)S(1)} %pad_maximum_fusion.2.f0), channel_id=1, source_target_pairs={{0,8},{4,12},{8,0},{12,4},{16,24},{20,28},{24,16},{28,20},{1,9},{5... | collective-permute-start | bytes 3538952 | tf_op jit(solution)/shard_map/ppermute | solution.py:33
  61.3 27.1 %collective-permute-start.7 = (bf16[3,6,32,1024]{3,2,1,0:T(8,128)(2,1)S(1)}, bf16[3,6,32,1024]{3,2,1,0:T(8,128)(2,1)S(1)}, u32[]{:S(2)}, u32[]{:S(2)}) collective-permute-start(bf16[3,6,32,1024]{3,2,1,0:T(8,128)(2,1)S(1)} %pad_maximum_fusion.2.f0), channel_id=1, source_target_pairs={{0,16},{4,20},{8,24},{12,28},{16,0},{20,4},{24,8},{28,12},{1,17},{... | collective-permute-start | bytes 3538952 | tf_op jit(solution)/shard_map/ppermute | solution.py:33
  62.4 34.4 %collective-permute-start.15 = (bf16[2,128,1024]{2,1,0:T(8,128)(2,1)S(1)}, bf16[2,128,1024]{2,1,0:T(8,128)(2,1)S(1)}, u32[]{:S(2)}, u32[]{:S(2)}) collective-permute-start(bf16[2,128,1024]{2,1,0:T(8,128)(2,1)S(1)} %copy-done.49), channel_id=1, source_target_pairs={{0,3},{1,0},{2,1},{3,2},{4,7},{5,4},{6,5},{7,6},{8,11},{9,8},{10,9... | collective-permute-start | bytes 1572872 | tf_op jit(solution)/shard_map/ppermute | solution.py:544
  62.5 44.5 %collective-permute-start.14 = (bf16[2,128,1024]{2,1,0:T(8,128)(2,1)S(1)}, bf16[2,128,1024]{2,1,0:T(8,128)(2,1)S(1)}, u32[]{:S(2)}, u32[]{:S(2)}) collective-permute-start(bf16[2,128,1024]{2,1,0:T(8,128)(2,1)S(1)} %copy-done.49), channel_id=1, source_target_pairs={{0,2},{1,3},{2,0},{3,1},{4,6},{5,7},{6,4},{7,5},{8,10},{9,11},{10,... | collective-permute-start | bytes 1572872 | tf_op jit(solution)/shard_map/ppermute | solution.py:544
  66.0 45.4 %collective-permute-start.13 = (bf16[2,128,1024]{2,1,0:T(8,128)(2,1)S(1)}, bf16[2,128,1024]{2,1,0:T(8,128)(2,1)S(1)}, u32[]{:S(2)}, u32[]{:S(2)}) collective-permute-start(bf16[2,128,1024]{2,1,0:T(8,128)(2,1)S(1)} %copy-done.49), channel_id=1, source_target_pairs={{0,1},{1,2},{2,3},{3,0},{4,5},{5,6},{6,7},{7,4},{8,9},{9,10},{10,1... | collective-permute-start | bytes 1572872 | tf_op jit(solution)/shard_map/ppermute | solution.py:544
  95.4 25.1 %collective-permute-start.17 = (bf16[3,3,32,1024]{3,2,1,0:T(8,128)(2,1)S(1)}, bf16[3,3,32,1024]{3,2,1,0:T(8,128)(2,1)S(1)}, u32[]{:S(2)}, u32[]{:S(2)}) collective-permute-start(bf16[3,3,32,1024]{3,2,1,0:T(8,128)(2,1)S(1)} %slice.304), channel_id=1, source_target_pairs={{0,8},{4,12},{8,0},{12,4},{16,24},{20,28},{24,16},{28,20},{1,9},{5... | collective-permute-start | bytes 1769480 | tf_op jit(solution)/shard_map/ppermute | solution.py:33
  96.8 23.7 %collective-permute-start.18 = (bf16[3,3,32,1024]{3,2,1,0:T(8,128)(2,1)S(1)}, bf16[3,3,32,1024]{3,2,1,0:T(8,128)(2,1)S(1)}, u32[]{:S(2)}, u32[]{:S(2)}) collective-permute-start(bf16[3,3,32,1024]{3,2,1,0:T(8,128)(2,1)S(1)} %slice.305), channel_id=1, source_target_pairs={{0,16},{4,20},{8,24},{12,28},{16,0},{20,4},{24,8},{28,12},{1,17},{... | collective-permute-start | bytes 1769480 | tf_op jit(solution)/shard_map/ppermute | solution.py:33
  114.7 38.3 %collective-permute-start.20 = (bf16[3,2,128,1024]{3,2,0,1:T(8,128)(2,1)S(1)}, bf16[3,2,128,1024]{3,2,0,1:T(8,128)(2,1)S(1)}, u32[]{:S(2)}, u32[]{:S(2)}) collective-permute-start(bf16[3,2,128,1024]{3,2,0,1:T(8,128)(2,1)S(1)} %pad_maximum_fusion.1), channel_id=1, source_target_pairs={{0,8},{4,12},{8,0},{12,4},{16,24},{20,28},{24,16},{28,20},{1,9},{5... | collective-permute-start | bytes 4718600 | tf_op jit(solution)/shard_map/ppermute | solution.py:33
  115.1 37.9 %collective-permute-start.21 = (bf16[3,2,128,1024]{3,2,0,1:T(8,128)(2,1)S(1)}, bf16[3,2,128,1024]{3,2,0,1:T(8,128)(2,1)S(1)}, u32[]{:S(2)}, u32[]{:S(2)}) collective-permute-start(bf16[3,2,128,1024]{3,2,0,1:T(8,128)(2,1)S(1)} %pad_maximum_fusion.1), channel_id=1, source_target_pairs={{0,16},{4,20},{8,24},{12,28},{16,0},{20,4},{24,8},{28,12},{1,17},{... | collective-permute-start | bytes 4718600 | tf_op jit(solution)/shard_map/ppermute | solution.py:33
  160.4 19.0 %collective-permute-start.24 = (bf16[512,1024]{1,0:T(8,128)(2,1)S(1)}, bf16[512,1024]{1,0:T(8,128)(2,1)S(1)}, u32[]{:S(2)}, u32[]{:S(2)}) collective-permute-start(bf16[512,1024]{1,0:T(8,128)(2,1)S(1)} %get-tuple-element.118.m0.a0), channel_id=1, source_target_pairs={{0,4},{4,0},{8,12},{12,8},{16,20},{20,16},{24,28},{28,24},{1,5},{5... | collective-permute-start | bytes 3145736 | tf_op jit(solution)/shard_map/ppermute | solution.py:33
  160.6 18.8 %collective-permute-start.22 = (bf16[3,1,128,1024]{3,2,0,1:T(8,128)(2,1)S(1)}, bf16[3,1,128,1024]{3,2,0,1:T(8,128)(2,1)S(1)}, u32[]{:S(2)}, u32[]{:S(2)}) collective-permute-start(bf16[3,1,128,1024]{3,2,0,1:T(8,128)(2,1)S(1)} %slice.306), channel_id=1, source_target_pairs={{0,8},{4,12},{8,0},{12,4},{16,24},{20,28},{24,16},{28,20},{1,9},{5... | collective-permute-start | bytes 2359304 | tf_op jit(solution)/shard_map/ppermute | solution.py:33
  163.0 32.3 %collective-permute-start.23 = (bf16[3,1,128,1024]{3,2,0,1:T(8,128)(2,1)S(1)}, bf16[3,1,128,1024]{3,2,0,1:T(8,128)(2,1)S(1)}, u32[]{:S(2)}, u32[]{:S(2)}) collective-permute-start(bf16[3,1,128,1024]{3,2,0,1:T(8,128)(2,1)S(1)} %slice.307), channel_id=1, source_target_pairs={{0,16},{4,20},{8,24},{12,28},{16,0},{20,4},{24,8},{28,12},{1,17},{... | collective-permute-start | bytes 2359304 | tf_op jit(solution)/shard_map/ppermute | solution.py:33
  247.9 48.5 %collective-permute-start.30 = (bf16[2,4,128,1024]{3,2,1,0:T(8,128)(2,1)}, bf16[2,4,128,1024]{3,2,1,0:T(8,128)(2,1)S(1)}, u32[]{:S(2)}, u32[]{:S(2)}) collective-permute-start(bf16[2,4,128,1024]{3,2,1,0:T(8,128)(2,1)} %get-tuple-element.143), channel_id=1, source_target_pairs={{0,16},{4,20},{8,24},{12,28},{16,0},{20,4},{24,8},{28,12},{1,17},{... | collective-permute-start | bytes 6291464 | tf_op jit(solution)/shard_map/ppermute | solution.py:33
  250.1 47.2 %collective-permute-start.31 = (bf16[2,4,128,1024]{3,2,1,0:T(8,128)(2,1)}, bf16[2,4,128,1024]{3,2,1,0:T(8,128)(2,1)S(1)}, u32[]{:S(2)}, u32[]{:S(2)}) collective-permute-start(bf16[2,4,128,1024]{3,2,1,0:T(8,128)(2,1)} %get-tuple-element.145), channel_id=1, source_target_pairs={{0,8},{4,12},{8,0},{12,4},{16,24},{20,28},{24,16},{28,20},{1,9},{5... | collective-permute-start | bytes 6291464 | tf_op jit(solution)/shard_map/ppermute | solution.py:33
  278.2 44.3 %collective-permute-start.28 = (bf16[512,1024]{1,0:T(8,128)(2,1)S(1)}, bf16[512,1024]{1,0:T(8,128)(2,1)}, u32[]{:S(2)}, u32[]{:S(2)}) collective-permute-start(bf16[512,1024]{1,0:T(8,128)(2,1)S(1)} %get-tuple-element.138), channel_id=1, source_target_pairs={{0,4},{4,0},{8,12},{12,8},{16,20},{20,16},{24,28},{28,24},{1,5},{5... | collective-permute-start | bytes 3145736 | tf_op jit(solution)/shard_map/ppermute | solution.py:33
  289.5 20.9 %collective-permute-start.36 = (bf16[128,1024]{1,0:T(8,128)(2,1)S(1)}, bf16[128,1024]{1,0:T(8,128)(2,1)S(1)}, u32[]{:S(2)}, u32[]{:S(2)}) collective-permute-start(bf16[128,1024]{1,0:T(8,128)(2,1)S(1)} %add_convert_fusion.14), channel_id=1, source_target_pairs={{4,0},{8,4},{12,8},{16,12},{20,16},{24,20},{28,24},{5,1},{9,5},{13... | collective-permute-start | bytes 786440 | tf_op jit(solution)/shard_map/ppermute | solution.py:39
  317.5 25.5 %collective-permute-start.43 = (bf16[4,128,1024]{2,1,0:T(8,128)(2,1)}, bf16[4,128,1024]{2,1,0:T(8,128)(2,1)}, u32[]{:S(2)}, u32[]{:S(2)}) collective-permute-start(bf16[4,128,1024]{2,1,0:T(8,128)(2,1)} %get-tuple-element.164), channel_id=1, source_target_pairs={{0,16},{4,20},{8,24},{12,28},{16,0},{20,4},{24,8},{28,12},{1,17},{... | collective-permute-start | bytes 3145736 | tf_op jit(solution)/shard_map/ppermute | solution.py:33
  317.5 25.4 %collective-permute-start.44 = (bf16[4,128,1024]{2,1,0:T(8,128)(2,1)}, bf16[4,128,1024]{2,1,0:T(8,128)(2,1)}, u32[]{:S(2)}, u32[]{:S(2)}) collective-permute-start(bf16[4,128,1024]{2,1,0:T(8,128)(2,1)} %get-tuple-element.166), channel_id=1, source_target_pairs={{0,8},{4,12},{8,0},{12,4},{16,24},{20,28},{24,16},{28,20},{1,9},{5... | collective-permute-start | bytes 3145736 | tf_op jit(solution)/shard_map/ppermute | solution.py:33
  342.9 35.7 %collective-permute-start.47 = (bf16[2,4,3,32,1024]{4,3,2,1,0:T(8,128)(2,1)}, bf16[2,4,3,32,1024]{4,3,2,1,0:T(8,128)(2,1)}, u32[]{:S(2)}, u32[]{:S(2)}) collective-permute-start(bf16[2,4,3,32,1024]{4,3,2,1,0:T(8,128)(2,1)} %get-tuple-element.171), channel_id=1, source_target_pairs={{0,16},{4,20},{8,24},{12,28},{16,0},{20,4},{24,8},{28,12},{1,17},{... | collective-permute-start | bytes 4718600 | tf_op jit(solution)/shard_map/ppermute | solution.py:33
  344.3 36.6 %collective-permute-start.45 = (bf16[2,4,3,32,1024]{4,3,2,1,0:T(8,128)(2,1)}, bf16[2,4,3,32,1024]{4,3,2,1,0:T(8,128)(2,1)}, u32[]{:S(2)}, u32[]{:S(2)}) collective-permute-start(bf16[2,4,3,32,1024]{4,3,2,1,0:T(8,128)(2,1)} %get-tuple-element.168), channel_id=1, source_target_pairs={{0,8},{4,12},{8,0},{12,4},{16,24},{20,28},{24,16},{28,20},{1,9},{5... | collective-permute-start | bytes 4718600 | tf_op jit(solution)/shard_map/ppermute | solution.py:33
  344.3 25.5 %collective-permute-start.37 = (bf16[512,1024]{1,0:T(8,128)(2,1)S(1)}, bf16[512,1024]{1,0:T(8,128)(2,1)}, u32[]{:S(2)}, u32[]{:S(2)}) collective-permute-start(bf16[512,1024]{1,0:T(8,128)(2,1)S(1)} %get-tuple-element.155), channel_id=1, source_target_pairs={{0,1},{1,2},{2,3},{4,5},{5,6},{6,7},{8,9},{9,10},{10,11},{12,13},{... | collective-permute-start | bytes 3145736 | tf_op jit(solution)/shard_map/ppermute | solution.py:46
  346.2 25.8 %collective-permute-start.38 = (bf16[512,1024]{1,0:T(8,128)(2,1)S(1)}, bf16[512,1024]{1,0:T(8,128)(2,1)}, u32[]{:S(2)}, u32[]{:S(2)}) collective-permute-start(bf16[512,1024]{1,0:T(8,128)(2,1)S(1)} %get-tuple-element.155), channel_id=1, source_target_pairs={{1,0},{2,1},{3,2},{5,4},{6,5},{7,6},{9,8},{10,9},{11,10},{13,12},{... | collective-permute-start | bytes 3145736 | tf_op jit(solution)/shard_map/ppermute | solution.py:48
  369.8 24.7 %collective-permute-start.41 = (bf16[512,1024]{1,0:T(8,128)(2,1)}, bf16[512,1024]{1,0:T(8,128)(2,1)S(1)}, u32[]{:S(2)}, u32[]{:S(2)}) collective-permute-start(bf16[512,1024]{1,0:T(8,128)(2,1)} %collective-permute-done.37), channel_id=1, source_target_pairs={{1,2},{2,3},{5,6},{6,7},{9,10},{10,11},{13,14},{14,15},{17,18},{18... | collective-permute-start | bytes 3145736 | tf_op jit(solution)/shard_map/ppermute | solution.py:46
  372.0 23.7 %collective-permute-start.39 = (bf16[512,1024]{1,0:T(8,128)(2,1)}, bf16[512,1024]{1,0:T(8,128)(2,1)S(1)}, u32[]{:S(2)}, u32[]{:S(2)}) collective-permute-start(bf16[512,1024]{1,0:T(8,128)(2,1)} %collective-permute-done.38), channel_id=1, source_target_pairs={{1,0},{2,1},{5,4},{6,5},{9,8},{10,9},{13,12},{14,13},{17,16},{18,1... | collective-permute-start | bytes 3145736 | tf_op jit(solution)/shard_map/ppermute | solution.py:48
  380.8 19.0 %collective-permute-start.48 = (bf16[4,3,32,1024]{3,2,1,0:T(8,128)(2,1)S(1)}, bf16[4,3,32,1024]{3,2,1,0:T(8,128)(2,1)S(1)}, u32[]{:S(2)}, u32[]{:S(2)}) collective-permute-start(bf16[4,3,32,1024]{3,2,1,0:T(8,128)(2,1)S(1)} %get-tuple-element.239), channel_id=1, source_target_pairs={{0,8},{4,12},{8,0},{12,4},{16,24},{20,28},{24,16},{28,20},{1,9},{5... | collective-permute-start | bytes 2359304 | tf_op jit(solution)/shard_map/ppermute | solution.py:33
  395.8 23.2 %collective-permute-start.42 = (bf16[512,1024]{1,0:T(8,128)(2,1)S(1)}, bf16[512,1024]{1,0:T(8,128)(2,1)S(1)}, u32[]{:S(2)}, u32[]{:S(2)}) collective-permute-start(bf16[512,1024]{1,0:T(8,128)(2,1)S(1)} %collective-permute-done.41), channel_id=1, source_target_pairs={{2,3},{6,7},{10,11},{14,15},{18,19},{22,23},{26,27},{30,31}} | collective-permute-start | bytes 3145736 | tf_op jit(solution)/shard_map/ppermute | solution.py:46
  399.9 20.6 %collective-permute-start.40 = (bf16[512,1024]{1,0:T(8,128)(2,1)S(1)}, bf16[512,1024]{1,0:T(8,128)(2,1)S(1)}, u32[]{:S(2)}, u32[]{:S(2)}) collective-permute-start(bf16[512,1024]{1,0:T(8,128)(2,1)S(1)} %collective-permute-done.39), channel_id=1, source_target_pairs={{1,0},{5,4},{9,8},{13,12},{17,16},{21,20},{25,24},{29,28}} | collective-permute-start | bytes 3145736 | tf_op jit(solution)/shard_map/ppermute | solution.py:48
  407.1 19.4 %collective-permute-start.66 = (bf16[2,128,1024]{2,1,0:T(8,128)(2,1)S(1)}, bf16[2,128,1024]{2,1,0:T(8,128)(2,1)S(1)}, u32[]{:S(2)}, u32[]{:S(2)}) collective-permute-start(bf16[2,128,1024]{2,1,0:T(8,128)(2,1)S(1)} %get-tuple-element.259), channel_id=1, source_target_pairs={{2,1},{3,2},{6,5},{7,6},{10,9},{11,10},{14,13},{15,14},{18,17},{19... | collective-permute-start | bytes 1572872 | tf_op jit(solution)/shard_map/ppermute | solution.py:73
  409.2 19.4 %collective-permute-start.63 = (bf16[2,128,1024]{2,1,0:T(8,128)(2,1)S(1)}, bf16[2,128,1024]{2,1,0:T(8,128)(2,1)S(1)}, u32[]{:S(2)}, u32[]{:S(2)}) collective-permute-start(bf16[2,128,1024]{2,1,0:T(8,128)(2,1)S(1)} %get-tuple-element.258), channel_id=1, source_target_pairs={{0,1},{1,2},{4,5},{5,6},{8,9},{9,10},{12,13},{13,14},{16,17},{17,1... | collective-permute-start | bytes 1572872 | tf_op jit(solution)/shard_map/ppermute | solution.py:72
  415.5 19.7 %collective-permute-start.53 = (bf16[2,3,32,1024]{3,2,1,0:T(8,128)(2,1)S(1)}, bf16[2,3,32,1024]{3,2,1,0:T(8,128)(2,1)S(1)}, u32[]{:S(2)}, u32[]{:S(2)}) collective-permute-start(bf16[2,3,32,1024]{3,2,1,0:T(8,128)(2,1)S(1)} %get-tuple-element.263), channel_id=1, source_target_pairs={{2,1},{3,2},{6,5},{7,6},{10,9},{11,10},{14,13},{15,14},{18,17},{19... | collective-permute-start | bytes 1179656 | tf_op jit(solution)/shard_map/ppermute | solution.py:73
  426.7 43.7 %collective-permute-start.67 = (bf16[2,128,1024]{2,1,0:T(8,128)(2,1)S(1)}, bf16[2,128,1024]{2,1,0:T(8,128)(2,1)}, u32[]{:S(2)}, u32[]{:S(2)}) collective-permute-start(bf16[2,128,1024]{2,1,0:T(8,128)(2,1)S(1)} %add_convert_fusion.9), channel_id=1, source_target_pairs={{1,0},{2,1},{3,2},{5,4},{6,5},{7,6},{9,8},{10,9},{11,10},{13,12},{... | collective-permute-start | bytes 1572872 | tf_op jit(solution)/shard_map/ppermute | solution.py:73
  429.6 41.2 %collective-permute-start.64 = (bf16[2,128,1024]{2,1,0:T(8,128)(2,1)}, bf16[2,128,1024]{2,1,0:T(8,128)(2,1)}, u32[]{:S(2)}, u32[]{:S(2)}) collective-permute-start(bf16[2,128,1024]{2,1,0:T(8,128)(2,1)} %add_convert_fusion.10), channel_id=1, source_target_pairs={{0,1},{1,2},{2,3},{4,5},{5,6},{6,7},{8,9},{9,10},{10,11},{12,13},{... | collective-permute-start | bytes 1572872 | tf_op jit(solution)/shard_map/ppermute | solution.py:72
  435.3 19.3 %collective-permute-start.54 = (bf16[2,3,32,1024]{3,2,1,0:T(8,128)(2,1)S(1)}, bf16[2,3,32,1024]{3,2,1,0:T(8,128)(2,1)S(1)}, u32[]{:S(2)}, u32[]{:S(2)}) collective-permute-start(bf16[2,3,32,1024]{3,2,1,0:T(8,128)(2,1)S(1)} %add_convert_fusion.12), channel_id=1, source_target_pairs={{1,0},{2,1},{3,2},{5,4},{6,5},{7,6},{9,8},{10,9},{11,10},{13,12},{... | collective-permute-start | bytes 1179656 | tf_op jit(solution)/shard_map/ppermute | solution.py:73
  454.8 21.4 %collective-permute-start.55 = (bf16[6,32,1024]{2,1,0:T(8,128)(2,1)S(1)}, bf16[6,32,1024]{2,1,0:T(8,128)(2,1)S(1)}, u32[]{:S(2)}, u32[]{:S(2)}) collective-permute-start(bf16[6,32,1024]{2,1,0:T(8,128)(2,1)S(1)} %bitcast.185), channel_id=1, source_target_pairs={{0,8},{4,12},{8,0},{12,4},{16,24},{20,28},{24,16},{28,20},{1,9},{5... | collective-permute-start | bytes 1179656 | tf_op jit(solution)/shard_map/ppermute | solution.py:33
  456.3 21.2 %collective-permute-start.56 = (bf16[6,32,1024]{2,1,0:T(8,128)(2,1)S(1)}, bf16[6,32,1024]{2,1,0:T(8,128)(2,1)}, u32[]{:S(2)}, u32[]{:S(2)}) collective-permute-start(bf16[6,32,1024]{2,1,0:T(8,128)(2,1)S(1)} %bitcast.186), channel_id=1, source_target_pairs={{0,16},{4,20},{8,24},{12,28},{16,0},{20,4},{24,8},{28,12},{1,17},{... | collective-permute-start | bytes 1179656 | tf_op jit(solution)/shard_map/ppermute | solution.py:33
  457.0 24.8 %collective-permute-start.57 = (bf16[6,32,1024]{2,1,0:T(8,128)(2,1)S(1)}, bf16[6,32,1024]{2,1,0:T(8,128)(2,1)}, u32[]{:S(2)}, u32[]{:S(2)}) collective-permute-start(bf16[6,32,1024]{2,1,0:T(8,128)(2,1)S(1)} %bitcast.187), channel_id=1, source_target_pairs={{0,24},{4,28},{8,16},{12,20},{16,8},{20,12},{24,0},{28,4},{1,25},{... | collective-permute-start | bytes 1179656 | tf_op jit(solution)/shard_map/ppermute | solution.py:33
  464.5 21.5 %all-to-all-start.1 = ((f32[32,24,128]{2,1,0:T(8,128)}), f32[32,24,128]{2,1,0:T(8,128)}, u32[]{:S(2)}, u32[]{:S(2)}) async-start(f32[32,24,128]{2,1,0:T(8,128)} %pad_maximum_fusion.7), calls=%async_computation.1 | async-start | bytes 786432 | tf_op jit(solution)/shard_map/all_to_all | solution.py:1249
  477.5 25.2 %collective-permute-start.70 = (bf16[2,128,1024]{2,1,0:T(8,128)(2,1)S(1)}, bf16[2,128,1024]{2,1,0:T(8,128)(2,1)S(1)}, u32[]{:S(2)}, u32[]{:S(2)}) collective-permute-start(bf16[2,128,1024]{2,1,0:T(8,128)(2,1)S(1)} %add_convert_fusion.8.n0), channel_id=1, source_target_pairs={{0,24},{4,28},{8,16},{12,20},{16,8},{20,12},{24,0},{28,4},{1,25},{... | collective-permute-start | bytes 1572872 | tf_op jit(solution)/shard_map/ppermute | solution.py:33
  481.8 21.8 %collective-permute-start.59 = (bf16[6,32,1024]{2,1,0:T(8,128)(2,1)S(1)}, bf16[6,32,1024]{2,1,0:T(8,128)(2,1)}, u32[]{:S(2)}, u32[]{:S(2)}) collective-permute-start(bf16[6,32,1024]{2,1,0:T(8,128)(2,1)S(1)} %collective-permute-done.55.n1), channel_id=1, source_target_pairs={{0,4},{4,0},{8,12},{12,8},{16,20},{20,16},{24,28},{28,24},{1,5},{5... | collective-permute-start | bytes 1179656 | tf_op jit(solution)/shard_map/ppermute | solution.py:33
  482.1 21.4 %collective-permute-start.60 = (bf16[6,32,1024]{2,1,0:T(8,128)(2,1)}, bf16[6,32,1024]{2,1,0:T(8,128)(2,1)}, u32[]{:S(2)}, u32[]{:S(2)}) collective-permute-start(bf16[6,32,1024]{2,1,0:T(8,128)(2,1)} %collective-permute-done.56.n2), channel_id=1, source_target_pairs={{0,4},{4,0},{8,12},{12,8},{16,20},{20,16},{24,28},{28,24},{1,5},{5... | collective-permute-start | bytes 1179656 | tf_op jit(solution)/shard_map/ppermute | solution.py:33
  492.6 20.1 %collective-permute-start.71 = (bf16[2,128,1024]{2,1,0:T(8,128)(2,1)S(1)}, bf16[2,128,1024]{2,1,0:T(8,128)(2,1)S(1)}, u32[]{:S(2)}, u32[]{:S(2)}) collective-permute-start(bf16[2,128,1024]{2,1,0:T(8,128)(2,1)S(1)} %add_convert_fusion.8.n0), channel_id=1, source_target_pairs={{0,4},{4,0},{8,12},{12,8},{16,20},{20,16},{24,28},{28,24},{1,5},{5... | collective-permute-start | bytes 1572872 | tf_op jit(solution)/shard_map/ppermute | solution.py:33
  (86 other events, 1358.3 us)
Sparse Core Ops, SparseCore 0:
  239.6 79.5 all-gather.2

commit v5 on v4

--- a/solution.py
+++ b/solution.py
@@ -737,23 +737,20 @@
     return jnp.where(x >= 0, 1.0 - tail, tail), bell * (1.0 / math.sqrt(2.0 * math.pi))
 
 
-def load_hidden(j, w, own, far, into):
-    rows = own.shape[2]
-
-    @pl.when(j == 0)
-    def _():
-        for p in range(4):
-            into[p * rows : (p + 1) * rows] = own[p, w]
-
-    @pl.when(j > 0)
-    def _():
-        for p in range(3):
-            into[p * rows : (p + 1) * rows] = far[p][0, w]
-        into[3 * rows :] = far[3 + w][0]
-
-
-def feed_in(place, m0, m1, own, f0, f1, f2, f3, act_ref, slope_ref, wh):
-    load_hidden(pl.program_id(0), 0, own, (f0, f1, f2, f3), wh)
+def load_hidden(p, w, own, far, first, into):
+    rows = into.shape[0] // 4
+    into[0:rows] = own[0, w]
+    for i, piece in enumerate(far):
+        @pl.when(p == first + i)
+        def _():
+            for slot in range(3):
+                held = piece[slot, w] if len(piece.shape) == 4 else piece[slot]
+                into[(1 + slot) * rows : (2 + slot) * rows] = held
+
+
+def feed_in(first, place, m0, m1, own, *rest):
+    *far, act_ref, slope_ref, wh = rest
+    load_hidden(pl.program_id(0) + first, 0, own, far, first, wh)
     rows = m0.shape[0]
     for half, m in enumerate((m0, m1)):
         saved = slice(half * rows, (half + 1) * rows)
@@ -763,26 +760,35 @@
         slope_ref[saved] = (part + pre * bell).astype(BF16)
 
 
-def feed_out(place, g0, g1, own, f0, f1, f2, f3, f4, act_ref, slope_ref,
+def feed_out(place, g0, g1, own, f0, f1, f2, h3, r3, act_a, slope_a, act_b, slope_b,
              mlp0, mlp1, mid0, mid1, pre_ref, wh, wr, mlp, mid):
-    j = pl.program_id(0)
-    load_hidden(j, 0, own, (f0, f1, f2, f3, f4), wh)
-    load_hidden(j, 1, own, (f0, f1, f2, f3, f4), wr)
+    p = pl.program_id(0)
+    load_hidden(p, 0, own, (f0, f1, f2, h3), 0, wh)
+    load_hidden(p, 1, own, (f0, f1, f2, r3), 0, wr)
     rows = g0.shape[0]
 
-    @pl.when(j == 0)
+    @pl.when(p == 0)
     def _():
         mlp[...] = jnp.zeros_like(mlp)
         mid[...] = jnp.zeros_like(mid)
 
-    for half, g in enumerate((g0, g1)):
-        saved = slice(half * rows, (half + 1) * rows)
-        back = dot(g[...], wr[...], NT)
-        pre_ref[saved] = (back * slope_ref[saved].astype(F32)).astype(BF16)
-        mlp[saved] += dot(act_ref[saved], wr[...], NN)
-        mid[saved] += dot(pre_ref[saved], wh[...], NN)
-
-    @pl.when(j == pl.num_programs(0) - 1)
+    def step(act, slope):
+        for half, g in enumerate((g0, g1)):
+            saved = slice(half * rows, (half + 1) * rows)
+            back = dot(g[...], wr[...], NT)
+            pre_ref[saved] = (back * slope[saved].astype(F32)).astype(BF16)
+            mlp[saved] += dot(act[saved], wr[...], NN)
+            mid[saved] += dot(pre_ref[saved], wh[...], NN)
+
+    @pl.when(p < 3)
+    def _():
+        step(act_a, slope_a)
+
+    @pl.when(p == 3)
+    def _():
+        step(act_b, slope_b)
+
+    @pl.when(p == 3)
     def _():
         mlp0[...] = mlp[0:rows].astype(mlp0.dtype)
         mlp1[...] = mlp[rows:].astype(mlp1.dtype)
@@ -790,14 +796,21 @@
         mid1[...] = mid[rows:].astype(mid1.dtype)
 
 
-def feed_weights(keeps, place, a0, a1, b_ref, keep, send):
+def feed_weights(keeps, place, a0, a1, *rest):
+    *parts, keep, send = rest
+    p = pl.program_id(0)
     rows = a0.shape[0]
     cut = keep.shape[2]
-    sends = [p for p in range(4) if p not in keeps]
-    grad = (dot(b_ref[0:rows], a0[...], TN) + dot(b_ref[rows:], a1[...], TN)).astype(BF16)
-    for p in range(4):
-        out, at = (keep, keeps.index(p)) if p in keeps else (send, sends.index(p))
-        out[at, 0] = grad[p * cut : (p + 1) * cut]
+
+    def step(b, out):
+        grad = (dot(b[0:rows], a0[...], TN) + dot(b[rows:], a1[...], TN)).astype(BF16)
+        for slot in range(4):
+            out[0, slot] = grad[slot * cut : (slot + 1) * cut]
+
+    for i in range(4):
+        @pl.when(p == i)
+        def _():
+            step(parts[-1] if i == 3 else parts[0], keep if i in keeps else send)
 
 
 def live_rows(place, count):
@@ -1079,35 +1092,55 @@
     )
     m_other = flip(m, 1)
 
-    hidden_own = whole((4, 2, wide, features))
-    hidden_far = [slot_spec(2, wide)] * 3 + [slot_spec(wide)]
     chunk = 4 * wide
-    act, slope = timed(14)(
-        feed_in, place, (slots,),
-        [full] * 2 + [hidden_own] + hidden_far,
-        [head(rows, chunk)] * 2,
-        [like((rows, slots * chunk))] * 2,
-        (m, m_other, own_m, *far_m[:4]),
-        [pltpu.VMEM((chunk, features), BF16)],
-    )
+    def fixed(shape):
+        return pl.BlockSpec(shape, lambda *_: (0,) * len(shape), pipeline_mode=pl.Buffered(1))
+
+    def own_spec_of(count, first):
+        return pl.BlockSpec((1, count, wide, features), lambda p, place: (p + first, 0, 0, 0))
+
+    def feeding(first, count, far, far_specs, earlier):
+        return timed(4 * count)(
+            partial(feed_in, first), place, (count,),
+            [full] * 2 + [own_spec_of(1, first)] + far_specs,
+            [head(rows, chunk)] * 2,
+            [like((rows, count * chunk))] * 2,
+            (after(m, *earlier), m_other, own_m, *far),
+            [pltpu.VMEM((chunk, features), BF16)],
+        )
+
+    act_a, slope_a = feeding(0, 3, far_m[:3], [fixed((3, 1, wide, features))] * 3, ())
+    act_b, slope_b = feeding(3, 1, far_m[3:4], [fixed((3, wide, features))], (act_a,))
+    early = pl.BlockSpec((rows, chunk), lambda p, place: (0, jnp.minimum(p, 2)))
+    last = fixed((rows, chunk))
     mlp, mlp_other, mid, mid_other, pre = timed(21)(
-        feed_out, place, (slots,),
-        [full] * 2 + [hidden_own] + hidden_far + hidden_far[3:] + [head(rows, chunk)] * 2,
+        feed_out, place, (4,),
+        [full] * 2 + [own_spec_of(2, 0)] + [fixed((3, 2, wide, features))] * 3
+        + [fixed((3, wide, features))] * 2 + [early] * 2 + [last] * 2,
         [full] * 4 + [head(rows, chunk)],
         [like((block_len, features), F32), like((block_len, features))] * 2
-        + [like((rows, slots * chunk))],
-        (grad_out, grad_out_other, own_m, *far_m, act, slope),
+        + [like((rows, 4 * chunk))],
+        (grad_out, grad_out_other, own_m, *far_m, act_a, slope_a, act_b, slope_b),
         [pltpu.VMEM((chunk, features), BF16)] * 2 + [pltpu.VMEM((rows, features), F32)] * 2,
     )
     mid_got, mlp_got = flip(mid_other, 1), flip(mlp_other, 1)
-    grad_spec = pl.BlockSpec((2, 1, wide, features), lambda j, place: (0, j, 0, 0))
-    hidden_grads = partial(
-        launch, place=place, grid=(slots,), us=8,
-        in_specs=[full] * 2 + [head(rows, chunk)], out_specs=[grad_spec] * 2,
-        outs=[like((2, slots, wide, features))] * 2,
-    )
+    def hidden_grads(keeps, keep_at, rows_of, parts, part_specs):
+        def spec(at):
+            return pl.BlockSpec(
+                (1, slots, wide, features), lambda p, place: (at(p), 0, 0, 0)
+            )
+
+        return timed(8)(
+            partial(feed_weights, keeps), place, (4,),
+            [full] * 2 + part_specs,
+            [spec(keep_at), spec(lambda p: jnp.maximum(p - 2, 0))],
+            [like((2, slots, wide, features))] * 2,
+            (*rows_of, *map(far_away, parts)),
+        )
+
     keep_r, send_r = hidden_grads(
-        partial(feed_weights, (0, 1)), operands=(grad_out, grad_out_other, far_away(after(act, pre)))
+        (0, 1), lambda p: jnp.minimum(p, 1), (grad_out, grad_out_other),
+        (after(act_a, pre), act_b), [early, last],
     )
     mlp_got = after(mlp_got, keep_r)
     mid_got = after(mid_got, keep_r)
@@ -1127,7 +1160,7 @@
     )
     resid_other = flip(resid_b, 1)
     keep_h, send_h = hidden_grads(
-        partial(feed_weights, (0, 2)), operands=(m, m_other, far_away(after(pre, resid_b)))
+        (0, 2), lambda p: p // 2, (m, m_other), (after(pre, resid_b),), [head(rows, chunk)]
     )
 
     grad_in, grad_in_other, grad_ctx, grad_ctx_other, d, ds = timed(27)(
@@ -1195,7 +1228,7 @@
         ]
     ).astype(F32)
     grad_gain, grad_moment = call(
-        scan_sums, [(grid, F32)] * 2, decay, after(start, grad_tokens), signal[:CTX], grad_conv
+        scan_sums, [(grid, F32)] * 2, decay, after(start, lefts[2], rights[2]), signal[:CTX], grad_conv
     )
     end_moment = block_len * block_power[1] * start + local_moment
     grad_rate = -gain * (grad_moment + end * end_moment)
@@ -1212,7 +1245,7 @@
     pairs = (near_h, more_h), (near_r, more_r)
     total_m = line_reduce(
         [jnp.stack([add(a[j], b[j]) for a, b in pairs]) for j in range(slots)],
-        list(zip(lefts[1:], rights[1:])),
+        [(lefts[1], rights[1])] + [()] * (slots - 2),
     )
     near_a, away_a = add(keep_a[0], got_a[0]), add(keep_a[1], got_a[1])
     near_b, away_b = add(keep_b[0], got_b[0]), add(keep_b[1], got_b[1])

time: 536 us -> 530 us (0.989)
  waiting for transfers between devices: 137 us -> 77.4 us
  starting transfers between devices: 122 us -> 154 us
  other arithmetic: 39.8 us -> 51.6 us
  local copies, waits for them, and re-layouts: 28.4 us -> 34.4 us
    ppermute x40, waiting for transfers between devices: 65.3 us -> 35 us  [flip(): return lax.ppermute(value, 'seq', [(i, i ^ mask) for i in range(count)])]
    ppermute x6, waiting for transfers between devices: 24.3 us -> 5.11 us  [line_reduce(): lax.ppermute(add(chunks[count - k], coming, k), 'tp', [(i, i - 1) for i i...]
    ppermute x40, starting transfers between devices: 37.6 us -> 55.6 us  [flip(): return lax.ppermute(value, 'seq', [(i, i ^ mask) for i in range(count)])]
    ppermute x3, waiting for transfers between devices: 18.7 us -> 6.03 us  [line_steps(): lax.ppermute(lefts[-1], 'tp', [(i, i + 1) for i in range(k - 1, count - 1)])]
    ppermute x3, starting transfers between devices: 7.27 us -> 14.7 us  [line_steps(): lax.ppermute(rights[-1], 'tp', [(i, i - 1) for i in range(1, count - k +...]
    convert_element_type x6, other arithmetic: 1.99 us -> 7.55 us  [add(): return a if b is None else (a.astype(F32) + b.astype(F32)).astype(BF16)]
    convert_element_type x8 -> x7, other arithmetic: 14.2 us -> 19 us  [add(): return (a.astype(F32) + b.astype(F32)).astype(BF16)]
    pallas_call x16 -> x17, Pallas kernels: 162 us -> 165 us  [launch(): pl.pallas_call(kernel, grid_spec=pltpu.PrefetchScalarGridSpec(num_scalar_...]
  transfers between devices with their start and end apart: 78 -> 78, of which waited for: 22 -> 20; matrix products, arithmetic and copies ran while one was open for 11% -> 14% of each run, Pallas kernels for 27% -> 28%
where the time goes in v5:
time: 530 us; the launch traced here: 521 us
  Pallas kernels  187 us (35%)
  starting transfers between devices  154 us (29%)
  waiting for transfers between devices  77.4 us (15%)
  other arithmetic  51.6 us (10%)
  local copies, waits for them, and re-layouts  34.4 us (6%)
  between operations  15.9 us (3%)
    pallas_call x17, Pallas kernels, launch(): pl.pallas_call(kernel, grid_spec=pltpu.PrefetchScalarGridSpec(num_scalar_...  165 us
    ppermute x40, starting transfers between devices, flip(): return lax.ppermute(value, 'seq', [(i, i ^ mask) for i in range(count)])  55.6 us
    ppermute x40, waiting for transfers between devices, flip(): return lax.ppermute(value, 'seq', [(i, i ^ mask) for i in range(count)])  35 us
    ppermute x11, starting transfers between devices, shifted(): lax.ppermute(value, 'seq', [(i, i + steps) for i in range(first, last)])  27.6 us
    pallas_call x6, Pallas kernels, call(): pl.pallas_call(kernel, out_shape=[jax.ShapeDtypeStruct(shape, dtype) for...  22.1 us
    convert_element_type x7, other arithmetic, add(): return (a.astype(F32) + b.astype(F32)).astype(BF16)  19 us
    ppermute x3, starting transfers between devices, line_steps(): lax.ppermute(rights[-1], 'tp', [(i, i - 1) for i in range(1, count - k +...  14.7 us
    ppermute x6, starting transfers between devices, line_reduce(): lax.ppermute(add(chunks[count - k], coming, k), 'tp', [(i, i - 1) for i i...  13.6 us
  transfers between devices with their start and end apart: 78, of which 20 were waited for; matrix products, arithmetic and copies ran while one was open for 14% of the time, Pallas kernels for 28%

profile of v5, /device:TPU:17, one launch (start us, length us, event | category | flops | bytes accessed | tf_op | source)
XLA Modules:
  0.0 521.2 jit_solution(8132912811718060227)
XLA Ops:
  13.7 3.2 collective-permute-start.2
  17.7 6.7 %all-to-all-start = ((f32[32,8,128]{2,1,0:T(8,128)}), f32[32,8,128]{2,1,0:T(8,128)S(1)}, u32[]{:S(2)}, u32[]{:S(2)}) async-start(f32[32,8,128]{2,1,0:T(8,128)} %broadcast_in_dim.11), calls=%async_computation | async-start | bytes 262144 | tf_op jit(solution)/shard_map/all_to_all | solution.py:1008
  26.2 3.3 collective-permute-start
  43.8 12.0 %all-to-all-done = f32[32,8,128]{2,1,0:T(8,128)S(1)} async-done(((f32[32,8,128]{2,1,0:T(8,128)}), f32[32,8,128]{2,1,0:T(8,128)S(1)}, u32[]{:S(2)}, u32[]{:S(2)}) %all-to-all-start) | async-done | bytes 131104 | tf_op jit(solution)/shard_map/all_to_all | solution.py:1008
  63.5 3.5 collective-permute-start.14
  67.0 8.5 %shard_map.257 = (f32[16,8,128]{2,1,0:T(8,128)S(1)}, f32[16,8,128]{2,1,0:T(8,128)S(1)}) custom-call(f32[16,8,128]{2,1,0:T(8,128)S(1)} %get-tuple-element.100.decay_ref, f32[512,8,128]{2,1,0:T(8,128)S(1)} %convert_multiply_fusion.1.u_ref), custom_call_target="tpu_custom_call" | custom-call | flops 8800000000 | tf_op jit(solution)/shard_map/pallas_call | solution.py:164
  75.5 13.6 %collective-permute-done.6.f1 = bf16[3,6,32,1024]{3,2,1,0:T(8,128)(2,1)S(1)} collective-permute-done((bf16[3,6,32,1024]{3,2,1,0:T(8,128)(2,1)S(1)}, bf16[3,6,32,1024]{3,2,1,0:T(8,128)(2,1)S(1)}, u32[]{:S(2)}, u32[]{:S(2)}) %collective-permute-start.6) | collective-permute-done | bytes 1179680 | tf_op jit(solution)/shard_map/ppermute | solution.py:33
  92.2 3.8 collective-permute-start.8
  98.5 9.5 %collective-permute-done.14 = bf16[2,128,1024]{2,1,0:T(8,128)(2,1)S(1)} collective-permute-done((bf16[2,128,1024]{2,1,0:T(8,128)(2,1)S(1)}, bf16[2,128,1024]{2,1,0:T(8,128)(2,1)S(1)}, u32[]{:S(2)}, u32[]{:S(2)}) %collective-permute-start.14) | collective-permute-done | bytes 524320 | tf_op jit(solution)/shard_map/ppermute | solution.py:544
  108.0 4.3 collective-permute-start.10
  112.4 3.1 collective-permute-start.11
  121.5 9.4 %shard_map.259 = (bf16[1024,512]{1,0:T(8,128)(2,1)S(1)}, bf16[1024,512]{1,0:T(8,128)(2,1)S(1)}, bf16[1024,512]{1,0:T(8,128)(2,1)}) custom-call(s32[3]{0:T(128)S(1)} %pad_add_fusion.place, bf16[512,1024]{1,0:T(8,128)(2,1)} %copy-done, bf16[512,1024]{1,0:T(8,128)(2,1)} %collective-permute-done.4.x1, bf16[4,6,32,1024]{3,2,1,0:T(8,128)(2,1)} %copy-done.18, ...), custom_call_target="tpu_custom_call" | custom-call | flops 8800000000 | tf_op jit(solution)/shard_map/pallas_call | solution.py:523
  132.8 21.0 %shard_map.260 = (f32[512,1024]{1,0:T(8,128)}, bf16[512,1024]{1,0:T(8,128)(2,1)S(1)}, bf16[256,1024]{1,0:T(8,128)(2,1)S(1)}, bf16[1024,512]{1,0:T(8,128)(2,1)}, f32[4,1024,1]{2,1,0:T(8,128)}) custom-call(s32[3]{0:T(128)S(1)} %pad_add_fusion.place, bf16[128,1024]{1,0:T(8,128)(2,1)S(1)} %bitcast.191, bf16[128,1024]{1,0:T(8,128)(2,1)S(1)} %collective-permute-done.16.c1, ...), custom_call_target="tpu_custom_call" | custom-call | flops 22000001024 | tf_op jit(solution)/shard_map/pallas_call | solution.py:523
  156.6 4.8 shard_map.261
  169.0 12.3 %shard_map.262 = (bf16[1024,1536]{1,0:T(8,128)(2,1)}, bf16[1024,1536]{1,0:T(8,128)(2,1)}) custom-call(s32[3]{0:T(128)S(1)} %pad_add_fusion.place, bf16[512,1024]{1,0:T(8,128)(2,1)S(1)} %get-tuple-element.121.m0.a0, bf16[512,1024]{1,0:T(8,128)(2,1)S(1)} %collective-permute-done.24.m1.a1, bf16[4,2,128,1024]{3,2,1,0:T(8,128)(2,1)} %copy-done.17, ...), custom_call_target="tpu_custom_call" | custom-call | flops 13200000000 | tf_op jit(solution)/shard_map/pallas_call | solution.py:523
  181.9 4.7 shard_map.263
  188.6 23.8 %shard_map.264 = (f32[512,1024]{1,0:T(8,128)}, bf16[512,1024]{1,0:T(8,128)(2,1)S(1)}, f32[512,1024]{1,0:T(8,128)}, bf16[512,1024]{1,0:T(8,128)(2,1)}, bf16[1024,2048]{1,0:T(8,128)(2,1)}) custom-call(s32[3]{0:T(128)S(1)} %pad_add_fusion.place, bf16[512,1024]{1,0:T(8,128)(2,1)} %copy-done.3, bf16[512,1024]{1,0:T(8,128)(2,1)} %copy-done.21, ...), custom_call_target="tpu_custom_call" | custom-call | flops 23100000256 | tf_op jit(solution)/shard_map/pallas_call | solution.py:523
  213.3 9.1 %shard_map.265 = (bf16[2,4,128,1024]{3,2,1,0:T(8,128)(2,1)}, bf16[2,4,128,1024]{3,2,1,0:T(8,128)(2,1)}) custom-call(s32[3]{0:T(128)S(1)} %pad_add_fusion.place, bf16[512,1024]{1,0:T(8,128)(2,1)S(1)} %copy-done.4, bf16[512,1024]{1,0:T(8,128)(2,1)S(1)} %copy-done.22, bf16[1024,1536]{1,0:T(8,128)(2,1)} %get-tuple-element.127.act_a.rest_0_, ...), custom_call_target="tpu_custom_call" | custom-call | flops 8800000000 | tf_op jit(solution)/shard_map/pallas_call | solution.py:523
  222.4 4.6 shard_map.266
  227.0 6.3 %shard_map.267 = (f32[512,1024]{1,0:T(8,128)}, bf16[512,1024]{1,0:T(8,128)(2,1)}, f32[1,1024]{1,0:T(1,128)S(1)}) custom-call(s32[3]{0:T(128)S(1)} %pad_add_fusion.place, f32[512,1024]{1,0:T(8,128)} %get-tuple-element.130.residual, f32[512,1024]{1,0:T(8,128)} %get-tuple-element.131.own, bf16[512,1024]{1,0:T(8,128)(2,1)} %collective-permute-done.26.got, ...), custom_call_target="tpu_custom_call" | custom-call | flops 5500000256 | tf_op jit(solution)/shard_map/pallas_call | solution.py:523
  233.8 9.1 %shard_map.268 = (bf16[2,4,128,1024]{3,2,1,0:T(8,128)(2,1)}, bf16[2,4,128,1024]{3,2,1,0:T(8,128)(2,1)}) custom-call(s32[3]{0:T(128)S(1)} %pad_add_fusion.place, bf16[512,1024]{1,0:T(8,128)(2,1)S(1)} %get-tuple-element.121.m0.a0, bf16[512,1024]{1,0:T(8,128)(2,1)S(1)} %copy-done.24, bf16[1024,2048]{1,0:T(8,128)(2,1)} %get-tuple-element.135.rest_0_), custom_call_target="tpu_custom_call" | custom-call | flops 8800000000 | tf_op jit(solution)/shard_map/pallas_call | solution.py:523
  246.1 26.9 %shard_map.269 = (f32[512,1024]{1,0:T(8,128)}, bf16[512,1024]{1,0:T(8,128)(2,1)S(1)}, f32[128,1024]{1,0:T(8,128)S(1)}, bf16[128,1024]{1,0:T(8,128)(2,1)S(1)}, bf...) custom-call(s32[3]{0:T(128)S(1)} %pad_add_fusion.place, bf16[512,1024]{1,0:T(8,128)(2,1)} %get-tuple-element.137.g0, ...), custom_call_target="tpu_custom_call" | custom-call | flops 29699999744 | tf_op jit(solution)/shard_map/pallas_call | solution.py:523
  273.8 10.5 %shard_map.271 = (bf16[2,4,3,32,1024]{4,3,2,1,0:T(8,128)(2,1)}, bf16[2,4,3,32,1024]{4,3,2,1,0:T(8,128)(2,1)}, bf16[2,4,3,32,1024]{4,3,2,1,0:T(8,128)(2,1)}, bf16[2,4,3,32,1024]{4,3,2,1,0:T(8,128)(2,1)}) custom-call(s32[3]{0:T(128)S(1)} %pad_add_fusion.place, bf16[512,1024]{1,0:T(8,128)(2,1)S(1)} %copy-done.1, bf16[512,1024]{1,0:T(8,128)(2,1)} %collective-permute-done.4.x1, ...), custom_call_target="tpu_custom_call" | custom-call | flops 11000000512 | tf_op jit(solution)/shard_map/pallas_call | solution.py:523
  286.7 4.6 collective-permute-done.30
  295.0 3.1 collective-permute-start.32
  305.6 4.1 collective-permute-done.34
  312.7 4.5 shard_map.272
  317.9 5.2 shard_map.273
  325.0 3.4 collective-permute-start.38
  328.3 9.7 %collective-permute-done.43 = bf16[4,128,1024]{2,1,0:T(8,128)(2,1)} collective-permute-done((bf16[4,128,1024]{2,1,0:T(8,128)(2,1)}, bf16[4,128,1024]{2,1,0:T(8,128)(2,1)}, u32[]{:S(2)}, u32[]{:S(2)}) %collective-permute-start.43) | collective-permute-done | bytes 1048608 | tf_op jit(solution)/shard_map/ppermute | solution.py:33
  339.4 3.2 fusion.26
  342.7 6.0 %collective-permute-done.37 = bf16[512,1024]{1,0:T(8,128)(2,1)S(1)} collective-permute-done((bf16[512,1024]{1,0:T(8,128)(2,1)S(1)}, bf16[512,1024]{1,0:T(8,128)(2,1)S(1)}, u32[]{:S(2)}, u32[]{:S(2)}) %collective-permute-start.37) | collective-permute-done | bytes 1048608 | tf_op jit(solution)/shard_map/ppermute | solution.py:46
  353.6 4.7 collective-permute-start.41
  358.3 9.7 %collective-permute-start.39 = (bf16[512,1024]{1,0:T(8,128)(2,1)}, bf16[512,1024]{1,0:T(8,128)(2,1)}, u32[]{:S(2)}, u32[]{:S(2)}) collective-permute-start(bf16[512,1024]{1,0:T(8,128)(2,1)} %copy-done.62), channel_id=1, source_target_pairs={{1,0},{2,1},{5,4},{6,5},{9,8},{10,9},{13,12},{14,13},{17,16},{18,1... | collective-permute-start | bytes 3145736 | tf_op jit(solution)/shard_map/ppermute | solution.py:48
  375.0 3.1 add_convert_fusion.5
  378.1 2.9 collective-permute-start.48
  381.0 3.3 add_convert_fusion.7
  386.8 5.5 %shard_map.274 = (f32[16,8,128]{2,1,0:T(8,128)S(1)}, f32[16,8,128]{2,1,0:T(8,128)S(1)}) custom-call(f32[16,8,128]{2,1,0:T(8,128)S(1)} %copy-done.33, f32[16,8,128]{2,1,0:T(8,128)S(1)} %copy-done.12, f32[128,8,128]{2,1,0:T(8,128)S(1)} %bitcast.181, f32[128,8,128]{2,1,0:T(8,128)S(1)} %bitcast.183), custom_call_target="tpu_custom_call" | custom-call | flops 5500000256 | tf_op jit(solution)/shard_map/pallas_call | solution.py:164
  399.3 4.1 collective-permute-start.67
  424.9 3.6 collective-permute-start.68
  431.1 4.5 collective-permute-start.70
  441.3 4.6 collective-permute-done.53
  454.5 10.1 %collective-permute-start.71 = (bf16[2,128,1024]{2,1,0:T(8,128)(2,1)S(1)}, bf16[2,128,1024]{2,1,0:T(8,128)(2,1)S(1)}, u32[]{:S(2)}, u32[]{:S(2)}) collective-permute-start(bf16[2,128,1024]{2,1,0:T(8,128)(2,1)S(1)} %add_convert_fusion.8.n0), channel_id=1, source_target_pairs={{0,4},{4,0},{8,12},{12,8},{16,20},{20,16},{24,28},{28,24},{1,5},{5... | collective-permute-start | bytes 1572872 | tf_op jit(solution)/shard_map/ppermute | solution.py:33
  465.5 9.7 %all-to-all-start.1 = ((f32[32,24,128]{2,1,0:T(8,128)}), f32[32,24,128]{2,1,0:T(8,128)}, u32[]{:S(2)}, u32[]{:S(2)}) async-start(f32[32,24,128]{2,1,0:T(8,128)} %pad_maximum_fusion.7), calls=%async_computation.1 | async-start | bytes 786432 | tf_op jit(solution)/shard_map/all_to_all | solution.py:1282
  475.3 5.3 %maximum_convert_fusion = f32[4,512,1024]{2,1,0:T(8,128)} fusion(bf16[1,512,1024]{2,1,0:T(8,128)(2,1)} %get-tuple-element.233, bf16[1,512,1024]{2,1,0:T(8,128)(2,1)} %get-tuple-element.234, bf16[1,512,1024]{2,1,0:T(8,128)(2,1)} %get-tuple-element.235, bf16[1,512,1024]{2,1,0:T(8,128)(2,1)} %get-tuple-element.232), kind=kLoop, calls=%fused_computation.1 | loop fusion | flops 8388608 | bytes 12582912 | tf_op jit(solution)/shard_map/convert_element_type | solution.py:1229
  484.4 6.0 %shard_map.276 = (f32[1024,1024]{1,0:T(8,128)}, f32[1024,1024]{1,0:T(8,128)}) custom-call(s32[3]{0:T(128)S(1)} %pad_add_fusion.place, bf16[2,128,1024]{2,1,0:T(8,128)(2,1)S(1)} %add_convert_fusion.8.n0, bf16[2,128,1024]{2,1,0:T(8,128)(2,1)S(1)} %collective-permute-done.68.n1, bf16[2,128,1024]{2,1,0:T(8,128)(2,1)S(1)} %collective-permute-done.69.n2, ...), custom_call_target="tpu_custom_call" | custom-call | flops 5500000256 | tf_op jit(solution)/shard_map/pallas_call | solution.py:523
  493.6 7.6 %collective-permute-start.60 = (bf16[6,32,1024]{2,1,0:T(8,128)(2,1)}, bf16[6,32,1024]{2,1,0:T(8,128)(2,1)S(1)}, u32[]{:S(2)}, u32[]{:S(2)}) collective-permute-start(bf16[6,32,1024]{2,1,0:T(8,128)(2,1)} %collective-permute-done.56.n2), channel_id=1, source_target_pairs={{0,4},{4,0},{8,12},{12,8},{16,20},{20,16},{24,28},{28,24},{1,5},{5... | collective-permute-start | bytes 1179656 | tf_op jit(solution)/shard_map/ppermute | solution.py:33
  505.7 6.4 %shard_map.275 = (f32[1024,256]{1,0:T(8,128)}, f32[1024,256]{1,0:T(8,128)}, f32[1024,256]{1,0:T(8,128)}, f32[256,1024]{1,0:T(8,128)}, f32[1024,256]{1,0:T(8,128)}, /*index=5*/f32[1024,256]{1,0:T(8,128)}) custom-call(s32[3]{0:T(128)S(1)} %pad_add_fusion.place, bf16[6,32,1024]{2,1,0:T(8,128)(2,1)S(1)} %bitcast.189, ...), custom_call_target="tpu_custom_call" | custom-call | flops 5500000256 | tf_op jit(solution)/shard_map/pallas_call | solution.py:523
  (391 shorter events, 156.5 us)
Async XLA Ops:
  13.5 46.8 %collective-permute-start.3 = (bf16[6,32,1024]{2,1,0:T(8,128)(2,1)}, bf16[6,32,1024]{2,1,0:T(8,128)(2,1)}, u32[]{:S(2)}, u32[]{:S(2)}) collective-permute-start(bf16[6,32,1024]{2,1,0:T(8,128)(2,1)} %slice_bitcast_fusion.1), channel_id=1, source_target_pairs={{0,3},{1,0},{2,1},{3,2},{4,7},{5,4},{6,5},{7,6},{8,11},{9,8},{10,9... | collective-permute-start | bytes 1179656 | tf_op jit(solution)/shard_map/ppermute | solution.py:544
  13.7 46.7 %collective-permute-start.2 = (bf16[6,32,1024]{2,1,0:T(8,128)(2,1)}, bf16[6,32,1024]{2,1,0:T(8,128)(2,1)}, u32[]{:S(2)}, u32[]{:S(2)}) collective-permute-start(bf16[6,32,1024]{2,1,0:T(8,128)(2,1)} %slice_bitcast_fusion.1), channel_id=1, source_target_pairs={{0,2},{1,3},{2,0},{3,1},{4,6},{5,7},{6,4},{7,5},{8,10},{9,11},{10,... | collective-permute-start | bytes 1179656 | tf_op jit(solution)/shard_map/ppermute | solution.py:544
  16.9 43.5 %collective-permute-start.1 = (bf16[6,32,1024]{2,1,0:T(8,128)(2,1)}, bf16[6,32,1024]{2,1,0:T(8,128)(2,1)}, u32[]{:S(2)}, u32[]{:S(2)}) collective-permute-start(bf16[6,32,1024]{2,1,0:T(8,128)(2,1)} %slice_bitcast_fusion.1), channel_id=1, source_target_pairs={{0,1},{1,2},{2,3},{3,0},{4,5},{5,6},{6,7},{7,4},{8,9},{9,10},{10,1... | collective-permute-start | bytes 1179656 | tf_op jit(solution)/shard_map/ppermute | solution.py:544
  17.7 38.0 %all-to-all-start = ((f32[32,8,128]{2,1,0:T(8,128)}), f32[32,8,128]{2,1,0:T(8,128)S(1)}, u32[]{:S(2)}, u32[]{:S(2)}) async-start(f32[32,8,128]{2,1,0:T(8,128)} %broadcast_in_dim.11), calls=%async_computation | async-start | bytes 262144 | tf_op jit(solution)/shard_map/all_to_all | solution.py:1008
  24.4 293.1 %all-gather.3.cloned.1.call-start = ((), (), s32[]{:S(2)}) async-start(), calls=%async_computation.2 | async-start | bytes 5242880 | tf_op jit(solution)/shard_map/all_gather | solution.py:1151
  26.2 33.2 %collective-permute-start = (bf16[128,1024]{1,0:T(8,128)(2,1)}, bf16[128,1024]{1,0:T(8,128)(2,1)S(1)}, u32[]{:S(2)}, u32[]{:S(2)}) collective-permute-start(bf16[128,1024]{1,0:T(8,128)(2,1)} %dynamic-slice_bitcast_fusion), channel_id=1, source_target_pairs={{0,4},{4,8},{8,12},{12,16},{16,20},{20,24},{24,28},{1,5},{5,9},{9,... | collective-permute-start | bytes 786440 | tf_op jit(solution)/shard_map/ppermute | solution.py:39
  34.2 29.2 %collective-permute-start.4 = (bf16[512,1024]{1,0:T(8,128)(2,1)S(1)}, bf16[512,1024]{1,0:T(8,128)(2,1)}, u32[]{:S(2)}, u32[]{:S(2)}) collective-permute-start(bf16[512,1024]{1,0:T(8,128)(2,1)S(1)} %fusion.5.x0), channel_id=1, source_target_pairs={{0,4},{4,0},{8,12},{12,8},{16,20},{20,16},{24,28},{28,24},{1,5},{5... | collective-permute-start | bytes 3145736 | tf_op jit(solution)/shard_map/ppermute | solution.py:33
  61.7 27.4 %collective-permute-start.6 = (bf16[3,6,32,1024]{3,2,1,0:T(8,128)(2,1)S(1)}, bf16[3,6,32,1024]{3,2,1,0:T(8,128)(2,1)S(1)}, u32[]{:S(2)}, u32[]{:S(2)}) collective-permute-start(bf16[3,6,32,1024]{3,2,1,0:T(8,128)(2,1)S(1)} %pad_maximum_fusion.2.f0), channel_id=1, source_target_pairs={{0,8},{4,12},{8,0},{12,4},{16,24},{20,28},{24,16},{28,20},{1,9},{5... | collective-permute-start | bytes 3538952 | tf_op jit(solution)/shard_map/ppermute | solution.py:33
  62.2 27.1 %collective-permute-start.7 = (bf16[3,6,32,1024]{3,2,1,0:T(8,128)(2,1)S(1)}, bf16[3,6,32,1024]{3,2,1,0:T(8,128)(2,1)S(1)}, u32[]{:S(2)}, u32[]{:S(2)}) collective-permute-start(bf16[3,6,32,1024]{3,2,1,0:T(8,128)(2,1)S(1)} %pad_maximum_fusion.2.f0), channel_id=1, source_target_pairs={{0,16},{4,20},{8,24},{12,28},{16,0},{20,4},{24,8},{28,12},{1,17},{... | collective-permute-start | bytes 3538952 | tf_op jit(solution)/shard_map/ppermute | solution.py:33
  63.4 34.4 %collective-permute-start.15 = (bf16[2,128,1024]{2,1,0:T(8,128)(2,1)S(1)}, bf16[2,128,1024]{2,1,0:T(8,128)(2,1)S(1)}, u32[]{:S(2)}, u32[]{:S(2)}) collective-permute-start(bf16[2,128,1024]{2,1,0:T(8,128)(2,1)S(1)} %copy-done.71), channel_id=1, source_target_pairs={{0,3},{1,0},{2,1},{3,2},{4,7},{5,4},{6,5},{7,6},{8,11},{9,8},{10,9... | collective-permute-start | bytes 1572872 | tf_op jit(solution)/shard_map/ppermute | solution.py:544
  63.5 44.5 %collective-permute-start.14 = (bf16[2,128,1024]{2,1,0:T(8,128)(2,1)S(1)}, bf16[2,128,1024]{2,1,0:T(8,128)(2,1)S(1)}, u32[]{:S(2)}, u32[]{:S(2)}) collective-permute-start(bf16[2,128,1024]{2,1,0:T(8,128)(2,1)S(1)} %copy-done.71), channel_id=1, source_target_pairs={{0,2},{1,3},{2,0},{3,1},{4,6},{5,7},{6,4},{7,5},{8,10},{9,11},{10,... | collective-permute-start | bytes 1572872 | tf_op jit(solution)/shard_map/ppermute | solution.py:544
  67.0 45.4 %collective-permute-start.13 = (bf16[2,128,1024]{2,1,0:T(8,128)(2,1)S(1)}, bf16[2,128,1024]{2,1,0:T(8,128)(2,1)S(1)}, u32[]{:S(2)}, u32[]{:S(2)}) collective-permute-start(bf16[2,128,1024]{2,1,0:T(8,128)(2,1)S(1)} %copy-done.71), channel_id=1, source_target_pairs={{0,1},{1,2},{2,3},{3,0},{4,5},{5,6},{6,7},{7,4},{8,9},{9,10},{10,1... | collective-permute-start | bytes 1572872 | tf_op jit(solution)/shard_map/ppermute | solution.py:544
  96.4 25.1 %collective-permute-start.17 = (bf16[3,3,32,1024]{3,2,1,0:T(8,128)(2,1)S(1)}, bf16[3,3,32,1024]{3,2,1,0:T(8,128)(2,1)S(1)}, u32[]{:S(2)}, u32[]{:S(2)}) collective-permute-start(bf16[3,3,32,1024]{3,2,1,0:T(8,128)(2,1)S(1)} %slice.304), channel_id=1, source_target_pairs={{0,8},{4,12},{8,0},{12,4},{16,24},{20,28},{24,16},{28,20},{1,9},{5... | collective-permute-start | bytes 1769480 | tf_op jit(solution)/shard_map/ppermute | solution.py:33
  97.7 23.7 %collective-permute-start.18 = (bf16[3,3,32,1024]{3,2,1,0:T(8,128)(2,1)S(1)}, bf16[3,3,32,1024]{3,2,1,0:T(8,128)(2,1)S(1)}, u32[]{:S(2)}, u32[]{:S(2)}) collective-permute-start(bf16[3,3,32,1024]{3,2,1,0:T(8,128)(2,1)S(1)} %slice.305), channel_id=1, source_target_pairs={{0,16},{4,20},{8,24},{12,28},{16,0},{20,4},{24,8},{28,12},{1,17},{... | collective-permute-start | bytes 1769480 | tf_op jit(solution)/shard_map/ppermute | solution.py:33
  115.6 38.3 %collective-permute-start.20 = (bf16[3,2,128,1024]{3,2,0,1:T(8,128)(2,1)S(1)}, bf16[3,2,128,1024]{3,2,0,1:T(8,128)(2,1)S(1)}, u32[]{:S(2)}, u32[]{:S(2)}) collective-permute-start(bf16[3,2,128,1024]{3,2,0,1:T(8,128)(2,1)S(1)} %pad_maximum_fusion.1), channel_id=1, source_target_pairs={{0,8},{4,12},{8,0},{12,4},{16,24},{20,28},{24,16},{28,20},{1,9},{5... | collective-permute-start | bytes 4718600 | tf_op jit(solution)/shard_map/ppermute | solution.py:33
  116.0 37.9 %collective-permute-start.21 = (bf16[3,2,128,1024]{3,2,0,1:T(8,128)(2,1)S(1)}, bf16[3,2,128,1024]{3,2,0,1:T(8,128)(2,1)S(1)}, u32[]{:S(2)}, u32[]{:S(2)}) collective-permute-start(bf16[3,2,128,1024]{3,2,0,1:T(8,128)(2,1)S(1)} %pad_maximum_fusion.1), channel_id=1, source_target_pairs={{0,16},{4,20},{8,24},{12,28},{16,0},{20,4},{24,8},{28,12},{1,17},{... | collective-permute-start | bytes 4718600 | tf_op jit(solution)/shard_map/ppermute | solution.py:33
  162.8 19.1 %collective-permute-start.22 = (bf16[3,1,128,1024]{3,2,0,1:T(8,128)(2,1)S(1)}, bf16[3,1,128,1024]{3,2,0,1:T(8,128)(2,1)S(1)}, u32[]{:S(2)}, u32[]{:S(2)}) collective-permute-start(bf16[3,1,128,1024]{3,2,0,1:T(8,128)(2,1)S(1)} %slice.306), channel_id=1, source_target_pairs={{0,8},{4,12},{8,0},{12,4},{16,24},{20,28},{24,16},{28,20},{1,9},{5... | collective-permute-start | bytes 2359304 | tf_op jit(solution)/shard_map/ppermute | solution.py:33
  164.0 24.6 %collective-permute-start.23 = (bf16[3,1,128,1024]{3,2,0,1:T(8,128)(2,1)S(1)}, bf16[3,1,128,1024]{3,2,0,1:T(8,128)(2,1)S(1)}, u32[]{:S(2)}, u32[]{:S(2)}) collective-permute-start(bf16[3,1,128,1024]{3,2,0,1:T(8,128)(2,1)S(1)} %slice.307), channel_id=1, source_target_pairs={{0,16},{4,20},{8,24},{12,28},{16,0},{20,4},{24,8},{28,12},{1,17},{... | collective-permute-start | bytes 2359304 | tf_op jit(solution)/shard_map/ppermute | solution.py:33
  242.9 48.5 %collective-permute-start.30 = (bf16[2,4,128,1024]{3,2,1,0:T(8,128)(2,1)}, bf16[2,4,128,1024]{3,2,1,0:T(8,128)(2,1)S(1)}, u32[]{:S(2)}, u32[]{:S(2)}) collective-permute-start(bf16[2,4,128,1024]{3,2,1,0:T(8,128)(2,1)} %get-tuple-element.146), channel_id=1, source_target_pairs={{0,16},{4,20},{8,24},{12,28},{16,0},{20,4},{24,8},{28,12},{1,17},{... | collective-permute-start | bytes 6291464 | tf_op jit(solution)/shard_map/ppermute | solution.py:33
  245.1 47.2 %collective-permute-start.31 = (bf16[2,4,128,1024]{3,2,1,0:T(8,128)(2,1)}, bf16[2,4,128,1024]{3,2,1,0:T(8,128)(2,1)S(1)}, u32[]{:S(2)}, u32[]{:S(2)}) collective-permute-start(bf16[2,4,128,1024]{3,2,1,0:T(8,128)(2,1)} %get-tuple-element.148), channel_id=1, source_target_pairs={{0,8},{4,12},{8,0},{12,4},{16,24},{20,28},{24,16},{28,20},{1,9},{5... | collective-permute-start | bytes 6291464 | tf_op jit(solution)/shard_map/ppermute | solution.py:33
  273.1 44.5 %collective-permute-start.28 = (bf16[512,1024]{1,0:T(8,128)(2,1)S(1)}, bf16[512,1024]{1,0:T(8,128)(2,1)}, u32[]{:S(2)}, u32[]{:S(2)}) collective-permute-start(bf16[512,1024]{1,0:T(8,128)(2,1)S(1)} %get-tuple-element.141), channel_id=1, source_target_pairs={{0,4},{4,0},{8,12},{12,8},{16,20},{20,16},{24,28},{28,24},{1,5},{5... | collective-permute-start | bytes 3145736 | tf_op jit(solution)/shard_map/ppermute | solution.py:33
  284.4 21.1 %collective-permute-start.36 = (bf16[128,1024]{1,0:T(8,128)(2,1)S(1)}, bf16[128,1024]{1,0:T(8,128)(2,1)S(1)}, u32[]{:S(2)}, u32[]{:S(2)}) collective-permute-start(bf16[128,1024]{1,0:T(8,128)(2,1)S(1)} %add_convert_fusion.14), channel_id=1, source_target_pairs={{4,0},{8,4},{12,8},{16,12},{20,16},{24,20},{28,24},{5,1},{9,5},{13... | collective-permute-start | bytes 786440 | tf_op jit(solution)/shard_map/ppermute | solution.py:39
  312.5 25.5 %collective-permute-start.43 = (bf16[4,128,1024]{2,1,0:T(8,128)(2,1)}, bf16[4,128,1024]{2,1,0:T(8,128)(2,1)}, u32[]{:S(2)}, u32[]{:S(2)}) collective-permute-start(bf16[4,128,1024]{2,1,0:T(8,128)(2,1)} %get-tuple-element.167), channel_id=1, source_target_pairs={{0,16},{4,20},{8,24},{12,28},{16,0},{20,4},{24,8},{28,12},{1,17},{... | collective-permute-start | bytes 3145736 | tf_op jit(solution)/shard_map/ppermute | solution.py:33
  312.6 25.4 %collective-permute-start.44 = (bf16[4,128,1024]{2,1,0:T(8,128)(2,1)}, bf16[4,128,1024]{2,1,0:T(8,128)(2,1)}, u32[]{:S(2)}, u32[]{:S(2)}) collective-permute-start(bf16[4,128,1024]{2,1,0:T(8,128)(2,1)} %get-tuple-element.169), channel_id=1, source_target_pairs={{0,8},{4,12},{8,0},{12,4},{16,24},{20,28},{24,16},{28,20},{1,9},{5... | collective-permute-start | bytes 3145736 | tf_op jit(solution)/shard_map/ppermute | solution.py:33
  323.0 25.7 %collective-permute-start.37 = (bf16[512,1024]{1,0:T(8,128)(2,1)S(1)}, bf16[512,1024]{1,0:T(8,128)(2,1)S(1)}, u32[]{:S(2)}, u32[]{:S(2)}) collective-permute-start(bf16[512,1024]{1,0:T(8,128)(2,1)S(1)} %get-tuple-element.158), channel_id=1, source_target_pairs={{0,1},{1,2},{2,3},{4,5},{5,6},{6,7},{8,9},{9,10},{10,11},{12,13},{... | collective-permute-start | bytes 3145736 | tf_op jit(solution)/shard_map/ppermute | solution.py:46
  325.0 25.7 %collective-permute-start.38 = (bf16[512,1024]{1,0:T(8,128)(2,1)S(1)}, bf16[512,1024]{1,0:T(8,128)(2,1)S(1)}, u32[]{:S(2)}, u32[]{:S(2)}) collective-permute-start(bf16[512,1024]{1,0:T(8,128)(2,1)S(1)} %get-tuple-element.158), channel_id=1, source_target_pairs={{1,0},{2,1},{3,2},{5,4},{6,5},{7,6},{9,8},{10,9},{11,10},{13,12},{... | collective-permute-start | bytes 3145736 | tf_op jit(solution)/shard_map/ppermute | solution.py:48
  338.0 35.7 %collective-permute-start.47 = (bf16[2,4,3,32,1024]{4,3,2,1,0:T(8,128)(2,1)}, bf16[2,4,3,32,1024]{4,3,2,1,0:T(8,128)(2,1)}, u32[]{:S(2)}, u32[]{:S(2)}) collective-permute-start(bf16[2,4,3,32,1024]{4,3,2,1,0:T(8,128)(2,1)} %get-tuple-element.174), channel_id=1, source_target_pairs={{0,16},{4,20},{8,24},{12,28},{16,0},{20,4},{24,8},{28,12},{1,17},{... | collective-permute-start | bytes 4718600 | tf_op jit(solution)/shard_map/ppermute | solution.py:33
  339.4 38.8 %collective-permute-start.45 = (bf16[2,4,3,32,1024]{4,3,2,1,0:T(8,128)(2,1)}, bf16[2,4,3,32,1024]{4,3,2,1,0:T(8,128)(2,1)}, u32[]{:S(2)}, u32[]{:S(2)}) collective-permute-start(bf16[2,4,3,32,1024]{4,3,2,1,0:T(8,128)(2,1)} %get-tuple-element.171), channel_id=1, source_target_pairs={{0,8},{4,12},{8,0},{12,4},{16,24},{20,28},{24,16},{28,20},{1,9},{5... | collective-permute-start | bytes 4718600 | tf_op jit(solution)/shard_map/ppermute | solution.py:33
  353.6 30.7 %collective-permute-start.41 = (bf16[512,1024]{1,0:T(8,128)(2,1)}, bf16[512,1024]{1,0:T(8,128)(2,1)}, u32[]{:S(2)}, u32[]{:S(2)}) collective-permute-start(bf16[512,1024]{1,0:T(8,128)(2,1)} %copy-done.60), channel_id=1, source_target_pairs={{1,2},{2,3},{5,6},{6,7},{9,10},{10,11},{13,14},{14,15},{17,18},{18... | collective-permute-start | bytes 3145736 | tf_op jit(solution)/shard_map/ppermute | solution.py:46
  358.3 28.5 %collective-permute-start.39 = (bf16[512,1024]{1,0:T(8,128)(2,1)}, bf16[512,1024]{1,0:T(8,128)(2,1)}, u32[]{:S(2)}, u32[]{:S(2)}) collective-permute-start(bf16[512,1024]{1,0:T(8,128)(2,1)} %copy-done.62), channel_id=1, source_target_pairs={{1,0},{2,1},{5,4},{6,5},{9,8},{10,9},{13,12},{14,13},{17,16},{18,1... | collective-permute-start | bytes 3145736 | tf_op jit(solution)/shard_map/ppermute | solution.py:48
  371.8 26.3 %collective-permute-start.66 = (bf16[2,128,1024]{2,1,0:T(8,128)(2,1)}, bf16[2,128,1024]{2,1,0:T(8,128)(2,1)}, u32[]{:S(2)}, u32[]{:S(2)}) collective-permute-start(bf16[2,128,1024]{2,1,0:T(8,128)(2,1)} %get-tuple-element.259), channel_id=1, source_target_pairs={{2,1},{3,2},{6,5},{7,6},{10,9},{11,10},{14,13},{15,14},{18,17},{19... | collective-permute-start | bytes 1572872 | tf_op jit(solution)/shard_map/ppermute | solution.py:73
  373.7 29.7 %collective-permute-start.63 = (bf16[2,128,1024]{2,1,0:T(8,128)(2,1)}, bf16[2,128,1024]{2,1,0:T(8,128)(2,1)}, u32[]{:S(2)}, u32[]{:S(2)}) collective-permute-start(bf16[2,128,1024]{2,1,0:T(8,128)(2,1)} %get-tuple-element.258), channel_id=1, source_target_pairs={{0,1},{1,2},{4,5},{5,6},{8,9},{9,10},{12,13},{13,14},{16,17},{17,1... | collective-permute-start | bytes 1572872 | tf_op jit(solution)/shard_map/ppermute | solution.py:72
  378.1 34.0 %collective-permute-start.48 = (bf16[4,3,32,1024]{3,2,1,0:T(8,128)(2,1)}, bf16[4,3,32,1024]{3,2,1,0:T(8,128)(2,1)}, u32[]{:S(2)}, u32[]{:S(2)}) collective-permute-start(bf16[4,3,32,1024]{3,2,1,0:T(8,128)(2,1)} %get-tuple-element.239), channel_id=1, source_target_pairs={{0,8},{4,12},{8,0},{12,4},{16,24},{20,28},{24,16},{28,20},{1,9},{5... | collective-permute-start | bytes 2359304 | tf_op jit(solution)/shard_map/ppermute | solution.py:33
  384.3 31.8 %collective-permute-start.46 = (bf16[4,3,32,1024]{3,2,1,0:T(8,128)(2,1)}, bf16[4,3,32,1024]{3,2,1,0:T(8,128)(2,1)}, u32[]{:S(2)}, u32[]{:S(2)}) collective-permute-start(bf16[4,3,32,1024]{3,2,1,0:T(8,128)(2,1)} %get-tuple-element.237), channel_id=1, source_target_pairs={{0,16},{4,20},{8,24},{12,28},{16,0},{20,4},{24,8},{28,12},{1,17},{... | collective-permute-start | bytes 2359304 | tf_op jit(solution)/shard_map/ppermute | solution.py:33
  399.3 21.7 %collective-permute-start.67 = (bf16[2,128,1024]{2,1,0:T(8,128)(2,1)S(1)}, bf16[2,128,1024]{2,1,0:T(8,128)(2,1)S(1)}, u32[]{:S(2)}, u32[]{:S(2)}) collective-permute-start(bf16[2,128,1024]{2,1,0:T(8,128)(2,1)S(1)} %add_convert_fusion.9), channel_id=1, source_target_pairs={{1,0},{2,1},{3,2},{5,4},{6,5},{7,6},{9,8},{10,9},{11,10},{13,12},{... | collective-permute-start | bytes 1572872 | tf_op jit(solution)/shard_map/ppermute | solution.py:73
  407.5 29.6 %collective-permute-start.42 = (bf16[512,1024]{1,0:T(8,128)(2,1)}, bf16[512,1024]{1,0:T(8,128)(2,1)}, u32[]{:S(2)}, u32[]{:S(2)}) collective-permute-start(bf16[512,1024]{1,0:T(8,128)(2,1)} %collective-permute-done.41), channel_id=1, source_target_pairs={{2,3},{6,7},{10,11},{14,15},{18,19},{22,23},{26,27},{30,31}} | collective-permute-start | bytes 3145736 | tf_op jit(solution)/shard_map/ppermute | solution.py:46
  412.1 27.5 %collective-permute-start.40 = (bf16[512,1024]{1,0:T(8,128)(2,1)}, bf16[512,1024]{1,0:T(8,128)(2,1)}, u32[]{:S(2)}, u32[]{:S(2)}) collective-permute-start(bf16[512,1024]{1,0:T(8,128)(2,1)} %collective-permute-done.39), channel_id=1, source_target_pairs={{1,0},{5,4},{9,8},{13,12},{17,16},{21,20},{25,24},{29,28}} | collective-permute-start | bytes 3145736 | tf_op jit(solution)/shard_map/ppermute | solution.py:48
  424.9 29.6 %collective-permute-start.68 = (bf16[2,128,1024]{2,1,0:T(8,128)(2,1)S(1)}, bf16[2,128,1024]{2,1,0:T(8,128)(2,1)S(1)}, u32[]{:S(2)}, u32[]{:S(2)}) collective-permute-start(bf16[2,128,1024]{2,1,0:T(8,128)(2,1)S(1)} %add_convert_fusion.8.n0), channel_id=1, source_target_pairs={{0,8},{4,12},{8,0},{12,4},{16,24},{20,28},{24,16},{28,20},{1,9},{5... | collective-permute-start | bytes 1572872 | tf_op jit(solution)/shard_map/ppermute | solution.py:33
  428.5 36.1 %collective-permute-start.69 = (bf16[2,128,1024]{2,1,0:T(8,128)(2,1)S(1)}, bf16[2,128,1024]{2,1,0:T(8,128)(2,1)S(1)}, u32[]{:S(2)}, u32[]{:S(2)}) collective-permute-start(bf16[2,128,1024]{2,1,0:T(8,128)(2,1)S(1)} %add_convert_fusion.8.n0), channel_id=1, source_target_pairs={{0,16},{4,20},{8,24},{12,28},{16,0},{20,4},{24,8},{28,12},{1,17},{... | collective-permute-start | bytes 1572872 | tf_op jit(solution)/shard_map/ppermute | solution.py:33
  431.1 33.6 %collective-permute-start.70 = (bf16[2,128,1024]{2,1,0:T(8,128)(2,1)S(1)}, bf16[2,128,1024]{2,1,0:T(8,128)(2,1)}, u32[]{:S(2)}, u32[]{:S(2)}) collective-permute-start(bf16[2,128,1024]{2,1,0:T(8,128)(2,1)S(1)} %add_convert_fusion.8.n0), channel_id=1, source_target_pairs={{0,24},{4,28},{8,16},{12,20},{16,8},{20,12},{24,0},{28,4},{1,25},{... | collective-permute-start | bytes 1572872 | tf_op jit(solution)/shard_map/ppermute | solution.py:33
  446.1 19.0 %collective-permute-start.54 = (bf16[2,3,32,1024]{3,2,1,0:T(8,128)(2,1)S(1)}, bf16[2,3,32,1024]{3,2,1,0:T(8,128)(2,1)S(1)}, u32[]{:S(2)}, u32[]{:S(2)}) collective-permute-start(bf16[2,3,32,1024]{3,2,1,0:T(8,128)(2,1)S(1)} %add_convert_fusion.12), channel_id=1, source_target_pairs={{1,0},{2,1},{3,2},{5,4},{6,5},{7,6},{9,8},{10,9},{11,10},{13,12},{... | collective-permute-start | bytes 1179656 | tf_op jit(solution)/shard_map/ppermute | solution.py:73
  454.5 27.2 %collective-permute-start.71 = (bf16[2,128,1024]{2,1,0:T(8,128)(2,1)S(1)}, bf16[2,128,1024]{2,1,0:T(8,128)(2,1)S(1)}, u32[]{:S(2)}, u32[]{:S(2)}) collective-permute-start(bf16[2,128,1024]{2,1,0:T(8,128)(2,1)S(1)} %add_convert_fusion.8.n0), channel_id=1, source_target_pairs={{0,4},{4,0},{8,12},{12,8},{16,20},{20,16},{24,28},{28,24},{1,5},{5... | collective-permute-start | bytes 1572872 | tf_op jit(solution)/shard_map/ppermute | solution.py:33
  464.6 18.3 %collective-permute-start.72 = (bf16[2,128,1024]{2,1,0:T(8,128)(2,1)S(1)}, bf16[2,128,1024]{2,1,0:T(8,128)(2,1)S(1)}, u32[]{:S(2)}, u32[]{:S(2)}) collective-permute-start(bf16[2,128,1024]{2,1,0:T(8,128)(2,1)S(1)} %collective-permute-done.68.n1), channel_id=1, source_target_pairs={{0,4},{4,0},{8,12},{12,8},{16,20},{20,16},{24,28},{28,24},{1,5},{5... | collective-permute-start | bytes 1572872 | tf_op jit(solution)/shard_map/ppermute | solution.py:33
  464.7 18.5 %collective-permute-start.73 = (bf16[2,128,1024]{2,1,0:T(8,128)(2,1)S(1)}, bf16[2,128,1024]{2,1,0:T(8,128)(2,1)}, u32[]{:S(2)}, u32[]{:S(2)}) collective-permute-start(bf16[2,128,1024]{2,1,0:T(8,128)(2,1)S(1)} %collective-permute-done.69.n2), channel_id=1, source_target_pairs={{0,4},{4,0},{8,12},{12,8},{16,20},{20,16},{24,28},{28,24},{1,5},{5... | collective-permute-start | bytes 1572872 | tf_op jit(solution)/shard_map/ppermute | solution.py:33
  465.1 19.3 %collective-permute-start.74 = (bf16[2,128,1024]{2,1,0:T(8,128)(2,1)}, bf16[2,128,1024]{2,1,0:T(8,128)(2,1)}, u32[]{:S(2)}, u32[]{:S(2)}) collective-permute-start(bf16[2,128,1024]{2,1,0:T(8,128)(2,1)} %collective-permute-done.70.n3), channel_id=1, source_target_pairs={{0,4},{4,0},{8,12},{12,8},{16,20},{20,16},{24,28},{28,24},{1,5},{5... | collective-permute-start | bytes 1572872 | tf_op jit(solution)/shard_map/ppermute | solution.py:33
  465.5 37.0 %all-to-all-start.1 = ((f32[32,24,128]{2,1,0:T(8,128)}), f32[32,24,128]{2,1,0:T(8,128)}, u32[]{:S(2)}, u32[]{:S(2)}) async-start(f32[32,24,128]{2,1,0:T(8,128)} %pad_maximum_fusion.7), calls=%async_computation.1 | async-start | bytes 786432 | tf_op jit(solution)/shard_map/all_to_all | solution.py:1282
  482.9 18.8 %collective-permute-start.57 = (bf16[6,32,1024]{2,1,0:T(8,128)(2,1)S(1)}, bf16[6,32,1024]{2,1,0:T(8,128)(2,1)}, u32[]{:S(2)}, u32[]{:S(2)}) collective-permute-start(bf16[6,32,1024]{2,1,0:T(8,128)(2,1)S(1)} %bitcast.187), channel_id=1, source_target_pairs={{0,24},{4,28},{8,16},{12,20},{16,8},{20,12},{24,0},{28,4},{1,25},{... | collective-permute-start | bytes 1179656 | tf_op jit(solution)/shard_map/ppermute | solution.py:33
  483.2 22.5 %collective-permute-start.58 = (bf16[6,32,1024]{2,1,0:T(8,128)(2,1)S(1)}, bf16[6,32,1024]{2,1,0:T(8,128)(2,1)}, u32[]{:S(2)}, u32[]{:S(2)}) collective-permute-start(bf16[6,32,1024]{2,1,0:T(8,128)(2,1)S(1)} %bitcast.188), channel_id=1, source_target_pairs={{0,4},{4,0},{8,12},{12,8},{16,20},{20,16},{24,28},{28,24},{1,5},{5... | collective-permute-start | bytes 1179656 | tf_op jit(solution)/shard_map/ppermute | solution.py:33
  (109 other events, 1273.2 us)
Sparse Core Ops, SparseCore 0:
  233.9 79.5 all-gather.2

commit v6 on v5

--- a/solution.py
+++ b/solution.py
@@ -544,7 +544,7 @@
     return lax.ppermute(value, "tp", [(i, (i + steps) % count) for i in range(count)])
 
 
-def pack_heads(place, wq, wk, wv, wsk, wsv, wo, out, turned):
+def pack_heads(place, wq, wk, wv, wsk, wsv, wo, out, mine, turned):
     chip = place[0] >> 1
     rows = out.shape[2]
     for w, ref in enumerate((wq, wk, wv, wsk, wsv, wo)):
@@ -552,9 +552,10 @@
         for p in range(4):
             cut = pl.ds(pl.multiple_of((chip ^ p) * rows, rows), rows)
             out[p, w] = turned[cut, :].astype(BF16)
-
-
-def pack_hidden(place, wh, wr, out, turned):
+        mine[w] = out[0, w]
+
+
+def pack_hidden(place, wh, wr, out, mine, turned):
     chip = place[0] >> 1
     rows = out.shape[2]
     for w, ref in enumerate((wh, wr)):
@@ -562,6 +563,7 @@
         for p in range(4):
             cut = pl.ds(pl.multiple_of((chip ^ p) * rows, rows), rows)
             out[p, w] = turned[cut, :].astype(BF16)
+        mine[w] = out[0, w]
 
 
 def load_heads(j, own, far, into, first, count):
@@ -965,27 +967,32 @@
     place = jnp.stack([seq_index, tp_index, length]).astype(jnp.int32)
 
     column = pl.BlockSpec((features, DH), lambda i, place: (0, place[0] & 1))
-    (own_w,) = timed(4)(
+    own_w, mine_w = timed(4)(
         pack_heads, place, (1,),
         [column] * 5 + [pl.BlockSpec((DH, features), lambda i, place: (place[0] & 1, 0))],
-        [whole((4, 6, cut, features))],
-        [like((4, 6, cut, features))],
+        [whole((4, 6, cut, features)), whole((6, cut, features))],
+        [like((4, 6, cut, features)), like((6, cut, features))],
         tuple(map(far_away, (
             query_weight, key_weight, value_weight, state_key_weight, state_value_weight, output_weight
         ))),
         [pltpu.VMEM((DH, features), F32)],
     )
-    (own_m,) = timed(5)(
+    own_m, mine_m = timed(5)(
         pack_hidden, place, (1,),
         [
             pl.BlockSpec((features, hidden_cols // 2), lambda i, place: (0, place[0] & 1)),
             pl.BlockSpec((hidden_cols // 2, features), lambda i, place: (place[0] & 1, 0)),
         ],
-        [whole((4, 2, wide, features))],
-        [like((4, 2, wide, features))],
+        [whole((4, 2, wide, features)), whole((2, wide, features))],
+        [like((4, 2, wide, features)), like((2, wide, features))],
         (far_away(hidden_weight), far_away(return_weight)),
         [pltpu.VMEM((hidden_cols // 2, features), F32)],
     )
+
+    def line_of(own):
+        return jnp.stack([cycle(own, j) for j in range(1, tp_count)])
+
+    line_w = line_of(mine_w)
 
     own_tokens = lax.dynamic_index_in_dim(tokens, tp_index, 0, keepdims=False)
     own_cot = lax.dynamic_index_in_dim(cotangent, tp_index, 0, keepdims=False)
@@ -1008,6 +1015,7 @@
     both = lax.all_to_all(
         jnp.broadcast_to(both, (devices,) + both.shape[1:]), ("seq", "tp"), 0, 0
     )
+    both = after(both, line_w)
     both = jnp.transpose(both.reshape(devices, 2, channels, states), (1, 3, 0, 2))
     both = both.reshape(2, states, features // 128, 128)
     rate, gain = both[0], both[1]
@@ -1018,16 +1026,12 @@
     )
     block_power = dict(zip((1, 2, 3, 6), blocks))
 
-    def line_of(own):
-        return jnp.stack([cycle(own, j) for j in range(1, tp_count)])
-
     def plane_of(line, by_x, by_y, half):
         return [line, by_x, by_y, flip(by_y[:, :half], 2), flip(by_x[:, half:], 4)]
 
-    line_w = line_of(own_w[0])
     near_w = flip(line_w, 2), flip(line_w, 4)
     far_w = plane_of(line_w, *near_w, 3)
-    line_m = line_of(after(own_m[0], line_w))
+    line_m = line_of(after(mine_m, line_w))
     near_m = flip(after(line_m, *near_w), 2), flip(after(line_m, *near_w), 4)
     far_m = plane_of(line_m, *near_m, 1)
     far_m[3:] = [value[:, 0] for value in far_m[3:]]
@@ -1251,7 +1255,8 @@
     near_b, away_b = add(keep_b[0], got_b[0]), add(keep_b[1], got_b[1])
     pairs = (near_a, flip(away_a, 4)), (near_b, flip(away_b, 2))
     total_a = line_reduce(
-        [jnp.stack([add(a[j], b[j]) for a, b in pairs]) for j in range(slots)]
+        [jnp.stack([add(a[j], b[j]) for a, b in pairs]) for j in range(slots)],
+        [()] * (slots - 2) + [(total_m,)],
     )
     pieces_m = regather(total_m)
     pieces_a = regather(total_a.reshape(6, cut, features))

time: 530 us -> 526 us (level)
    all_to_all x1, waiting for transfers between devices: 12 us -> 0.01 us  [fast_body(): lax.all_to_all(jnp.broadcast_to(both, (devices,) + both.shape[1:]), ('seq...]
    ppermute x6, waiting for transfers between devices: 9.55 us -> 18.8 us  [cycle(): lax.ppermute(value, 'tp', [(i, (i + steps) % count) for i in range(count)])]
    ppermute x40, waiting for transfers between devices: 35 us -> 28.5 us  [flip(): return lax.ppermute(value, 'seq', [(i, i ^ mask) for i in range(count)])]
    unnamed x166 -> x122, local copies, waits for them, and re-layouts: 13 us -> 9.8 us
where the time goes in v6:
time: 526 us; the launch traced here: 517 us
  Pallas kernels  189 us (36%)
  starting transfers between devices  155 us (29%)
  waiting for transfers between devices  74 us (14%)
  other arithmetic  51.3 us (10%)
  local copies, waits for them, and re-layouts  32.1 us (6%)
  between operations  15.8 us (3%)
    pallas_call x17, Pallas kernels, launch(): pl.pallas_call(kernel, grid_spec=pltpu.PrefetchScalarGridSpec(num_scalar_...  167 us
    ppermute x40, starting transfers between devices, flip(): return lax.ppermute(value, 'seq', [(i, i ^ mask) for i in range(count)])  57.9 us
    ppermute x11, starting transfers between devices, shifted(): lax.ppermute(value, 'seq', [(i, i + steps) for i in range(first, last)])  30.6 us
    ppermute x40, waiting for transfers between devices, flip(): return lax.ppermute(value, 'seq', [(i, i ^ mask) for i in range(count)])  28.5 us
    pallas_call x6, Pallas kernels, call(): pl.pallas_call(kernel, out_shape=[jax.ShapeDtypeStruct(shape, dtype) for...  22.1 us
    ppermute x6, waiting for transfers between devices, cycle(): lax.ppermute(value, 'tp', [(i, (i + steps) % count) for i in range(count)])  18.8 us
    convert_element_type x7, other arithmetic, add(): return (a.astype(F32) + b.astype(F32)).astype(BF16)  17.2 us
    ppermute x3, starting transfers between devices, line_steps(): lax.ppermute(rights[-1], 'tp', [(i, i - 1) for i in range(1, count - k +...  13.9 us
  transfers between devices with their start and end apart: 78, of which 20 were waited for; matrix products, arithmetic and copies ran while one was open for 14% of the time, Pallas kernels for 28%

profile of v6, /device:TPU:17, one launch (start us, length us, event | category | flops | bytes accessed | tf_op | source)
XLA Modules:
  0.0 516.6 jit_solution(16277876825661992835)
XLA Ops:
  9.2 3.2 shard_map.254
  13.7 3.2 collective-permute-start.1
  17.7 6.7 %all-to-all-start = ((f32[32,8,128]{2,1,0:T(8,128)}), f32[32,8,128]{2,1,0:T(8,128)}, u32[]{:S(2)}, u32[]{:S(2)}) async-start(f32[32,8,128]{2,1,0:T(8,128)} %broadcast_in_dim.11), calls=%async_computation | async-start | bytes 262144 | tf_op jit(solution)/shard_map/all_to_all | solution.py:1015
  26.2 3.3 collective-permute-start.3
  36.5 3.6 shard_map.256
  45.1 3.4 collective-permute-done.1
  48.5 3.6 collective-permute-done
  65.2 8.5 %shard_map.257 = (f32[16,8,128]{2,1,0:T(8,128)S(1)}, f32[16,8,128]{2,1,0:T(8,128)S(1)}) custom-call(f32[16,8,128]{2,1,0:T(8,128)S(1)} %get-tuple-element.109.decay_ref, f32[512,8,128]{2,1,0:T(8,128)S(1)} %convert_multiply_fusion.1.u_ref), custom_call_target="tpu_custom_call" | custom-call | flops 8800000000 | tf_op jit(solution)/shard_map/pallas_call | solution.py:164
  73.7 6.5 %collective-permute-done.6.f1 = bf16[3,6,32,1024]{3,2,1,0:T(8,128)(2,1)} collective-permute-done((bf16[3,6,32,1024]{3,2,1,0:T(8,128)(2,1)}, bf16[3,6,32,1024]{3,2,1,0:T(8,128)(2,1)}, u32[]{:S(2)}, u32[]{:S(2)}) %collective-permute-start.6) | collective-permute-done | bytes 1179680 | tf_op jit(solution)/shard_map/ppermute | solution.py:33
  83.3 7.4 %collective-permute-start.8 = (f32[16,8,128]{2,1,0:T(8,128)S(1)}, f32[16,8,128]{2,1,0:T(8,128)S(1)}, u32[]{:S(2)}, u32[]{:S(2)}) collective-permute-start(f32[16,8,128]{2,1,0:T(8,128)S(1)} %get-tuple-element.113), channel_id=1, source_target_pairs={{0,4},{4,8},{8,12},{12,16},{16,20},{20,24},{24,28},{1,5},{5,9},{9,... | collective-permute-start | bytes 196616 | tf_op jit(solution)/shard_map/ppermute | solution.py:39
  94.6 11.8 %collective-permute-done.14 = bf16[2,128,1024]{2,1,0:T(8,128)(2,1)} collective-permute-done((bf16[2,128,1024]{2,1,0:T(8,128)(2,1)}, bf16[2,128,1024]{2,1,0:T(8,128)(2,1)}, u32[]{:S(2)}, u32[]{:S(2)}) %collective-permute-start.14) | collective-permute-done | bytes 524320 | tf_op jit(solution)/shard_map/ppermute | solution.py:544
  106.4 5.2 %collective-permute-start.10 = (f32[16,8,128]{2,1,0:T(8,128)S(1)}, f32[16,8,128]{2,1,0:T(8,128)S(1)}, u32[]{:S(2)}, u32[]{:S(2)}) collective-permute-start(f32[16,8,128]{2,1,0:T(8,128)S(1)} %multiply_add_fusion.2), channel_id=1, source_target_pairs={{0,4},{4,8},{8,12},{12,16},{16,20},{20,24},{24,28},{1,5},{5,9},{9,... | collective-permute-start | bytes 196616 | tf_op jit(solution)/shard_map/ppermute | solution.py:39
  119.4 9.4 %shard_map.259 = (bf16[1024,512]{1,0:T(8,128)(2,1)S(1)}, bf16[1024,512]{1,0:T(8,128)(2,1)S(1)}, bf16[1024,512]{1,0:T(8,128)(2,1)}) custom-call(s32[3]{0:T(128)S(1)} %pad_add_fusion.place, bf16[512,1024]{1,0:T(8,128)(2,1)} %copy-done, bf16[512,1024]{1,0:T(8,128)(2,1)} %collective-permute-done.4.x1, bf16[4,6,32,1024]{3,2,1,0:T(8,128)(2,1)} %copy-done.23, ...), custom_call_target="tpu_custom_call" | custom-call | flops 8800000000 | tf_op jit(solution)/shard_map/pallas_call | solution.py:523
  130.7 21.0 %shard_map.260 = (f32[512,1024]{1,0:T(8,128)}, bf16[512,1024]{1,0:T(8,128)(2,1)S(1)}, bf16[256,1024]{1,0:T(8,128)(2,1)S(1)}, bf16[1024,512]{1,0:T(8,128)(2,1)}, f32[4,1024,1]{2,1,0:T(8,128)}) custom-call(s32[3]{0:T(128)S(1)} %pad_add_fusion.place, bf16[128,1024]{1,0:T(8,128)(2,1)S(1)} %bitcast.183, bf16[128,1024]{1,0:T(8,128)(2,1)S(1)} %collective-permute-done.16.c1, ...), custom_call_target="tpu_custom_call" | custom-call | flops 22000001024 | tf_op jit(solution)/shard_map/pallas_call | solution.py:523
  154.4 4.8 shard_map.261
  165.3 12.3 %shard_map.262 = (bf16[1024,1536]{1,0:T(8,128)(2,1)}, bf16[1024,1536]{1,0:T(8,128)(2,1)}) custom-call(s32[3]{0:T(128)S(1)} %pad_add_fusion.place, bf16[512,1024]{1,0:T(8,128)(2,1)S(1)} %get-tuple-element.133.m0.a0, bf16[512,1024]{1,0:T(8,128)(2,1)S(1)} %collective-permute-done.24.m1.a1, bf16[4,2,128,1024]{3,2,1,0:T(8,128)(2,1)} %copy-done.22, ...), custom_call_target="tpu_custom_call" | custom-call | flops 13200000000 | tf_op jit(solution)/shard_map/pallas_call | solution.py:523
  178.4 4.7 shard_map.263
  185.1 23.0 %shard_map.264 = (f32[512,1024]{1,0:T(8,128)}, bf16[512,1024]{1,0:T(8,128)(2,1)S(1)}, f32[512,1024]{1,0:T(8,128)}, bf16[512,1024]{1,0:T(8,128)(2,1)S(1)}, bf16[1024,2048]{1,0:T(8,128)(2,1)}) custom-call(s32[3]{0:T(128)S(1)} %pad_add_fusion.place, bf16[512,1024]{1,0:T(8,128)(2,1)} %fusion.6.g0.a0, bf16[512,1024]{1,0:T(8,128)(2,1)} %collective-permute-done.5.g1.a1, ...), custom_call_target="tpu_custom_call" | custom-call | flops 23100000256 | tf_op jit(solution)/shard_map/pallas_call | solution.py:523
  209.5 9.7 %shard_map.265 = (bf16[2,4,128,1024]{3,2,1,0:T(8,128)(2,1)}, bf16[2,4,128,1024]{3,2,1,0:T(8,128)(2,1)}) custom-call(s32[3]{0:T(128)S(1)} %pad_add_fusion.place, bf16[512,1024]{1,0:T(8,128)(2,1)} %fusion.6.g0.a0, bf16[512,1024]{1,0:T(8,128)(2,1)} %collective-permute-done.5.g1.a1, bf16[1024,1536]{1,0:T(8,128)(2,1)} %get-tuple-element.139.act_a.rest_0_, ...), custom_call_target="tpu_custom_call" | custom-call | flops 8800000000 | tf_op jit(solution)/shard_map/pallas_call | solution.py:523
  219.2 4.6 shard_map.266
  223.8 6.3 %shard_map.267 = (f32[512,1024]{1,0:T(8,128)}, bf16[512,1024]{1,0:T(8,128)(2,1)}, f32[1,1024]{1,0:T(1,128)S(1)}) custom-call(s32[3]{0:T(128)S(1)} %pad_add_fusion.place, f32[512,1024]{1,0:T(8,128)} %get-tuple-element.142.residual, f32[512,1024]{1,0:T(8,128)} %get-tuple-element.143.own, bf16[512,1024]{1,0:T(8,128)(2,1)} %collective-permute-done.26.got, ...), custom_call_target="tpu_custom_call" | custom-call | flops 5500000256 | tf_op jit(solution)/shard_map/pallas_call | solution.py:523
  230.6 9.1 %shard_map.268 = (bf16[2,4,128,1024]{3,2,1,0:T(8,128)(2,1)}, bf16[2,4,128,1024]{3,2,1,0:T(8,128)(2,1)}) custom-call(s32[3]{0:T(128)S(1)} %pad_add_fusion.place, bf16[512,1024]{1,0:T(8,128)(2,1)S(1)} %get-tuple-element.133.m0.a0, bf16[512,1024]{1,0:T(8,128)(2,1)S(1)} %copy-done.18, bf16[1024,2048]{1,0:T(8,128)(2,1)} %get-tuple-element.147.rest_0_), custom_call_target="tpu_custom_call" | custom-call | flops 8800000000 | tf_op jit(solution)/shard_map/pallas_call | solution.py:523
  242.5 26.9 %shard_map.269 = (f32[512,1024]{1,0:T(8,128)}, bf16[512,1024]{1,0:T(8,128)(2,1)S(1)}, f32[128,1024]{1,0:T(8,128)S(1)}, bf16[128,1024]{1,0:T(8,128)(2,1)S(1)}, bf...) custom-call(s32[3]{0:T(128)S(1)} %pad_add_fusion.place, bf16[512,1024]{1,0:T(8,128)(2,1)} %get-tuple-element.149.g0, ...), custom_call_target="tpu_custom_call" | custom-call | flops 29699999744 | tf_op jit(solution)/shard_map/pallas_call | solution.py:523
  270.1 10.5 %shard_map.271 = (bf16[2,4,3,32,1024]{4,3,2,1,0:T(8,128)(2,1)}, bf16[2,4,3,32,1024]{4,3,2,1,0:T(8,128)(2,1)}, bf16[2,4,3,32,1024]{4,3,2,1,0:T(8,128)(2,1)}, bf16[2,4,3,32,1024]{4,3,2,1,0:T(8,128)(2,1)}) custom-call(s32[3]{0:T(128)S(1)} %pad_add_fusion.place, bf16[512,1024]{1,0:T(8,128)(2,1)S(1)} %copy-done.1, bf16[512,1024]{1,0:T(8,128)(2,1)} %collective-permute-done.4.x1, ...), custom_call_target="tpu_custom_call" | custom-call | flops 11000000512 | tf_op jit(solution)/shard_map/pallas_call | solution.py:523
  283.1 4.6 collective-permute-done.30
  301.9 4.1 collective-permute-done.34
  309.1 4.5 shard_map.272
  314.3 5.2 %shard_map.273 = (bf16[512,1024]{1,0:T(8,128)(2,1)S(1)}, f32[1,1024]{1,0:T(1,128)S(1)}) custom-call(s32[3]{0:T(128)S(1)} %pad_add_fusion.place, bf16[4,512,1024]{2,1,0:T(8,128)(2,1)} %tokens.3, f32[512,1024]{1,0:T(8,128)} %get-tuple-element.152.own, bf16[512,1024]{1,0:T(8,128)(2,1)} %collective-permute-done.28.got, bf16[512,1024]{1,0:T(8,128)(2,1)S(1)} %bitcast.170, ...), custom_call_target="tpu_custom_call" | custom-call | flops 5500000256 | tf_op jit(solution)/shard_map/pallas_call | solution.py:523
  321.4 3.4 collective-permute-start.38
  324.7 9.5 %collective-permute-done.43 = bf16[4,128,1024]{2,1,0:T(8,128)(2,1)} collective-permute-done((bf16[4,128,1024]{2,1,0:T(8,128)(2,1)}, bf16[4,128,1024]{2,1,0:T(8,128)(2,1)}, u32[]{:S(2)}, u32[]{:S(2)}) %collective-permute-start.43) | collective-permute-done | bytes 1048608 | tf_op jit(solution)/shard_map/ppermute | solution.py:33
  335.9 3.2 fusion.26
  339.2 6.1 %collective-permute-done.37 = bf16[512,1024]{1,0:T(8,128)(2,1)S(1)} collective-permute-done((bf16[512,1024]{1,0:T(8,128)(2,1)S(1)}, bf16[512,1024]{1,0:T(8,128)(2,1)S(1)}, u32[]{:S(2)}, u32[]{:S(2)}) %collective-permute-start.37) | collective-permute-done | bytes 1048608 | tf_op jit(solution)/shard_map/ppermute | solution.py:46
  350.2 4.7 collective-permute-start.41
  354.9 9.8 %collective-permute-start.39 = (bf16[512,1024]{1,0:T(8,128)(2,1)}, bf16[512,1024]{1,0:T(8,128)(2,1)}, u32[]{:S(2)}, u32[]{:S(2)}) collective-permute-start(bf16[512,1024]{1,0:T(8,128)(2,1)} %copy-done.47), channel_id=1, source_target_pairs={{1,0},{2,1},{5,4},{6,5},{9,8},{10,9},{13,12},{14,13},{17,16},{18,1... | collective-permute-start | bytes 3145736 | tf_op jit(solution)/shard_map/ppermute | solution.py:48
  378.0 3.3 add_convert_fusion.7
  383.6 5.5 %shard_map.274 = (f32[16,8,128]{2,1,0:T(8,128)S(1)}, f32[16,8,128]{2,1,0:T(8,128)S(1)}) custom-call(f32[16,8,128]{2,1,0:T(8,128)S(1)} %copy-done.28, f32[16,8,128]{2,1,0:T(8,128)S(1)} %copy-done.10, f32[128,8,128]{2,1,0:T(8,128)S(1)} %bitcast.173, f32[128,8,128]{2,1,0:T(8,128)S(1)} %bitcast.175), custom_call_target="tpu_custom_call" | custom-call | flops 5500000256 | tf_op jit(solution)/shard_map/pallas_call | solution.py:164
  396.1 4.1 collective-permute-start.54
  413.4 4.0 collective-permute-start.68
  419.6 5.7 %collective-permute-start.70 = (bf16[2,128,1024]{2,1,0:T(8,128)(2,1)S(1)}, bf16[2,128,1024]{2,1,0:T(8,128)(2,1)}, u32[]{:S(2)}, u32[]{:S(2)}) collective-permute-start(bf16[2,128,1024]{2,1,0:T(8,128)(2,1)S(1)} %add_convert_fusion.8.n0), channel_id=1, source_target_pairs={{0,24},{4,28},{8,16},{12,20},{16,8},{20,12},{24,0},{28,4},{1,25},{... | collective-permute-start | bytes 1572872 | tf_op jit(solution)/shard_map/ppermute | solution.py:33
  425.6 5.2 collective-permute-done.42
  434.2 5.4 %collective-permute-done.59 = bf16[2,3,32,1024]{3,2,1,0:T(8,128)(2,1)S(1)} collective-permute-done((bf16[2,3,32,1024]{3,2,1,0:T(8,128)(2,1)S(1)}, bf16[2,3,32,1024]{3,2,1,0:T(8,128)(2,1)S(1)}, u32[]{:S(2)}, u32[]{:S(2)}) %collective-permute-start.59) | collective-permute-done | bytes 393248 | tf_op jit(solution)/shard_map/ppermute | solution.py:73
  442.1 3.2 collective-permute-start.57
  447.9 11.8 %collective-permute-start.71 = (bf16[2,128,1024]{2,1,0:T(8,128)(2,1)S(1)}, bf16[2,128,1024]{2,1,0:T(8,128)(2,1)S(1)}, u32[]{:S(2)}, u32[]{:S(2)}) collective-permute-start(bf16[2,128,1024]{2,1,0:T(8,128)(2,1)S(1)} %add_convert_fusion.8.n0), channel_id=1, source_target_pairs={{0,4},{4,0},{8,12},{12,8},{16,20},{20,16},{24,28},{28,24},{1,5},{5... | collective-permute-start | bytes 1572872 | tf_op jit(solution)/shard_map/ppermute | solution.py:33
  460.9 9.9 %all-to-all-start.1 = ((f32[32,24,128]{2,1,0:T(8,128)}), f32[32,24,128]{2,1,0:T(8,128)}, u32[]{:S(2)}, u32[]{:S(2)}) async-start(f32[32,24,128]{2,1,0:T(8,128)} %pad_maximum_fusion.7), calls=%async_computation.1 | async-start | bytes 786432 | tf_op jit(solution)/shard_map/all_to_all | solution.py:1287
  470.8 5.3 %maximum_convert_fusion = f32[4,512,1024]{2,1,0:T(8,128)} fusion(bf16[1,512,1024]{2,1,0:T(8,128)(2,1)} %get-tuple-element.247, bf16[1,512,1024]{2,1,0:T(8,128)(2,1)} %get-tuple-element.248, bf16[1,512,1024]{2,1,0:T(8,128)(2,1)} %get-tuple-element.249, bf16[1,512,1024]{2,1,0:T(8,128)(2,1)} %get-tuple-element.246), kind=kLoop, calls=%fused_computation.1 | loop fusion | flops 8388608 | bytes 12582912 | tf_op jit(solution)/shard_map/convert_element_type | solution.py:1233
  480.0 6.0 %shard_map.276 = (f32[1024,1024]{1,0:T(8,128)}, f32[1024,1024]{1,0:T(8,128)}) custom-call(s32[3]{0:T(128)S(1)} %pad_add_fusion.place, bf16[2,128,1024]{2,1,0:T(8,128)(2,1)S(1)} %add_convert_fusion.8.n0, bf16[2,128,1024]{2,1,0:T(8,128)(2,1)S(1)} %collective-permute-done.68.n1, bf16[2,128,1024]{2,1,0:T(8,128)(2,1)S(1)} %collective-permute-done.69.n2, ...), custom_call_target="tpu_custom_call" | custom-call | flops 5500000256 | tf_op jit(solution)/shard_map/pallas_call | solution.py:523
  489.1 7.7 %collective-permute-start.66 = (bf16[6,32,1024]{2,1,0:T(8,128)(2,1)}, bf16[6,32,1024]{2,1,0:T(8,128)(2,1)S(1)}, u32[]{:S(2)}, u32[]{:S(2)}) collective-permute-start(bf16[6,32,1024]{2,1,0:T(8,128)(2,1)} %collective-permute-done.62.n2), channel_id=1, source_target_pairs={{0,4},{4,0},{8,12},{12,8},{16,20},{20,16},{24,28},{28,24},{1,5},{5... | collective-permute-start | bytes 1179656 | tf_op jit(solution)/shard_map/ppermute | solution.py:33
  501.3 6.3 %shard_map.275 = (f32[1024,256]{1,0:T(8,128)}, f32[1024,256]{1,0:T(8,128)}, f32[1024,256]{1,0:T(8,128)}, f32[256,1024]{1,0:T(8,128)}, f32[1024,256]{1,0:T(8,128)}, /*index=5*/f32[1024,256]{1,0:T(8,128)}) custom-call(s32[3]{0:T(128)S(1)} %pad_add_fusion.place, bf16[6,32,1024]{2,1,0:T(8,128)(2,1)S(1)} %bitcast.181, ...), custom_call_target="tpu_custom_call" | custom-call | flops 5500000256 | tf_op jit(solution)/shard_map/pallas_call | solution.py:523
  (346 shorter events, 154.0 us)
Async XLA Ops:
  13.5 31.6 %collective-permute-start.2 = (bf16[6,32,1024]{2,1,0:T(8,128)(2,1)}, bf16[6,32,1024]{2,1,0:T(8,128)(2,1)}, u32[]{:S(2)}, u32[]{:S(2)}) collective-permute-start(bf16[6,32,1024]{2,1,0:T(8,128)(2,1)} %get-tuple-element.107), channel_id=1, source_target_pairs={{0,3},{1,0},{2,1},{3,2},{4,7},{5,4},{6,5},{7,6},{8,11},{9,8},{10,9... | collective-permute-start | bytes 1179656 | tf_op jit(solution)/shard_map/ppermute | solution.py:544
  13.7 34.8 %collective-permute-start.1 = (bf16[6,32,1024]{2,1,0:T(8,128)(2,1)}, bf16[6,32,1024]{2,1,0:T(8,128)(2,1)}, u32[]{:S(2)}, u32[]{:S(2)}) collective-permute-start(bf16[6,32,1024]{2,1,0:T(8,128)(2,1)} %get-tuple-element.107), channel_id=1, source_target_pairs={{0,2},{1,3},{2,0},{3,1},{4,6},{5,7},{6,4},{7,5},{8,10},{9,11},{10,... | collective-permute-start | bytes 1179656 | tf_op jit(solution)/shard_map/ppermute | solution.py:544
  16.9 35.1 %collective-permute-start = (bf16[6,32,1024]{2,1,0:T(8,128)(2,1)}, bf16[6,32,1024]{2,1,0:T(8,128)(2,1)}, u32[]{:S(2)}, u32[]{:S(2)}) collective-permute-start(bf16[6,32,1024]{2,1,0:T(8,128)(2,1)} %get-tuple-element.107), channel_id=1, source_target_pairs={{0,1},{1,2},{2,3},{3,0},{4,5},{5,6},{6,7},{7,4},{8,9},{9,10},{10,1... | collective-permute-start | bytes 1179656 | tf_op jit(solution)/shard_map/ppermute | solution.py:544
  17.7 40.0 %all-to-all-start = ((f32[32,8,128]{2,1,0:T(8,128)}), f32[32,8,128]{2,1,0:T(8,128)}, u32[]{:S(2)}, u32[]{:S(2)}) async-start(f32[32,8,128]{2,1,0:T(8,128)} %broadcast_in_dim.11), calls=%async_computation | async-start | bytes 262144 | tf_op jit(solution)/shard_map/all_to_all | solution.py:1015
  24.5 289.5 %all-gather.3.cloned.1.call-start = ((), (), s32[]{:S(2)}) async-start(), calls=%async_computation.2 | async-start | bytes 5242880 | tf_op jit(solution)/shard_map/all_gather | solution.py:1155
  34.3 29.3 %collective-permute-start.4 = (bf16[512,1024]{1,0:T(8,128)(2,1)S(1)}, bf16[512,1024]{1,0:T(8,128)(2,1)}, u32[]{:S(2)}, u32[]{:S(2)}) collective-permute-start(bf16[512,1024]{1,0:T(8,128)(2,1)S(1)} %fusion.5.x0), channel_id=1, source_target_pairs={{0,4},{4,0},{8,12},{12,8},{16,20},{20,16},{24,28},{28,24},{1,5},{5... | collective-permute-start | bytes 3145736 | tf_op jit(solution)/shard_map/ppermute | solution.py:33
  43.3 21.3 %collective-permute-start.5 = (bf16[512,1024]{1,0:T(8,128)(2,1)}, bf16[512,1024]{1,0:T(8,128)(2,1)}, u32[]{:S(2)}, u32[]{:S(2)}) collective-permute-start(bf16[512,1024]{1,0:T(8,128)(2,1)} %fusion.6.g0.a0), channel_id=1, source_target_pairs={{0,4},{4,0},{8,12},{12,8},{16,20},{20,16},{24,28},{28,24},{1,5},{5... | collective-permute-start | bytes 3145736 | tf_op jit(solution)/shard_map/ppermute | solution.py:33
  54.4 25.8 %collective-permute-start.6 = (bf16[3,6,32,1024]{3,2,1,0:T(8,128)(2,1)}, bf16[3,6,32,1024]{3,2,1,0:T(8,128)(2,1)}, u32[]{:S(2)}, u32[]{:S(2)}) collective-permute-start(bf16[3,6,32,1024]{3,2,1,0:T(8,128)(2,1)} %pad_maximum_fusion.2.f0), channel_id=1, source_target_pairs={{0,8},{4,12},{8,0},{12,4},{16,24},{20,28},{24,16},{28,20},{1,9},{5... | collective-permute-start | bytes 3538952 | tf_op jit(solution)/shard_map/ppermute | solution.py:33
  55.6 25.5 %collective-permute-start.7 = (bf16[3,6,32,1024]{3,2,1,0:T(8,128)(2,1)}, bf16[3,6,32,1024]{3,2,1,0:T(8,128)(2,1)}, u32[]{:S(2)}, u32[]{:S(2)}) collective-permute-start(bf16[3,6,32,1024]{3,2,1,0:T(8,128)(2,1)} %pad_maximum_fusion.2.f0), channel_id=1, source_target_pairs={{0,16},{4,20},{8,24},{12,28},{16,0},{20,4},{24,8},{28,12},{1,17},{... | collective-permute-start | bytes 3538952 | tf_op jit(solution)/shard_map/ppermute | solution.py:33
  63.4 30.5 %collective-permute-start.15 = (bf16[2,128,1024]{2,1,0:T(8,128)(2,1)}, bf16[2,128,1024]{2,1,0:T(8,128)(2,1)}, u32[]{:S(2)}, u32[]{:S(2)}) collective-permute-start(bf16[2,128,1024]{2,1,0:T(8,128)(2,1)} %get-tuple-element.119), channel_id=1, source_target_pairs={{0,3},{1,0},{2,1},{3,2},{4,7},{5,4},{6,5},{7,6},{8,11},{9,8},{10,9... | collective-permute-start | bytes 1572872 | tf_op jit(solution)/shard_map/ppermute | solution.py:544
  63.6 42.9 %collective-permute-start.14 = (bf16[2,128,1024]{2,1,0:T(8,128)(2,1)}, bf16[2,128,1024]{2,1,0:T(8,128)(2,1)}, u32[]{:S(2)}, u32[]{:S(2)}) collective-permute-start(bf16[2,128,1024]{2,1,0:T(8,128)(2,1)} %get-tuple-element.119), channel_id=1, source_target_pairs={{0,2},{1,3},{2,0},{3,1},{4,6},{5,7},{6,4},{7,5},{8,10},{9,11},{10,... | collective-permute-start | bytes 1572872 | tf_op jit(solution)/shard_map/ppermute | solution.py:544
  64.6 47.1 %collective-permute-start.13 = (bf16[2,128,1024]{2,1,0:T(8,128)(2,1)}, bf16[2,128,1024]{2,1,0:T(8,128)(2,1)}, u32[]{:S(2)}, u32[]{:S(2)}) collective-permute-start(bf16[2,128,1024]{2,1,0:T(8,128)(2,1)} %get-tuple-element.119), channel_id=1, source_target_pairs={{0,1},{1,2},{2,3},{3,0},{4,5},{5,6},{6,7},{7,4},{8,9},{9,10},{10,1... | collective-permute-start | bytes 1572872 | tf_op jit(solution)/shard_map/ppermute | solution.py:544
  93.6 25.8 %collective-permute-start.17 = (bf16[3,3,32,1024]{3,2,1,0:T(8,128)(2,1)S(1)}, bf16[3,3,32,1024]{3,2,1,0:T(8,128)(2,1)S(1)}, u32[]{:S(2)}, u32[]{:S(2)}) collective-permute-start(bf16[3,3,32,1024]{3,2,1,0:T(8,128)(2,1)S(1)} %slice.294), channel_id=1, source_target_pairs={{0,8},{4,12},{8,0},{12,4},{16,24},{20,28},{24,16},{28,20},{1,9},{5... | collective-permute-start | bytes 1769480 | tf_op jit(solution)/shard_map/ppermute | solution.py:33
  93.9 25.5 %collective-permute-start.18 = (bf16[3,3,32,1024]{3,2,1,0:T(8,128)(2,1)S(1)}, bf16[3,3,32,1024]{3,2,1,0:T(8,128)(2,1)S(1)}, u32[]{:S(2)}, u32[]{:S(2)}) collective-permute-start(bf16[3,3,32,1024]{3,2,1,0:T(8,128)(2,1)S(1)} %slice.295), channel_id=1, source_target_pairs={{0,16},{4,20},{8,24},{12,28},{16,0},{20,4},{24,8},{28,12},{1,17},{... | collective-permute-start | bytes 1769480 | tf_op jit(solution)/shard_map/ppermute | solution.py:33
  93.9 21.6 %collective-permute-start.12 = (f32[16,8,128]{2,1,0:T(8,128)S(1)}, f32[16,8,128]{2,1,0:T(8,128)S(1)}, u32[]{:S(2)}, u32[]{:S(2)}) collective-permute-start(f32[16,8,128]{2,1,0:T(8,128)S(1)} %multiply_add_fusion.2), channel_id=1, source_target_pairs={{0,28},{1,29},{2,30},{3,31}} | collective-permute-start | bytes 196616 | tf_op jit(solution)/shard_map/ppermute | solution.py:39
  115.5 36.2 %collective-permute-start.20 = (bf16[3,2,128,1024]{3,2,0,1:T(8,128)(2,1)S(1)}, bf16[3,2,128,1024]{3,2,0,1:T(8,128)(2,1)S(1)}, u32[]{:S(2)}, u32[]{:S(2)}) collective-permute-start(bf16[3,2,128,1024]{3,2,0,1:T(8,128)(2,1)S(1)} %pad_maximum_fusion.1), channel_id=1, source_target_pairs={{0,8},{4,12},{8,0},{12,4},{16,24},{20,28},{24,16},{28,20},{1,9},{5... | collective-permute-start | bytes 4718600 | tf_op jit(solution)/shard_map/ppermute | solution.py:33
  115.9 35.9 %collective-permute-start.21 = (bf16[3,2,128,1024]{3,2,0,1:T(8,128)(2,1)S(1)}, bf16[3,2,128,1024]{3,2,0,1:T(8,128)(2,1)S(1)}, u32[]{:S(2)}, u32[]{:S(2)}) collective-permute-start(bf16[3,2,128,1024]{3,2,0,1:T(8,128)(2,1)S(1)} %pad_maximum_fusion.1), channel_id=1, source_target_pairs={{0,16},{4,20},{8,24},{12,28},{16,0},{20,4},{24,8},{28,12},{1,17},{... | collective-permute-start | bytes 4718600 | tf_op jit(solution)/shard_map/ppermute | solution.py:33
  159.6 18.8 %collective-permute-start.22 = (bf16[3,1,128,1024]{3,2,0,1:T(8,128)(2,1)S(1)}, bf16[3,1,128,1024]{3,2,0,1:T(8,128)(2,1)S(1)}, u32[]{:S(2)}, u32[]{:S(2)}) collective-permute-start(bf16[3,1,128,1024]{3,2,0,1:T(8,128)(2,1)S(1)} %slice.296), channel_id=1, source_target_pairs={{0,8},{4,12},{8,0},{12,4},{16,24},{20,28},{24,16},{28,20},{1,9},{5... | collective-permute-start | bytes 2359304 | tf_op jit(solution)/shard_map/ppermute | solution.py:33
  160.9 24.3 %collective-permute-start.23 = (bf16[3,1,128,1024]{3,2,0,1:T(8,128)(2,1)S(1)}, bf16[3,1,128,1024]{3,2,0,1:T(8,128)(2,1)S(1)}, u32[]{:S(2)}, u32[]{:S(2)}) collective-permute-start(bf16[3,1,128,1024]{3,2,0,1:T(8,128)(2,1)S(1)} %slice.297), channel_id=1, source_target_pairs={{0,16},{4,20},{8,24},{12,28},{16,0},{20,4},{24,8},{28,12},{1,17},{... | collective-permute-start | bytes 2359304 | tf_op jit(solution)/shard_map/ppermute | solution.py:33
  239.7 48.0 %collective-permute-start.30 = (bf16[2,4,128,1024]{3,2,1,0:T(8,128)(2,1)}, bf16[2,4,128,1024]{3,2,1,0:T(8,128)(2,1)S(1)}, u32[]{:S(2)}, u32[]{:S(2)}) collective-permute-start(bf16[2,4,128,1024]{3,2,1,0:T(8,128)(2,1)} %get-tuple-element.158), channel_id=1, source_target_pairs={{0,16},{4,20},{8,24},{12,28},{16,0},{20,4},{24,8},{28,12},{1,17},{... | collective-permute-start | bytes 6291464 | tf_op jit(solution)/shard_map/ppermute | solution.py:33
  241.4 47.2 %collective-permute-start.31 = (bf16[2,4,128,1024]{3,2,1,0:T(8,128)(2,1)}, bf16[2,4,128,1024]{3,2,1,0:T(8,128)(2,1)S(1)}, u32[]{:S(2)}, u32[]{:S(2)}) collective-permute-start(bf16[2,4,128,1024]{3,2,1,0:T(8,128)(2,1)} %get-tuple-element.160), channel_id=1, source_target_pairs={{0,8},{4,12},{8,0},{12,4},{16,24},{20,28},{24,16},{28,20},{1,9},{5... | collective-permute-start | bytes 6291464 | tf_op jit(solution)/shard_map/ppermute | solution.py:33
  269.4 44.6 %collective-permute-start.28 = (bf16[512,1024]{1,0:T(8,128)(2,1)S(1)}, bf16[512,1024]{1,0:T(8,128)(2,1)}, u32[]{:S(2)}, u32[]{:S(2)}) collective-permute-start(bf16[512,1024]{1,0:T(8,128)(2,1)S(1)} %get-tuple-element.153), channel_id=1, source_target_pairs={{0,4},{4,0},{8,12},{12,8},{16,20},{20,16},{24,28},{28,24},{1,5},{5... | collective-permute-start | bytes 3145736 | tf_op jit(solution)/shard_map/ppermute | solution.py:33
  280.7 21.0 %collective-permute-start.36 = (bf16[128,1024]{1,0:T(8,128)(2,1)S(1)}, bf16[128,1024]{1,0:T(8,128)(2,1)S(1)}, u32[]{:S(2)}, u32[]{:S(2)}) collective-permute-start(bf16[128,1024]{1,0:T(8,128)(2,1)S(1)} %add_convert_fusion.14), channel_id=1, source_target_pairs={{4,0},{8,4},{12,8},{16,12},{20,16},{24,20},{28,24},{5,1},{9,5},{13... | collective-permute-start | bytes 786440 | tf_op jit(solution)/shard_map/ppermute | solution.py:39
  308.9 25.3 %collective-permute-start.43 = (bf16[4,128,1024]{2,1,0:T(8,128)(2,1)}, bf16[4,128,1024]{2,1,0:T(8,128)(2,1)}, u32[]{:S(2)}, u32[]{:S(2)}) collective-permute-start(bf16[4,128,1024]{2,1,0:T(8,128)(2,1)} %get-tuple-element.179), channel_id=1, source_target_pairs={{0,16},{4,20},{8,24},{12,28},{16,0},{20,4},{24,8},{28,12},{1,17},{... | collective-permute-start | bytes 3145736 | tf_op jit(solution)/shard_map/ppermute | solution.py:33
  309.0 25.2 %collective-permute-start.44 = (bf16[4,128,1024]{2,1,0:T(8,128)(2,1)}, bf16[4,128,1024]{2,1,0:T(8,128)(2,1)}, u32[]{:S(2)}, u32[]{:S(2)}) collective-permute-start(bf16[4,128,1024]{2,1,0:T(8,128)(2,1)} %get-tuple-element.181), channel_id=1, source_target_pairs={{0,8},{4,12},{8,0},{12,4},{16,24},{20,28},{24,16},{28,20},{1,9},{5... | collective-permute-start | bytes 3145736 | tf_op jit(solution)/shard_map/ppermute | solution.py:33
  319.5 25.8 %collective-permute-start.37 = (bf16[512,1024]{1,0:T(8,128)(2,1)S(1)}, bf16[512,1024]{1,0:T(8,128)(2,1)S(1)}, u32[]{:S(2)}, u32[]{:S(2)}) collective-permute-start(bf16[512,1024]{1,0:T(8,128)(2,1)S(1)} %get-tuple-element.170), channel_id=1, source_target_pairs={{0,1},{1,2},{2,3},{4,5},{5,6},{6,7},{8,9},{9,10},{10,11},{12,13},{... | collective-permute-start | bytes 3145736 | tf_op jit(solution)/shard_map/ppermute | solution.py:46
  321.4 25.8 %collective-permute-start.38 = (bf16[512,1024]{1,0:T(8,128)(2,1)S(1)}, bf16[512,1024]{1,0:T(8,128)(2,1)S(1)}, u32[]{:S(2)}, u32[]{:S(2)}) collective-permute-start(bf16[512,1024]{1,0:T(8,128)(2,1)S(1)} %get-tuple-element.170), channel_id=1, source_target_pairs={{1,0},{2,1},{3,2},{5,4},{6,5},{7,6},{9,8},{10,9},{11,10},{13,12},{... | collective-permute-start | bytes 3145736 | tf_op jit(solution)/shard_map/ppermute | solution.py:48
  334.3 36.1 %collective-permute-start.47 = (bf16[2,4,3,32,1024]{4,3,2,1,0:T(8,128)(2,1)}, bf16[2,4,3,32,1024]{4,3,2,1,0:T(8,128)(2,1)}, u32[]{:S(2)}, u32[]{:S(2)}) collective-permute-start(bf16[2,4,3,32,1024]{4,3,2,1,0:T(8,128)(2,1)} %get-tuple-element.186), channel_id=1, source_target_pairs={{0,16},{4,20},{8,24},{12,28},{16,0},{20,4},{24,8},{28,12},{1,17},{... | collective-permute-start | bytes 4718600 | tf_op jit(solution)/shard_map/ppermute | solution.py:33
  335.9 38.9 %collective-permute-start.45 = (bf16[2,4,3,32,1024]{4,3,2,1,0:T(8,128)(2,1)}, bf16[2,4,3,32,1024]{4,3,2,1,0:T(8,128)(2,1)}, u32[]{:S(2)}, u32[]{:S(2)}) collective-permute-start(bf16[2,4,3,32,1024]{4,3,2,1,0:T(8,128)(2,1)} %get-tuple-element.183), channel_id=1, source_target_pairs={{0,8},{4,12},{8,0},{12,4},{16,24},{20,28},{24,16},{28,20},{1,9},{5... | collective-permute-start | bytes 4718600 | tf_op jit(solution)/shard_map/ppermute | solution.py:33
  350.2 31.1 %collective-permute-start.41 = (bf16[512,1024]{1,0:T(8,128)(2,1)}, bf16[512,1024]{1,0:T(8,128)(2,1)}, u32[]{:S(2)}, u32[]{:S(2)}) collective-permute-start(bf16[512,1024]{1,0:T(8,128)(2,1)} %copy-done.45), channel_id=1, source_target_pairs={{1,2},{2,3},{5,6},{6,7},{9,10},{10,11},{13,14},{14,15},{17,18},{18... | collective-permute-start | bytes 3145736 | tf_op jit(solution)/shard_map/ppermute | solution.py:46
  354.9 28.7 %collective-permute-start.39 = (bf16[512,1024]{1,0:T(8,128)(2,1)}, bf16[512,1024]{1,0:T(8,128)(2,1)}, u32[]{:S(2)}, u32[]{:S(2)}) collective-permute-start(bf16[512,1024]{1,0:T(8,128)(2,1)} %copy-done.47), channel_id=1, source_target_pairs={{1,0},{2,1},{5,4},{6,5},{9,8},{10,9},{13,12},{14,13},{17,16},{18,1... | collective-permute-start | bytes 3145736 | tf_op jit(solution)/shard_map/ppermute | solution.py:48
  368.5 26.4 %collective-permute-start.53 = (bf16[2,128,1024]{2,1,0:T(8,128)(2,1)}, bf16[2,128,1024]{2,1,0:T(8,128)(2,1)}, u32[]{:S(2)}, u32[]{:S(2)}) collective-permute-start(bf16[2,128,1024]{2,1,0:T(8,128)(2,1)} %get-tuple-element.273), channel_id=1, source_target_pairs={{2,1},{3,2},{6,5},{7,6},{10,9},{11,10},{14,13},{15,14},{18,17},{19... | collective-permute-start | bytes 1572872 | tf_op jit(solution)/shard_map/ppermute | solution.py:73
  370.4 29.8 %collective-permute-start.50 = (bf16[2,128,1024]{2,1,0:T(8,128)(2,1)}, bf16[2,128,1024]{2,1,0:T(8,128)(2,1)}, u32[]{:S(2)}, u32[]{:S(2)}) collective-permute-start(bf16[2,128,1024]{2,1,0:T(8,128)(2,1)} %get-tuple-element.272), channel_id=1, source_target_pairs={{0,1},{1,2},{4,5},{5,6},{8,9},{9,10},{12,13},{13,14},{16,17},{17,1... | collective-permute-start | bytes 1572872 | tf_op jit(solution)/shard_map/ppermute | solution.py:72
  374.8 31.4 %collective-permute-start.48 = (bf16[4,3,32,1024]{3,2,1,0:T(8,128)(2,1)}, bf16[4,3,32,1024]{3,2,1,0:T(8,128)(2,1)}, u32[]{:S(2)}, u32[]{:S(2)}) collective-permute-start(bf16[4,3,32,1024]{3,2,1,0:T(8,128)(2,1)} %get-tuple-element.253), channel_id=1, source_target_pairs={{0,8},{4,12},{8,0},{12,4},{16,24},{20,28},{24,16},{28,20},{1,9},{5... | collective-permute-start | bytes 2359304 | tf_op jit(solution)/shard_map/ppermute | solution.py:33
  381.2 27.3 %collective-permute-start.46 = (bf16[4,3,32,1024]{3,2,1,0:T(8,128)(2,1)}, bf16[4,3,32,1024]{3,2,1,0:T(8,128)(2,1)}, u32[]{:S(2)}, u32[]{:S(2)}) collective-permute-start(bf16[4,3,32,1024]{3,2,1,0:T(8,128)(2,1)} %get-tuple-element.251), channel_id=1, source_target_pairs={{0,16},{4,20},{8,24},{12,28},{16,0},{20,4},{24,8},{28,12},{1,17},{... | collective-permute-start | bytes 2359304 | tf_op jit(solution)/shard_map/ppermute | solution.py:33
  403.5 27.2 %collective-permute-start.42 = (bf16[512,1024]{1,0:T(8,128)(2,1)}, bf16[512,1024]{1,0:T(8,128)(2,1)S(1)}, u32[]{:S(2)}, u32[]{:S(2)}) collective-permute-start(bf16[512,1024]{1,0:T(8,128)(2,1)} %collective-permute-done.41), channel_id=1, source_target_pairs={{2,3},{6,7},{10,11},{14,15},{18,19},{22,23},{26,27},{30,31}} | collective-permute-start | bytes 3145736 | tf_op jit(solution)/shard_map/ppermute | solution.py:46
  406.2 26.6 %collective-permute-start.40 = (bf16[512,1024]{1,0:T(8,128)(2,1)}, bf16[512,1024]{1,0:T(8,128)(2,1)S(1)}, u32[]{:S(2)}, u32[]{:S(2)}) collective-permute-start(bf16[512,1024]{1,0:T(8,128)(2,1)} %collective-permute-done.39), channel_id=1, source_target_pairs={{1,0},{5,4},{9,8},{13,12},{17,16},{21,20},{25,24},{29,28}} | collective-permute-start | bytes 3145736 | tf_op jit(solution)/shard_map/ppermute | solution.py:48
  413.4 34.5 %collective-permute-start.68 = (bf16[2,128,1024]{2,1,0:T(8,128)(2,1)S(1)}, bf16[2,128,1024]{2,1,0:T(8,128)(2,1)S(1)}, u32[]{:S(2)}, u32[]{:S(2)}) collective-permute-start(bf16[2,128,1024]{2,1,0:T(8,128)(2,1)S(1)} %add_convert_fusion.8.n0), channel_id=1, source_target_pairs={{0,8},{4,12},{8,0},{12,4},{16,24},{20,28},{24,16},{28,20},{1,9},{5... | collective-permute-start | bytes 1572872 | tf_op jit(solution)/shard_map/ppermute | solution.py:33
  417.4 42.4 %collective-permute-start.69 = (bf16[2,128,1024]{2,1,0:T(8,128)(2,1)S(1)}, bf16[2,128,1024]{2,1,0:T(8,128)(2,1)S(1)}, u32[]{:S(2)}, u32[]{:S(2)}) collective-permute-start(bf16[2,128,1024]{2,1,0:T(8,128)(2,1)S(1)} %add_convert_fusion.8.n0), channel_id=1, source_target_pairs={{0,16},{4,20},{8,24},{12,28},{16,0},{20,4},{24,8},{28,12},{1,17},{... | collective-permute-start | bytes 1572872 | tf_op jit(solution)/shard_map/ppermute | solution.py:33
  419.6 40.2 %collective-permute-start.70 = (bf16[2,128,1024]{2,1,0:T(8,128)(2,1)S(1)}, bf16[2,128,1024]{2,1,0:T(8,128)(2,1)}, u32[]{:S(2)}, u32[]{:S(2)}) collective-permute-start(bf16[2,128,1024]{2,1,0:T(8,128)(2,1)S(1)} %add_convert_fusion.8.n0), channel_id=1, source_target_pairs={{0,24},{4,28},{8,16},{12,20},{16,8},{20,12},{24,0},{28,4},{1,25},{... | collective-permute-start | bytes 1572872 | tf_op jit(solution)/shard_map/ppermute | solution.py:33
  439.8 20.5 %collective-permute-start.60 = (bf16[2,3,32,1024]{3,2,1,0:T(8,128)(2,1)S(1)}, bf16[2,3,32,1024]{3,2,1,0:T(8,128)(2,1)S(1)}, u32[]{:S(2)}, u32[]{:S(2)}) collective-permute-start(bf16[2,3,32,1024]{3,2,1,0:T(8,128)(2,1)S(1)} %add_convert_fusion.12), channel_id=1, source_target_pairs={{1,0},{2,1},{3,2},{5,4},{6,5},{7,6},{9,8},{10,9},{11,10},{13,12},{... | collective-permute-start | bytes 1179656 | tf_op jit(solution)/shard_map/ppermute | solution.py:73
  447.9 29.3 %collective-permute-start.71 = (bf16[2,128,1024]{2,1,0:T(8,128)(2,1)S(1)}, bf16[2,128,1024]{2,1,0:T(8,128)(2,1)S(1)}, u32[]{:S(2)}, u32[]{:S(2)}) collective-permute-start(bf16[2,128,1024]{2,1,0:T(8,128)(2,1)S(1)} %add_convert_fusion.8.n0), channel_id=1, source_target_pairs={{0,4},{4,0},{8,12},{12,8},{16,20},{20,16},{24,28},{28,24},{1,5},{5... | collective-permute-start | bytes 1572872 | tf_op jit(solution)/shard_map/ppermute | solution.py:33
  459.8 18.7 %collective-permute-start.72 = (bf16[2,128,1024]{2,1,0:T(8,128)(2,1)S(1)}, bf16[2,128,1024]{2,1,0:T(8,128)(2,1)S(1)}, u32[]{:S(2)}, u32[]{:S(2)}) collective-permute-start(bf16[2,128,1024]{2,1,0:T(8,128)(2,1)S(1)} %collective-permute-done.68.n1), channel_id=1, source_target_pairs={{0,4},{4,0},{8,12},{12,8},{16,20},{20,16},{24,28},{28,24},{1,5},{5... | collective-permute-start | bytes 1572872 | tf_op jit(solution)/shard_map/ppermute | solution.py:33
  459.8 18.9 %collective-permute-start.73 = (bf16[2,128,1024]{2,1,0:T(8,128)(2,1)S(1)}, bf16[2,128,1024]{2,1,0:T(8,128)(2,1)}, u32[]{:S(2)}, u32[]{:S(2)}) collective-permute-start(bf16[2,128,1024]{2,1,0:T(8,128)(2,1)S(1)} %collective-permute-done.69.n2), channel_id=1, source_target_pairs={{0,4},{4,0},{8,12},{12,8},{16,20},{20,16},{24,28},{28,24},{1,5},{5... | collective-permute-start | bytes 1572872 | tf_op jit(solution)/shard_map/ppermute | solution.py:33
  460.3 19.7 %collective-permute-start.74 = (bf16[2,128,1024]{2,1,0:T(8,128)(2,1)}, bf16[2,128,1024]{2,1,0:T(8,128)(2,1)}, u32[]{:S(2)}, u32[]{:S(2)}) collective-permute-start(bf16[2,128,1024]{2,1,0:T(8,128)(2,1)} %collective-permute-done.70.n3), channel_id=1, source_target_pairs={{0,4},{4,0},{8,12},{12,8},{16,20},{20,16},{24,28},{28,24},{1,5},{5... | collective-permute-start | bytes 1572872 | tf_op jit(solution)/shard_map/ppermute | solution.py:33
  460.9 37.2 %all-to-all-start.1 = ((f32[32,24,128]{2,1,0:T(8,128)}), f32[32,24,128]{2,1,0:T(8,128)}, u32[]{:S(2)}, u32[]{:S(2)}) async-start(f32[32,24,128]{2,1,0:T(8,128)} %pad_maximum_fusion.7), calls=%async_computation.1 | async-start | bytes 786432 | tf_op jit(solution)/shard_map/all_to_all | solution.py:1287
  478.5 18.8 %collective-permute-start.63 = (bf16[6,32,1024]{2,1,0:T(8,128)(2,1)S(1)}, bf16[6,32,1024]{2,1,0:T(8,128)(2,1)}, u32[]{:S(2)}, u32[]{:S(2)}) collective-permute-start(bf16[6,32,1024]{2,1,0:T(8,128)(2,1)S(1)} %bitcast.179), channel_id=1, source_target_pairs={{0,24},{4,28},{8,16},{12,20},{16,8},{20,12},{24,0},{28,4},{1,25},{... | collective-permute-start | bytes 1179656 | tf_op jit(solution)/shard_map/ppermute | solution.py:33
  478.8 22.5 %collective-permute-start.64 = (bf16[6,32,1024]{2,1,0:T(8,128)(2,1)S(1)}, bf16[6,32,1024]{2,1,0:T(8,128)(2,1)}, u32[]{:S(2)}, u32[]{:S(2)}) collective-permute-start(bf16[6,32,1024]{2,1,0:T(8,128)(2,1)S(1)} %bitcast.180), channel_id=1, source_target_pairs={{0,4},{4,0},{8,12},{12,8},{16,20},{20,16},{24,28},{28,24},{1,5},{5... | collective-permute-start | bytes 1179656 | tf_op jit(solution)/shard_map/ppermute | solution.py:33
  (87 other events, 1204.2 us)
Sparse Core Ops, SparseCore 0:
  230.7 80.0 all-gather.2

commit v7 on v6

--- a/solution.py
+++ b/solution.py
@@ -1082,7 +1082,7 @@
         ],
     )
     part, part_other, state, mix, lse = attended
-    group = 128
+    group = 256
     steps = block_len // group
     row_spec = pl.BlockSpec((group, features), lambda i, place: (i, 0))
     seq_spec = pl.BlockSpec((1, group, features), lambda i, place: (place[1], i, 0))

time: 526 us -> 522 us (level)
  transfers between devices with their start and end apart: 78 -> 78, of which waited for: 20 -> 22; matrix products, arithmetic and copies ran while one was open for 14% -> 14% of each run, Pallas kernels for 28% -> 28%
where the time goes in v7:
time: 522 us; the launch traced here: 513 us
  Pallas kernels  185 us (35%)
  starting transfers between devices  154 us (30%)
  waiting for transfers between devices  74.5 us (14%)
  other arithmetic  51.3 us (10%)
  local copies, waits for them, and re-layouts  32.1 us (6%)
  between operations  15.8 us (3%)
    pallas_call x17, Pallas kernels, launch(): pl.pallas_call(kernel, grid_spec=pltpu.PrefetchScalarGridSpec(num_scalar_...  163 us
    ppermute x40, starting transfers between devices, flip(): return lax.ppermute(value, 'seq', [(i, i ^ mask) for i in range(count)])  57.4 us
    ppermute x11, starting transfers between devices, shifted(): lax.ppermute(value, 'seq', [(i, i + steps) for i in range(first, last)])  30.6 us
    ppermute x40, waiting for transfers between devices, flip(): return lax.ppermute(value, 'seq', [(i, i ^ mask) for i in range(count)])  29.8 us
    pallas_call x6, Pallas kernels, call(): pl.pallas_call(kernel, out_shape=[jax.ShapeDtypeStruct(shape, dtype) for...  22.1 us
    ppermute x6, waiting for transfers between devices, cycle(): lax.ppermute(value, 'tp', [(i, (i + steps) % count) for i in range(count)])  18.8 us
    convert_element_type x7, other arithmetic, add(): return (a.astype(F32) + b.astype(F32)).astype(BF16)  17.2 us
    ppermute x3, starting transfers between devices, line_steps(): lax.ppermute(rights[-1], 'tp', [(i, i - 1) for i in range(1, count - k +...  13.9 us
  transfers between devices with their start and end apart: 78, of which 22 were waited for; matrix products, arithmetic and copies ran while one was open for 14% of the time, Pallas kernels for 28%

profile of v7, /device:TPU:17, one launch (start us, length us, event | category | flops | bytes accessed | tf_op | source)
XLA Modules:
  0.0 513.0 jit_solution(7963407864482035164)
XLA Ops:
  9.2 3.2 shard_map.254
  13.7 3.2 collective-permute-start.1
  17.7 6.7 %all-to-all-start = ((f32[32,8,128]{2,1,0:T(8,128)}), f32[32,8,128]{2,1,0:T(8,128)}, u32[]{:S(2)}, u32[]{:S(2)}) async-start(f32[32,8,128]{2,1,0:T(8,128)} %broadcast_in_dim.11), calls=%async_computation | async-start | bytes 262144 | tf_op jit(solution)/shard_map/all_to_all | solution.py:1015
  26.2 3.3 collective-permute-start.3
  36.5 3.6 shard_map.256
  45.1 3.4 collective-permute-done.1
  48.5 3.6 collective-permute-done
  65.2 8.5 %shard_map.257 = (f32[16,8,128]{2,1,0:T(8,128)S(1)}, f32[16,8,128]{2,1,0:T(8,128)S(1)}) custom-call(f32[16,8,128]{2,1,0:T(8,128)S(1)} %get-tuple-element.109.decay_ref, f32[512,8,128]{2,1,0:T(8,128)S(1)} %convert_multiply_fusion.1.u_ref), custom_call_target="tpu_custom_call" | custom-call | flops 8800000000 | tf_op jit(solution)/shard_map/pallas_call | solution.py:164
  73.7 6.5 %collective-permute-done.6.f1 = bf16[3,6,32,1024]{3,2,1,0:T(8,128)(2,1)} collective-permute-done((bf16[3,6,32,1024]{3,2,1,0:T(8,128)(2,1)}, bf16[3,6,32,1024]{3,2,1,0:T(8,128)(2,1)}, u32[]{:S(2)}, u32[]{:S(2)}) %collective-permute-start.6) | collective-permute-done | bytes 1179680 | tf_op jit(solution)/shard_map/ppermute | solution.py:33
  83.3 7.4 %collective-permute-start.8 = (f32[16,8,128]{2,1,0:T(8,128)S(1)}, f32[16,8,128]{2,1,0:T(8,128)S(1)}, u32[]{:S(2)}, u32[]{:S(2)}) collective-permute-start(f32[16,8,128]{2,1,0:T(8,128)S(1)} %get-tuple-element.113), channel_id=1, source_target_pairs={{0,4},{4,8},{8,12},{12,16},{16,20},{20,24},{24,28},{1,5},{5,9},{9,... | collective-permute-start | bytes 196616 | tf_op jit(solution)/shard_map/ppermute | solution.py:39
  94.6 11.8 %collective-permute-done.14 = bf16[2,128,1024]{2,1,0:T(8,128)(2,1)} collective-permute-done((bf16[2,128,1024]{2,1,0:T(8,128)(2,1)}, bf16[2,128,1024]{2,1,0:T(8,128)(2,1)}, u32[]{:S(2)}, u32[]{:S(2)}) %collective-permute-start.14) | collective-permute-done | bytes 524320 | tf_op jit(solution)/shard_map/ppermute | solution.py:544
  106.4 5.2 %collective-permute-start.10 = (f32[16,8,128]{2,1,0:T(8,128)S(1)}, f32[16,8,128]{2,1,0:T(8,128)S(1)}, u32[]{:S(2)}, u32[]{:S(2)}) collective-permute-start(f32[16,8,128]{2,1,0:T(8,128)S(1)} %multiply_add_fusion.2), channel_id=1, source_target_pairs={{0,4},{4,8},{8,12},{12,16},{16,20},{20,24},{24,28},{1,5},{5,9},{9,... | collective-permute-start | bytes 196616 | tf_op jit(solution)/shard_map/ppermute | solution.py:39
  119.4 9.4 %shard_map.259 = (bf16[1024,512]{1,0:T(8,128)(2,1)S(1)}, bf16[1024,512]{1,0:T(8,128)(2,1)S(1)}, bf16[1024,512]{1,0:T(8,128)(2,1)}) custom-call(s32[3]{0:T(128)S(1)} %pad_add_fusion.place, bf16[512,1024]{1,0:T(8,128)(2,1)} %copy-done, bf16[512,1024]{1,0:T(8,128)(2,1)} %collective-permute-done.4.x1, bf16[4,6,32,1024]{3,2,1,0:T(8,128)(2,1)} %copy-done.23, ...), custom_call_target="tpu_custom_call" | custom-call | flops 8800000000 | tf_op jit(solution)/shard_map/pallas_call | solution.py:523
  130.7 21.0 %shard_map.260 = (f32[512,1024]{1,0:T(8,128)}, bf16[512,1024]{1,0:T(8,128)(2,1)S(1)}, bf16[256,1024]{1,0:T(8,128)(2,1)S(1)}, bf16[1024,512]{1,0:T(8,128)(2,1)}, f32[4,1024,1]{2,1,0:T(8,128)}) custom-call(s32[3]{0:T(128)S(1)} %pad_add_fusion.place, bf16[128,1024]{1,0:T(8,128)(2,1)S(1)} %bitcast.183, bf16[128,1024]{1,0:T(8,128)(2,1)S(1)} %collective-permute-done.16.c1, ...), custom_call_target="tpu_custom_call" | custom-call | flops 22000001024 | tf_op jit(solution)/shard_map/pallas_call | solution.py:523
  154.4 3.7 shard_map.261
  164.3 12.3 %shard_map.262 = (bf16[1024,1536]{1,0:T(8,128)(2,1)}, bf16[1024,1536]{1,0:T(8,128)(2,1)}) custom-call(s32[3]{0:T(128)S(1)} %pad_add_fusion.place, bf16[512,1024]{1,0:T(8,128)(2,1)S(1)} %get-tuple-element.133.m0.a0, bf16[512,1024]{1,0:T(8,128)(2,1)S(1)} %collective-permute-done.24.m1.a1, bf16[4,2,128,1024]{3,2,1,0:T(8,128)(2,1)} %copy-done.22, ...), custom_call_target="tpu_custom_call" | custom-call | flops 13200000000 | tf_op jit(solution)/shard_map/pallas_call | solution.py:523
  177.4 4.7 shard_map.263
  184.1 23.0 %shard_map.264 = (f32[512,1024]{1,0:T(8,128)}, bf16[512,1024]{1,0:T(8,128)(2,1)S(1)}, f32[512,1024]{1,0:T(8,128)}, bf16[512,1024]{1,0:T(8,128)(2,1)S(1)}, bf16[1024,2048]{1,0:T(8,128)(2,1)}) custom-call(s32[3]{0:T(128)S(1)} %pad_add_fusion.place, bf16[512,1024]{1,0:T(8,128)(2,1)} %fusion.6.g0.a0, bf16[512,1024]{1,0:T(8,128)(2,1)} %collective-permute-done.5.g1.a1, ...), custom_call_target="tpu_custom_call" | custom-call | flops 23100000256 | tf_op jit(solution)/shard_map/pallas_call | solution.py:523
  208.4 9.7 %shard_map.265 = (bf16[2,4,128,1024]{3,2,1,0:T(8,128)(2,1)}, bf16[2,4,128,1024]{3,2,1,0:T(8,128)(2,1)}) custom-call(s32[3]{0:T(128)S(1)} %pad_add_fusion.place, bf16[512,1024]{1,0:T(8,128)(2,1)} %fusion.6.g0.a0, bf16[512,1024]{1,0:T(8,128)(2,1)} %collective-permute-done.5.g1.a1, bf16[1024,1536]{1,0:T(8,128)(2,1)} %get-tuple-element.139.act_a.rest_0_, ...), custom_call_target="tpu_custom_call" | custom-call | flops 8800000000 | tf_op jit(solution)/shard_map/pallas_call | solution.py:523
  218.1 3.7 shard_map.266
  221.8 5.4 %shard_map.267 = (f32[512,1024]{1,0:T(8,128)}, bf16[512,1024]{1,0:T(8,128)(2,1)}, f32[1,1024]{1,0:T(1,128)S(1)}) custom-call(s32[3]{0:T(128)S(1)} %pad_add_fusion.place, f32[512,1024]{1,0:T(8,128)} %get-tuple-element.142.residual, f32[512,1024]{1,0:T(8,128)} %get-tuple-element.143.own, bf16[512,1024]{1,0:T(8,128)(2,1)} %collective-permute-done.26.got, ...), custom_call_target="tpu_custom_call" | custom-call | flops 5500000256 | tf_op jit(solution)/shard_map/pallas_call | solution.py:523
  227.7 9.1 %shard_map.268 = (bf16[2,4,128,1024]{3,2,1,0:T(8,128)(2,1)}, bf16[2,4,128,1024]{3,2,1,0:T(8,128)(2,1)}) custom-call(s32[3]{0:T(128)S(1)} %pad_add_fusion.place, bf16[512,1024]{1,0:T(8,128)(2,1)S(1)} %get-tuple-element.133.m0.a0, bf16[512,1024]{1,0:T(8,128)(2,1)S(1)} %copy-done.18, bf16[1024,2048]{1,0:T(8,128)(2,1)} %get-tuple-element.147.rest_0_), custom_call_target="tpu_custom_call" | custom-call | flops 8800000000 | tf_op jit(solution)/shard_map/pallas_call | solution.py:523
  239.7 26.9 %shard_map.269 = (f32[512,1024]{1,0:T(8,128)}, bf16[512,1024]{1,0:T(8,128)(2,1)S(1)}, f32[128,1024]{1,0:T(8,128)S(1)}, bf16[128,1024]{1,0:T(8,128)(2,1)S(1)}, bf...) custom-call(s32[3]{0:T(128)S(1)} %pad_add_fusion.place, bf16[512,1024]{1,0:T(8,128)(2,1)} %get-tuple-element.149.g0, ...), custom_call_target="tpu_custom_call" | custom-call | flops 29699999744 | tf_op jit(solution)/shard_map/pallas_call | solution.py:523
  267.3 10.5 %shard_map.271 = (bf16[2,4,3,32,1024]{4,3,2,1,0:T(8,128)(2,1)}, bf16[2,4,3,32,1024]{4,3,2,1,0:T(8,128)(2,1)}, bf16[2,4,3,32,1024]{4,3,2,1,0:T(8,128)(2,1)}, bf16[2,4,3,32,1024]{4,3,2,1,0:T(8,128)(2,1)}) custom-call(s32[3]{0:T(128)S(1)} %pad_add_fusion.place, bf16[512,1024]{1,0:T(8,128)(2,1)S(1)} %copy-done.1, bf16[512,1024]{1,0:T(8,128)(2,1)} %collective-permute-done.4.x1, ...), custom_call_target="tpu_custom_call" | custom-call | flops 11000000512 | tf_op jit(solution)/shard_map/pallas_call | solution.py:523
  280.2 4.6 collective-permute-done.30
  299.0 4.1 collective-permute-done.34
  306.2 4.5 shard_map.272
  311.4 4.5 shard_map.273
  317.8 3.4 collective-permute-start.38
  321.1 10.2 %collective-permute-done.43 = bf16[4,128,1024]{2,1,0:T(8,128)(2,1)} collective-permute-done((bf16[4,128,1024]{2,1,0:T(8,128)(2,1)}, bf16[4,128,1024]{2,1,0:T(8,128)(2,1)}, u32[]{:S(2)}, u32[]{:S(2)}) %collective-permute-start.43) | collective-permute-done | bytes 1048608 | tf_op jit(solution)/shard_map/ppermute | solution.py:33
  333.0 3.2 fusion.26
  336.3 5.3 %collective-permute-done.37 = bf16[512,1024]{1,0:T(8,128)(2,1)S(1)} collective-permute-done((bf16[512,1024]{1,0:T(8,128)(2,1)S(1)}, bf16[512,1024]{1,0:T(8,128)(2,1)S(1)}, u32[]{:S(2)}, u32[]{:S(2)}) %collective-permute-start.37) | collective-permute-done | bytes 1048608 | tf_op jit(solution)/shard_map/ppermute | solution.py:46
  346.6 4.7 collective-permute-start.41
  351.3 9.8 %collective-permute-start.39 = (bf16[512,1024]{1,0:T(8,128)(2,1)}, bf16[512,1024]{1,0:T(8,128)(2,1)}, u32[]{:S(2)}, u32[]{:S(2)}) collective-permute-start(bf16[512,1024]{1,0:T(8,128)(2,1)} %copy-done.47), channel_id=1, source_target_pairs={{1,0},{2,1},{5,4},{6,5},{9,8},{10,9},{13,12},{14,13},{17,16},{18,1... | collective-permute-start | bytes 3145736 | tf_op jit(solution)/shard_map/ppermute | solution.py:48
  374.4 3.3 add_convert_fusion.7
  380.0 5.5 %shard_map.274 = (f32[16,8,128]{2,1,0:T(8,128)S(1)}, f32[16,8,128]{2,1,0:T(8,128)S(1)}) custom-call(f32[16,8,128]{2,1,0:T(8,128)S(1)} %copy-done.28, f32[16,8,128]{2,1,0:T(8,128)S(1)} %copy-done.10, f32[128,8,128]{2,1,0:T(8,128)S(1)} %bitcast.173, f32[128,8,128]{2,1,0:T(8,128)S(1)} %bitcast.175), custom_call_target="tpu_custom_call" | custom-call | flops 5500000256 | tf_op jit(solution)/shard_map/pallas_call | solution.py:164
  392.5 4.1 collective-permute-start.54
  409.8 4.0 collective-permute-start.68
  416.0 5.7 %collective-permute-start.70 = (bf16[2,128,1024]{2,1,0:T(8,128)(2,1)S(1)}, bf16[2,128,1024]{2,1,0:T(8,128)(2,1)}, u32[]{:S(2)}, u32[]{:S(2)}) collective-permute-start(bf16[2,128,1024]{2,1,0:T(8,128)(2,1)S(1)} %add_convert_fusion.8.n0), channel_id=1, source_target_pairs={{0,24},{4,28},{8,16},{12,20},{16,8},{20,12},{24,0},{28,4},{1,25},{... | collective-permute-start | bytes 1572872 | tf_op jit(solution)/shard_map/ppermute | solution.py:33
  422.0 5.2 %collective-permute-done.42 = bf16[512,1024]{1,0:T(8,128)(2,1)S(1)} collective-permute-done((bf16[512,1024]{1,0:T(8,128)(2,1)}, bf16[512,1024]{1,0:T(8,128)(2,1)S(1)}, u32[]{:S(2)}, u32[]{:S(2)}) %collective-permute-start.42) | collective-permute-done | bytes 1048608 | tf_op jit(solution)/shard_map/ppermute | solution.py:46
  430.9 5.2 %collective-permute-done.59 = bf16[2,3,32,1024]{3,2,1,0:T(8,128)(2,1)S(1)} collective-permute-done((bf16[2,3,32,1024]{3,2,1,0:T(8,128)(2,1)S(1)}, bf16[2,3,32,1024]{3,2,1,0:T(8,128)(2,1)S(1)}, u32[]{:S(2)}, u32[]{:S(2)}) %collective-permute-start.59) | collective-permute-done | bytes 393248 | tf_op jit(solution)/shard_map/ppermute | solution.py:73
  438.5 3.2 collective-permute-start.57
  444.3 11.8 %collective-permute-start.71 = (bf16[2,128,1024]{2,1,0:T(8,128)(2,1)S(1)}, bf16[2,128,1024]{2,1,0:T(8,128)(2,1)S(1)}, u32[]{:S(2)}, u32[]{:S(2)}) collective-permute-start(bf16[2,128,1024]{2,1,0:T(8,128)(2,1)S(1)} %add_convert_fusion.8.n0), channel_id=1, source_target_pairs={{0,4},{4,0},{8,12},{12,8},{16,20},{20,16},{24,28},{28,24},{1,5},{5... | collective-permute-start | bytes 1572872 | tf_op jit(solution)/shard_map/ppermute | solution.py:33
  457.3 9.9 %all-to-all-start.1 = ((f32[32,24,128]{2,1,0:T(8,128)}), f32[32,24,128]{2,1,0:T(8,128)}, u32[]{:S(2)}, u32[]{:S(2)}) async-start(f32[32,24,128]{2,1,0:T(8,128)} %pad_maximum_fusion.7), calls=%async_computation.1 | async-start | bytes 786432 | tf_op jit(solution)/shard_map/all_to_all | solution.py:1287
  467.2 5.3 %maximum_convert_fusion = f32[4,512,1024]{2,1,0:T(8,128)} fusion(bf16[1,512,1024]{2,1,0:T(8,128)(2,1)} %get-tuple-element.247, bf16[1,512,1024]{2,1,0:T(8,128)(2,1)} %get-tuple-element.248, bf16[1,512,1024]{2,1,0:T(8,128)(2,1)} %get-tuple-element.249, bf16[1,512,1024]{2,1,0:T(8,128)(2,1)} %get-tuple-element.246), kind=kLoop, calls=%fused_computation.1 | loop fusion | flops 8388608 | bytes 12582912 | tf_op jit(solution)/shard_map/convert_element_type | solution.py:1233
  476.4 6.0 %shard_map.276 = (f32[1024,1024]{1,0:T(8,128)}, f32[1024,1024]{1,0:T(8,128)}) custom-call(s32[3]{0:T(128)S(1)} %pad_add_fusion.place, bf16[2,128,1024]{2,1,0:T(8,128)(2,1)S(1)} %add_convert_fusion.8.n0, bf16[2,128,1024]{2,1,0:T(8,128)(2,1)S(1)} %collective-permute-done.68.n1, bf16[2,128,1024]{2,1,0:T(8,128)(2,1)S(1)} %collective-permute-done.69.n2, ...), custom_call_target="tpu_custom_call" | custom-call | flops 5500000256 | tf_op jit(solution)/shard_map/pallas_call | solution.py:523
  485.5 7.7 %collective-permute-start.66 = (bf16[6,32,1024]{2,1,0:T(8,128)(2,1)}, bf16[6,32,1024]{2,1,0:T(8,128)(2,1)S(1)}, u32[]{:S(2)}, u32[]{:S(2)}) collective-permute-start(bf16[6,32,1024]{2,1,0:T(8,128)(2,1)} %collective-permute-done.62.n2), channel_id=1, source_target_pairs={{0,4},{4,0},{8,12},{12,8},{16,20},{20,16},{24,28},{28,24},{1,5},{5... | collective-permute-start | bytes 1179656 | tf_op jit(solution)/shard_map/ppermute | solution.py:33
  497.7 6.3 %shard_map.275 = (f32[1024,256]{1,0:T(8,128)}, f32[1024,256]{1,0:T(8,128)}, f32[1024,256]{1,0:T(8,128)}, f32[256,1024]{1,0:T(8,128)}, f32[1024,256]{1,0:T(8,128)}, /*index=5*/f32[1024,256]{1,0:T(8,128)}) custom-call(s32[3]{0:T(128)S(1)} %pad_add_fusion.place, bf16[6,32,1024]{2,1,0:T(8,128)(2,1)S(1)} %bitcast.181, ...), custom_call_target="tpu_custom_call" | custom-call | flops 5500000256 | tf_op jit(solution)/shard_map/pallas_call | solution.py:523
  (346 shorter events, 154.3 us)
Async XLA Ops:
  13.5 31.6 %collective-permute-start.2 = (bf16[6,32,1024]{2,1,0:T(8,128)(2,1)}, bf16[6,32,1024]{2,1,0:T(8,128)(2,1)}, u32[]{:S(2)}, u32[]{:S(2)}) collective-permute-start(bf16[6,32,1024]{2,1,0:T(8,128)(2,1)} %get-tuple-element.107), channel_id=1, source_target_pairs={{0,3},{1,0},{2,1},{3,2},{4,7},{5,4},{6,5},{7,6},{8,11},{9,8},{10,9... | collective-permute-start | bytes 1179656 | tf_op jit(solution)/shard_map/ppermute | solution.py:544
  13.7 34.8 %collective-permute-start.1 = (bf16[6,32,1024]{2,1,0:T(8,128)(2,1)}, bf16[6,32,1024]{2,1,0:T(8,128)(2,1)}, u32[]{:S(2)}, u32[]{:S(2)}) collective-permute-start(bf16[6,32,1024]{2,1,0:T(8,128)(2,1)} %get-tuple-element.107), channel_id=1, source_target_pairs={{0,2},{1,3},{2,0},{3,1},{4,6},{5,7},{6,4},{7,5},{8,10},{9,11},{10,... | collective-permute-start | bytes 1179656 | tf_op jit(solution)/shard_map/ppermute | solution.py:544
  16.9 35.1 %collective-permute-start = (bf16[6,32,1024]{2,1,0:T(8,128)(2,1)}, bf16[6,32,1024]{2,1,0:T(8,128)(2,1)}, u32[]{:S(2)}, u32[]{:S(2)}) collective-permute-start(bf16[6,32,1024]{2,1,0:T(8,128)(2,1)} %get-tuple-element.107), channel_id=1, source_target_pairs={{0,1},{1,2},{2,3},{3,0},{4,5},{5,6},{6,7},{7,4},{8,9},{9,10},{10,1... | collective-permute-start | bytes 1179656 | tf_op jit(solution)/shard_map/ppermute | solution.py:544
  17.7 40.0 %all-to-all-start = ((f32[32,8,128]{2,1,0:T(8,128)}), f32[32,8,128]{2,1,0:T(8,128)}, u32[]{:S(2)}, u32[]{:S(2)}) async-start(f32[32,8,128]{2,1,0:T(8,128)} %broadcast_in_dim.11), calls=%async_computation | async-start | bytes 262144 | tf_op jit(solution)/shard_map/all_to_all | solution.py:1015
  24.5 286.6 %all-gather.3.cloned.1.call-start = ((), (), s32[]{:S(2)}) async-start(), calls=%async_computation.2 | async-start | bytes 5242880 | tf_op jit(solution)/shard_map/all_gather | solution.py:1155
  34.3 29.3 %collective-permute-start.4 = (bf16[512,1024]{1,0:T(8,128)(2,1)S(1)}, bf16[512,1024]{1,0:T(8,128)(2,1)}, u32[]{:S(2)}, u32[]{:S(2)}) collective-permute-start(bf16[512,1024]{1,0:T(8,128)(2,1)S(1)} %fusion.5.x0), channel_id=1, source_target_pairs={{0,4},{4,0},{8,12},{12,8},{16,20},{20,16},{24,28},{28,24},{1,5},{5... | collective-permute-start | bytes 3145736 | tf_op jit(solution)/shard_map/ppermute | solution.py:33
  43.3 21.3 %collective-permute-start.5 = (bf16[512,1024]{1,0:T(8,128)(2,1)}, bf16[512,1024]{1,0:T(8,128)(2,1)}, u32[]{:S(2)}, u32[]{:S(2)}) collective-permute-start(bf16[512,1024]{1,0:T(8,128)(2,1)} %fusion.6.g0.a0), channel_id=1, source_target_pairs={{0,4},{4,0},{8,12},{12,8},{16,20},{20,16},{24,28},{28,24},{1,5},{5... | collective-permute-start | bytes 3145736 | tf_op jit(solution)/shard_map/ppermute | solution.py:33
  54.4 25.8 %collective-permute-start.6 = (bf16[3,6,32,1024]{3,2,1,0:T(8,128)(2,1)}, bf16[3,6,32,1024]{3,2,1,0:T(8,128)(2,1)}, u32[]{:S(2)}, u32[]{:S(2)}) collective-permute-start(bf16[3,6,32,1024]{3,2,1,0:T(8,128)(2,1)} %pad_maximum_fusion.2.f0), channel_id=1, source_target_pairs={{0,8},{4,12},{8,0},{12,4},{16,24},{20,28},{24,16},{28,20},{1,9},{5... | collective-permute-start | bytes 3538952 | tf_op jit(solution)/shard_map/ppermute | solution.py:33
  55.6 25.5 %collective-permute-start.7 = (bf16[3,6,32,1024]{3,2,1,0:T(8,128)(2,1)}, bf16[3,6,32,1024]{3,2,1,0:T(8,128)(2,1)}, u32[]{:S(2)}, u32[]{:S(2)}) collective-permute-start(bf16[3,6,32,1024]{3,2,1,0:T(8,128)(2,1)} %pad_maximum_fusion.2.f0), channel_id=1, source_target_pairs={{0,16},{4,20},{8,24},{12,28},{16,0},{20,4},{24,8},{28,12},{1,17},{... | collective-permute-start | bytes 3538952 | tf_op jit(solution)/shard_map/ppermute | solution.py:33
  63.4 30.5 %collective-permute-start.15 = (bf16[2,128,1024]{2,1,0:T(8,128)(2,1)}, bf16[2,128,1024]{2,1,0:T(8,128)(2,1)}, u32[]{:S(2)}, u32[]{:S(2)}) collective-permute-start(bf16[2,128,1024]{2,1,0:T(8,128)(2,1)} %get-tuple-element.119), channel_id=1, source_target_pairs={{0,3},{1,0},{2,1},{3,2},{4,7},{5,4},{6,5},{7,6},{8,11},{9,8},{10,9... | collective-permute-start | bytes 1572872 | tf_op jit(solution)/shard_map/ppermute | solution.py:544
  63.6 42.9 %collective-permute-start.14 = (bf16[2,128,1024]{2,1,0:T(8,128)(2,1)}, bf16[2,128,1024]{2,1,0:T(8,128)(2,1)}, u32[]{:S(2)}, u32[]{:S(2)}) collective-permute-start(bf16[2,128,1024]{2,1,0:T(8,128)(2,1)} %get-tuple-element.119), channel_id=1, source_target_pairs={{0,2},{1,3},{2,0},{3,1},{4,6},{5,7},{6,4},{7,5},{8,10},{9,11},{10,... | collective-permute-start | bytes 1572872 | tf_op jit(solution)/shard_map/ppermute | solution.py:544
  64.6 47.1 %collective-permute-start.13 = (bf16[2,128,1024]{2,1,0:T(8,128)(2,1)}, bf16[2,128,1024]{2,1,0:T(8,128)(2,1)}, u32[]{:S(2)}, u32[]{:S(2)}) collective-permute-start(bf16[2,128,1024]{2,1,0:T(8,128)(2,1)} %get-tuple-element.119), channel_id=1, source_target_pairs={{0,1},{1,2},{2,3},{3,0},{4,5},{5,6},{6,7},{7,4},{8,9},{9,10},{10,1... | collective-permute-start | bytes 1572872 | tf_op jit(solution)/shard_map/ppermute | solution.py:544
  93.6 25.8 %collective-permute-start.17 = (bf16[3,3,32,1024]{3,2,1,0:T(8,128)(2,1)S(1)}, bf16[3,3,32,1024]{3,2,1,0:T(8,128)(2,1)S(1)}, u32[]{:S(2)}, u32[]{:S(2)}) collective-permute-start(bf16[3,3,32,1024]{3,2,1,0:T(8,128)(2,1)S(1)} %slice.294), channel_id=1, source_target_pairs={{0,8},{4,12},{8,0},{12,4},{16,24},{20,28},{24,16},{28,20},{1,9},{5... | collective-permute-start | bytes 1769480 | tf_op jit(solution)/shard_map/ppermute | solution.py:33
  93.9 25.5 %collective-permute-start.18 = (bf16[3,3,32,1024]{3,2,1,0:T(8,128)(2,1)S(1)}, bf16[3,3,32,1024]{3,2,1,0:T(8,128)(2,1)S(1)}, u32[]{:S(2)}, u32[]{:S(2)}) collective-permute-start(bf16[3,3,32,1024]{3,2,1,0:T(8,128)(2,1)S(1)} %slice.295), channel_id=1, source_target_pairs={{0,16},{4,20},{8,24},{12,28},{16,0},{20,4},{24,8},{28,12},{1,17},{... | collective-permute-start | bytes 1769480 | tf_op jit(solution)/shard_map/ppermute | solution.py:33
  93.9 21.6 %collective-permute-start.12 = (f32[16,8,128]{2,1,0:T(8,128)S(1)}, f32[16,8,128]{2,1,0:T(8,128)S(1)}, u32[]{:S(2)}, u32[]{:S(2)}) collective-permute-start(f32[16,8,128]{2,1,0:T(8,128)S(1)} %multiply_add_fusion.2), channel_id=1, source_target_pairs={{0,28},{1,29},{2,30},{3,31}} | collective-permute-start | bytes 196616 | tf_op jit(solution)/shard_map/ppermute | solution.py:39
  115.5 36.2 %collective-permute-start.20 = (bf16[3,2,128,1024]{3,2,0,1:T(8,128)(2,1)S(1)}, bf16[3,2,128,1024]{3,2,0,1:T(8,128)(2,1)S(1)}, u32[]{:S(2)}, u32[]{:S(2)}) collective-permute-start(bf16[3,2,128,1024]{3,2,0,1:T(8,128)(2,1)S(1)} %pad_maximum_fusion.1), channel_id=1, source_target_pairs={{0,8},{4,12},{8,0},{12,4},{16,24},{20,28},{24,16},{28,20},{1,9},{5... | collective-permute-start | bytes 4718600 | tf_op jit(solution)/shard_map/ppermute | solution.py:33
  115.9 35.9 %collective-permute-start.21 = (bf16[3,2,128,1024]{3,2,0,1:T(8,128)(2,1)S(1)}, bf16[3,2,128,1024]{3,2,0,1:T(8,128)(2,1)S(1)}, u32[]{:S(2)}, u32[]{:S(2)}) collective-permute-start(bf16[3,2,128,1024]{3,2,0,1:T(8,128)(2,1)S(1)} %pad_maximum_fusion.1), channel_id=1, source_target_pairs={{0,16},{4,20},{8,24},{12,28},{16,0},{20,4},{24,8},{28,12},{1,17},{... | collective-permute-start | bytes 4718600 | tf_op jit(solution)/shard_map/ppermute | solution.py:33
  158.5 18.8 %collective-permute-start.22 = (bf16[3,1,128,1024]{3,2,0,1:T(8,128)(2,1)S(1)}, bf16[3,1,128,1024]{3,2,0,1:T(8,128)(2,1)S(1)}, u32[]{:S(2)}, u32[]{:S(2)}) collective-permute-start(bf16[3,1,128,1024]{3,2,0,1:T(8,128)(2,1)S(1)} %slice.296), channel_id=1, source_target_pairs={{0,8},{4,12},{8,0},{12,4},{16,24},{20,28},{24,16},{28,20},{1,9},{5... | collective-permute-start | bytes 2359304 | tf_op jit(solution)/shard_map/ppermute | solution.py:33
  159.8 24.3 %collective-permute-start.23 = (bf16[3,1,128,1024]{3,2,0,1:T(8,128)(2,1)S(1)}, bf16[3,1,128,1024]{3,2,0,1:T(8,128)(2,1)S(1)}, u32[]{:S(2)}, u32[]{:S(2)}) collective-permute-start(bf16[3,1,128,1024]{3,2,0,1:T(8,128)(2,1)S(1)} %slice.297), channel_id=1, source_target_pairs={{0,16},{4,20},{8,24},{12,28},{16,0},{20,4},{24,8},{28,12},{1,17},{... | collective-permute-start | bytes 2359304 | tf_op jit(solution)/shard_map/ppermute | solution.py:33
  236.8 48.0 %collective-permute-start.30 = (bf16[2,4,128,1024]{3,2,1,0:T(8,128)(2,1)}, bf16[2,4,128,1024]{3,2,1,0:T(8,128)(2,1)S(1)}, u32[]{:S(2)}, u32[]{:S(2)}) collective-permute-start(bf16[2,4,128,1024]{3,2,1,0:T(8,128)(2,1)} %get-tuple-element.158), channel_id=1, source_target_pairs={{0,16},{4,20},{8,24},{12,28},{16,0},{20,4},{24,8},{28,12},{1,17},{... | collective-permute-start | bytes 6291464 | tf_op jit(solution)/shard_map/ppermute | solution.py:33
  238.5 47.2 %collective-permute-start.31 = (bf16[2,4,128,1024]{3,2,1,0:T(8,128)(2,1)}, bf16[2,4,128,1024]{3,2,1,0:T(8,128)(2,1)S(1)}, u32[]{:S(2)}, u32[]{:S(2)}) collective-permute-start(bf16[2,4,128,1024]{3,2,1,0:T(8,128)(2,1)} %get-tuple-element.160), channel_id=1, source_target_pairs={{0,8},{4,12},{8,0},{12,4},{16,24},{20,28},{24,16},{28,20},{1,9},{5... | collective-permute-start | bytes 6291464 | tf_op jit(solution)/shard_map/ppermute | solution.py:33
  266.6 44.6 %collective-permute-start.28 = (bf16[512,1024]{1,0:T(8,128)(2,1)S(1)}, bf16[512,1024]{1,0:T(8,128)(2,1)}, u32[]{:S(2)}, u32[]{:S(2)}) collective-permute-start(bf16[512,1024]{1,0:T(8,128)(2,1)S(1)} %get-tuple-element.153), channel_id=1, source_target_pairs={{0,4},{4,0},{8,12},{12,8},{16,20},{20,16},{24,28},{28,24},{1,5},{5... | collective-permute-start | bytes 3145736 | tf_op jit(solution)/shard_map/ppermute | solution.py:33
  277.9 21.0 %collective-permute-start.36 = (bf16[128,1024]{1,0:T(8,128)(2,1)S(1)}, bf16[128,1024]{1,0:T(8,128)(2,1)S(1)}, u32[]{:S(2)}, u32[]{:S(2)}) collective-permute-start(bf16[128,1024]{1,0:T(8,128)(2,1)S(1)} %add_convert_fusion.14), channel_id=1, source_target_pairs={{4,0},{8,4},{12,8},{16,12},{20,16},{24,20},{28,24},{5,1},{9,5},{13... | collective-permute-start | bytes 786440 | tf_op jit(solution)/shard_map/ppermute | solution.py:39
  306.0 25.3 %collective-permute-start.43 = (bf16[4,128,1024]{2,1,0:T(8,128)(2,1)}, bf16[4,128,1024]{2,1,0:T(8,128)(2,1)}, u32[]{:S(2)}, u32[]{:S(2)}) collective-permute-start(bf16[4,128,1024]{2,1,0:T(8,128)(2,1)} %get-tuple-element.179), channel_id=1, source_target_pairs={{0,16},{4,20},{8,24},{12,28},{16,0},{20,4},{24,8},{28,12},{1,17},{... | collective-permute-start | bytes 3145736 | tf_op jit(solution)/shard_map/ppermute | solution.py:33
  306.1 25.2 %collective-permute-start.44 = (bf16[4,128,1024]{2,1,0:T(8,128)(2,1)}, bf16[4,128,1024]{2,1,0:T(8,128)(2,1)}, u32[]{:S(2)}, u32[]{:S(2)}) collective-permute-start(bf16[4,128,1024]{2,1,0:T(8,128)(2,1)} %get-tuple-element.181), channel_id=1, source_target_pairs={{0,8},{4,12},{8,0},{12,4},{16,24},{20,28},{24,16},{28,20},{1,9},{5... | collective-permute-start | bytes 3145736 | tf_op jit(solution)/shard_map/ppermute | solution.py:33
  315.8 25.8 %collective-permute-start.37 = (bf16[512,1024]{1,0:T(8,128)(2,1)S(1)}, bf16[512,1024]{1,0:T(8,128)(2,1)S(1)}, u32[]{:S(2)}, u32[]{:S(2)}) collective-permute-start(bf16[512,1024]{1,0:T(8,128)(2,1)S(1)} %get-tuple-element.170), channel_id=1, source_target_pairs={{0,1},{1,2},{2,3},{4,5},{5,6},{6,7},{8,9},{9,10},{10,11},{12,13},{... | collective-permute-start | bytes 3145736 | tf_op jit(solution)/shard_map/ppermute | solution.py:46
  317.8 25.8 %collective-permute-start.38 = (bf16[512,1024]{1,0:T(8,128)(2,1)S(1)}, bf16[512,1024]{1,0:T(8,128)(2,1)S(1)}, u32[]{:S(2)}, u32[]{:S(2)}) collective-permute-start(bf16[512,1024]{1,0:T(8,128)(2,1)S(1)} %get-tuple-element.170), channel_id=1, source_target_pairs={{1,0},{2,1},{3,2},{5,4},{6,5},{7,6},{9,8},{10,9},{11,10},{13,12},{... | collective-permute-start | bytes 3145736 | tf_op jit(solution)/shard_map/ppermute | solution.py:48
  331.4 35.9 %collective-permute-start.47 = (bf16[2,4,3,32,1024]{4,3,2,1,0:T(8,128)(2,1)}, bf16[2,4,3,32,1024]{4,3,2,1,0:T(8,128)(2,1)}, u32[]{:S(2)}, u32[]{:S(2)}) collective-permute-start(bf16[2,4,3,32,1024]{4,3,2,1,0:T(8,128)(2,1)} %get-tuple-element.186), channel_id=1, source_target_pairs={{0,16},{4,20},{8,24},{12,28},{16,0},{20,4},{24,8},{28,12},{1,17},{... | collective-permute-start | bytes 4718600 | tf_op jit(solution)/shard_map/ppermute | solution.py:33
  333.0 38.7 %collective-permute-start.45 = (bf16[2,4,3,32,1024]{4,3,2,1,0:T(8,128)(2,1)}, bf16[2,4,3,32,1024]{4,3,2,1,0:T(8,128)(2,1)}, u32[]{:S(2)}, u32[]{:S(2)}) collective-permute-start(bf16[2,4,3,32,1024]{4,3,2,1,0:T(8,128)(2,1)} %get-tuple-element.183), channel_id=1, source_target_pairs={{0,8},{4,12},{8,0},{12,4},{16,24},{20,28},{24,16},{28,20},{1,9},{5... | collective-permute-start | bytes 4718600 | tf_op jit(solution)/shard_map/ppermute | solution.py:33
  346.6 31.1 %collective-permute-start.41 = (bf16[512,1024]{1,0:T(8,128)(2,1)}, bf16[512,1024]{1,0:T(8,128)(2,1)}, u32[]{:S(2)}, u32[]{:S(2)}) collective-permute-start(bf16[512,1024]{1,0:T(8,128)(2,1)} %copy-done.45), channel_id=1, source_target_pairs={{1,2},{2,3},{5,6},{6,7},{9,10},{10,11},{13,14},{14,15},{17,18},{18... | collective-permute-start | bytes 3145736 | tf_op jit(solution)/shard_map/ppermute | solution.py:46
  351.3 28.7 %collective-permute-start.39 = (bf16[512,1024]{1,0:T(8,128)(2,1)}, bf16[512,1024]{1,0:T(8,128)(2,1)}, u32[]{:S(2)}, u32[]{:S(2)}) collective-permute-start(bf16[512,1024]{1,0:T(8,128)(2,1)} %copy-done.47), channel_id=1, source_target_pairs={{1,0},{2,1},{5,4},{6,5},{9,8},{10,9},{13,12},{14,13},{17,16},{18,1... | collective-permute-start | bytes 3145736 | tf_op jit(solution)/shard_map/ppermute | solution.py:48
  364.9 26.4 %collective-permute-start.53 = (bf16[2,128,1024]{2,1,0:T(8,128)(2,1)}, bf16[2,128,1024]{2,1,0:T(8,128)(2,1)}, u32[]{:S(2)}, u32[]{:S(2)}) collective-permute-start(bf16[2,128,1024]{2,1,0:T(8,128)(2,1)} %get-tuple-element.273), channel_id=1, source_target_pairs={{2,1},{3,2},{6,5},{7,6},{10,9},{11,10},{14,13},{15,14},{18,17},{19... | collective-permute-start | bytes 1572872 | tf_op jit(solution)/shard_map/ppermute | solution.py:73
  367.3 29.3 %collective-permute-start.50 = (bf16[2,128,1024]{2,1,0:T(8,128)(2,1)}, bf16[2,128,1024]{2,1,0:T(8,128)(2,1)}, u32[]{:S(2)}, u32[]{:S(2)}) collective-permute-start(bf16[2,128,1024]{2,1,0:T(8,128)(2,1)} %get-tuple-element.272), channel_id=1, source_target_pairs={{0,1},{1,2},{4,5},{5,6},{8,9},{9,10},{12,13},{13,14},{16,17},{17,1... | collective-permute-start | bytes 1572872 | tf_op jit(solution)/shard_map/ppermute | solution.py:72
  371.8 30.9 %collective-permute-start.48 = (bf16[4,3,32,1024]{3,2,1,0:T(8,128)(2,1)}, bf16[4,3,32,1024]{3,2,1,0:T(8,128)(2,1)}, u32[]{:S(2)}, u32[]{:S(2)}) collective-permute-start(bf16[4,3,32,1024]{3,2,1,0:T(8,128)(2,1)} %get-tuple-element.253), channel_id=1, source_target_pairs={{0,8},{4,12},{8,0},{12,4},{16,24},{20,28},{24,16},{28,20},{1,9},{5... | collective-permute-start | bytes 2359304 | tf_op jit(solution)/shard_map/ppermute | solution.py:33
  377.6 27.2 %collective-permute-start.46 = (bf16[4,3,32,1024]{3,2,1,0:T(8,128)(2,1)}, bf16[4,3,32,1024]{3,2,1,0:T(8,128)(2,1)}, u32[]{:S(2)}, u32[]{:S(2)}) collective-permute-start(bf16[4,3,32,1024]{3,2,1,0:T(8,128)(2,1)} %get-tuple-element.251), channel_id=1, source_target_pairs={{0,16},{4,20},{8,24},{12,28},{16,0},{20,4},{24,8},{28,12},{1,17},{... | collective-permute-start | bytes 2359304 | tf_op jit(solution)/shard_map/ppermute | solution.py:33
  399.9 27.2 %collective-permute-start.42 = (bf16[512,1024]{1,0:T(8,128)(2,1)}, bf16[512,1024]{1,0:T(8,128)(2,1)S(1)}, u32[]{:S(2)}, u32[]{:S(2)}) collective-permute-start(bf16[512,1024]{1,0:T(8,128)(2,1)} %collective-permute-done.41), channel_id=1, source_target_pairs={{2,3},{6,7},{10,11},{14,15},{18,19},{22,23},{26,27},{30,31}} | collective-permute-start | bytes 3145736 | tf_op jit(solution)/shard_map/ppermute | solution.py:46
  402.6 26.8 %collective-permute-start.40 = (bf16[512,1024]{1,0:T(8,128)(2,1)}, bf16[512,1024]{1,0:T(8,128)(2,1)S(1)}, u32[]{:S(2)}, u32[]{:S(2)}) collective-permute-start(bf16[512,1024]{1,0:T(8,128)(2,1)} %collective-permute-done.39), channel_id=1, source_target_pairs={{1,0},{5,4},{9,8},{13,12},{17,16},{21,20},{25,24},{29,28}} | collective-permute-start | bytes 3145736 | tf_op jit(solution)/shard_map/ppermute | solution.py:48
  409.8 34.5 %collective-permute-start.68 = (bf16[2,128,1024]{2,1,0:T(8,128)(2,1)S(1)}, bf16[2,128,1024]{2,1,0:T(8,128)(2,1)S(1)}, u32[]{:S(2)}, u32[]{:S(2)}) collective-permute-start(bf16[2,128,1024]{2,1,0:T(8,128)(2,1)S(1)} %add_convert_fusion.8.n0), channel_id=1, source_target_pairs={{0,8},{4,12},{8,0},{12,4},{16,24},{20,28},{24,16},{28,20},{1,9},{5... | collective-permute-start | bytes 1572872 | tf_op jit(solution)/shard_map/ppermute | solution.py:33
  413.8 42.4 %collective-permute-start.69 = (bf16[2,128,1024]{2,1,0:T(8,128)(2,1)S(1)}, bf16[2,128,1024]{2,1,0:T(8,128)(2,1)S(1)}, u32[]{:S(2)}, u32[]{:S(2)}) collective-permute-start(bf16[2,128,1024]{2,1,0:T(8,128)(2,1)S(1)} %add_convert_fusion.8.n0), channel_id=1, source_target_pairs={{0,16},{4,20},{8,24},{12,28},{16,0},{20,4},{24,8},{28,12},{1,17},{... | collective-permute-start | bytes 1572872 | tf_op jit(solution)/shard_map/ppermute | solution.py:33
  416.0 40.2 %collective-permute-start.70 = (bf16[2,128,1024]{2,1,0:T(8,128)(2,1)S(1)}, bf16[2,128,1024]{2,1,0:T(8,128)(2,1)}, u32[]{:S(2)}, u32[]{:S(2)}) collective-permute-start(bf16[2,128,1024]{2,1,0:T(8,128)(2,1)S(1)} %add_convert_fusion.8.n0), channel_id=1, source_target_pairs={{0,24},{4,28},{8,16},{12,20},{16,8},{20,12},{24,0},{28,4},{1,25},{... | collective-permute-start | bytes 1572872 | tf_op jit(solution)/shard_map/ppermute | solution.py:33
  436.2 20.5 %collective-permute-start.60 = (bf16[2,3,32,1024]{3,2,1,0:T(8,128)(2,1)S(1)}, bf16[2,3,32,1024]{3,2,1,0:T(8,128)(2,1)S(1)}, u32[]{:S(2)}, u32[]{:S(2)}) collective-permute-start(bf16[2,3,32,1024]{3,2,1,0:T(8,128)(2,1)S(1)} %add_convert_fusion.12), channel_id=1, source_target_pairs={{1,0},{2,1},{3,2},{5,4},{6,5},{7,6},{9,8},{10,9},{11,10},{13,12},{... | collective-permute-start | bytes 1179656 | tf_op jit(solution)/shard_map/ppermute | solution.py:73
  444.3 29.3 %collective-permute-start.71 = (bf16[2,128,1024]{2,1,0:T(8,128)(2,1)S(1)}, bf16[2,128,1024]{2,1,0:T(8,128)(2,1)S(1)}, u32[]{:S(2)}, u32[]{:S(2)}) collective-permute-start(bf16[2,128,1024]{2,1,0:T(8,128)(2,1)S(1)} %add_convert_fusion.8.n0), channel_id=1, source_target_pairs={{0,4},{4,0},{8,12},{12,8},{16,20},{20,16},{24,28},{28,24},{1,5},{5... | collective-permute-start | bytes 1572872 | tf_op jit(solution)/shard_map/ppermute | solution.py:33
  456.2 18.7 %collective-permute-start.72 = (bf16[2,128,1024]{2,1,0:T(8,128)(2,1)S(1)}, bf16[2,128,1024]{2,1,0:T(8,128)(2,1)S(1)}, u32[]{:S(2)}, u32[]{:S(2)}) collective-permute-start(bf16[2,128,1024]{2,1,0:T(8,128)(2,1)S(1)} %collective-permute-done.68.n1), channel_id=1, source_target_pairs={{0,4},{4,0},{8,12},{12,8},{16,20},{20,16},{24,28},{28,24},{1,5},{5... | collective-permute-start | bytes 1572872 | tf_op jit(solution)/shard_map/ppermute | solution.py:33
  456.2 18.9 %collective-permute-start.73 = (bf16[2,128,1024]{2,1,0:T(8,128)(2,1)S(1)}, bf16[2,128,1024]{2,1,0:T(8,128)(2,1)}, u32[]{:S(2)}, u32[]{:S(2)}) collective-permute-start(bf16[2,128,1024]{2,1,0:T(8,128)(2,1)S(1)} %collective-permute-done.69.n2), channel_id=1, source_target_pairs={{0,4},{4,0},{8,12},{12,8},{16,20},{20,16},{24,28},{28,24},{1,5},{5... | collective-permute-start | bytes 1572872 | tf_op jit(solution)/shard_map/ppermute | solution.py:33
  456.7 19.7 %collective-permute-start.74 = (bf16[2,128,1024]{2,1,0:T(8,128)(2,1)}, bf16[2,128,1024]{2,1,0:T(8,128)(2,1)}, u32[]{:S(2)}, u32[]{:S(2)}) collective-permute-start(bf16[2,128,1024]{2,1,0:T(8,128)(2,1)} %collective-permute-done.70.n3), channel_id=1, source_target_pairs={{0,4},{4,0},{8,12},{12,8},{16,20},{20,16},{24,28},{28,24},{1,5},{5... | collective-permute-start | bytes 1572872 | tf_op jit(solution)/shard_map/ppermute | solution.py:33
  457.3 37.2 %all-to-all-start.1 = ((f32[32,24,128]{2,1,0:T(8,128)}), f32[32,24,128]{2,1,0:T(8,128)}, u32[]{:S(2)}, u32[]{:S(2)}) async-start(f32[32,24,128]{2,1,0:T(8,128)} %pad_maximum_fusion.7), calls=%async_computation.1 | async-start | bytes 786432 | tf_op jit(solution)/shard_map/all_to_all | solution.py:1287
  474.9 18.8 %collective-permute-start.63 = (bf16[6,32,1024]{2,1,0:T(8,128)(2,1)S(1)}, bf16[6,32,1024]{2,1,0:T(8,128)(2,1)}, u32[]{:S(2)}, u32[]{:S(2)}) collective-permute-start(bf16[6,32,1024]{2,1,0:T(8,128)(2,1)S(1)} %bitcast.179), channel_id=1, source_target_pairs={{0,24},{4,28},{8,16},{12,20},{16,8},{20,12},{24,0},{28,4},{1,25},{... | collective-permute-start | bytes 1179656 | tf_op jit(solution)/shard_map/ppermute | solution.py:33
  475.2 22.5 %collective-permute-start.64 = (bf16[6,32,1024]{2,1,0:T(8,128)(2,1)S(1)}, bf16[6,32,1024]{2,1,0:T(8,128)(2,1)}, u32[]{:S(2)}, u32[]{:S(2)}) collective-permute-start(bf16[6,32,1024]{2,1,0:T(8,128)(2,1)S(1)} %bitcast.180), channel_id=1, source_target_pairs={{0,4},{4,0},{8,12},{12,8},{16,20},{20,16},{24,28},{28,24},{1,5},{5... | collective-permute-start | bytes 1179656 | tf_op jit(solution)/shard_map/ppermute | solution.py:33
  (87 other events, 1198.5 us)
Sparse Core Ops, SparseCore 0:
  227.8 80.0 all-gather.2
